TPU v7x, 256 devices: a whole 4x4x8 slice. The times are simulated.
256 devices in a mesh: section: 2 (over x_lo), tensor: 128 (over y, z, x_hi, core).
Axes of the slice: x: 4 (x_hi: 2, x_lo: 2; x = x_hi * 2 + x_lo), y: 4, z: 8, core: 2. Of those that a mesh axis runs over, the one named last changes fastest.
Arguments:
- resid_in: bfloat16 [256, 8192], P(None, 'tensor'), may hold values from -6 to 6
- contexts: bfloat16 [2, 256, 16384], P('section', None, 'tensor'), may hold values from -6 to 6
- out_proj: bfloat16 [2, 16384, 8192], P('section', 'tensor'), may hold values from -0.046875 to 0.046875
- encoder: bfloat16 [8192, 32768], P(None, ('section', 'tensor')), may hold values from -0.0625 to 0.0625
- enc_bias: bfloat16 [32768], P(('section', 'tensor')), may hold values from -3 to 3
- decoder: bfloat16 [32768, 8192], P(('section', 'tensor')), may hold values from -0.125 to 0.125
- dec_bias: bfloat16 [8192], replicated, may hold values from -3 to 3
- token_ids: int32 [256], replicated, may hold values from 0 to 128000, as said below
- owner_map: int32 [128], replicated, may hold values from 0 to 127, each once
Outputs:
- owned_error: bfloat16 [256, 8192], P('tensor', 'section')
- new_encoder: bfloat16 [8192, 32768], P(None, ('section', 'tensor'))
- new_decoder: bfloat16 [32768, 8192], P(('section', 'tensor'))
Inputs may be any that keep to these rules, and one draw needn't show every extreme that they name: `token_ids`: 128000 marks a document start and stands at the first token of every micro-batch; all other ids lie below 128000.
All inputs are finite; a program needn't handle non-finite values.
Results may differ from a plain program's by a relative error of at most 0.02005.
Values may be sent and summed in bfloat16 or wider, within the bound.
No kernel may reach another device: no remote copies, remote signals or barrier semaphores. Data moves between devices by JAX's collectives and lax.ppermute only.
A program may use at most 128 MiB of HBM per device.

v0:
```python
import jax
import jax.numpy as jnp
from jax import lax
from jax.sharding import PartitionSpec as P

BOS = 128000


STEP_RATE = 0.5


def from_behind(block, axis, distance):
    devices = range(lax.axis_size(axis))
    route = [(i - distance, i) for i in devices if i - distance in devices]
    return lax.ppermute(block, axis, route)


def from_root(value, axis, source):
    kept = jnp.where(lax.axis_index(axis) == source, value, 0).astype(value.dtype)
    return lax.psum(kept, axis)


def shards(
    resid_in, contexts, out_proj, encoder, enc_bias, decoder, dec_bias, token_ids, owner_map
):
    section_count = lax.axis_size("section")
    tokens = resid_in.shape[0]
    model_width = decoder.shape[1]
    context_part = contexts[0]
    proj_part = out_proj[0]
    own_sum = lax.psum_scatter(
        lax.dot_general(
            proj_part,
            context_part,
            (((0,), (0 + 1,)), ((), ())),
            preferred_element_type=jnp.float32,
        ),
        "tensor",
        scatter_dimension=0,
        tiled=True,
    ).T
    before = (resid_in.astype(jnp.float32) + own_sum).astype(jnp.bfloat16)
    arrived = from_behind(before, "section", 1)
    last_resid = (arrived.astype(jnp.float32) + own_sum).astype(jnp.bfloat16)
    blocks = owner_map.shape[0]
    block_rows = tokens // blocks
    inverse = jnp.zeros((blocks,), jnp.int32).at[owner_map].set(jnp.arange(blocks, dtype=jnp.int32))
    last_resid = last_resid.reshape(blocks, block_rows, -1)[inverse].reshape(tokens, -1)
    kept_ids = token_ids.reshape(blocks, block_rows)[inverse].reshape(tokens)
    kept_rows = (kept_ids != BOS).astype(jnp.float32)[:, None]
    full_rows = lax.all_gather(last_resid, "tensor", axis=1, tiled=True)
    full_rows = from_root(full_rows, "section", 1)
    values = full_rows.astype(jnp.float32)
    inverse_rms = lax.rsqrt(jnp.mean(values * values, axis=1, keepdims=True) + 1e-05)
    centred = (values * inverse_rms - dec_bias.astype(jnp.float32)).astype(jnp.bfloat16)
    before_relu = jnp.dot(centred, encoder, preferred_element_type=jnp.float32) + enc_bias.astype(
        jnp.float32
    )
    latents = jnp.maximum(before_relu, 0.0).astype(jnp.bfloat16)
    tensor_rank = lax.axis_index("tensor")
    section_rank = lax.axis_index("section")
    half_width = model_width // section_count
    row_sum = lax.psum_scatter(
        jnp.dot(latents, decoder, preferred_element_type=jnp.float32),
        "tensor",
        scatter_dimension=0,
        tiled=True,
    )
    summed = lax.psum_scatter(
        row_sum.astype(jnp.bfloat16), "section", scatter_dimension=1, tiled=True
    ).astype(jnp.float32)
    row_start = tensor_rank * block_rows
    target = lax.dynamic_slice(
        centred, (row_start, section_rank * half_width), (block_rows, half_width)
    ).astype(jnp.float32)
    mask_rows = lax.dynamic_slice_in_dim(kept_rows, row_start, block_rows, 0)
    owned_error = (mask_rows * (summed - target)).astype(jnp.bfloat16)
    error_full = lax.all_gather(owned_error, "section", axis=1, tiled=True)
    error_all = lax.all_gather(error_full, "tensor", axis=0, tiled=True)
    grad_dec = lax.dot_general(
        latents, error_all, (((0,), (0,)), ((), ())), preferred_element_type=jnp.float32
    )
    backward = lax.dot_general(
        error_all, decoder, (((1,), (1,)), ((), ())), preferred_element_type=jnp.float32
    )
    pre_grad = jnp.where(before_relu > 0.0, backward, 0.0).astype(jnp.bfloat16)
    grad_enc = lax.dot_general(
        centred, pre_grad, (((0,), (0,)), ((), ())), preferred_element_type=jnp.float32
    )
    step_size = STEP_RATE / tokens
    new_encoder = (encoder.astype(jnp.float32) - step_size * grad_enc).astype(jnp.bfloat16)
    new_decoder = (decoder.astype(jnp.float32) - step_size * grad_dec).astype(jnp.bfloat16)
    return (owned_error, new_encoder, new_decoder)


def solution(mesh):
    return jax.shard_map(
        shards,
        mesh=mesh,
        in_specs=(
            P(None, "tensor"),
            P("section", None, "tensor"),
            P("section", "tensor", None),
            P(None, ("section", "tensor")),
            P(("section", "tensor")),
            P(("section", "tensor"), None),
            P(),
            P(),
            P(),
        ),
        out_specs=(
            P("tensor", "section"),
            P(None, ("section", "tensor")),
            P(("section", "tensor"), None),
        ),
        check_vma=False,
    )
```

profile of v0, /device:TPU:1, one launch (start us, length us, event | category | flops | bytes accessed | tf_op | source)
XLA Modules:
  0.0 1881.4 jit_solution(8152221970186845736)
XLA Ops:
  7.2 1.5 copy-done
  8.8 5.3 fusion.7
  14.8 1.0 scatter_custom_fusion
  15.8 667.1 %reduce-scatter.5.cloned.1.call-done = f32[64,256]{1,0:T(8,128)} async-done(((f32[8192,256]{1,0:T(8,128)}), f32[64,256]{1,0:T(8,128)}) %reduce-scatter.5.cloned.1.call-update) | async-done | bytes 65552 | tf_op jit(solution)/shard_map/reduce_scatter | solution.py:31
  682.8 0.8 fusion.11
  683.7 2.5 collective-permute-start
  686.2 1.0 collective-permute-done
  687.2 0.8 fusion.12
  688.2 0.7 gather_fusion.1
  688.9 0.7 copy.22
  689.7 121.1 %all-gather.4.cloned.1.call-done = bf16[256,8192]{0,1:T(8,128)(2,1)} async-done(((bf16[256,64]{0,1:T(8,128)(2,1)}), bf16[256,8192]{0,1:T(8,128)(2,1)}) %all-gather.4.cloned.1.call-update) | async-done | bytes 4194320 | tf_op jit(solution)/shard_map/all_gather | solution.py:51
  810.8 6.4 copy.23
  817.2 2.2 broadcast_select_fusion
  820.3 0.6 gather_fusion
  821.0 0.6 dynamic-slice.4
  822.2 115.5 %all-reduce.4.cloned.1.call-done = bf16[256,8192]{1,0:T(8,128)(2,1)} async-done(((bf16[256,8192]{1,0:T(8,128)(2,1)}), bf16[256,8192]{1,0:T(8,128)(2,1)}) %all-reduce.4.cloned.1.call-update) | async-done | bytes 4194320 | tf_op jit(solution)/shard_map/psum | solution.py:20
  937.7 3.3 fusion.4
  941.2 1.1 fusion.6
  942.3 2.0 copy-done.1
  944.2 1.3 convolution_add_fusion
  945.8 4.5 fusion.15
  950.3 734.5 %all-reduce.5 = bf16[256,8192]{1,0:T(8,128)(2,1)} all-reduce(f32[256,8192]{1,0:T(8,128)} %fusion.15), channel_id=3, replica_groups=mesh['section'=2,'tensor'=128] {'tensor'}, use_global_device_ids=true, to_apply=%region_4.5.clone | all-reduce | flops 2097152 | bytes 12582912
  1684.8 0.9 dynamic-slice_convert_fusion
  1685.7 1.8 copy.24
  1687.9 35.2 %reduce-scatter.7.cloned.1.call-done = bf16[4096,2]{1,0:T(8,128)(2,1)} async-done(((bf16[8192,2]{1,0:T(8,128)(2,1)}), bf16[4096,2]{1,0:T(8,128)(2,1)}) %reduce-scatter.7.cloned.1.call-update) | async-done | bytes 16400
  1723.1 1.6 copy.25
  1724.7 1.0 multiply_convert_fusion
  1725.6 3.6 all_gather.10
  1729.2 122.5 %all-gather.6.cloned.1.call-done = bf16[128,2,8192]{2,1,0:T(2,128)(2,1)} async-done(((bf16[1,2,8192]{2,1,0:T(2,128)(2,1)}), bf16[128,2,8192]{2,1,0:T(2,128)(2,1)}) %all-gather.6.cloned.1.call-update) | async-done | bytes 4194320 | tf_op jit(solution)/shard_map/all_gather | solution.py:79
  1851.7 7.3 reshape.64
  1859.0 10.6 fusion.2
  1869.6 5.3 fusion.3
  (44 shorter events, 2.5 us)
Async XLA Ops:
  7.2 1.6 copy-start
  7.2 675.7 %reduce-scatter.5.cloned.1.call-start = ((), (), s32[]{:S(2)}) async-start(), calls=%async_computation.2 | async-start | bytes 8454144 | tf_op jit(solution)/shard_map/reduce_scatter | solution.py:31
  14.1 0.7 copy-start.9
  14.1 668.7 %copy-start.6 = (bf16[256,64]{0,1:T(8,128)(2,1)S(1)}, bf16[256,64]{0,1:T(8,128)(2,1)}, u32[]{:S(2)}) copy-start(bf16[256,64]{0,1:T(8,128)(2,1)} %param.9) | copy-start | bytes 98308
  14.1 796.6 %all-gather.4.cloned.1.call-start = ((), (), s32[]{:S(2)}) async-start(), calls=%async_computation.3 | async-start | bytes 4227072 | tf_op jit(solution)/shard_map/all_gather | solution.py:51
  683.7 3.5 collective-permute-start
  689.7 248.0 %all-reduce.4.cloned.1.call-start = ((), (), s32[]{:S(2)}) async-start(), calls=%async_computation.4 | async-start | bytes 8388608 | tf_op jit(solution)/shard_map/psum | solution.py:20
  819.4 0.7 copy-start.10
  819.4 0.7 copy-start.7
  819.4 0.7 copy-start.8
  819.4 1.5 copy-start.11
  819.5 903.6 %reduce-scatter.7.cloned.1.call-start = ((), (), s32[]{:S(2)}) async-start(), calls=%async_computation.6 | async-start | bytes 3145728
  937.7 3.4 copy-start.4
  941.2 3.1 copy-start.3
  942.3 2.0 copy-start.1
  944.2 1.6 copy-start.2
  1687.6 164.2 %all-gather.6.cloned.1.call-start = ((), (), s32[]{:S(2)}) async-start(), calls=%async_computation.5 | async-start | bytes 4227072 | tf_op jit(solution)/shard_map/all_gather | solution.py:79
  1725.6 133.4 %copy-start.5 = (bf16[2,4096]{1,0:T(2,128)(2,1)}, bf16[2,4096]{1,0:T(2,128)(2,1)S(1)}, u32[]{:S(2)}) copy-start(bf16[2,4096]{1,0:T(2,128)(2,1)S(1)} %multiply_convert_fusion) | copy-start | bytes 49156
Sparse Core Ops, SparseCore 0:
  14.3 668.5 reduce-scatter.4
  689.8 120.9 all-gather.3
  819.6 118.0 all-reduce.3
  1687.7 35.3 reduce-scatter.6
  1729.3 122.3 all-gather.5
where the time goes:
time: 1880 us
  waiting for transfers between devices  1060 us (56%)
  blocking collectives  738 us (39%)
  local copies, waits for them, and re-layouts  27.4 us (1%)
  matrix products  27 us (1%)
    unnamed x1, blocking collectives  734 us
    reduce_scatter x1, waiting for transfers between devices, shards(): lax.psum_scatter(lax.dot_general(proj_part, context_part, (((0,), (0 + 1,...  667 us
    all_gather x1, waiting for transfers between devices, shards(): error_all = lax.all_gather(error_full, 'tensor', axis=0, tiled=True)  123 us
    all_gather x1, waiting for transfers between devices, shards(): full_rows = lax.all_gather(last_resid, 'tensor', axis=1, tiled=True)  121 us
    psum x1, waiting for transfers between devices, from_root(): return lax.psum(kept, axis)  115 us
  transfers between devices with their start and end apart: 6, of which 6 were waited for; matrix products, arithmetic and copies ran while one was open for 0% of the time, Pallas kernels for 0%

commit v1 on v0

v1 whole, which is shorter than its diff:
```python
import jax
import jax.numpy as jnp
from jax import lax
from jax.sharding import Mesh
from jax.sharding import PartitionSpec as P

BOS = 128000


STEP_RATE = 0.5

AXES = ("xl", "y", "z", "xh", "c")
PLANE = ("y", "xh", "xl")
TENSOR = ("y", "z", "xh", "c")


def exchange(value, swap):
    sizes = [lax.axis_size(a) for a in AXES]
    route = []
    for source in range(sizes[0] * sizes[1] * sizes[2] * sizes[3] * sizes[4]):
        rest, place = source, {}
        for axis, size in zip(AXES[::-1], sizes[::-1]):
            place[axis] = rest % size
            rest //= size
        place = swap(place)
        target = 0
        for axis, size in zip(AXES, sizes):
            target = target * size + place[axis]
        route.append((source, target))
    return lax.ppermute(value, AXES, route)


def other_core(value):
    return exchange(value, lambda p: {**p, "c": 1 - p["c"]})


def core_and_section(value):
    return exchange(value, lambda p: {**p, "c": p["xl"], "xl": p["c"]})


def reduce_rows(partial, plane, depth):
    width = partial.shape[1]
    pieces = lax.all_to_all(partial.reshape(plane, -1, width), PLANE, 0, 0, tiled=True)
    chunk = jnp.sum(pieces.astype(jnp.float32), axis=0).astype(jnp.bfloat16)
    pieces = lax.all_to_all(chunk.reshape(depth, -1, width), "z", 0, 0, tiled=True)
    return jnp.sum(pieces.astype(jnp.float32), axis=0)


def gather_rows(rows, plane, depth):
    width = rows.shape[1]
    rows = lax.all_to_all(
        jnp.broadcast_to(rows[None], (depth,) + rows.shape), "z", 0, 0, tiled=True
    ).reshape(-1, width)
    return lax.all_to_all(
        jnp.broadcast_to(rows[None], (plane,) + rows.shape), PLANE, 0, 0, tiled=True
    ).reshape(-1, width)


def matmul(a, b, dims=((1,), (0,))):
    return lax.dot_general(a, b, (dims, ((), ())), preferred_element_type=jnp.float32)


def shards(
    resid_in, contexts, out_proj, encoder, enc_bias, decoder, dec_bias, token_ids, owner_map
):
    tokens = resid_in.shape[0]
    features = decoder.shape[1]
    half = features // 2
    blocks = owner_map.shape[0]
    block_rows = tokens // blocks
    depth = lax.axis_size("z")
    plane = lax.axis_size("y") * lax.axis_size("xh") * lax.axis_size("xl")
    y, z, xh, xl, core = (lax.axis_index(a) for a in ("y", "z", "xh", "xl", "c"))
    size_xh, size_xl = lax.axis_size("xh"), lax.axis_size("xl")

    row = lax.broadcasted_iota(jnp.int32, (tokens, tokens), 0)
    old = lax.broadcasted_iota(jnp.int32, (tokens, tokens), 1)
    slot = row // block_rows
    at_z, at_plane = slot % depth, slot // depth
    at_y, at_x = at_plane // (size_xh * size_xl), at_plane % (size_xh * size_xl)
    position = (at_y * depth + at_z) * (size_xh * size_xl) + at_x
    owner_of_row = jnp.repeat(owner_map, block_rows)
    order = (
        (owner_of_row[None, :] == position) & (old % block_rows == row % block_rows)
    ).astype(jnp.bfloat16)
    my_position = ((y * depth + z) * size_xh + xh) * size_xl + xl
    kept = (token_ids.reshape(blocks, block_rows) != BOS).astype(jnp.float32)
    mask_rows = jnp.sum(
        jnp.where((owner_map == my_position)[:, None], kept, 0.0), axis=0
    )[:, None]

    def mine(weight, axis):
        return lax.dynamic_slice_in_dim(weight, core * half, half, axis)

    def theirs(weight, axis):
        return lax.dynamic_slice_in_dim(weight, (1 - core) * half, half, axis)

    proj = out_proj[0]
    proj_other = other_core(theirs(proj, 1))
    dec_other = other_core(theirs(decoder, 1))
    context = matmul(order, contexts[0]).astype(jnp.bfloat16)
    resid = matmul(order, resid_in).astype(jnp.bfloat16)
    context_other = other_core(context)
    resid_other = other_core(resid)

    partial = (matmul(context, mine(proj, 1)) + matmul(context_other, proj_other)).astype(
        jnp.bfloat16
    )
    columns = jnp.where(
        core == 0,
        jnp.concatenate([resid, resid_other], axis=1),
        jnp.concatenate([resid_other, resid], axis=1),
    ).astype(jnp.float32)
    start = ((y * depth + z) * size_xh + xh) * columns.shape[1]
    owns = (start // half == core) & (xl == 0)
    start = start % half
    here = lax.dynamic_slice_in_dim(partial, start, columns.shape[1], 1).astype(jnp.float32)
    partial = lax.dynamic_update_slice_in_dim(
        partial, (here + jnp.where(owns, columns, 0.0)).astype(jnp.bfloat16), start, 1
    )
    values = (
        reduce_rows(partial, plane, depth).astype(jnp.bfloat16).astype(jnp.float32)
    )
    squares = jnp.sum(values * values, axis=1, keepdims=True)
    squares = squares + other_core(squares)
    inverse_rms = lax.rsqrt(squares / features + 1e-05)
    my_centred = (values * inverse_rms - mine(dec_bias, 0).astype(jnp.float32)).astype(
        jnp.bfloat16
    )
    centred = gather_rows(my_centred, plane, depth)
    centred_other = other_core(centred)
    low, high = (
        jnp.where(core == 0, centred, centred_other),
        jnp.where(core == 0, centred_other, centred),
    )
    before_relu = (
        matmul(low, encoder[:half])
        + matmul(high, encoder[half:])
        + enc_bias.astype(jnp.float32)
    )
    latents = jnp.maximum(before_relu, 0.0).astype(jnp.bfloat16)
    latents_other = other_core(latents)
    rebuilt = reduce_rows(
        (matmul(latents, mine(decoder, 1)) + matmul(latents_other, dec_other)).astype(
            jnp.bfloat16
        ),
        plane,
        depth,
    )
    my_error = (mask_rows * (rebuilt - my_centred.astype(jnp.float32))).astype(jnp.bfloat16)
    owned_error = core_and_section(my_error)
    error = gather_rows(my_error, plane, depth)
    error_other = other_core(error)
    error_low, error_high = (
        jnp.where(core == 0, error, error_other),
        jnp.where(core == 0, error_other, error),
    )
    backward = matmul(error_low, decoder[:, :half], ((1,), (1,))) + matmul(
        error_high, decoder[:, half:], ((1,), (1,))
    )
    pre_grad = jnp.where(before_relu > 0.0, backward, 0.0).astype(jnp.bfloat16)
    step_size = STEP_RATE / tokens

    def stepped(weight, grad):
        return (weight.astype(jnp.float32) - step_size * grad).astype(jnp.bfloat16)

    over_rows = ((0,), (0,))
    new_encoder = jnp.concatenate(
        [
            stepped(encoder[:half], matmul(low, pre_grad, over_rows)),
            stepped(encoder[half:], matmul(high, pre_grad, over_rows)),
        ],
        axis=0,
    )
    new_decoder = jnp.concatenate(
        [
            stepped(decoder[:, :half], matmul(latents, error_low, over_rows)),
            stepped(decoder[:, half:], matmul(latents, error_high, over_rows)),
        ],
        axis=1,
    )
    return (owned_error, new_encoder, new_decoder)


def solution(mesh):
    cut = Mesh(mesh.devices.reshape(2, 4, 8, 2, 2), AXES)
    return jax.shard_map(
        shards,
        mesh=cut,
        in_specs=(
            P(None, TENSOR),
            P("xl", None, TENSOR),
            P("xl", TENSOR, None),
            P(None, AXES),
            P(AXES),
            P(AXES, None),
            P(),
            P(),
            P(),
        ),
        out_specs=(
            P(TENSOR, "xl"),
            P(None, AXES),
            P(AXES, None),
        ),
        check_vma=False,
    )
```

time: 1880 us -> 235 us (0.12)
  waiting for transfers between devices: 1060 us -> 56.2 us
  blocking collectives: 738 us -> 112 us
  starting transfers between devices: 2.72 us -> 33.1 us
  local copies, waits for them, and re-layouts: 27.4 us -> 8.5 us
    unnamed x1 -> x0, blocking collectives: 734 us -> none
    reduce_scatter x1 -> x0, waiting for transfers between devices: 667 us -> none  [shards(): lax.psum_scatter(lax.dot_general(proj_part, context_part, (((0,), (0 + 1,...]
    all_gather x2 -> x0, waiting for transfers between devices: 244 us -> none  [the longest x1 123 us: shards(): error_all = lax.all_gather(error_full, 'tensor', axis=0, tiled=True)]
    psum x1 -> x0, waiting for transfers between devices: 115 us -> none  [from_root(): return lax.psum(kept, axis)]
    all_to_all x0 -> x5, blocking collectives: none -> 112 us  [the longest x2 57.7 us: gather_rows(): lax.all_to_all(jnp.broadcast_to(rows[None], (plane,) + rows.shape), PLANE...]
    all_to_all x0 -> x3, waiting for transfers between devices: none -> 48.6 us  [the longest x1 33 us: reduce_rows(): lax.all_to_all(partial.reshape(plane, -1, width), PLANE, 0, 0, tiled=True)]
    unnamed x6 -> x0, waiting for transfers between devices: 35.3 us -> none
  transfers between devices with their start and end apart: 6 -> 12, of which waited for: 6 -> 7; matrix products, arithmetic and copies ran while one was open for 0% -> 4% of each run, Pallas kernels for 0% -> 0%
where the time goes in v1:
time: 235 us; the launch traced here: 234 us
  blocking collectives  112 us (48%)
  waiting for transfers between devices  56.2 us (24%)
  starting transfers between devices  33.1 us (14%)
  matrix products  15.8 us (7%)
  local copies, waits for them, and re-layouts  8.5 us (4%)
  other arithmetic  7.65 us (3%)
    all_to_all x2, blocking collectives, gather_rows(): lax.all_to_all(jnp.broadcast_to(rows[None], (plane,) + rows.shape), PLANE...  57.7 us
    all_to_all x1, waiting for transfers between devices, reduce_rows(): lax.all_to_all(partial.reshape(plane, -1, width), PLANE, 0, 0, tiled=True)  33 us
    all_to_all x1, blocking collectives, reduce_rows(): lax.all_to_all(partial.reshape(plane, -1, width), PLANE, 0, 0, tiled=True)  33 us
    all_to_all x2, blocking collectives, gather_rows(): lax.all_to_all(jnp.broadcast_to(rows[None], (depth,) + rows.shape), 'z',...  21.3 us
    ppermute x9, starting transfers between devices, exchange(): return lax.ppermute(value, AXES, route)  16.8 us
    dot_general x14, matrix products, matmul(): lax.dot_general(a, b, (dims, ((), ())), preferred_element_type=jnp.float32)  15.8 us
    all_to_all x2, waiting for transfers between devices, reduce_rows(): lax.all_to_all(chunk.reshape(depth, -1, width), 'z', 0, 0, tiled=True)  15.7 us
    all_to_all x2, starting transfers between devices, reduce_rows(): lax.all_to_all(chunk.reshape(depth, -1, width), 'z', 0, 0, tiled=True)  11.7 us
  transfers between devices with their start and end apart: 12, of which 7 were waited for; matrix products, arithmetic and copies ran while one was open for 4% of the time, Pallas kernels for 0%

profile of v1, /device:TPU:1, one launch (start us, length us, event | category | flops | bytes accessed | tf_op | source)
XLA Modules:
  0.0 234.1 jit_solution(16590066357938584992)
XLA Ops:
  0.7 1.6 copy-done
  2.2 1.1 dynamic-slice_bitcast_fusion
  3.3 3.2 %collective-permute-start.1 = (bf16[128,4096]{1,0:T(8,128)(2,1)}, bf16[128,4096]{1,0:T(8,128)(2,1)S(1)}, u32[]{:S(2)}, u32[]{:S(2)}) collective-permute-start(bf16[128,4096]{1,0:T(8,128)(2,1)} %dynamic-slice_bitcast_fusion), channel_id=1, source_target_pairs={{0,1},{1,0},{2,3},{3,2},{4,5},{5,4},{6,7},{7,6},{8,9},{9,8},{10,11... | collective-permute-start | bytes 3145736 | tf_op jit(solution)/shard_map/ppermute | solution.py:30
  8.5 2.7 %fusion.11 = f32[256,4096]{1,0:T(8,128)} fusion(bf16[256,128]{1,0:T(8,128)(2,1)S(1)} %convolution_convert_fusion.1, bf16[1,128,8192]{2,1,0:T(8,128)(2,1)S(1)} %copy-done, s32[]{:T(128)S(6)} %select_n.106), kind=kOutput, calls=%fused_computation.27 | convolution fusion | flops 268435456 | bytes 5308420 | tf_op jit(solution)/shard_map/dot_general | solution.py:60
  11.2 2.9 %fusion = bf16[256,4096]{1,0:T(8,128)(2,1)S(1)} fusion(f32[256,4096]{1,0:T(8,128)} %fusion.11, bf16[256,128]{1,0:T(8,128)(2,1)S(1)} %collective-permute-done, bf16[128,4096]{1,0:T(8,128)(2,1)S(1)} %collective-permute-done.1), kind=kOutput, calls=%fused_computation.2 | convolution fusion | flops 270532608 | bytes 7405568 | tf_op jit(solution)/shard_map/dot_general | solution.py:60
  14.2 33.0 %all_to_all.40 = bf16[16,16,4096]{2,1,0:T(8,128)(2,1)} all-to-all(bf16[16,16,4096]{2,1,0:T(8,128)(2,1)S(1)} %bitcast.32), channel_id=1, replica_groups=mesh['xl'=2,'y'=4,'z'=8,'xh'=2,'c'=2] {'y','xh','xl'}, dimensions={0} | all-to-all | bytes 4194304 | tf_op jit(solution)/shard_map/all_to_all | solution.py:43
  47.2 1.9 reduce_sum.64
  49.8 8.2 %all-to-all-start.1 = ((bf16[8,2,4096]{2,1,0:T(2,128)(2,1)}), bf16[8,2,4096]{2,1,0:T(2,128)(2,1)S(1)}, u32[]{:S(2)}, u32[]{:S(2)}) async-start(bf16[8,2,4096]{2,1,0:T(2,128)(2,1)} %reshape.115), calls=%async_computation.1 | async-start | bytes 262144 | tf_op jit(solution)/shard_map/all_to_all | solution.py:45
  58.1 7.9 %all-to-all-done.1 = bf16[8,2,4096]{2,1,0:T(2,128)(2,1)S(1)} async-done(((bf16[8,2,4096]{2,1,0:T(2,128)(2,1)}), bf16[8,2,4096]{2,1,0:T(2,128)(2,1)S(1)}, u32[]{:S(2)}, u32[]{:S(2)}) %all-to-all-start.1) | async-done | bytes 131104 | tf_op jit(solution)/shard_map/all_to_all | solution.py:45
  66.2 2.9 %collective-permute-start.3 = (f32[2,1]{0,1:T(1,128)S(1)}, f32[2,1]{0,1:T(1,128)S(1)}, u32[]{:S(2)}, u32[]{:S(2)}) collective-permute-start(f32[2,1]{0,1:T(1,128)S(1)} %bitcast.39), channel_id=1, source_target_pairs={{0,1},{1,0},{2,3},{3,2},{4,5},{5,4},{6,7},{7,6},{8,9},{9,8},{10,11... | collective-permute-start | bytes 32 | tf_op jit(solution)/shard_map/ppermute | solution.py:30
  69.2 0.8 collective-permute-done.3
  70.2 10.9 %all_to_all.41 = bf16[8,2,4096]{2,1,0:T(2,128)(2,1)S(1)} all-to-all(bf16[8,2,4096]{2,1,0:T(2,128)(2,1)S(1)} %broadcast_in_dim.59), channel_id=1, replica_groups=mesh['xl'=2,'y'=4,'z'=8,'xh'=2,'c'=2] {'z'}, dimensions={0} | all-to-all | bytes 262144 | tf_op jit(solution)/shard_map/all_to_all | solution.py:51
  81.4 29.8 %all_to_all.42 = bf16[16,16,4096]{2,1,0:T(8,128)(2,1)S(1)} all-to-all(bf16[16,16,4096]{2,1,0:T(8,128)(2,1)S(1)} %broadcast_in_dim.61), channel_id=1, replica_groups=mesh['xl'=2,'y'=4,'z'=8,'xh'=2,'c'=2] {'y','xh','xl'}, dimensions={0} | all-to-all | bytes 4194304 | tf_op jit(solution)/shard_map/all_to_all | solution.py:54
  111.2 2.5 %collective-permute-start.4 = (bf16[256,4096]{1,0:T(8,128)(2,1)S(1)}, bf16[256,4096]{1,0:T(8,128)(2,1)S(1)}, u32[]{:S(2)}, u32[]{:S(2)}) collective-permute-start(bf16[256,4096]{1,0:T(8,128)(2,1)S(1)} %bitcast.34), channel_id=1, source_target_pairs={{0,1},{1,0},{2,3},{3,2},{4,5},{5,4},{6,7},{7,6},{8,9},{9,8},{10,11... | collective-permute-start | bytes 6291464 | tf_op jit(solution)/shard_map/ppermute | solution.py:30
  113.9 3.6 %collective-permute-done.4 = bf16[256,4096]{1,0:T(8,128)(2,1)S(1)} collective-permute-done((bf16[256,4096]{1,0:T(8,128)(2,1)S(1)}, bf16[256,4096]{1,0:T(8,128)(2,1)S(1)}, u32[]{:S(2)}, u32[]{:S(2)}) %collective-permute-start.4) | collective-permute-done | bytes 2097184 | tf_op jit(solution)/shard_map/ppermute | solution.py:30
  117.4 0.8 fusion.19
  118.8 0.8 maximum_convert_fusion
  120.9 2.0 fusion.1
  123.0 4.6 %all-to-all-start.4 = ((bf16[16,16,4096]{2,1,0:T(8,128)(2,1)}), bf16[16,16,4096]{2,1,0:T(8,128)(2,1)}, u32[]{:S(2)}, u32[]{:S(2)}) async-start(bf16[16,16,4096]{2,1,0:T(8,128)(2,1)} %bitcast.33), calls=%async_computation.4 | async-start | bytes 4194304 | tf_op jit(solution)/shard_map/all_to_all | solution.py:43
  127.7 33.0 %all-to-all-done.4 = bf16[16,16,4096]{2,1,0:T(8,128)(2,1)} async-done(((bf16[16,16,4096]{2,1,0:T(8,128)(2,1)}), bf16[16,16,4096]{2,1,0:T(8,128)(2,1)}, u32[]{:S(2)}, u32[]{:S(2)}) %all-to-all-start.4) | async-done | bytes 2097184 | tf_op jit(solution)/shard_map/all_to_all | solution.py:43
  160.7 1.9 reduce_sum.67
  163.4 3.6 %all-to-all-start.5 = ((bf16[8,2,4096]{2,1,0:T(2,128)(2,1)}), bf16[8,2,4096]{2,1,0:T(2,128)(2,1)S(1)}, u32[]{:S(2)}, u32[]{:S(2)}) async-start(bf16[8,2,4096]{2,1,0:T(2,128)(2,1)} %reshape.118), calls=%async_computation.5 | async-start | bytes 262144 | tf_op jit(solution)/shard_map/all_to_all | solution.py:45
  167.0 7.7 %all-to-all-done.5 = bf16[8,2,4096]{2,1,0:T(2,128)(2,1)S(1)} async-done(((bf16[8,2,4096]{2,1,0:T(2,128)(2,1)}), bf16[8,2,4096]{2,1,0:T(2,128)(2,1)S(1)}, u32[]{:S(2)}, u32[]{:S(2)}) %all-to-all-start.5) | async-done | bytes 131104 | tf_op jit(solution)/shard_map/all_to_all | solution.py:45
  175.1 10.4 %all_to_all.43 = bf16[8,2,4096]{2,1,0:T(2,128)(2,1)S(1)} all-to-all(bf16[8,2,4096]{2,1,0:T(2,128)(2,1)S(1)} %broadcast_in_dim.62), channel_id=1, replica_groups=mesh['xl'=2,'y'=4,'z'=8,'xh'=2,'c'=2] {'z'}, dimensions={0} | all-to-all | bytes 262144 | tf_op jit(solution)/shard_map/all_to_all | solution.py:51
  185.8 27.9 %all_to_all.44 = bf16[16,16,4096]{2,1,0:T(8,128)(2,1)S(1)} all-to-all(bf16[16,16,4096]{2,1,0:T(8,128)(2,1)S(1)} %broadcast_in_dim.64), channel_id=1, replica_groups=mesh['xl'=2,'y'=4,'z'=8,'xh'=2,'c'=2] {'y','xh','xl'}, dimensions={0} | all-to-all | bytes 4194304 | tf_op jit(solution)/shard_map/all_to_all | solution.py:54
  213.7 4.8 %collective-permute-start.8 = (bf16[256,4096]{1,0:T(8,128)(2,1)S(1)}, bf16[256,4096]{1,0:T(8,128)(2,1)S(1)}, u32[]{:S(2)}, u32[]{:S(2)}) collective-permute-start(bf16[256,4096]{1,0:T(8,128)(2,1)S(1)} %bitcast.27), channel_id=1, source_target_pairs={{0,1},{1,0},{2,3},{3,2},{4,5},{5,4},{6,7},{7,6},{8,9},{9,8},{10,11... | collective-permute-start | bytes 6291464 | tf_op jit(solution)/shard_map/ppermute | solution.py:30
  218.5 2.1 collective-permute-start.7
  220.7 2.9 %collective-permute-done.7 = bf16[2,4096]{1,0:T(2,128)(2,1)S(1)} collective-permute-done((bf16[2,4096]{1,0:T(2,128)(2,1)S(1)}, bf16[2,4096]{1,0:T(2,128)(2,1)S(1)}, u32[]{:S(2)}, u32[]{:S(2)}) %collective-permute-start.7) | collective-permute-done | bytes 16416 | tf_op jit(solution)/shard_map/ppermute | solution.py:30
  227.2 1.0 fusion.7
  228.2 1.0 fusion.6
  229.2 1.5 pad_maximum_fusion
  232.0 1.5 pad_maximum_fusion.1
  (74 shorter events, 12.8 us)
Async XLA Ops:
  0.6 1.6 copy-start
  0.6 5.9 %copy-start.7 = (s32[128]{0:T(128)S(1)}, s32[128]{0:T(128)}, u32[]{:S(2)}) copy-start(s32[128]{0:T(128)} %param.17) | copy-start | bytes 1540
  0.7 6.1 %copy-start.12 = (bf16[1,256,128]{2,1,0:T(8,128)(2,1)S(1)}, bf16[1,256,128]{2,1,0:T(8,128)(2,1)}, u32[]{:S(2)}) copy-start(bf16[1,256,128]{2,1,0:T(8,128)(2,1)} %param.10) | copy-start | bytes 196612
  3.3 4.1 %copy-start.13 = (bf16[256,64]{0,1:T(8,128)(2,1)S(1)}, bf16[256,64]{0,1:T(8,128)(2,1)}, u32[]{:S(2)}) copy-start(bf16[256,64]{0,1:T(8,128)(2,1)} %param.9) | copy-start | bytes 98308
  3.3 7.9 %collective-permute-start.1 = (bf16[128,4096]{1,0:T(8,128)(2,1)}, bf16[128,4096]{1,0:T(8,128)(2,1)S(1)}, u32[]{:S(2)}, u32[]{:S(2)}) collective-permute-start(bf16[128,4096]{1,0:T(8,128)(2,1)} %dynamic-slice_bitcast_fusion), channel_id=1, source_target_pairs={{0,1},{1,0},{2,3},{3,2},{4,5},{5,4},{6,7},{7,6},{8,9},{9,8},{10,11... | collective-permute-start | bytes 3145736 | tf_op jit(solution)/shard_map/ppermute | solution.py:30
  7.3 3.8 %collective-permute-start = (bf16[256,128]{1,0:T(8,128)(2,1)S(1)}, bf16[256,128]{1,0:T(8,128)(2,1)S(1)}, u32[]{:S(2)}, u32[]{:S(2)}) collective-permute-start(bf16[256,128]{1,0:T(8,128)(2,1)S(1)} %convolution_convert_fusion.1), channel_id=1, source_target_pairs={{0,1},{1,0},{2,3},{3,2},{4,5},{5,4},{6,7},{7,6},{8,9},{9,8},{10,11... | collective-permute-start | bytes 196616 | tf_op jit(solution)/shard_map/ppermute | solution.py:30
  7.9 6.1 %collective-permute-start.2 = (bf16[256,64]{1,0:T(8,128)(2,1)S(1)}, bf16[256,64]{1,0:T(8,128)(2,1)S(1)}, u32[]{:S(2)}, u32[]{:S(2)}) collective-permute-start(bf16[256,64]{1,0:T(8,128)(2,1)S(1)} %convolution_convert_fusion), channel_id=1, source_target_pairs={{0,1},{1,0},{2,3},{3,2},{4,5},{5,4},{6,7},{7,6},{8,9},{9,8},{10,11... | collective-permute-start | bytes 98312 | tf_op jit(solution)/shard_map/ppermute | solution.py:30
  47.2 10.9 %copy-start.5 = (bf16[8192]{0:T(1024)(128)(2,1)S(1)}, bf16[8192]{0:T(1024)(128)(2,1)}, u32[]{:S(2)}) copy-start(bf16[8192]{0:T(1024)(128)(2,1)} %param.15) | copy-start | bytes 49156
  49.8 16.1 %all-to-all-start.1 = ((bf16[8,2,4096]{2,1,0:T(2,128)(2,1)}), bf16[8,2,4096]{2,1,0:T(2,128)(2,1)S(1)}, u32[]{:S(2)}, u32[]{:S(2)}) async-start(bf16[8,2,4096]{2,1,0:T(2,128)(2,1)} %reshape.115), calls=%async_computation.1 | async-start | bytes 262144 | tf_op jit(solution)/shard_map/all_to_all | solution.py:45
  66.2 3.7 %collective-permute-start.3 = (f32[2,1]{0,1:T(1,128)S(1)}, f32[2,1]{0,1:T(1,128)S(1)}, u32[]{:S(2)}, u32[]{:S(2)}) collective-permute-start(f32[2,1]{0,1:T(1,128)S(1)} %bitcast.39), channel_id=1, source_target_pairs={{0,1},{1,0},{2,3},{3,2},{4,5},{5,4},{6,7},{7,6},{8,9},{9,8},{10,11... | collective-permute-start | bytes 32 | tf_op jit(solution)/shard_map/ppermute | solution.py:30
  81.3 32.3 %copy-start.1 = (bf16[128,8192]{1,0:T(8,128)(2,1)S(1)}, bf16[128,8192]{1,0:T(8,128)(2,1)}, u32[]{:S(2)}) copy-start(bf16[128,8192]{1,0:T(8,128)(2,1)} %param.14) | copy-start | bytes 6291460
  111.2 7.1 %copy-start.3 = (bf16[16,16,4096]{2,1,0:T(8,128)(2,1)}, bf16[16,16,4096]{2,1,0:T(8,128)(2,1)S(1)}, u32[]{:S(2)}) copy-start(bf16[16,16,4096]{2,1,0:T(8,128)(2,1)S(1)} %all_to_all.42) | copy-start | bytes 6291460
  111.2 2.7 %copy-start.14 = (bf16[128]{0:T(256)(128)(2,1)S(1)}, bf16[128]{0:T(256)(128)(2,1)}, u32[]{:S(2)}) copy-start(bf16[128]{0:T(256)(128)(2,1)} %param.13) | copy-start | bytes 772
  111.2 6.3 %copy-start.8 = (bf16[8192,128]{1,0:T(8,128)(2,1)S(1)}, bf16[8192,128]{1,0:T(8,128)(2,1)}, u32[]{:S(2)}) copy-start(bf16[8192,128]{1,0:T(8,128)(2,1)} %param.12) | copy-start | bytes 6291460
  111.2 6.3 %collective-permute-start.4 = (bf16[256,4096]{1,0:T(8,128)(2,1)S(1)}, bf16[256,4096]{1,0:T(8,128)(2,1)S(1)}, u32[]{:S(2)}, u32[]{:S(2)}) collective-permute-start(bf16[256,4096]{1,0:T(8,128)(2,1)S(1)} %bitcast.34), channel_id=1, source_target_pairs={{0,1},{1,0},{2,3},{3,2},{4,5},{5,4},{6,7},{7,6},{8,9},{9,8},{10,11... | collective-permute-start | bytes 6291464 | tf_op jit(solution)/shard_map/ppermute | solution.py:30
  113.7 7.0 %collective-permute-start.6 = (bf16[128,4096]{1,0:T(8,128)(2,1)S(1)}, bf16[128,4096]{1,0:T(8,128)(2,1)S(1)}, u32[]{:S(2)}, u32[]{:S(2)}) collective-permute-start(bf16[128,4096]{1,0:T(8,128)(2,1)S(1)} %constant_dynamic-slice_fusion), channel_id=1, source_target_pairs={{0,1},{1,0},{2,3},{3,2},{4,5},{5,4},{6,7},{7,6},{8,9},{9,8},{10,11... | collective-permute-start | bytes 3145736 | tf_op jit(solution)/shard_map/ppermute | solution.py:30
  117.4 1.3 copy-start.10
  119.6 1.4 collective-permute-start.5
  123.0 4.6 %copy-start.6 = (s32[256]{0:T(256)S(1)}, s32[256]{0:T(256)}, u32[]{:S(2)}) copy-start(s32[256]{0:T(256)} %param.16) | copy-start | bytes 3076
  123.0 37.7 %all-to-all-start.4 = ((bf16[16,16,4096]{2,1,0:T(8,128)(2,1)}), bf16[16,16,4096]{2,1,0:T(8,128)(2,1)}, u32[]{:S(2)}, u32[]{:S(2)}) async-start(bf16[16,16,4096]{2,1,0:T(8,128)(2,1)} %bitcast.33), calls=%async_computation.4 | async-start | bytes 4194304 | tf_op jit(solution)/shard_map/all_to_all | solution.py:43
  163.4 11.4 %all-to-all-start.5 = ((bf16[8,2,4096]{2,1,0:T(2,128)(2,1)}), bf16[8,2,4096]{2,1,0:T(2,128)(2,1)S(1)}, u32[]{:S(2)}, u32[]{:S(2)}) async-start(bf16[8,2,4096]{2,1,0:T(2,128)(2,1)} %reshape.118), calls=%async_computation.5 | async-start | bytes 262144 | tf_op jit(solution)/shard_map/all_to_all | solution.py:45
  185.8 37.8 %copy-start.2 = (bf16[128,8192]{1,0:T(8,128)(2,1)S(1)}, bf16[128,8192]{1,0:T(8,128)(2,1)}, u32[]{:S(2)}) copy-start(bf16[128,8192]{1,0:T(8,128)(2,1)} %param.14) | copy-start | bytes 6291460
  213.7 9.8 %collective-permute-start.8 = (bf16[256,4096]{1,0:T(8,128)(2,1)S(1)}, bf16[256,4096]{1,0:T(8,128)(2,1)S(1)}, u32[]{:S(2)}, u32[]{:S(2)}) collective-permute-start(bf16[256,4096]{1,0:T(8,128)(2,1)S(1)} %bitcast.27), channel_id=1, source_target_pairs={{0,1},{1,0},{2,3},{3,2},{4,5},{5,4},{6,7},{7,6},{8,9},{9,8},{10,11... | collective-permute-start | bytes 6291464 | tf_op jit(solution)/shard_map/ppermute | solution.py:30
  218.5 5.0 %collective-permute-start.7 = (bf16[2,4096]{1,0:T(2,128)(2,1)S(1)}, bf16[2,4096]{1,0:T(2,128)(2,1)S(1)}, u32[]{:S(2)}, u32[]{:S(2)}) collective-permute-start(bf16[2,4096]{1,0:T(2,128)(2,1)S(1)} %multiply_convert_fusion), channel_id=1, source_target_pairs={{0,0},{1,128},{2,2},{3,130},{4,4},{5,132},{6,6},{7,134},{8,8},{9,1... | collective-permute-start | bytes 49160 | tf_op jit(solution)/shard_map/ppermute | solution.py:30
  224.3 1.6 copy-start.4
  224.3 2.2 copy-start.9
  224.3 2.8 %copy-start.11 = (bf16[256,4096]{1,0:T(8,128)(2,1)S(1)}, bf16[256,4096]{1,0:T(8,128)(2,1)}, u32[]{:S(2)}) copy-start(bf16[256,4096]{1,0:T(8,128)(2,1)} %copy-done.10) | copy-start | bytes 6291460

commit v2 on v1

v2 whole, which is shorter than its diff:
```python
import jax
import jax.numpy as jnp
from jax import lax
from jax.sharding import Mesh
from jax.sharding import PartitionSpec as P

BOS = 128000


STEP_RATE = 0.5

AXES = ("xl", "y", "zh", "zl", "xh", "c")
SIZES = (2, 4, 4, 2, 2, 2)
NEAR = ("y", "xh", "xl", "zl")
FAR = "zh"
TENSOR = ("y", "zh", "zl", "xh", "c")


def exchange(value, swap):
    route = []
    for source in range(256):
        rest, place = source, {}
        for axis, size in zip(AXES[::-1], SIZES[::-1]):
            place[axis] = rest % size
            rest //= size
        place = swap(place)
        target = 0
        for axis, size in zip(AXES, SIZES):
            target = target * size + place[axis]
        route.append((source, target))
    return lax.ppermute(value, AXES, route)


def other_core(value):
    return exchange(value, lambda p: {**p, "c": 1 - p["c"]})


def core_and_section(value):
    return exchange(value, lambda p: {**p, "c": p["xl"], "xl": p["c"]})


def matmul(a, b, dims=((1,), (0,))):
    return lax.dot_general(a, b, (dims, ((), ())), preferred_element_type=jnp.float32)


def spread(value, axes, count):
    return lax.all_to_all(
        jnp.broadcast_to(value[None], (count,) + value.shape), axes, 0, 0, tiled=True
    )


def sum_pieces(partial, near, far):
    tokens, width = partial.shape
    depth = tokens // near
    pieces = lax.all_to_all(partial.reshape(near, depth, width), NEAR, 0, 0, tiled=True)
    to = lax.broadcasted_iota(jnp.int32, (depth, tokens), 0)
    of = lax.broadcasted_iota(jnp.int32, (depth, tokens), 1)
    adds = (of % depth == to).astype(jnp.bfloat16)
    chunk = matmul(adds, pieces.reshape(tokens, width)).astype(jnp.bfloat16)
    return jnp.sum(spread(chunk, FAR, far).astype(jnp.float32), axis=0)


def shards(
    resid_in, contexts, out_proj, encoder, enc_bias, decoder, dec_bias, token_ids, owner_map
):
    tokens = resid_in.shape[0]
    features = decoder.shape[1]
    own = decoder.shape[0]
    half = features // 2
    blocks = owner_map.shape[0]
    block_rows = tokens // blocks
    far = lax.axis_size(FAR)
    near = blocks // far
    depth = tokens // near
    y, zh, zl, xh, xl, core = (
        lax.axis_index(a) for a in ("y", "zh", "zl", "xh", "xl", "c")
    )

    row = lax.broadcasted_iota(jnp.int32, (tokens, tokens), 0)
    old = lax.broadcasted_iota(jnp.int32, (tokens, tokens), 1)
    slot = row // block_rows
    position = (
        (slot // 32) * 32 + (slot % 4) * 8 + (slot // 4 % 2) * 4 + (slot // 8 % 4)
    )
    owner_of_row = jnp.repeat(owner_map, block_rows)
    order = (
        (owner_of_row[None, :] == position) & (old % block_rows == row % block_rows)
    ).astype(jnp.bfloat16)
    my_slot = ((y * 2 + xh) * 2 + xl) * 2 + zl
    kept = (token_ids != BOS).astype(jnp.bfloat16)
    mask_rows = lax.dynamic_slice_in_dim(
        matmul(order, kept[:, None]), my_slot * depth, depth, 0
    )

    def mine(weight, axis):
        return lax.dynamic_slice_in_dim(weight, core * half, half, axis)

    def theirs(weight, axis):
        return lax.dynamic_slice_in_dim(weight, (1 - core) * half, half, axis)

    proj = out_proj[0]
    proj_both = jnp.concatenate([mine(proj, 1), other_core(theirs(proj, 1))], axis=0)
    context = matmul(order, contexts[0]).astype(jnp.bfloat16)
    resid = matmul(order, resid_in).astype(jnp.bfloat16)
    context_both = jnp.concatenate([context, other_core(context)], axis=1)
    resid_other = other_core(resid)
    partial = matmul(context_both, proj_both).astype(jnp.bfloat16)
    columns = jnp.where(
        core == 0,
        jnp.concatenate([resid, resid_other], axis=1),
        jnp.concatenate([resid_other, resid], axis=1),
    ).astype(jnp.float32)
    start = (((y * 4 + zh) * 2 + zl) * 2 + xh) * columns.shape[1]
    owns = (start // half == core) & (xl == 0)
    start = start % half
    here = lax.dynamic_slice_in_dim(partial, start, columns.shape[1], 1).astype(jnp.float32)
    partial = lax.dynamic_update_slice_in_dim(
        partial, (here + jnp.where(owns, columns, 0.0)).astype(jnp.bfloat16), start, 1
    )
    values = sum_pieces(partial, near, far).astype(jnp.bfloat16).astype(jnp.float32)
    squares = jnp.sum(values * values, axis=1, keepdims=True)
    squares = squares + other_core(squares)
    inverse_rms = lax.rsqrt(squares / features + 1e-05)
    my_centred = (values * inverse_rms - mine(dec_bias, 0).astype(jnp.float32)).astype(
        jnp.bfloat16
    )
    encoder_both = jnp.concatenate([mine(encoder, 0), other_core(theirs(encoder, 0))], axis=1)
    decoder_both = jnp.concatenate([mine(decoder, 1), other_core(theirs(decoder, 1))], axis=0)
    centred = spread(my_centred, NEAR, near).reshape(tokens, half)
    products = matmul(centred, encoder_both)
    before_relu = (
        products[:, :own]
        + other_core(products[:, own:])
        + enc_bias.astype(jnp.float32)
    )
    latents = jnp.maximum(before_relu, 0.0).astype(jnp.bfloat16)
    latents_both = jnp.concatenate([latents, other_core(latents)], axis=1)
    partial = matmul(latents_both, decoder_both).astype(jnp.bfloat16)
    later, _ = lax.optimization_barrier((centred, partial))
    centred_other = other_core(later)
    centred_full = jnp.where(
        core == 0,
        jnp.concatenate([later, centred_other], axis=1),
        jnp.concatenate([centred_other, later], axis=1),
    )
    rebuilt = sum_pieces(partial, near, far)
    my_error = (mask_rows * (rebuilt - my_centred.astype(jnp.float32))).astype(jnp.bfloat16)
    owned_error = core_and_section(
        lax.dynamic_slice_in_dim(my_error, zh * block_rows, block_rows, 0)
    )
    error = spread(my_error, NEAR, near).reshape(tokens, half)
    step_size = STEP_RATE / tokens

    def stepped(weight, grad):
        return (weight.astype(jnp.float32) - step_size * grad).astype(jnp.bfloat16)

    over_rows = ((0,), (0,))
    products = matmul(error, decoder_both, ((1,), (1,)))
    backward = products[:, :own] + other_core(products[:, own:])
    pre_grad = jnp.where(before_relu > 0.0, backward, 0.0).astype(jnp.bfloat16)
    stepped_both = stepped(decoder_both, matmul(latents_both, error, over_rows))
    kept_half, back_half = stepped_both[:own], other_core(stepped_both[own:])
    new_decoder = jnp.where(
        core == 0,
        jnp.concatenate([kept_half, back_half], axis=1),
        jnp.concatenate([back_half, kept_half], axis=1),
    )
    new_encoder = stepped(encoder, matmul(centred_full, pre_grad, over_rows))
    return (owned_error, new_encoder, new_decoder)


def solution(mesh):
    cut = Mesh(mesh.devices.reshape(SIZES), AXES)
    return jax.shard_map(
        shards,
        mesh=cut,
        in_specs=(
            P(None, TENSOR),
            P("xl", None, TENSOR),
            P("xl", TENSOR, None),
            P(None, AXES),
            P(AXES),
            P(AXES, None),
            P(),
            P(),
            P(),
        ),
        out_specs=(
            P(TENSOR, "xl"),
            P(None, AXES),
            P(AXES, None),
        ),
        check_vma=False,
    )
```

time: 235 us -> 218 us (0.928)
  blocking collectives: 112 us -> 0 us
  waiting for transfers between devices: 56.2 us -> 124 us
  starting transfers between devices: 33.1 us -> 56.6 us
  matrix products: 15.8 us -> 21.9 us
  other arithmetic: 7.65 us -> 3.85 us
    all_to_all x5 -> x0, blocking collectives: 112 us -> none  [the longest x2 57.7 us: gather_rows(): lax.all_to_all(jnp.broadcast_to(rows[None], (plane,) + rows.shape), PLANE...]
    all_to_all x3 -> x6, waiting for transfers between devices: 48.6 us -> 118 us  [the longest x4 61.4 us: spread(): lax.all_to_all(jnp.broadcast_to(value[None], (count,) + value.shape), axe...]
    all_to_all x3 -> x6, starting transfers between devices: 16.3 us -> 33.9 us  [the longest x4 21.9 us: spread(): lax.all_to_all(jnp.broadcast_to(value[None], (count,) + value.shape), axe...]
    dot_general x14 -> x11, matrix products: 15.8 us -> 21.9 us  [matmul(): lax.dot_general(a, b, (dims, ((), ())), preferred_element_type=jnp.float32)]
    ppermute x9 -> x12, starting transfers between devices: 16.8 us -> 22.7 us  [exchange(): return lax.ppermute(value, AXES, route)]
    reduce_sum x5 -> x2, other arithmetic: 4.19 us -> 0.07 us  [sum_pieces(): return jnp.sum(spread(chunk, FAR, far).astype(jnp.float32), axis=0)]
    broadcast_in_dim x6 -> x4, local copies, waits for them, and re-layouts: 0.7 us -> 4.57 us  [spread(): jnp.broadcast_to(value[None], (count,) + value.shape)]
    unnamed x31 -> x65, local copies, waits for them, and re-layouts: 4.76 us -> 1.02 us
  transfers between devices with their start and end apart: 12 -> 18, of which waited for: 7 -> 11; matrix products, arithmetic and copies ran while one was open for 4% -> 9% of each run, Pallas kernels for 0% -> 0%
where the time goes in v2:
time: 218 us; the launch traced here: 217 us
  waiting for transfers between devices  124 us (57%)
  starting transfers between devices  56.6 us (26%)
  matrix products  21.9 us (10%)
  local copies, waits for them, and re-layouts  9.1 us (4%)
  other arithmetic  3.85 us (2%)
    all_to_all x4, waiting for transfers between devices, spread(): lax.all_to_all(jnp.broadcast_to(value[None], (count,) + value.shape), axe...  61.4 us
    all_to_all x2, waiting for transfers between devices, sum_pieces(): lax.all_to_all(partial.reshape(near, depth, width), NEAR, 0, 0, tiled=True)  56.7 us
    ppermute x12, starting transfers between devices, exchange(): return lax.ppermute(value, AXES, route)  22.7 us
    dot_general x11, matrix products, matmul(): lax.dot_general(a, b, (dims, ((), ())), preferred_element_type=jnp.float32)  21.9 us
    all_to_all x4, starting transfers between devices, spread(): lax.all_to_all(jnp.broadcast_to(value[None], (count,) + value.shape), axe...  21.9 us
    all_to_all x2, starting transfers between devices, sum_pieces(): lax.all_to_all(partial.reshape(near, depth, width), NEAR, 0, 0, tiled=True)  12 us
    ppermute x12, waiting for transfers between devices, exchange(): return lax.ppermute(value, AXES, route)  6.3 us
    broadcast_in_dim x4, local copies, waits for them, and re-layouts, spread(): jnp.broadcast_to(value[None], (count,) + value.shape)  4.57 us
  transfers between devices with their start and end apart: 18, of which 11 were waited for; matrix products, arithmetic and copies ran while one was open for 9% of the time, Pallas kernels for 0%

profile of v2, /device:TPU:1, one launch (start us, length us, event | category | flops | bytes accessed | tf_op | source)
XLA Modules:
  0.0 217.1 jit_solution(5455007577812050768)
XLA Ops:
  0.7 1.7 dynamic-slice_bitcast_fusion.1
  2.4 3.3 %collective-permute-start.1 = (bf16[128,4096]{1,0:T(8,128)(2,1)S(1)}, bf16[128,4096]{1,0:T(8,128)(2,1)S(1)}, u32[]{:S(2)}, u32[]{:S(2)}) collective-permute-start(bf16[128,4096]{1,0:T(8,128)(2,1)S(1)} %get-tuple-element.8), channel_id=1, source_target_pairs={{0,1},{1,0},{2,3},{3,2},{4,5},{5,4},{6,7},{7,6},{8,9},{9,8},{10,11... | collective-permute-start | bytes 3145736 | tf_op jit(solution)/shard_map/ppermute | solution.py:31
  8.1 2.1 convolution_convert_fusion.1
  10.1 1.6 fusion.52
  11.7 6.7 %all-to-all-start = ((bf16[32,8,4096]{2,1,0:T(8,128)(2,1)}), bf16[32,8,4096]{2,1,0:T(8,128)(2,1)S(1)}, u32[]{:S(2)}, u32[]{:S(2)}) async-start(bf16[32,8,4096]{2,1,0:T(8,128)(2,1)} %bitcast.4), calls=%async_computation | async-start | bytes 4194304 | tf_op jit(solution)/shard_map/all_to_all | solution.py:55
  18.4 28.4 %all-to-all-done = bf16[32,8,4096]{2,1,0:T(8,128)(2,1)S(1)} async-done(((bf16[32,8,4096]{2,1,0:T(8,128)(2,1)}), bf16[32,8,4096]{2,1,0:T(8,128)(2,1)S(1)}, u32[]{:S(2)}, u32[]{:S(2)}) %all-to-all-start) | async-done | bytes 2097184 | tf_op jit(solution)/shard_map/all_to_all | solution.py:55
  47.9 7.3 %all-to-all-start.1 = ((bf16[4,8,4096]{2,1,0:T(8,128)(2,1)}), bf16[4,8,4096]{2,1,0:T(8,128)(2,1)S(1)}, u32[]{:S(2)}, u32[]{:S(2)}) async-start(bf16[4,8,4096]{2,1,0:T(8,128)(2,1)} %broadcast_in_dim.19), calls=%async_computation.1 | async-start | bytes 524288 | tf_op jit(solution)/shard_map/all_to_all | solution.py:47
  55.2 8.1 %all-to-all-done.1 = bf16[4,8,4096]{2,1,0:T(8,128)(2,1)S(1)} async-done(((bf16[4,8,4096]{2,1,0:T(8,128)(2,1)}), bf16[4,8,4096]{2,1,0:T(8,128)(2,1)S(1)}, u32[]{:S(2)}, u32[]{:S(2)}) %all-to-all-start.1) | async-done | bytes 262176 | tf_op jit(solution)/shard_map/all_to_all | solution.py:47
  63.5 3.5 %collective-permute-start.3 = (f32[8,1]{0,1:T(1,128)S(1)}, f32[8,1]{0,1:T(1,128)S(1)}, u32[]{:S(2)}, u32[]{:S(2)}) collective-permute-start(f32[8,1]{0,1:T(1,128)S(1)} %bitcast.33), channel_id=1, source_target_pairs={{0,1},{1,0},{2,3},{3,2},{4,5},{5,4},{6,7},{7,6},{8,9},{9,8},{10,11... | collective-permute-start | bytes 104 | tf_op jit(solution)/shard_map/ppermute | solution.py:31
  68.0 1.6 broadcast_in_dim.21
  69.5 5.7 %all-to-all-start.2 = ((bf16[32,8,4096]{2,1,0:T(8,128)(2,1)}), bf16[32,8,4096]{2,1,0:T(8,128)(2,1)}, u32[]{:S(2)}, u32[]{:S(2)}) async-start(bf16[32,8,4096]{2,1,0:T(8,128)(2,1)} %broadcast_in_dim.21), calls=%async_computation.2 | async-start | bytes 4194304 | tf_op jit(solution)/shard_map/all_to_all | solution.py:47
  75.2 1.1 constant_dynamic-slice_fusion.3
  78.0 1.3 collective-permute-done.4
  79.4 24.3 %all-to-all-done.2 = bf16[32,8,4096]{2,1,0:T(8,128)(2,1)} async-done(((bf16[32,8,4096]{2,1,0:T(8,128)(2,1)}), bf16[32,8,4096]{2,1,0:T(8,128)(2,1)}, u32[]{:S(2)}, u32[]{:S(2)}) %all-to-all-start.2) | async-done | bytes 2097184 | tf_op jit(solution)/shard_map/all_to_all | solution.py:47
  103.7 2.6 %fusion.11 = f32[256,256]{1,0:T(8,128)S(1)} fusion(bf16[4096,128]{1,0:T(8,128)(2,1)} %collective-permute-done.4, bf16[4096,128]{1,0:T(8,128)(2,1)S(1)} %copy-done.4, bf16[32,8,4096]{2,1,0:T(8,128)(2,1)} %all-to-all-done.2), kind=kOutput, calls=%fused_computation.19 | convolution fusion | flops 541065216 | bytes 4456448 | tf_op jit(solution)/shard_map/dot_general | solution.py:43
  106.3 1.8 collective-permute-start.5
  110.5 3.3 %convolution_convert_fusion = bf16[256,4096]{1,0:T(8,128)(2,1)} fusion(bf16[128,4096]{1,0:T(8,128)(2,1)} %collective-permute-done.7, bf16[128,4096]{1,0:T(8,128)(2,1)S(1)} %get-tuple-element.11, bf16[256,128]{1,0:T(8,128)(2,1)S(1)} %collective-permute-done.6, bf16[256,128]{1,0:T(8,128)(2,1)S(1)} %maximum_convert_fusion), kind=kOutput, calls=%fused_computation.4 | convolution fusion | flops 542375936 | bytes 4325376 | tf_op jit(solution)/shard_map/dot_general | solution.py:43
  113.8 5.4 %all-to-all-start.3 = ((bf16[32,8,4096]{2,1,0:T(8,128)(2,1)}), bf16[32,8,4096]{2,1,0:T(8,128)(2,1)S(1)}, u32[]{:S(2)}, u32[]{:S(2)}) async-start(bf16[32,8,4096]{2,1,0:T(8,128)(2,1)} %bitcast.32), calls=%async_computation.3 | async-start | bytes 4194304 | tf_op jit(solution)/shard_map/all_to_all | solution.py:55
  119.3 28.3 %all-to-all-done.3 = bf16[32,8,4096]{2,1,0:T(8,128)(2,1)S(1)} async-done(((bf16[32,8,4096]{2,1,0:T(8,128)(2,1)}), bf16[32,8,4096]{2,1,0:T(8,128)(2,1)S(1)}, u32[]{:S(2)}, u32[]{:S(2)}) %all-to-all-start.3) | async-done | bytes 2097184 | tf_op jit(solution)/shard_map/all_to_all | solution.py:55
  148.7 3.4 %all-to-all-start.4 = ((bf16[4,8,4096]{2,1,0:T(8,128)(2,1)}), bf16[4,8,4096]{2,1,0:T(8,128)(2,1)S(1)}, u32[]{:S(2)}, u32[]{:S(2)}) async-start(bf16[4,8,4096]{2,1,0:T(8,128)(2,1)} %broadcast_in_dim.22), calls=%async_computation.4 | async-start | bytes 524288 | tf_op jit(solution)/shard_map/all_to_all | solution.py:47
  152.9 7.3 %all-to-all-done.4 = bf16[4,8,4096]{2,1,0:T(8,128)(2,1)S(1)} async-done(((bf16[4,8,4096]{2,1,0:T(8,128)(2,1)}), bf16[4,8,4096]{2,1,0:T(8,128)(2,1)S(1)}, u32[]{:S(2)}, u32[]{:S(2)}) %all-to-all-start.4) | async-done | bytes 262176 | tf_op jit(solution)/shard_map/all_to_all | solution.py:47
  160.4 1.6 broadcast_in_dim.23
  161.9 5.5 %all-to-all-start.5 = ((bf16[32,8,4096]{2,1,0:T(8,128)(2,1)}), bf16[32,8,4096]{2,1,0:T(8,128)(2,1)S(1)}, u32[]{:S(2)}, u32[]{:S(2)}) async-start(bf16[32,8,4096]{2,1,0:T(8,128)(2,1)} %broadcast_in_dim.23), calls=%async_computation.5 | async-start | bytes 4194304 | tf_op jit(solution)/shard_map/all_to_all | solution.py:47
  167.5 3.8 %collective-permute-start.9 = (bf16[256,4096]{1,0:T(8,128)(2,1)}, bf16[256,4096]{1,0:T(8,128)(2,1)}, u32[]{:S(2)}, u32[]{:S(2)}) collective-permute-start(bf16[256,4096]{1,0:T(8,128)(2,1)} %bitcast.8), channel_id=1, source_target_pairs={{0,1},{1,0},{2,3},{3,2},{4,5},{5,4},{6,7},{7,6},{8,9},{9,8},{10,11... | collective-permute-start | bytes 6291464 | tf_op jit(solution)/shard_map/ppermute | solution.py:31
  171.2 21.6 %all-to-all-done.5 = bf16[32,8,4096]{2,1,0:T(8,128)(2,1)S(1)} async-done(((bf16[32,8,4096]{2,1,0:T(8,128)(2,1)}), bf16[32,8,4096]{2,1,0:T(8,128)(2,1)S(1)}, u32[]{:S(2)}, u32[]{:S(2)}) %all-to-all-start.5) | async-done | bytes 2097184 | tf_op jit(solution)/shard_map/all_to_all | solution.py:47
  192.8 2.0 fusion.16
  194.8 4.8 %collective-permute-start.10 = (f32[256,128]{1,0:T(8,128)S(1)}, f32[256,128]{1,0:T(8,128)S(1)}, u32[]{:S(2)}, u32[]{:S(2)}) collective-permute-start(f32[256,128]{1,0:T(8,128)S(1)} %slice.27), channel_id=1, source_target_pairs={{0,1},{1,0},{2,3},{3,2},{4,5},{5,4},{6,7},{7,6},{8,9},{9,8},{10,11... | collective-permute-start | bytes 393224 | tf_op jit(solution)/shard_map/ppermute | solution.py:31
  199.7 2.0 subtract_convert_fusion
  202.0 3.0 %collective-permute-start.8 = (bf16[2,4096]{1,0:T(2,128)(2,1)S(1)}, bf16[2,4096]{1,0:T(2,128)(2,1)S(1)}, u32[]{:S(2)}, u32[]{:S(2)}) collective-permute-start(bf16[2,4096]{1,0:T(2,128)(2,1)S(1)} %constant_dynamic-slice_fusion.4), channel_id=1, source_target_pairs={{0,0},{1,128},{2,2},{3,130},{4,4},{5,132},{6,6},{7,134},{8,8},{9,1... | collective-permute-start | bytes 49160 | tf_op jit(solution)/shard_map/ppermute | solution.py:31
  205.0 2.2 %collective-permute-done.8 = bf16[2,4096]{1,0:T(2,128)(2,1)S(1)} collective-permute-done((bf16[2,4096]{1,0:T(2,128)(2,1)S(1)}, bf16[2,4096]{1,0:T(2,128)(2,1)S(1)}, u32[]{:S(2)}, u32[]{:S(2)}) %collective-permute-start.8) | collective-permute-done | bytes 16416 | tf_op jit(solution)/shard_map/ppermute | solution.py:31
  207.2 7.4 %fusion.1 = bf16[8192,128]{1,0:T(8,128)(2,1)} fusion(bf16[256,4096]{1,0:T(8,128)(2,1)} %collective-permute-done.9, bf16[256,4096]{1,0:T(8,128)(2,1)} %bitcast.8, bf16[8192,128]{1,0:T(8,128)(2,1)S(1)} %copy-done.3, pred[]{:T(512)S(6)} %eq.48, f32[256,128]{1,0:T(8,128)S(1)} %collective-permute-done.10, f32[256,256]{1,0:T(8,128)S(1)} %fusion.16, ...), kind=kOutput, calls=%fused_computation.2 | convolution fusion | flops 560136192 | bytes 8913409 | tf_op jit(solution)/shard_map/dot_general | solution.py:43
  214.7 1.8 maximum_select_fusion.2
  (112 shorter events, 11.5 us)
Async XLA Ops:
  2.4 5.7 %collective-permute-start.1 = (bf16[128,4096]{1,0:T(8,128)(2,1)S(1)}, bf16[128,4096]{1,0:T(8,128)(2,1)S(1)}, u32[]{:S(2)}, u32[]{:S(2)}) collective-permute-start(bf16[128,4096]{1,0:T(8,128)(2,1)S(1)} %get-tuple-element.8), channel_id=1, source_target_pairs={{0,1},{1,0},{2,3},{3,2},{4,5},{5,4},{6,7},{7,6},{8,9},{9,8},{10,11... | collective-permute-start | bytes 3145736 | tf_op jit(solution)/shard_map/ppermute | solution.py:31
  6.7 1.4 collective-permute-start
  7.5 2.6 %collective-permute-start.2 = (bf16[256,64]{1,0:T(8,128)(2,1)S(1)}, bf16[256,64]{1,0:T(8,128)(2,1)S(1)}, u32[]{:S(2)}, u32[]{:S(2)}) collective-permute-start(bf16[256,64]{1,0:T(8,128)(2,1)S(1)} %convolution_convert_fusion.4), channel_id=1, source_target_pairs={{0,1},{1,0},{2,3},{3,2},{4,5},{5,4},{6,7},{7,6},{8,9},{9,8},{10,11... | collective-permute-start | bytes 98312 | tf_op jit(solution)/shard_map/ppermute | solution.py:31
  11.7 35.1 %all-to-all-start = ((bf16[32,8,4096]{2,1,0:T(8,128)(2,1)}), bf16[32,8,4096]{2,1,0:T(8,128)(2,1)S(1)}, u32[]{:S(2)}, u32[]{:S(2)}) async-start(bf16[32,8,4096]{2,1,0:T(8,128)(2,1)} %bitcast.4), calls=%async_computation | async-start | bytes 4194304 | tf_op jit(solution)/shard_map/all_to_all | solution.py:55
  18.4 36.8 %copy-start.7 = (bf16[8192]{0:T(1024)(128)(2,1)S(1)}, bf16[8192]{0:T(1024)(128)(2,1)}, u32[]{:S(2)}) copy-start(bf16[8192]{0:T(1024)(128)(2,1)} %param.15) | copy-start | bytes 49156
  47.9 15.4 %all-to-all-start.1 = ((bf16[4,8,4096]{2,1,0:T(8,128)(2,1)}), bf16[4,8,4096]{2,1,0:T(8,128)(2,1)S(1)}, u32[]{:S(2)}, u32[]{:S(2)}) async-start(bf16[4,8,4096]{2,1,0:T(8,128)(2,1)} %broadcast_in_dim.19), calls=%async_computation.1 | async-start | bytes 524288 | tf_op jit(solution)/shard_map/all_to_all | solution.py:47
  63.5 4.4 %collective-permute-start.3 = (f32[8,1]{0,1:T(1,128)S(1)}, f32[8,1]{0,1:T(1,128)S(1)}, u32[]{:S(2)}, u32[]{:S(2)}) collective-permute-start(f32[8,1]{0,1:T(1,128)S(1)} %bitcast.33), channel_id=1, source_target_pairs={{0,1},{1,0},{2,3},{3,2},{4,5},{5,4},{6,7},{7,6},{8,9},{9,8},{10,11... | collective-permute-start | bytes 104 | tf_op jit(solution)/shard_map/ppermute | solution.py:31
  69.5 5.7 %copy-start.2 = (bf16[8192,128]{1,0:T(8,128)(2,1)S(1)}, bf16[8192,128]{1,0:T(8,128)(2,1)}, u32[]{:S(2)}) copy-start(bf16[8192,128]{1,0:T(8,128)(2,1)} %param.12) | copy-start | bytes 6291460
  69.5 34.2 %all-to-all-start.2 = ((bf16[32,8,4096]{2,1,0:T(8,128)(2,1)}), bf16[32,8,4096]{2,1,0:T(8,128)(2,1)}, u32[]{:S(2)}, u32[]{:S(2)}) async-start(bf16[32,8,4096]{2,1,0:T(8,128)(2,1)} %broadcast_in_dim.21), calls=%async_computation.2 | async-start | bytes 4194304 | tf_op jit(solution)/shard_map/all_to_all | solution.py:47
  76.4 27.4 %copy-start.4 = (bf16[4096,128]{1,0:T(8,128)(2,1)S(1)}, bf16[4096,128]{1,0:T(8,128)(2,1)}, u32[]{:S(2)}) copy-start(bf16[4096,128]{1,0:T(8,128)(2,1)} %get-tuple-element.9) | copy-start | bytes 3145732
  76.4 3.0 %collective-permute-start.4 = (bf16[4096,128]{1,0:T(8,128)(2,1)S(1)}, bf16[4096,128]{1,0:T(8,128)(2,1)}, u32[]{:S(2)}, u32[]{:S(2)}) collective-permute-start(bf16[4096,128]{1,0:T(8,128)(2,1)S(1)} %get-tuple-element.10), channel_id=1, source_target_pairs={{0,1},{1,0},{2,3},{3,2},{4,5},{5,4},{6,7},{7,6},{8,9},{9,8},{10,11... | collective-permute-start | bytes 3145736 | tf_op jit(solution)/shard_map/ppermute | solution.py:31
  77.3 32.3 %collective-permute-start.7 = (bf16[128,4096]{1,0:T(8,128)(2,1)S(1)}, bf16[128,4096]{1,0:T(8,128)(2,1)}, u32[]{:S(2)}, u32[]{:S(2)}) collective-permute-start(bf16[128,4096]{1,0:T(8,128)(2,1)S(1)} %get-tuple-element.12), channel_id=1, source_target_pairs={{0,1},{1,0},{2,3},{3,2},{4,5},{5,4},{6,7},{7,6},{8,9},{9,8},{10,11... | collective-permute-start | bytes 3145736 | tf_op jit(solution)/shard_map/ppermute | solution.py:31
  106.3 2.8 %collective-permute-start.5 = (f32[256,128]{1,0:T(8,128)S(1)}, f32[256,128]{1,0:T(8,128)S(1)}, u32[]{:S(2)}, u32[]{:S(2)}) collective-permute-start(f32[256,128]{1,0:T(8,128)S(1)} %slice.25), channel_id=1, source_target_pairs={{0,1},{1,0},{2,3},{3,2},{4,5},{5,4},{6,7},{7,6},{8,9},{9,8},{10,11... | collective-permute-start | bytes 393224 | tf_op jit(solution)/shard_map/ppermute | solution.py:31
  108.1 5.7 %copy-start.21 = (f32[128]{0:T(128)}, f32[128]{0:T(128)S(1)}, u32[]{:S(2)}) copy-start(f32[128]{0:T(128)S(1)} %convert_element_type.104) | copy-start | bytes 1540
  109.2 1.4 collective-permute-start.6
  113.8 33.8 %all-to-all-start.3 = ((bf16[32,8,4096]{2,1,0:T(8,128)(2,1)}), bf16[32,8,4096]{2,1,0:T(8,128)(2,1)S(1)}, u32[]{:S(2)}, u32[]{:S(2)}) async-start(bf16[32,8,4096]{2,1,0:T(8,128)(2,1)} %bitcast.32), calls=%async_computation.3 | async-start | bytes 4194304 | tf_op jit(solution)/shard_map/all_to_all | solution.py:55
  119.2 32.9 %copy-start.26 = (s32[256]{0:T(256)S(1)}, s32[256]{0:T(256)}, u32[]{:S(2)}) copy-start(s32[256]{0:T(256)} %param.16) | copy-start | bytes 3076
  119.2 33.0 %copy-start.11 = (s32[256]{0:T(256)S(1)}, s32[256]{0:T(256)}, u32[]{:S(2)}) copy-start(s32[256]{0:T(256)} %copy-done.10) | copy-start | bytes 3076
  119.2 33.0 %copy-start.13 = (s32[256]{0:T(256)S(1)}, s32[256]{0:T(256)}, u32[]{:S(2)}) copy-start(s32[256]{0:T(256)} %copy-done.12) | copy-start | bytes 3076
  119.2 33.0 %copy-start.15 = (s32[256]{0:T(256)S(1)}, s32[256]{0:T(256)}, u32[]{:S(2)}) copy-start(s32[256]{0:T(256)} %copy-done.14) | copy-start | bytes 3076
  119.2 33.0 %copy-start.17 = (s32[256]{0:T(256)S(1)}, s32[256]{0:T(256)}, u32[]{:S(2)}) copy-start(s32[256]{0:T(256)} %copy-done.16) | copy-start | bytes 3076
  119.2 33.0 %copy-start.19 = (s32[256]{0:T(256)S(1)}, s32[256]{0:T(256)}, u32[]{:S(2)}) copy-start(s32[256]{0:T(256)} %copy-done.18) | copy-start | bytes 3076
  119.2 33.0 %copy-start.29 = (pred[256]{0:T(512)(128)(4,1)S(1)}, pred[256]{0:T(512)(128)(4,1)}, u32[]{:S(2)}) copy-start(pred[256]{0:T(512)(128)(4,1)} %copy-done.28) | copy-start | bytes 772
  119.2 33.0 %copy-start.31 = (pred[256]{0:T(512)(128)(4,1)S(1)}, pred[256]{0:T(512)(128)(4,1)}, u32[]{:S(2)}) copy-start(pred[256]{0:T(512)(128)(4,1)} %copy-done.30) | copy-start | bytes 772
  148.7 11.5 %all-to-all-start.4 = ((bf16[4,8,4096]{2,1,0:T(8,128)(2,1)}), bf16[4,8,4096]{2,1,0:T(8,128)(2,1)S(1)}, u32[]{:S(2)}, u32[]{:S(2)}) async-start(bf16[4,8,4096]{2,1,0:T(8,128)(2,1)} %broadcast_in_dim.22), calls=%async_computation.4 | async-start | bytes 524288 | tf_op jit(solution)/shard_map/all_to_all | solution.py:47
  152.2 8.0 %copy-start.9 = (f32[8]{0:T(128)S(1)}, f32[8]{0:T(128)}, u32[]{:S(2)}) copy-start(f32[8]{0:T(128)} %copy-done.8) | copy-start | bytes 100
  161.9 30.9 %all-to-all-start.5 = ((bf16[32,8,4096]{2,1,0:T(8,128)(2,1)}), bf16[32,8,4096]{2,1,0:T(8,128)(2,1)S(1)}, u32[]{:S(2)}, u32[]{:S(2)}) async-start(bf16[32,8,4096]{2,1,0:T(8,128)(2,1)} %broadcast_in_dim.23), calls=%async_computation.5 | async-start | bytes 4194304 | tf_op jit(solution)/shard_map/all_to_all | solution.py:47
  167.5 32.2 %copy-start.24 = (bf16[256,128]{1,0:T(8,128)(2,1)S(1)}, bf16[256,128]{1,0:T(8,128)(2,1)}, u32[]{:S(2)}) copy-start(bf16[256,128]{1,0:T(8,128)(2,1)} %copy-done.23) | copy-start | bytes 196612
  167.5 39.8 %collective-permute-start.9 = (bf16[256,4096]{1,0:T(8,128)(2,1)}, bf16[256,4096]{1,0:T(8,128)(2,1)}, u32[]{:S(2)}, u32[]{:S(2)}) collective-permute-start(bf16[256,4096]{1,0:T(8,128)(2,1)} %bitcast.8), channel_id=1, source_target_pairs={{0,1},{1,0},{2,3},{3,2},{4,5},{5,4},{6,7},{7,6},{8,9},{9,8},{10,11... | collective-permute-start | bytes 6291464 | tf_op jit(solution)/shard_map/ppermute | solution.py:31
  194.8 12.4 %collective-permute-start.10 = (f32[256,128]{1,0:T(8,128)S(1)}, f32[256,128]{1,0:T(8,128)S(1)}, u32[]{:S(2)}, u32[]{:S(2)}) collective-permute-start(f32[256,128]{1,0:T(8,128)S(1)} %slice.27), channel_id=1, source_target_pairs={{0,1},{1,0},{2,3},{3,2},{4,5},{5,4},{6,7},{7,6},{8,9},{9,8},{10,11... | collective-permute-start | bytes 393224 | tf_op jit(solution)/shard_map/ppermute | solution.py:31
  201.9 12.8 %collective-permute-start.11 = (bf16[128,4096]{1,0:T(8,128)(2,1)S(1)}, bf16[128,4096]{1,0:T(8,128)(2,1)S(1)}, u32[]{:S(2)}, u32[]{:S(2)}) collective-permute-start(bf16[128,4096]{1,0:T(8,128)(2,1)S(1)} %get-tuple-element.6), channel_id=1, source_target_pairs={{0,1},{1,0},{2,3},{3,2},{4,5},{5,4},{6,7},{7,6},{8,9},{9,8},{10,11... | collective-permute-start | bytes 3145736 | tf_op jit(solution)/shard_map/ppermute | solution.py:31
  202.0 5.2 %collective-permute-start.8 = (bf16[2,4096]{1,0:T(2,128)(2,1)S(1)}, bf16[2,4096]{1,0:T(2,128)(2,1)S(1)}, u32[]{:S(2)}, u32[]{:S(2)}) collective-permute-start(bf16[2,4096]{1,0:T(2,128)(2,1)S(1)} %constant_dynamic-slice_fusion.4), channel_id=1, source_target_pairs={{0,0},{1,128},{2,2},{3,130},{4,4},{5,132},{6,6},{7,134},{8,8},{9,1... | collective-permute-start | bytes 49160 | tf_op jit(solution)/shard_map/ppermute | solution.py:31
  (18 other events, 48.8 us)

commit v3 on v2

--- a/solution.py
+++ b/solution.py
@@ -49,14 +49,17 @@
     )
 
 
-def sum_pieces(partial, near, far):
+def near_sum(partial, near):
     tokens, width = partial.shape
     depth = tokens // near
     pieces = lax.all_to_all(partial.reshape(near, depth, width), NEAR, 0, 0, tiled=True)
     to = lax.broadcasted_iota(jnp.int32, (depth, tokens), 0)
     of = lax.broadcasted_iota(jnp.int32, (depth, tokens), 1)
     adds = (of % depth == to).astype(jnp.bfloat16)
-    chunk = matmul(adds, pieces.reshape(tokens, width)).astype(jnp.bfloat16)
+    return matmul(adds, pieces.reshape(tokens, width)).astype(jnp.bfloat16)
+
+
+def far_sum(chunk, far):
     return jnp.sum(spread(chunk, FAR, far).astype(jnp.float32), axis=0)
 
 
@@ -99,33 +102,44 @@
         return lax.dynamic_slice_in_dim(weight, (1 - core) * half, half, axis)
 
     proj = out_proj[0]
-    proj_both = jnp.concatenate([mine(proj, 1), other_core(theirs(proj, 1))], axis=0)
-    context = matmul(order, contexts[0]).astype(jnp.bfloat16)
-    resid = matmul(order, resid_in).astype(jnp.bfloat16)
-    context_both = jnp.concatenate([context, other_core(context)], axis=1)
-    resid_other = other_core(resid)
-    partial = matmul(context_both, proj_both).astype(jnp.bfloat16)
-    columns = jnp.where(
-        core == 0,
-        jnp.concatenate([resid, resid_other], axis=1),
-        jnp.concatenate([resid_other, resid], axis=1),
-    ).astype(jnp.float32)
-    start = (((y * 4 + zh) * 2 + zl) * 2 + xh) * columns.shape[1]
+    proj_other = other_core(theirs(proj, 1))
+    width = resid_in.shape[1]
+    joined = matmul(order, jnp.concatenate([contexts[0], resid_in], axis=1)).astype(
+        jnp.bfloat16
+    )
+    joined_both = jnp.concatenate([joined, other_core(joined)], axis=1)
+    start = (((y * 4 + zh) * 2 + zl) * 2 + xh) * 2 * width
     owns = (start // half == core) & (xl == 0)
-    start = start % half
-    here = lax.dynamic_slice_in_dim(partial, start, columns.shape[1], 1).astype(jnp.float32)
-    partial = lax.dynamic_update_slice_in_dim(
-        partial, (here + jnp.where(owns, columns, 0.0)).astype(jnp.bfloat16), start, 1
-    )
-    values = sum_pieces(partial, near, far).astype(jnp.bfloat16).astype(jnp.float32)
+
+    def placed(which):
+        column = lax.broadcasted_iota(jnp.int32, (width, half), 1)
+        target = lax.broadcasted_iota(jnp.int32, (width, half), 0) + (
+            start % half + which * width
+        )
+        return ((column == target) & owns).astype(jnp.bfloat16)
+
+    proj_both = jnp.concatenate(
+        [mine(proj, 1), placed(core), proj_other, placed(1 - core)], axis=0
+    )
+    partial = matmul(joined_both, proj_both).astype(jnp.bfloat16)
+
+    encoder_late, decoder_late, _ = lax.optimization_barrier((encoder, decoder, partial))
+    encoder_both = jnp.concatenate(
+        [mine(encoder_late, 0), other_core(theirs(encoder_late, 0))], axis=1
+    )
+    decoder_both = jnp.concatenate(
+        [mine(decoder_late, 1), other_core(theirs(decoder_late, 1))], axis=0
+    )
+    my_bias = mine(dec_bias, 0).astype(jnp.float32)
+    chunk = near_sum(partial, near)
+    chunk, encoder_both, decoder_both, mask_rows, my_bias = lax.optimization_barrier(
+        (chunk, encoder_both, decoder_both, mask_rows, my_bias)
+    )
+    values = far_sum(chunk, far).astype(jnp.bfloat16).astype(jnp.float32)
     squares = jnp.sum(values * values, axis=1, keepdims=True)
     squares = squares + other_core(squares)
     inverse_rms = lax.rsqrt(squares / features + 1e-05)
-    my_centred = (values * inverse_rms - mine(dec_bias, 0).astype(jnp.float32)).astype(
-        jnp.bfloat16
-    )
-    encoder_both = jnp.concatenate([mine(encoder, 0), other_core(theirs(encoder, 0))], axis=1)
-    decoder_both = jnp.concatenate([mine(decoder, 1), other_core(theirs(decoder, 1))], axis=0)
+    my_centred = (values * inverse_rms - my_bias).astype(jnp.bfloat16)
     centred = spread(my_centred, NEAR, near).reshape(tokens, half)
     products = matmul(centred, encoder_both)
     before_relu = (
@@ -143,11 +157,10 @@
         jnp.concatenate([later, centred_other], axis=1),
         jnp.concatenate([centred_other, later], axis=1),
     )
-    rebuilt = sum_pieces(partial, near, far)
+    chunk = near_sum(partial, near)
+    chunk, centred_full = lax.optimization_barrier((chunk, centred_full))
+    rebuilt = far_sum(chunk, far)
     my_error = (mask_rows * (rebuilt - my_centred.astype(jnp.float32))).astype(jnp.bfloat16)
-    owned_error = core_and_section(
-        lax.dynamic_slice_in_dim(my_error, zh * block_rows, block_rows, 0)
-    )
     error = spread(my_error, NEAR, near).reshape(tokens, half)
     step_size = STEP_RATE / tokens
 
@@ -157,13 +170,20 @@
     over_rows = ((0,), (0,))
     products = matmul(error, decoder_both, ((1,), (1,)))
     backward = products[:, :own] + other_core(products[:, own:])
-    pre_grad = jnp.where(before_relu > 0.0, backward, 0.0).astype(jnp.bfloat16)
-    stepped_both = stepped(decoder_both, matmul(latents_both, error, over_rows))
-    kept_half, back_half = stepped_both[:own], other_core(stepped_both[own:])
-    new_decoder = jnp.where(
-        core == 0,
-        jnp.concatenate([kept_half, back_half], axis=1),
-        jnp.concatenate([back_half, kept_half], axis=1),
+    pre_grad = lax.optimization_barrier(
+        jnp.where(before_relu > 0.0, backward, 0.0).astype(jnp.bfloat16)
+    )
+    error_late, _ = lax.optimization_barrier((error, products))
+    stepped_both = stepped(decoder_both, matmul(latents_both, error_late, over_rows))
+    own_rows, _ = lax.optimization_barrier((my_error, products))
+    owned_error = core_and_section(
+        lax.dynamic_slice_in_dim(own_rows, zh * block_rows, block_rows, 0)
+    )
+    new_decoder = lax.dynamic_update_slice_in_dim(
+        decoder, stepped_both[:own], core * half, 1
+    )
+    new_decoder = lax.dynamic_update_slice_in_dim(
+        new_decoder, other_core(stepped_both[own:]), (1 - core) * half, 1
     )
     new_encoder = stepped(encoder, matmul(centred_full, pre_grad, over_rows))
     return (owned_error, new_encoder, new_decoder)

time: 218 us -> 222 us (1.018)
  blocking collectives: 0 us -> 59 us
  waiting for transfers between devices: 124 us -> 77.2 us
  starting transfers between devices: 56.6 us -> 36.6 us
  local copies, waits for them, and re-layouts: 9.1 us -> 16.9 us
  other arithmetic: 3.85 us -> 9.58 us
    all_to_all x0 -> x3, blocking collectives: none -> 59 us  [spread(): lax.all_to_all(jnp.broadcast_to(value[None], (count,) + value.shape), axe...]
    all_to_all x4 -> x1, waiting for transfers between devices: 61.4 us -> 27.2 us  [spread(): lax.all_to_all(jnp.broadcast_to(value[None], (count,) + value.shape), axe...]
    all_to_all x4 -> x1, starting transfers between devices: 21.9 us -> 6.75 us  [spread(): lax.all_to_all(jnp.broadcast_to(value[None], (count,) + value.shape), axe...]
    all_to_all x2, waiting for transfers between devices: 56.7 us -> 41.8 us  [near_sum(): lax.all_to_all(partial.reshape(near, depth, width), NEAR, 0, 0, tiled=True)]
    unnamed x65 -> x40, local copies, waits for them, and re-layouts: 1.02 us -> 6.36 us
    ppermute x12 -> x11, starting transfers between devices: 22.7 us -> 18.1 us  [exchange(): return lax.ppermute(value, AXES, route)]
    select_n x1, other arithmetic: 1.8 us -> 5.93 us  [shards(): jnp.where(core == 0, jnp.concatenate([later, centred_other], axis=1), jnp...]
    optimization_barrier x0 -> x1, local copies, waits for them, and re-layouts: none -> 3.24 us  [shards(): lax.optimization_barrier((encoder, decoder, partial))]
  transfers between devices with their start and end apart: 18 -> 14, of which waited for: 11 -> 9; matrix products, arithmetic and copies ran while one was open for 9% -> 10% of each run, Pallas kernels for 0% -> 0%
where the time goes in v3:
time: 222 us; the launch traced here: 221 us
  waiting for transfers between devices  77.2 us (35%)
  blocking collectives  59 us (27%)
  starting transfers between devices  36.6 us (16%)
  matrix products  20.5 us (9%)
  local copies, waits for them, and re-layouts  16.9 us (8%)
  other arithmetic  9.58 us (4%)
    all_to_all x3, blocking collectives, spread(): lax.all_to_all(jnp.broadcast_to(value[None], (count,) + value.shape), axe...  59 us
    all_to_all x2, waiting for transfers between devices, near_sum(): lax.all_to_all(partial.reshape(near, depth, width), NEAR, 0, 0, tiled=True)  41.8 us
    all_to_all x1, waiting for transfers between devices, spread(): lax.all_to_all(jnp.broadcast_to(value[None], (count,) + value.shape), axe...  27.2 us
    dot_general x10, matrix products, matmul(): lax.dot_general(a, b, (dims, ((), ())), preferred_element_type=jnp.float32)  20.5 us
    ppermute x11, starting transfers between devices, exchange(): return lax.ppermute(value, AXES, route)  18.1 us
    all_to_all x2, starting transfers between devices, near_sum(): lax.all_to_all(partial.reshape(near, depth, width), NEAR, 0, 0, tiled=True)  11.7 us
    ppermute x11, waiting for transfers between devices, exchange(): return lax.ppermute(value, AXES, route)  8.21 us
    all_to_all x1, starting transfers between devices, spread(): lax.all_to_all(jnp.broadcast_to(value[None], (count,) + value.shape), axe...  6.75 us
  transfers between devices with their start and end apart: 14, of which 9 were waited for; matrix products, arithmetic and copies ran while one was open for 10% of the time, Pallas kernels for 0%

profile of v3, /device:TPU:1, one launch (start us, length us, event | category | flops | bytes accessed | tf_op | source)
XLA Modules:
  0.0 220.9 jit_solution(11910885557394823884)
XLA Ops:
  0.6 3.2 %copy.27 = bf16[128,8192]{1,0:T(8,128)(2,1)} copy(bf16[128,8192]{1,0:T(8,128)(2,1)} %param.14) | data formatting | bytes 4194304 | tf_op jit(solution)/shard_map/optimization_barrier | solution.py:126
  3.9 1.2 dynamic-slice_bitcast_fusion.1
  5.1 3.2 %collective-permute-start.1 = (bf16[128,4096]{1,0:T(8,128)(2,1)}, bf16[128,4096]{1,0:T(8,128)(2,1)S(1)}, u32[]{:S(2)}, u32[]{:S(2)}) collective-permute-start(bf16[128,4096]{1,0:T(8,128)(2,1)} %get-tuple-element.34), channel_id=1, source_target_pairs={{0,1},{1,0},{2,3},{3,2},{4,5},{5,4},{6,7},{7,6},{8,9},{9,8},{10,11... | collective-permute-start | bytes 3145736 | tf_op jit(solution)/shard_map/ppermute | solution.py:31
  10.8 2.5 %convolution_convert_fusion.1 = bf16[256,4096]{1,0:T(8,128)(2,1)} fusion(bf16[64,4096]{1,0:T(8,128)(2,1)S(1)} %get-tuple-element.40, bf16[128,4096]{1,0:T(8,128)(2,1)S(1)} %collective-permute-done.1, bf16[64,4096]{1,0:T(8,128)(2,1)S(1)} %get-tuple-element.39, bf16[128,4096]{1,0:T(8,128)(2,1)S(1)} %get-tuple-element.33, ...), kind=kOutput, calls=%fused_computation.6 | convolution fusion | flops 819331072 | bytes 5439488 | tf_op jit(solution)/shard_map/dot_general | solution.py:43
  13.3 6.9 %all-to-all-start = ((bf16[32,8,4096]{2,1,0:T(8,128)(2,1)}), bf16[32,8,4096]{2,1,0:T(8,128)(2,1)}, u32[]{:S(2)}, u32[]{:S(2)}) async-start(bf16[32,8,4096]{2,1,0:T(8,128)(2,1)} %bitcast.37), calls=%async_computation | async-start | bytes 4194304 | tf_op jit(solution)/shard_map/all_to_all | solution.py:55
  23.6 1.5 pad_maximum_fusion
  25.3 23.3 %all-to-all-done = bf16[32,8,4096]{2,1,0:T(8,128)(2,1)} async-done(((bf16[32,8,4096]{2,1,0:T(8,128)(2,1)}), bf16[32,8,4096]{2,1,0:T(8,128)(2,1)}, u32[]{:S(2)}, u32[]{:S(2)}) %all-to-all-start) | async-done | bytes 2097184 | tf_op jit(solution)/shard_map/all_to_all | solution.py:55
  48.6 2.0 convolution_convert_fusion.3
  50.6 15.6 %all_to_all.30 = bf16[4,8,4096]{2,1,0:T(8,128)(2,1)S(1)} all-to-all(bf16[4,8,4096]{2,1,0:T(8,128)(2,1)S(1)} %broadcast_in_dim.14), channel_id=1, replica_groups=mesh['xl'=2,'y'=4,'zh'=4,'zl'=2,'xh'=2,'c'=2] {'zh'}, dimensions={0} | all-to-all | bytes 524288 | tf_op jit(solution)/shard_map/all_to_all | solution.py:47
  66.4 4.3 %collective-permute-start.4 = (f32[8,1]{0,1:T(1,128)S(1)}, f32[8,1]{0,1:T(1,128)S(1)}, u32[]{:S(2)}, u32[]{:S(2)}) collective-permute-start(f32[8,1]{0,1:T(1,128)S(1)} %bitcast.39), channel_id=1, source_target_pairs={{0,1},{1,0},{2,3},{3,2},{4,5},{5,4},{6,7},{7,6},{8,9},{9,8},{10,11... | collective-permute-start | bytes 104 | tf_op jit(solution)/shard_map/ppermute | solution.py:31
  71.8 32.5 %all_to_all.31 = bf16[32,8,4096]{2,1,0:T(8,128)(2,1)S(1)} all-to-all(bf16[32,8,4096]{2,1,0:T(8,128)(2,1)S(1)} %broadcast_in_dim.16), channel_id=1, replica_groups=mesh['xl'=2,'y'=4,'zh'=4,'zl'=2,'xh'=2,'c'=2] {'y','xh','xl','zl'}, dimensions={0} | all-to-all | bytes 4194304 | tf_op jit(solution)/shard_map/all_to_all | solution.py:47
  105.8 1.8 collective-permute-start.5
  110.0 2.1 convolution_convert_fusion
  112.1 4.8 %all-to-all-start.3 = ((bf16[32,8,4096]{2,1,0:T(8,128)(2,1)}), bf16[32,8,4096]{2,1,0:T(8,128)(2,1)}, u32[]{:S(2)}, u32[]{:S(2)}) async-start(bf16[32,8,4096]{2,1,0:T(8,128)(2,1)} %bitcast.36), calls=%async_computation.3 | async-start | bytes 4194304 | tf_op jit(solution)/shard_map/all_to_all | solution.py:55
  117.5 4.1 %collective-permute-done.7 = bf16[256,4096]{1,0:T(8,128)(2,1)} collective-permute-done((bf16[256,4096]{1,0:T(8,128)(2,1)}, bf16[256,4096]{1,0:T(8,128)(2,1)}, u32[]{:S(2)}, u32[]{:S(2)}) %collective-permute-start.7) | collective-permute-done | bytes 2097184 | tf_op jit(solution)/shard_map/ppermute | solution.py:31
  121.6 5.9 %maximum_select_fusion = bf16[256,8192]{1,0:T(8,128)(2,1)} fusion(bf16[256,4096]{1,0:T(8,128)(2,1)} %collective-permute-done.7, bf16[256,4096]{1,0:T(8,128)(2,1)} %bitcast.35, pred[]{:T(512)S(6)} %eq.55), kind=kLoop, calls=%fused_computation.10 | loop fusion | flops 18874368 | bytes 8388609 | tf_op jit(solution)/shard_map/jit(_where)/select_n | solution.py:155
  127.6 18.4 %all-to-all-done.3 = bf16[32,8,4096]{2,1,0:T(8,128)(2,1)} async-done(((bf16[32,8,4096]{2,1,0:T(8,128)(2,1)}), bf16[32,8,4096]{2,1,0:T(8,128)(2,1)}, u32[]{:S(2)}, u32[]{:S(2)}) %all-to-all-start.3) | async-done | bytes 2097184 | tf_op jit(solution)/shard_map/all_to_all | solution.py:55
  146.0 2.0 convolution_convert_fusion.2
  148.0 10.9 %all_to_all.32 = bf16[4,8,4096]{2,1,0:T(8,128)(2,1)S(1)} all-to-all(bf16[4,8,4096]{2,1,0:T(8,128)(2,1)S(1)} %broadcast_in_dim.17), channel_id=1, replica_groups=mesh['xl'=2,'y'=4,'zh'=4,'zl'=2,'xh'=2,'c'=2] {'zh'}, dimensions={0} | all-to-all | bytes 524288 | tf_op jit(solution)/shard_map/all_to_all | solution.py:47
  159.0 1.6 broadcast_in_dim.18
  160.6 6.7 %all-to-all-start.5 = ((bf16[32,8,4096]{2,1,0:T(8,128)(2,1)}), bf16[32,8,4096]{2,1,0:T(8,128)(2,1)}, u32[]{:S(2)}, u32[]{:S(2)}) async-start(bf16[32,8,4096]{2,1,0:T(8,128)(2,1)} %broadcast_in_dim.18), calls=%async_computation.5 | async-start | bytes 4194304 | tf_op jit(solution)/shard_map/all_to_all | solution.py:47
  167.3 27.2 %all-to-all-done.5 = bf16[32,8,4096]{2,1,0:T(8,128)(2,1)} async-done(((bf16[32,8,4096]{2,1,0:T(8,128)(2,1)}), bf16[32,8,4096]{2,1,0:T(8,128)(2,1)}, u32[]{:S(2)}, u32[]{:S(2)}) %all-to-all-start.5) | async-done | bytes 2097184 | tf_op jit(solution)/shard_map/all_to_all | solution.py:47
  194.6 2.3 %fusion.61 = f32[256,256]{1,0:T(8,128)S(1)} fusion(bf16[256,4096]{1,0:T(8,128)(2,1)S(1)} %pad_maximum_fusion.1, bf16[32,8,4096]{2,1,0:T(8,128)(2,1)} %all-to-all-done.5), kind=kOutput, calls=%fused_computation.126 | convolution fusion | flops 536870912 | bytes 4456448 | tf_op jit(solution)/shard_map/dot_general | solution.py:43
  198.3 3.1 %collective-permute-start.9 = (f32[256,128]{0,1:T(8,128)}, f32[256,128]{0,1:T(8,128)}, u32[]{:S(2)}, u32[]{:S(2)}) collective-permute-start(f32[256,128]{0,1:T(8,128)} %copy.22), channel_id=1, source_target_pairs={{0,1},{1,0},{2,3},{3,2},{4,5},{5,4},{6,7},{7,6},{8,9},{9,8},{10,11... | collective-permute-start | bytes 393224 | tf_op jit(solution)/shard_map/ppermute | solution.py:31
  201.4 2.5 %fusion.3 = bf16[256,4096]{1,0:T(8,128)(2,1)S(1)} fusion(bf16[256,4096]{1,0:T(8,128)(2,1)} %bitcast.13, bf16[256,4096]{1,0:T(8,128)(2,1)S(1)} %pad_maximum_fusion.1, bf16[256,128]{0,1:T(8,128)(2,1)S(1)} %collective-permute-done.6, bf16[256,128]{0,1:T(8,128)(2,1)S(1)} %maximum_convert_fusion), kind=kOutput, calls=%fused_computation.7 | convolution fusion | flops 541327360 | bytes 6422528 | tf_op jit(solution)/shard_map/dot_general | solution.py:43
  204.1 1.3 copy-done.5
  205.4 1.5 constant_dynamic-slice_fusion
  206.9 3.1 %collective-permute-start.8 = (bf16[2,4096]{1,0:T(2,128)(2,1)}, bf16[2,4096]{1,0:T(2,128)(2,1)S(1)}, u32[]{:S(2)}, u32[]{:S(2)}) collective-permute-start(bf16[2,4096]{1,0:T(2,128)(2,1)} %constant_dynamic-slice_fusion), channel_id=1, source_target_pairs={{0,0},{1,128},{2,2},{3,130},{4,4},{5,132},{6,6},{7,134},{8,8},{9,1... | collective-permute-start | bytes 49160 | tf_op jit(solution)/shard_map/ppermute | solution.py:31
  210.0 1.7 copy.21
  212.2 1.1 select_convert_fusion
  213.2 5.0 %fusion.1 = bf16[8192,128]{1,0:T(8,128)(2,1)} fusion(bf16[256,8192]{1,0:T(8,128)(2,1)} %maximum_select_fusion, bf16[256,128]{0,1:T(8,128)(2,1)S(1)} %select_convert_fusion, bf16[8192,128]{1,0:T(8,128)(2,1)S(1)} %copy-done.2), kind=kOutput, calls=%fused_computation.2 | convolution fusion | flops 541065216 | bytes 8454144 | tf_op jit(solution)/shard_map/dot_general | solution.py:43
  218.2 1.3 constant_dynamic-update-slice_fusion
  (88 shorter events, 15.2 us)
Async XLA Ops:
  0.6 3.3 %copy-start.9 = (bf16[1,128,8192]{2,1,0:T(8,128)(2,1)S(1)}, bf16[1,128,8192]{2,1,0:T(8,128)(2,1)}, u32[]{:S(2)}) copy-start(bf16[1,128,8192]{2,1,0:T(8,128)(2,1)} %param.11) | copy-start | bytes 6291460
  3.9 4.4 %copy-start.11 = (bf16[256,64]{0,1:T(8,128)(2,1)S(1)}, bf16[256,64]{0,1:T(8,128)(2,1)}, u32[]{:S(2)}) copy-start(bf16[256,64]{0,1:T(8,128)(2,1)} %param.9) | copy-start | bytes 98308
  3.9 4.6 %copy-start.14 = (s32[128]{0:T(128)S(1)}, s32[128]{0:T(128)}, u32[]{:S(2)}) copy-start(s32[128]{0:T(128)} %param.17) | copy-start | bytes 1540
  3.9 4.8 %copy-start.15 = (bf16[1,256,128]{2,1,0:T(8,128)(2,1)S(1)}, bf16[1,256,128]{2,1,0:T(8,128)(2,1)}, u32[]{:S(2)}) copy-start(bf16[1,256,128]{2,1,0:T(8,128)(2,1)} %param.10) | copy-start | bytes 196612
  5.1 5.7 %collective-permute-start.1 = (bf16[128,4096]{1,0:T(8,128)(2,1)}, bf16[128,4096]{1,0:T(8,128)(2,1)S(1)}, u32[]{:S(2)}, u32[]{:S(2)}) collective-permute-start(bf16[128,4096]{1,0:T(8,128)(2,1)} %get-tuple-element.34), channel_id=1, source_target_pairs={{0,1},{1,0},{2,3},{3,2},{4,5},{5,4},{6,7},{7,6},{8,9},{9,8},{10,11... | collective-permute-start | bytes 3145736 | tf_op jit(solution)/shard_map/ppermute | solution.py:31
  9.4 1.4 collective-permute-start
  13.3 6.9 %copy-start.16 = (s32[256]{0:T(256)S(1)}, s32[256]{0:T(256)}, u32[]{:S(2)}) copy-start(s32[256]{0:T(256)} %param.16) | copy-start | bytes 3076
  13.3 7.0 %copy-start.1 = (bf16[8192,128]{1,0:T(8,128)(2,1)S(1)}, bf16[8192,128]{1,0:T(8,128)(2,1)}, u32[]{:S(2)}) copy-start(bf16[8192,128]{1,0:T(8,128)(2,1)} %param.12) | copy-start | bytes 6291460
  13.3 35.3 %all-to-all-start = ((bf16[32,8,4096]{2,1,0:T(8,128)(2,1)}), bf16[32,8,4096]{2,1,0:T(8,128)(2,1)}, u32[]{:S(2)}, u32[]{:S(2)}) async-start(bf16[32,8,4096]{2,1,0:T(8,128)(2,1)} %bitcast.37), calls=%async_computation | async-start | bytes 4194304 | tf_op jit(solution)/shard_map/all_to_all | solution.py:55
  20.3 1.6 copy-start.3
  20.5 3.1 %collective-permute-start.2 = (bf16[4096,128]{1,0:T(8,128)(2,1)S(1)}, bf16[4096,128]{1,0:T(8,128)(2,1)S(1)}, u32[]{:S(2)}, u32[]{:S(2)}) collective-permute-start(bf16[4096,128]{1,0:T(8,128)(2,1)S(1)} %get-tuple-element.32), channel_id=1, source_target_pairs={{0,1},{1,0},{2,3},{3,2},{4,5},{5,4},{6,7},{7,6},{8,9},{9,8},{10,11... | collective-permute-start | bytes 3145736 | tf_op jit(solution)/shard_map/ppermute | solution.py:31
  22.1 1.5 copy-start.12
  22.1 3.0 %collective-permute-start.3 = (bf16[128,4096]{1,0:T(8,128)(2,1)S(1)}, bf16[128,4096]{1,0:T(8,128)(2,1)S(1)}, u32[]{:S(2)}, u32[]{:S(2)}) collective-permute-start(bf16[128,4096]{1,0:T(8,128)(2,1)S(1)} %get-tuple-element.30), channel_id=1, source_target_pairs={{0,1},{1,0},{2,3},{3,2},{4,5},{5,4},{6,7},{7,6},{8,9},{9,8},{10,11... | collective-permute-start | bytes 3145736 | tf_op jit(solution)/shard_map/ppermute | solution.py:31
  66.4 5.1 %collective-permute-start.4 = (f32[8,1]{0,1:T(1,128)S(1)}, f32[8,1]{0,1:T(1,128)S(1)}, u32[]{:S(2)}, u32[]{:S(2)}) collective-permute-start(f32[8,1]{0,1:T(1,128)S(1)} %bitcast.39), channel_id=1, source_target_pairs={{0,1},{1,0},{2,3},{3,2},{4,5},{5,4},{6,7},{7,6},{8,9},{9,8},{10,11... | collective-permute-start | bytes 104 | tf_op jit(solution)/shard_map/ppermute | solution.py:31
  71.8 32.5 %copy-start.8 = (bf16[4096,256]{1,0:T(8,128)(2,1)S(1)}, bf16[4096,256]{1,0:T(8,128)(2,1)}, u32[]{:S(2)}) copy-start(bf16[4096,256]{1,0:T(8,128)(2,1)} %pad_maximum_fusion) | copy-start | bytes 6291460
  104.4 1.4 copy-start
  104.4 3.2 %copy-start.17 = (bf16[128]{0:T(256)(128)(2,1)S(1)}, bf16[128]{0:T(256)(128)(2,1)}, u32[]{:S(2)}) copy-start(bf16[128]{0:T(256)(128)(2,1)} %param.13) | copy-start | bytes 772
  105.8 2.8 %collective-permute-start.5 = (f32[256,128]{0,1:T(8,128)S(1)}, f32[256,128]{0,1:T(8,128)S(1)}, u32[]{:S(2)}, u32[]{:S(2)}) collective-permute-start(f32[256,128]{0,1:T(8,128)S(1)} %slice.25), channel_id=1, source_target_pairs={{0,1},{1,0},{2,3},{3,2},{4,5},{5,4},{6,7},{7,6},{8,9},{9,8},{10,11... | collective-permute-start | bytes 393224 | tf_op jit(solution)/shard_map/ppermute | solution.py:31
  107.6 4.5 %copy-start.13 = (f32[128]{0:T(128)}, f32[128]{0:T(128)S(1)}, u32[]{:S(2)}) copy-start(f32[128]{0:T(128)S(1)} %convert_element_type.96) | copy-start | bytes 1540
  108.7 1.4 collective-permute-start.6
  112.1 33.9 %all-to-all-start.3 = ((bf16[32,8,4096]{2,1,0:T(8,128)(2,1)}), bf16[32,8,4096]{2,1,0:T(8,128)(2,1)}, u32[]{:S(2)}, u32[]{:S(2)}) async-start(bf16[32,8,4096]{2,1,0:T(8,128)(2,1)} %bitcast.36), calls=%async_computation.3 | async-start | bytes 4194304 | tf_op jit(solution)/shard_map/all_to_all | solution.py:55
  116.9 4.8 %collective-permute-start.7 = (bf16[256,4096]{1,0:T(8,128)(2,1)}, bf16[256,4096]{1,0:T(8,128)(2,1)}, u32[]{:S(2)}, u32[]{:S(2)}) collective-permute-start(bf16[256,4096]{1,0:T(8,128)(2,1)} %bitcast.34), channel_id=1, source_target_pairs={{0,1},{1,0},{2,3},{3,2},{4,5},{5,4},{6,7},{7,6},{8,9},{9,8},{10,11... | collective-permute-start | bytes 6291464 | tf_op jit(solution)/shard_map/ppermute | solution.py:31
  159.0 1.6 copy-start.10
  160.6 34.0 %all-to-all-start.5 = ((bf16[32,8,4096]{2,1,0:T(8,128)(2,1)}), bf16[32,8,4096]{2,1,0:T(8,128)(2,1)}, u32[]{:S(2)}, u32[]{:S(2)}) async-start(bf16[32,8,4096]{2,1,0:T(8,128)(2,1)} %broadcast_in_dim.18), calls=%async_computation.5 | async-start | bytes 4194304 | tf_op jit(solution)/shard_map/all_to_all | solution.py:47
  198.3 13.8 %collective-permute-start.9 = (f32[256,128]{0,1:T(8,128)}, f32[256,128]{0,1:T(8,128)}, u32[]{:S(2)}, u32[]{:S(2)}) collective-permute-start(f32[256,128]{0,1:T(8,128)} %copy.22), channel_id=1, source_target_pairs={{0,1},{1,0},{2,3},{3,2},{4,5},{5,4},{6,7},{7,6},{8,9},{9,8},{10,11... | collective-permute-start | bytes 393224 | tf_op jit(solution)/shard_map/ppermute | solution.py:31
  201.4 2.5 %copy-start.4 = (bf16[128,8192]{1,0:T(8,128)(2,1)S(1)}, bf16[128,8192]{1,0:T(8,128)(2,1)}, u32[]{:S(2)}) copy-start(bf16[128,8192]{1,0:T(8,128)(2,1)} %copy.27) | copy-start | bytes 6291460
  203.9 9.3 %copy-start.2 = (bf16[8192,128]{1,0:T(8,128)(2,1)S(1)}, bf16[8192,128]{1,0:T(8,128)(2,1)}, u32[]{:S(2)}) copy-start(bf16[8192,128]{1,0:T(8,128)(2,1)} %param.12) | copy-start | bytes 6291460
  204.1 1.3 copy-start.5
  205.4 12.8 %collective-permute-start.10 = (bf16[128,4096]{1,0:T(8,128)(2,1)S(1)}, bf16[128,4096]{1,0:T(8,128)(2,1)}, u32[]{:S(2)}, u32[]{:S(2)}) collective-permute-start(bf16[128,4096]{1,0:T(8,128)(2,1)S(1)} %get-tuple-element.27), channel_id=1, source_target_pairs={{0,1},{1,0},{2,3},{3,2},{4,5},{5,4},{6,7},{7,6},{8,9},{9,8},{10,11... | collective-permute-start | bytes 3145736 | tf_op jit(solution)/shard_map/ppermute | solution.py:31
  206.9 5.3 %collective-permute-start.8 = (bf16[2,4096]{1,0:T(2,128)(2,1)}, bf16[2,4096]{1,0:T(2,128)(2,1)S(1)}, u32[]{:S(2)}, u32[]{:S(2)}) collective-permute-start(bf16[2,4096]{1,0:T(2,128)(2,1)} %constant_dynamic-slice_fusion), channel_id=1, source_target_pairs={{0,0},{1,128},{2,2},{3,130},{4,4},{5,132},{6,6},{7,134},{8,8},{9,1... | collective-permute-start | bytes 49160 | tf_op jit(solution)/shard_map/ppermute | solution.py:31
  213.2 5.0 %copy-start.6 = (bf16[128,8192]{1,0:T(8,128)(2,1)S(1)}, bf16[128,8192]{1,0:T(8,128)(2,1)}, u32[]{:S(2)}) copy-start(bf16[128,8192]{1,0:T(8,128)(2,1)} %copy-done.5) | copy-start | bytes 6291460
  219.6 1.3 copy-start.7

commit v4 on v3

v4 whole, which is shorter than its diff:
```python
import jax
import jax.numpy as jnp
from jax import lax
from jax.experimental import pallas as pl
from jax.experimental.pallas import tpu as pltpu
from jax.sharding import Mesh
from jax.sharding import PartitionSpec as P

BOS = 128000


STEP_RATE = 0.5

AXES = ("xl", "y", "z", "xh", "c")
SIZES = (2, 4, 8, 2, 2)
TENSOR = ("y", "z", "xh", "c")
NEAR = 8
FAR = 16


def device(x, y, z, c):
    return (((x % 2 * 4 + y) * 8 + z % 8) * 2 + x // 2) * 2 + c


NEAR_GROUPS = [
    [device(x, y, 2 * w + p, 0) for x in range(4) for p in range(2)]
    for y in range(4)
    for w in range(4)
] + [
    [device(x, y, 2 * w + 1 + p, 1) for y in range(4) for p in range(2)]
    for x in range(4)
    for w in range(4)
]
FAR_GROUPS = [
    [device(x, y, 2 * w + p, 0) for y in range(4) for w in range(4)]
    for x in range(4)
    for p in range(2)
] + [
    [device(x, y, 2 * w + 1 + p, 1) for x in range(4) for w in range(4)]
    for y in range(4)
    for p in range(2)
]


def chip_of(slot, core):
    near, far = slot // FAR, slot % FAR
    line, pair, other, deep = near // 2, near % 2, far // 4, far % 4
    x = jnp.where(core == 0, line, other)
    y = jnp.where(core == 0, other, line)
    z = (2 * deep + pair + core) % 8
    return (y * 8 + z) * 4 + x


def exchange(value, swap):
    route = []
    for xl in range(2):
        for y in range(4):
            for z in range(8):
                for xh in range(2):
                    for c in range(2):
                        xl2, c2 = swap(xl, c)
                        route.append(
                            (device(xh * 2 + xl, y, z, c), device(xh * 2 + xl2, y, z, c2))
                        )
    return lax.ppermute(value, AXES, route)


def other_core(value):
    return exchange(value, lambda xl, c: (xl, 1 - c))


def core_and_section(value):
    return exchange(value, lambda xl, c: (c, xl))


def matmul(a, b, dims=((1,), (0,)), **how):
    return lax.dot_general(
        a, b, (dims, ((), ())), preferred_element_type=jnp.float32, **how
    )


def all_to_all(pieces, groups):
    return lax.all_to_all(pieces, AXES, 0, 0, axis_index_groups=groups, tiled=True)


def spread(value, groups, count):
    stacked = jnp.broadcast_to(value[None], (count,) + value.shape)
    return all_to_all(stacked, groups).reshape(-1, value.shape[1])


def near_sum(partial):
    tokens, width = partial.shape
    depth = tokens // NEAR
    pieces = all_to_all(partial.reshape(NEAR, depth, width), NEAR_GROUPS)
    to = lax.broadcasted_iota(jnp.int32, (depth, tokens), 0)
    of = lax.broadcasted_iota(jnp.int32, (depth, tokens), 1)
    adds = (of % depth == to).astype(jnp.bfloat16)
    return matmul(adds, pieces.reshape(tokens, width)).astype(jnp.bfloat16)


def far_sum(chunk):
    pieces = all_to_all(chunk.reshape(FAR, -1, chunk.shape[1]), FAR_GROUPS)
    return jnp.sum(pieces.astype(jnp.float32), axis=0)


def place(core_ref, kept_ref, back_ref, out_ref, sems):
    half = kept_ref.shape[1]
    core = core_ref[0]
    copies = [
        pltpu.make_async_copy(
            ref, out_ref.at[:, pl.ds(pl.multiple_of(at * half, half), half)], sems.at[i]
        )
        for i, (ref, at) in enumerate(((kept_ref, core), (back_ref, 1 - core)))
    ]
    for copy in copies:
        copy.start()
    for copy in copies:
        copy.wait()


def join_columns(core, kept, back):
    rows, half = kept.shape
    return pl.pallas_call(
        place,
        grid_spec=pltpu.PrefetchScalarGridSpec(
            num_scalar_prefetch=1,
            grid=(1,),
            in_specs=[pl.BlockSpec(memory_space=pl.ANY)] * 2,
            out_specs=pl.BlockSpec(memory_space=pl.ANY),
            scratch_shapes=[pltpu.SemaphoreType.DMA((2,))],
        ),
        out_shape=jax.ShapeDtypeStruct((rows, 2 * half), kept.dtype),
        cost_estimate=pl.CostEstimate(
            flops=0, bytes_accessed=8 * rows * half, transcendentals=0
        ),
    )(jnp.reshape(core, (1,)).astype(jnp.int32), kept, back)


def shards(
    resid_in, contexts, out_proj, encoder, enc_bias, decoder, dec_bias, token_ids, owner_map
):
    tokens, width = resid_in.shape
    own, features = decoder.shape
    half = features // 2
    blocks = owner_map.shape[0]
    block_rows = tokens // blocks
    y, z, xh, xl, core = (lax.axis_index(a) for a in ("y", "z", "xh", "xl", "c"))
    chip = (y * 8 + z) * 4 + xh * 2 + xl

    def mine(weight, axis):
        return lax.dynamic_slice_in_dim(weight, core * half, half, axis)

    def theirs(weight, axis):
        return lax.dynamic_slice_in_dim(weight, (1 - core) * half, half, axis)

    proj = out_proj[0]
    proj_other = other_core(theirs(proj, 1))
    context_other = other_core(contexts[0])
    resid_other = other_core(resid_in)

    row = lax.broadcasted_iota(jnp.int32, (tokens, tokens), 0)
    old = lax.broadcasted_iota(jnp.int32, (tokens, tokens), 1)
    same_place = row % block_rows == old % block_rows
    at = chip_of(row // block_rows, core)
    owner_of_row = jnp.repeat(owner_map, block_rows)
    order = ((owner_of_row[None, :] == at) & same_place).astype(jnp.bfloat16)
    across = (chip_of(old // block_rows, 1 - core) == at) & same_place
    kept = (token_ids.reshape(blocks, block_rows) != BOS).astype(jnp.float32)
    mask_rows = jnp.sum(jnp.where((owner_map == chip)[:, None], kept, 0.0), axis=0)[:, None]

    start = ((y * 8 + z) * 2 + xh) * 2 * width
    owns = (start // half == core) & (xl == 0)

    def placed(which):
        column = lax.broadcasted_iota(jnp.int32, (width, half), 1)
        target = lax.broadcasted_iota(jnp.int32, (width, half), 0) + (
            start % half + which * width
        )
        return ((column == target) & owns).astype(jnp.bfloat16)

    joined = matmul(
        order,
        jnp.concatenate([contexts[0], context_other, resid_in, resid_other], axis=1),
    ).astype(jnp.bfloat16)
    proj_both = jnp.concatenate(
        [mine(proj, 1), proj_other, placed(core), placed(1 - core)], axis=0
    )
    partial = matmul(joined, proj_both).astype(jnp.bfloat16)

    encoder_out, decoder_out, _ = lax.optimization_barrier(
        (theirs(encoder, 0), theirs(decoder, 1), partial)
    )
    encoder_own, encoder_other = mine(encoder, 0), other_core(encoder_out)
    decoder_both = jnp.concatenate([mine(decoder, 1), other_core(decoder_out)], axis=0)
    my_bias = mine(dec_bias, 0).astype(jnp.float32)
    chunk = near_sum(partial)
    chunk, encoder_own, encoder_other, decoder_both, mask_rows, my_bias, across = (
        lax.optimization_barrier(
            (chunk, encoder_own, encoder_other, decoder_both, mask_rows, my_bias, across)
        )
    )
    values = far_sum(chunk).astype(jnp.bfloat16).astype(jnp.float32)
    squares = jnp.sum(values * values, axis=1, keepdims=True)
    squares = squares + other_core(squares)
    inverse_rms = lax.rsqrt(squares / features + 1e-05)
    my_centred = (values * inverse_rms - my_bias).astype(jnp.bfloat16)
    centred = spread(spread(my_centred, FAR_GROUPS, FAR), NEAR_GROUPS, NEAR)

    exact = dict(precision=lax.Precision.HIGHEST)

    def both_halves(own_weight, other_weight, values, dims):
        sent = other_core(matmul(other_weight, values, dims))
        kept = matmul(own_weight, values, dims)
        return kept + matmul(sent, across.astype(jnp.float32), ((1,), (1,)), **exact)

    before_relu = both_halves(encoder_own, encoder_other, centred, ((0,), (1,)))
    before_relu = before_relu + enc_bias.astype(jnp.float32)[:, None]
    latents = jnp.maximum(before_relu, 0.0).astype(jnp.bfloat16)
    across_low = across.astype(jnp.bfloat16)
    latents_other = matmul(other_core(latents), across_low, ((1,), (1,))).astype(jnp.bfloat16)
    latents_both = jnp.concatenate([latents, latents_other], axis=0)
    partial = matmul(latents_both, decoder_both, ((0,), (0,))).astype(jnp.bfloat16)
    later, _ = lax.optimization_barrier((centred, partial))
    centred_other = matmul(
        other_core(later), across_low, ((0,), (1,))
    ).astype(jnp.bfloat16)
    centred_own = later.T
    centred_full = jnp.where(
        core == 0,
        jnp.concatenate([centred_own, centred_other], axis=0),
        jnp.concatenate([centred_other, centred_own], axis=0),
    )
    chunk = near_sum(partial)
    chunk, centred_full = lax.optimization_barrier((chunk, centred_full))
    rebuilt = far_sum(chunk)
    my_error = (mask_rows * (rebuilt - my_centred.astype(jnp.float32))).astype(jnp.bfloat16)
    owned_error = core_and_section(my_error)
    error = spread(spread(my_error, FAR_GROUPS, FAR), NEAR_GROUPS, NEAR)
    step_size = STEP_RATE / tokens

    def stepped(weight, grad):
        return (weight.astype(jnp.float32) - step_size * grad).astype(jnp.bfloat16)

    decoder_own, decoder_other = decoder_both[:own], decoder_both[own:]
    backward = both_halves(decoder_own, decoder_other, error, ((1,), (1,)))
    pre_grad = lax.optimization_barrier(
        jnp.where(before_relu > 0.0, backward, 0.0).astype(jnp.bfloat16)
    )
    back = other_core(stepped(decoder_other, matmul(latents_other, error)))
    new_decoder = join_columns(core, stepped(decoder_own, matmul(latents, error)), back)
    new_encoder = stepped(encoder, matmul(centred_full, pre_grad, ((1,), (1,))))
    return (owned_error, new_encoder, new_decoder)


def solution(mesh):
    cut = Mesh(mesh.devices.reshape(SIZES), AXES)
    return jax.shard_map(
        shards,
        mesh=cut,
        in_specs=(
            P(None, TENSOR),
            P("xl", None, TENSOR),
            P("xl", TENSOR, None),
            P(None, AXES),
            P(AXES),
            P(AXES, None),
            P(),
            P(),
            P(),
        ),
        out_specs=(
            P(TENSOR, "xl"),
            P(None, AXES),
            P(AXES, None),
        ),
        check_vma=False,
    )
```

time: 222 us -> 267 us (1.20)
  Pallas kernels: 0 us -> 64.6 us
  waiting for transfers between devices: 77.2 us -> 31 us
  blocking collectives: 59 us -> 84.9 us
  matrix products: 20.5 us -> 25.2 us
  other arithmetic: 9.58 us -> 6.36 us
    pallas_call x0 -> x1, Pallas kernels: none -> 64.6 us  [join_columns(): pl.pallas_call(place, grid_spec=pltpu.PrefetchScalarGridSpec(num_scalar_p...]
    all_to_all x3, waiting for transfers between devices: 69 us -> 12.9 us  [all_to_all(): lax.all_to_all(pieces, AXES, 0, 0, axis_index_groups=groups, tiled=True)]
    all_to_all x3 -> x5, blocking collectives: 59 us -> 84.9 us  [all_to_all(): lax.all_to_all(pieces, AXES, 0, 0, axis_index_groups=groups, tiled=True)]
    ppermute x11 -> x12, waiting for transfers between devices: 8.21 us -> 18.1 us  [exchange(): return lax.ppermute(value, AXES, route)]
    dot_general x10 -> x15, matrix products: 20.5 us -> 25.2 us  [matmul(): lax.dot_general(a, b, (dims, ((), ())), preferred_element_type=jnp.float3...]
    select_n x1, other arithmetic: 5.93 us -> 2.56 us  [shards(): jnp.where(core == 0, jnp.concatenate([centred_own, centred_other], axis=0...]
    unnamed x40 -> x34, local copies, waits for them, and re-layouts: 6.36 us -> 5.04 us
    ppermute x11 -> x12, starting transfers between devices: 18.1 us -> 18.7 us  [exchange(): return lax.ppermute(value, AXES, route)]
  transfers between devices with their start and end apart: 14 -> 15, of which waited for: 9 -> 9; matrix products, arithmetic and copies ran while one was open for 10% -> 8% of each run, Pallas kernels for 0% -> 0%
where the time goes in v4:
time: 267 us; the launch traced here: 266 us
  blocking collectives  84.9 us (32%)
  Pallas kernels  64.6 us (24%)
  starting transfers between devices  37.1 us (14%)
  waiting for transfers between devices  31 us (12%)
  matrix products  25.2 us (9%)
  local copies, waits for them, and re-layouts  16.2 us (6%)
  other arithmetic  6.36 us (2%)
    all_to_all x5, blocking collectives, all_to_all(): lax.all_to_all(pieces, AXES, 0, 0, axis_index_groups=groups, tiled=True)  84.9 us
    pallas_call x1, Pallas kernels, join_columns(): pl.pallas_call(place, grid_spec=pltpu.PrefetchScalarGridSpec(num_scalar_p...  64.6 us
    dot_general x15, matrix products, matmul(): lax.dot_general(a, b, (dims, ((), ())), preferred_element_type=jnp.float3...  25.2 us
    ppermute x12, starting transfers between devices, exchange(): return lax.ppermute(value, AXES, route)  18.7 us
    all_to_all x3, starting transfers between devices, all_to_all(): lax.all_to_all(pieces, AXES, 0, 0, axis_index_groups=groups, tiled=True)  18.4 us
    ppermute x12, waiting for transfers between devices, exchange(): return lax.ppermute(value, AXES, route)  18.1 us
    all_to_all x3, waiting for transfers between devices, all_to_all(): lax.all_to_all(pieces, AXES, 0, 0, axis_index_groups=groups, tiled=True)  12.9 us
  transfers between devices with their start and end apart: 15, of which 9 were waited for; matrix products, arithmetic and copies ran while one was open for 8% of the time, Pallas kernels for 0%

profile of v4, /device:TPU:1, one launch (start us, length us, event | category | flops | bytes accessed | tf_op | source)
XLA Modules:
  0.0 266.5 jit_solution(9104831972193570183)
XLA Ops:
  1.5 3.3 %collective-permute-start.1 = (bf16[256,64]{1,0:T(8,128)(2,1)S(1)}, bf16[256,64]{1,0:T(8,128)(2,1)S(1)}, u32[]{:S(2)}, u32[]{:S(2)}) collective-permute-start(bf16[256,64]{1,0:T(8,128)(2,1)S(1)} %copy.16), channel_id=1, source_target_pairs={{0,1},{1,0},{2,3},{3,2},{4,5},{5,4},{6,7},{7,6},{8,9},{9,8},{10,11... | collective-permute-start | bytes 98312 | tf_op jit(solution)/shard_map/ppermute | solution.py:65
  4.9 1.7 dynamic-slice_bitcast_fusion.1
  7.9 1.7 collective-permute-done.2
  9.6 4.5 %convolution_convert_fusion.2 = bf16[256,4096]{1,0:T(8,128)(2,1)} fusion(bf16[64,4096]{1,0:T(8,128)(2,1)S(1)} %get-tuple-element.38, bf16[64,4096]{1,0:T(8,128)(2,1)S(1)} %get-tuple-element.37, bf16[128,4096]{1,0:T(8,128)(2,1)} %collective-permute-done.2, bf16[128,4096]{1,0:T(8,128)(2,1)S(1)} %get-tuple-element.31, ...), kind=kOutput, calls=%fused_computation.5 | convolution fusion | flops 875593728 | bytes 5445125 | tf_op jit(solution)/shard_map/dot_general | solution.py:77
  14.0 8.2 %all-to-all-start = ((bf16[8,32,4096]{2,1,0:T(8,128)(2,1)}), bf16[8,32,4096]{2,1,0:T(8,128)(2,1)}, u32[]{:S(2)}, u32[]{:S(2)}) async-start(bf16[8,32,4096]{2,1,0:T(8,128)(2,1)} %bitcast.52), calls=%async_computation | async-start | bytes 4194304 | tf_op jit(solution)/shard_map/all_to_all | solution.py:83
  29.0 1.7 pad_maximum_fusion
  30.7 6.8 %all-to-all-done = bf16[8,32,4096]{2,1,0:T(8,128)(2,1)} async-done(((bf16[8,32,4096]{2,1,0:T(8,128)(2,1)}), bf16[8,32,4096]{2,1,0:T(8,128)(2,1)}, u32[]{:S(2)}, u32[]{:S(2)}) %all-to-all-start) | async-done | bytes 2097184 | tf_op jit(solution)/shard_map/all_to_all | solution.py:83
  37.4 2.0 convolution_convert_fusion.4
  40.4 18.3 %all_to_all.40 = bf16[16,2,4096]{2,1,0:T(2,128)(2,1)S(1)} all-to-all(bf16[16,2,4096]{2,1,0:T(2,128)(2,1)} %reshape.128), channel_id=1, replica_groups={{0,8,16,24,32,40,48,56,64,72,80,88,96,104,112,120},{4,12,20,28,36,44,52..., dimensions={0} | all-to-all | bytes 524288 | tf_op jit(solution)/shard_map/all_to_all | solution.py:83
  59.1 2.1 collective-permute-start.5
  62.3 14.8 %all_to_all.41 = bf16[16,2,4096]{2,1,0:T(2,128)(2,1)} all-to-all(bf16[16,2,4096]{2,1,0:T(2,128)(2,1)S(1)} %broadcast_in_dim.57), channel_id=1, replica_groups={{0,8,16,24,32,40,48,56,64,72,80,88,96,104,112,120},{4,12,20,28,36,44,52..., dimensions={0} | all-to-all | bytes 524288 | tf_op jit(solution)/shard_map/all_to_all | solution.py:83
  78.4 21.0 %all_to_all.42 = bf16[8,32,4096]{2,1,0:T(8,128)(2,1)S(1)} all-to-all(bf16[8,32,4096]{2,1,0:T(8,128)(2,1)S(1)} %broadcast_in_dim.59), channel_id=1, replica_groups={{0,4,128,132,2,6,130,134},{8,12,136,140,10,14,138,142},{16,20,144,148,1..., dimensions={0} | all-to-all | bytes 4194304 | tf_op jit(solution)/shard_map/all_to_all | solution.py:83
  99.4 2.8 %fusion.123 = f32[128,256]{1,0:T(8,128)S(1)} fusion(bf16[4096,128]{1,0:T(8,128)(2,1)} %collective-permute-done.3, bf16[256,4096]{1,0:T(8,128)(2,1)S(1)} %bitcast.46), kind=kOutput, calls=%fused_computation.186 | convolution fusion | flops 268435456 | bytes 3276800 | tf_op jit(solution)/shard_map/dot_general | solution.py:77
  102.2 3.2 %collective-permute-start.6 = (f32[128,256]{1,0:T(8,128)S(1)}, f32[128,256]{1,0:T(8,128)S(1)}, u32[]{:S(2)}, u32[]{:S(2)}) collective-permute-start(f32[128,256]{1,0:T(8,128)S(1)} %fusion.123), channel_id=1, source_target_pairs={{0,1},{1,0},{2,3},{3,2},{4,5},{5,4},{6,7},{7,6},{8,9},{9,8},{10,11... | collective-permute-start | bytes 393224 | tf_op jit(solution)/shard_map/ppermute | solution.py:65
  109.2 2.1 convolution_convert_fusion.1
  111.3 4.7 %all-to-all-start.4 = ((bf16[8,32,4096]{2,1,0:T(8,128)(2,1)}), bf16[8,32,4096]{2,1,0:T(8,128)(2,1)}, u32[]{:S(2)}, u32[]{:S(2)}) async-start(bf16[8,32,4096]{2,1,0:T(8,128)(2,1)} %bitcast.50), calls=%async_computation.4 | async-start | bytes 4194304 | tf_op jit(solution)/shard_map/all_to_all | solution.py:83
  116.4 2.4 copy.17
  120.3 2.4 convolution_convert_fusion
  122.7 2.6 maximum_select_fusion
  125.3 6.2 %all-to-all-done.4 = bf16[8,32,4096]{2,1,0:T(8,128)(2,1)} async-done(((bf16[8,32,4096]{2,1,0:T(8,128)(2,1)}), bf16[8,32,4096]{2,1,0:T(8,128)(2,1)}, u32[]{:S(2)}, u32[]{:S(2)}) %all-to-all-start.4) | async-done | bytes 2097184 | tf_op jit(solution)/shard_map/all_to_all | solution.py:83
  131.4 2.0 convolution_convert_fusion.3
  133.7 14.9 %all_to_all.43 = bf16[16,2,4096]{2,1,0:T(2,128)(2,1)S(1)} all-to-all(bf16[16,2,4096]{2,1,0:T(2,128)(2,1)S(1)} %reshape.132), channel_id=1, replica_groups={{0,8,16,24,32,40,48,56,64,72,80,88,96,104,112,120},{4,12,20,28,36,44,52..., dimensions={0} | all-to-all | bytes 524288 | tf_op jit(solution)/shard_map/all_to_all | solution.py:83
  149.1 15.9 %all_to_all.44 = bf16[16,2,4096]{2,1,0:T(2,128)(2,1)S(1)} all-to-all(bf16[16,2,4096]{2,1,0:T(2,128)(2,1)S(1)} %broadcast_in_dim.60), channel_id=1, replica_groups={{0,8,16,24,32,40,48,56,64,72,80,88,96,104,112,120},{4,12,20,28,36,44,52..., dimensions={0} | all-to-all | bytes 524288 | tf_op jit(solution)/shard_map/all_to_all | solution.py:83
  165.1 1.6 broadcast_in_dim.62
  166.7 5.5 %all-to-all-start.7 = ((bf16[8,32,4096]{2,1,0:T(8,128)(2,1)}), bf16[8,32,4096]{2,1,0:T(8,128)(2,1)S(1)}, u32[]{:S(2)}, u32[]{:S(2)}) async-start(bf16[8,32,4096]{2,1,0:T(8,128)(2,1)} %broadcast_in_dim.62), calls=%async_computation.7 | async-start | bytes 4194304 | tf_op jit(solution)/shard_map/all_to_all | solution.py:83
  172.2 5.4 %collective-permute-start.9 = (bf16[2,4096]{1,0:T(2,128)(2,1)S(1)}, bf16[2,4096]{1,0:T(2,128)(2,1)S(1)}, u32[]{:S(2)}, u32[]{:S(2)}) collective-permute-start(bf16[2,4096]{1,0:T(2,128)(2,1)S(1)} %multiply_convert_fusion), channel_id=1, source_target_pairs={{0,0},{1,128},{2,2},{3,130},{4,4},{5,132},{6,6},{7,134},{8,8},{9,1... | collective-permute-start | bytes 49160 | tf_op jit(solution)/shard_map/ppermute | solution.py:65
  177.6 11.3 %collective-permute-done.9 = bf16[2,4096]{1,0:T(2,128)(2,1)S(1)} collective-permute-done((bf16[2,4096]{1,0:T(2,128)(2,1)S(1)}, bf16[2,4096]{1,0:T(2,128)(2,1)S(1)}, u32[]{:S(2)}, u32[]{:S(2)}) %collective-permute-start.9) | collective-permute-done | bytes 16416 | tf_op jit(solution)/shard_map/ppermute | solution.py:65
  188.8 2.2 fusion.16
  191.6 2.5 collective-permute-start.10
  194.2 1.6 subtract_convert_fusion.1.kept_ref
  197.7 2.6 fusion.1
  201.2 64.6 %shard_map.112 = bf16[128,8192]{1,0:T(8,128)(2,1)} custom-call(s32[1]{0:T(128)} %bitcast.14.core_ref, bf16[128,4096]{1,0:T(8,128)(2,1)} %subtract_convert_fusion.1.kept_ref, bf16[128,4096]{1,0:T(8,128)(2,1)} %copy-done.9), custom_call_target="tpu_custom_call" | custom-call | bytes 4194304 | tf_op jit(solution)/shard_map/pallas_call | solution.py:123
  (90 shorter events, 23.0 us)
Async XLA Ops:
  1.5 6.3 %collective-permute-start.1 = (bf16[256,64]{1,0:T(8,128)(2,1)S(1)}, bf16[256,64]{1,0:T(8,128)(2,1)S(1)}, u32[]{:S(2)}, u32[]{:S(2)}) collective-permute-start(bf16[256,64]{1,0:T(8,128)(2,1)S(1)} %copy.16), channel_id=1, source_target_pairs={{0,1},{1,0},{2,3},{3,2},{4,5},{5,4},{6,7},{7,6},{8,9},{9,8},{10,11... | collective-permute-start | bytes 98312 | tf_op jit(solution)/shard_map/ppermute | solution.py:65
  4.8 3.0 %collective-permute-start = (bf16[256,128]{1,0:T(8,128)(2,1)}, bf16[256,128]{1,0:T(8,128)(2,1)S(1)}, u32[]{:S(2)}, u32[]{:S(2)}) collective-permute-start(bf16[256,128]{1,0:T(8,128)(2,1)} %bitcast.54), channel_id=1, source_target_pairs={{0,1},{1,0},{2,3},{3,2},{4,5},{5,4},{6,7},{7,6},{8,9},{9,8},{10,11... | collective-permute-start | bytes 196616 | tf_op jit(solution)/shard_map/ppermute | solution.py:65
  4.9 2.7 %copy-start.13 = (s32[128]{0:T(128)S(1)}, s32[128]{0:T(128)}, u32[]{:S(2)}) copy-start(s32[128]{0:T(128)} %param.17) | copy-start | bytes 1540
  4.9 4.6 %copy-start.14 = (bf16[1,256,128]{2,1,0:T(8,128)(2,1)S(1)}, bf16[1,256,128]{2,1,0:T(8,128)(2,1)}, u32[]{:S(2)}) copy-start(bf16[1,256,128]{2,1,0:T(8,128)(2,1)} %param.10) | copy-start | bytes 196612
  6.6 2.9 %collective-permute-start.2 = (bf16[128,4096]{1,0:T(8,128)(2,1)S(1)}, bf16[128,4096]{1,0:T(8,128)(2,1)}, u32[]{:S(2)}, u32[]{:S(2)}) collective-permute-start(bf16[128,4096]{1,0:T(8,128)(2,1)S(1)} %get-tuple-element.32), channel_id=1, source_target_pairs={{0,1},{1,0},{2,3},{3,2},{4,5},{5,4},{6,7},{7,6},{8,9},{9,8},{10,11... | collective-permute-start | bytes 3145736 | tf_op jit(solution)/shard_map/ppermute | solution.py:65
  14.0 8.2 %copy-start.8 = (bf16[128,8192]{1,0:T(8,128)(2,1)S(1)}, bf16[128,8192]{1,0:T(8,128)(2,1)}, u32[]{:S(2)}) copy-start(bf16[128,8192]{1,0:T(8,128)(2,1)} %param.14) | copy-start | bytes 6291460
  14.0 23.4 %all-to-all-start = ((bf16[8,32,4096]{2,1,0:T(8,128)(2,1)}), bf16[8,32,4096]{2,1,0:T(8,128)(2,1)}, u32[]{:S(2)}, u32[]{:S(2)}) async-start(bf16[8,32,4096]{2,1,0:T(8,128)(2,1)} %bitcast.52), calls=%async_computation | async-start | bytes 4194304 | tf_op jit(solution)/shard_map/all_to_all | solution.py:83
  22.2 2.0 copy-start.5
  24.2 1.1 copy-start.12
  24.2 2.7 %copy-start.11 = (bf16[8192]{0:T(1024)(128)(2,1)S(1)}, bf16[8192]{0:T(1024)(128)(2,1)}, u32[]{:S(2)}) copy-start(bf16[8192]{0:T(1024)(128)(2,1)} %param.15) | copy-start | bytes 49156
  25.3 2.7 collective-permute-start.4
  26.2 13.3 %collective-permute-start.3 = (bf16[4096,128]{1,0:T(8,128)(2,1)}, bf16[4096,128]{1,0:T(8,128)(2,1)}, u32[]{:S(2)}, u32[]{:S(2)}) collective-permute-start(bf16[4096,128]{1,0:T(8,128)(2,1)} %get-tuple-element.15), channel_id=1, source_target_pairs={{0,1},{1,0},{2,3},{3,2},{4,5},{5,4},{6,7},{7,6},{8,9},{9,8},{10,11... | collective-permute-start | bytes 3145736 | tf_op jit(solution)/shard_map/ppermute | solution.py:65
  28.0 1.0 copy-start.10
  30.7 78.6 %copy-start = (bf16[256,4096]{1,0:T(8,128)(2,1)}, bf16[256,4096]{1,0:T(8,128)(2,1)S(1)}, u32[]{:S(2)}) copy-start(bf16[256,4096]{1,0:T(8,128)(2,1)S(1)} %pad_maximum_fusion) | copy-start | bytes 6291460
  59.1 2.9 %collective-permute-start.5 = (f32[2,1]{0,1:T(1,128)S(1)}, f32[2,1]{0,1:T(1,128)S(1)}, u32[]{:S(2)}, u32[]{:S(2)}) collective-permute-start(f32[2,1]{0,1:T(1,128)S(1)} %bitcast.53), channel_id=1, source_target_pairs={{0,1},{1,0},{2,3},{3,2},{4,5},{5,4},{6,7},{7,6},{8,9},{9,8},{10,11... | collective-permute-start | bytes 32 | tf_op jit(solution)/shard_map/ppermute | solution.py:65
  99.4 8.3 %copy-start.2 = (bf16[8,32,4096]{2,1,0:T(8,128)(2,1)}, bf16[8,32,4096]{2,1,0:T(8,128)(2,1)S(1)}, u32[]{:S(2)}) copy-start(bf16[8,32,4096]{2,1,0:T(8,128)(2,1)S(1)} %all_to_all.42) | copy-start | bytes 6291460
  99.4 6.1 %copy-start.15 = (bf16[128]{0:T(256)(128)(2,1)S(1)}, bf16[128]{0:T(256)(128)(2,1)}, u32[]{:S(2)}) copy-start(bf16[128]{0:T(256)(128)(2,1)} %param.13) | copy-start | bytes 772
  102.2 4.2 %collective-permute-start.6 = (f32[128,256]{1,0:T(8,128)S(1)}, f32[128,256]{1,0:T(8,128)S(1)}, u32[]{:S(2)}, u32[]{:S(2)}) collective-permute-start(f32[128,256]{1,0:T(8,128)S(1)} %fusion.123), channel_id=1, source_target_pairs={{0,1},{1,0},{2,3},{3,2},{4,5},{5,4},{6,7},{7,6},{8,9},{9,8},{10,11... | collective-permute-start | bytes 393224 | tf_op jit(solution)/shard_map/ppermute | solution.py:65
  107.7 1.4 collective-permute-start.7
  111.3 4.7 %copy-start.3 = (bf16[8,32,4096]{2,1,0:T(8,128)(2,1)S(1)}, bf16[8,32,4096]{2,1,0:T(8,128)(2,1)}, u32[]{:S(2)}) copy-start(bf16[8,32,4096]{2,1,0:T(8,128)(2,1)} %copy-done.2) | copy-start | bytes 6291460
  111.3 20.1 %all-to-all-start.4 = ((bf16[8,32,4096]{2,1,0:T(8,128)(2,1)}), bf16[8,32,4096]{2,1,0:T(8,128)(2,1)}, u32[]{:S(2)}, u32[]{:S(2)}) async-start(bf16[8,32,4096]{2,1,0:T(8,128)(2,1)} %bitcast.50), calls=%async_computation.4 | async-start | bytes 4194304 | tf_op jit(solution)/shard_map/all_to_all | solution.py:83
  115.9 4.4 %collective-permute-start.8 = (bf16[256,4096]{1,0:T(8,128)(2,1)S(1)}, bf16[256,4096]{1,0:T(8,128)(2,1)}, u32[]{:S(2)}, u32[]{:S(2)}) collective-permute-start(bf16[256,4096]{1,0:T(8,128)(2,1)S(1)} %bitcast.48), channel_id=1, source_target_pairs={{0,1},{1,0},{2,3},{3,2},{4,5},{5,4},{6,7},{7,6},{8,9},{9,8},{10,11... | collective-permute-start | bytes 6291464 | tf_op jit(solution)/shard_map/ppermute | solution.py:65
  118.8 3.8 %copy-start.7 = (bf16[256,4096]{0,1:T(8,128)(2,1)S(1)}, bf16[256,4096]{0,1:T(8,128)(2,1)}, u32[]{:S(2)}) copy-start(bf16[256,4096]{0,1:T(8,128)(2,1)} %copy.17) | copy-start | bytes 6291460
  166.7 22.2 %all-to-all-start.7 = ((bf16[8,32,4096]{2,1,0:T(8,128)(2,1)}), bf16[8,32,4096]{2,1,0:T(8,128)(2,1)S(1)}, u32[]{:S(2)}, u32[]{:S(2)}) async-start(bf16[8,32,4096]{2,1,0:T(8,128)(2,1)} %broadcast_in_dim.62), calls=%async_computation.7 | async-start | bytes 4194304 | tf_op jit(solution)/shard_map/all_to_all | solution.py:83
  172.2 16.6 %collective-permute-start.9 = (bf16[2,4096]{1,0:T(2,128)(2,1)S(1)}, bf16[2,4096]{1,0:T(2,128)(2,1)S(1)}, u32[]{:S(2)}, u32[]{:S(2)}) collective-permute-start(bf16[2,4096]{1,0:T(2,128)(2,1)S(1)} %multiply_convert_fusion), channel_id=1, source_target_pairs={{0,0},{1,128},{2,2},{3,130},{4,4},{5,132},{6,6},{7,134},{8,8},{9,1... | collective-permute-start | bytes 49160 | tf_op jit(solution)/shard_map/ppermute | solution.py:65
  188.8 2.2 copy-start.1
  191.6 4.2 %collective-permute-start.10 = (f32[128,256]{1,0:T(8,128)S(1)}, f32[128,256]{1,0:T(8,128)S(1)}, u32[]{:S(2)}, u32[]{:S(2)}) collective-permute-start(f32[128,256]{1,0:T(8,128)S(1)} %fusion.16), channel_id=1, source_target_pairs={{0,1},{1,0},{2,3},{3,2},{4,5},{5,4},{6,7},{7,6},{8,9},{9,8},{10,11... | collective-permute-start | bytes 393224 | tf_op jit(solution)/shard_map/ppermute | solution.py:65
  194.1 6.1 %collective-permute-start.11 = (bf16[128,4096]{1,0:T(8,128)(2,1)S(1)}, bf16[128,4096]{1,0:T(8,128)(2,1)S(1)}, u32[]{:S(2)}, u32[]{:S(2)}) collective-permute-start(bf16[128,4096]{1,0:T(8,128)(2,1)S(1)} %subtract_convert_fusion), channel_id=1, source_target_pairs={{0,1},{1,0},{2,3},{3,2},{4,5},{5,4},{6,7},{7,6},{8,9},{9,8},{10,11... | collective-permute-start | bytes 3145736 | tf_op jit(solution)/shard_map/ppermute | solution.py:65
  194.2 2.8 %copy-start.4 = (bf16[8192,256]{1,0:T(8,128)(2,1)S(1)}, bf16[8192,256]{1,0:T(8,128)(2,1)}, u32[]{:S(2)}) copy-start(bf16[8192,256]{1,0:T(8,128)(2,1)} %maximum_select_fusion) | copy-start | bytes 12582916
  195.8 1.9 copy-start.6
  200.2 1.0 copy-start.9

commit v5 on v4

--- a/solution.py
+++ b/solution.py
@@ -103,37 +103,113 @@
     return jnp.sum(pieces.astype(jnp.float32), axis=0)
 
 
-def place(core_ref, kept_ref, back_ref, out_ref, sems):
-    half = kept_ref.shape[1]
-    core = core_ref[0]
-    copies = [
-        pltpu.make_async_copy(
-            ref, out_ref.at[:, pl.ds(pl.multiple_of(at * half, half), half)], sems.at[i]
-        )
-        for i, (ref, at) in enumerate(((kept_ref, core), (back_ref, 1 - core)))
-    ]
-    for copy in copies:
-        copy.start()
-    for copy in copies:
-        copy.wait()
-
-
-def join_columns(core, kept, back):
-    rows, half = kept.shape
+def project(
+    at_ref, order_ref, context_ref, context2_ref, resid_ref, resid2_ref, own_ref, other_ref,
+    out_ref, context_rows, context2_rows, resid_rows, resid2_rows,
+):
+    tile = pl.program_id(0)
+
+    @pl.when(tile == 0)
+    def _():
+        for source, rows in (
+            (context_ref, context_rows),
+            (context2_ref, context2_rows),
+            (resid_ref, resid_rows),
+            (resid2_ref, resid2_rows),
+        ):
+            rows[...] = matmul(order_ref[...], source[...]).astype(jnp.bfloat16)
+
+    width, columns = resid_ref.shape[1], out_ref.shape[1]
+    shift = lax.broadcasted_iota(jnp.int32, (width, columns), 1) - lax.broadcasted_iota(
+        jnp.int32, (width, columns), 0
+    )
+    total = matmul(context_rows[...], own_ref[...]) + matmul(context2_rows[...], other_ref[...])
+    for rows, which in ((resid_rows, 0), (resid2_rows, 1)):
+        placed = jnp.where(shift == at_ref[1 + which] - tile * columns, 1.0, 0.0)
+        total += matmul(rows[...], placed.astype(jnp.bfloat16))
+    out_ref[...] = total.astype(jnp.bfloat16)
+
+
+def project_both(at, order, context, context2, resid, resid2, proj, proj_other):
+    tokens, depth = context.shape
+    half = proj_other.shape[1]
+    columns = half // 8
+    whole = lambda array: pl.BlockSpec(array.shape, lambda j, at: (0, 0))
     return pl.pallas_call(
-        place,
+        project,
         grid_spec=pltpu.PrefetchScalarGridSpec(
             num_scalar_prefetch=1,
-            grid=(1,),
-            in_specs=[pl.BlockSpec(memory_space=pl.ANY)] * 2,
-            out_specs=pl.BlockSpec(memory_space=pl.ANY),
-            scratch_shapes=[pltpu.SemaphoreType.DMA((2,))],
-        ),
-        out_shape=jax.ShapeDtypeStruct((rows, 2 * half), kept.dtype),
+            grid=(8,),
+            in_specs=[
+                whole(order),
+                whole(context),
+                whole(context2),
+                whole(resid),
+                whole(resid2),
+                pl.BlockSpec((depth, columns), lambda j, at: (0, at[0] * 8 + j)),
+                pl.BlockSpec((depth, columns), lambda j, at: (0, j)),
+            ],
+            out_specs=pl.BlockSpec((tokens, columns), lambda j, at: (0, j)),
+            scratch_shapes=[
+                pltpu.VMEM(array.shape, jnp.bfloat16)
+                for array in (context, context2, resid, resid2)
+            ],
+        ),
+        out_shape=jax.ShapeDtypeStruct((tokens, half), jnp.bfloat16),
         cost_estimate=pl.CostEstimate(
-            flops=0, bytes_accessed=8 * rows * half, transcendentals=0
-        ),
-    )(jnp.reshape(core, (1,)).astype(jnp.int32), kept, back)
+            flops=6 * tokens * depth * half,
+            bytes_accessed=4 * half * (depth + tokens // 2),
+            transcendentals=0,
+        ),
+    )(at, order, context, context2, resid, resid2, proj, proj_other)
+
+
+def products(dims, core_ref, rows_ref, own_ref, other_ref, to_other_ref, kept_ref, sent_ref):
+    tile = pl.program_id(0)
+
+    @pl.when(tile == 0)
+    def _():
+        kept_ref[...] = jnp.zeros_like(kept_ref)
+        sent_ref[...] = jnp.zeros_like(sent_ref)
+
+    kept_ref[...] += matmul(rows_ref[...], own_ref[...], dims)
+    sent_ref[...] += matmul(rows_ref[...], other_ref[...], dims)
+
+    @pl.when(tile == pl.num_programs(0) - 1)
+    def _():
+        sent_ref[...] = matmul(
+            to_other_ref[...], sent_ref[...], precision=lax.Precision.HIGHEST
+        )
+
+
+def both_products(core, rows, weight, other, to_other, along):
+    tokens, half = rows.shape
+    own = weight.shape[1 - along]
+    steps = 4
+    tile = half // steps
+    shape = (tile, own) if along == 0 else (own, tile)
+    spot = lambda at: (at, 0) if along == 0 else (0, at)
+    result = jax.ShapeDtypeStruct((tokens, own), jnp.float32)
+    return pl.pallas_call(
+        lambda *refs: products(((1,), (along,)), *refs),
+        grid_spec=pltpu.PrefetchScalarGridSpec(
+            num_scalar_prefetch=1,
+            grid=(steps,),
+            in_specs=[
+                pl.BlockSpec((tokens, tile), lambda k, core: (0, k)),
+                pl.BlockSpec(shape, lambda k, core: spot(core[0] * steps + k)),
+                pl.BlockSpec(shape, lambda k, core: spot(k)),
+                pl.BlockSpec((tokens, tokens), lambda k, core: (0, 0)),
+            ],
+            out_specs=[pl.BlockSpec((tokens, own), lambda k, core: (0, 0))] * 2,
+        ),
+        out_shape=[result, result],
+        cost_estimate=pl.CostEstimate(
+            flops=4 * tokens * half * own,
+            bytes_accessed=2 * half * (tokens + 2 * own),
+            transcendentals=0,
+        ),
+    )(core, rows, weight, other, to_other)
 
 
 def shards(
@@ -164,39 +240,41 @@
     at = chip_of(row // block_rows, core)
     owner_of_row = jnp.repeat(owner_map, block_rows)
     order = ((owner_of_row[None, :] == at) & same_place).astype(jnp.bfloat16)
-    across = (chip_of(old // block_rows, 1 - core) == at) & same_place
+    across = ((chip_of(old // block_rows, 1 - core) == at) & same_place).astype(jnp.bfloat16)
+    to_other = (
+        (chip_of(row // block_rows, 1 - core) == chip_of(old // block_rows, core)) & same_place
+    ).astype(jnp.float32)
     kept = (token_ids.reshape(blocks, block_rows) != BOS).astype(jnp.float32)
     mask_rows = jnp.sum(jnp.where((owner_map == chip)[:, None], kept, 0.0), axis=0)[:, None]
 
     start = ((y * 8 + z) * 2 + xh) * 2 * width
     owns = (start // half == core) & (xl == 0)
-
-    def placed(which):
-        column = lax.broadcasted_iota(jnp.int32, (width, half), 1)
-        target = lax.broadcasted_iota(jnp.int32, (width, half), 0) + (
-            start % half + which * width
-        )
-        return ((column == target) & owns).astype(jnp.bfloat16)
-
-    joined = matmul(
-        order,
-        jnp.concatenate([contexts[0], context_other, resid_in, resid_other], axis=1),
-    ).astype(jnp.bfloat16)
-    proj_both = jnp.concatenate(
-        [mine(proj, 1), proj_other, placed(core), placed(1 - core)], axis=0
-    )
-    partial = matmul(joined, proj_both).astype(jnp.bfloat16)
+    start = jnp.where(owns, start % half, -features)
+    core_at = jnp.reshape(core, (1,)).astype(jnp.int32)
+    places = jnp.stack([core, start + core * width, start + (1 - core) * width]).astype(jnp.int32)
+    partial = project_both(
+        places, order, contexts[0], context_other, resid_in, resid_other, proj, proj_other
+    )
 
     encoder_out, decoder_out, _ = lax.optimization_barrier(
         (theirs(encoder, 0), theirs(decoder, 1), partial)
     )
-    encoder_own, encoder_other = mine(encoder, 0), other_core(encoder_out)
-    decoder_both = jnp.concatenate([mine(decoder, 1), other_core(decoder_out)], axis=0)
+    encoder_other, decoder_other = other_core(encoder_out), other_core(decoder_out)
+    decoder_both = jnp.concatenate([mine(decoder, 1), decoder_other], axis=0)
     my_bias = mine(dec_bias, 0).astype(jnp.float32)
     chunk = near_sum(partial)
-    chunk, encoder_own, encoder_other, decoder_both, mask_rows, my_bias, across = (
+    chunk, encoder_other, decoder_other, decoder_both, mask_rows, my_bias, across, to_other = (
         lax.optimization_barrier(
-            (chunk, encoder_own, encoder_other, decoder_both, mask_rows, my_bias, across)
+            (
+                chunk,
+                encoder_other,
+                decoder_other,
+                decoder_both,
+                mask_rows,
+                my_bias,
+                across,
+                to_other,
+            )
         )
     )
     values = far_sum(chunk).astype(jnp.bfloat16).astype(jnp.float32)
@@ -206,23 +284,19 @@
     my_centred = (values * inverse_rms - my_bias).astype(jnp.bfloat16)
     centred = spread(spread(my_centred, FAR_GROUPS, FAR), NEAR_GROUPS, NEAR)
 
-    exact = dict(precision=lax.Precision.HIGHEST)
-
-    def both_halves(own_weight, other_weight, values, dims):
-        sent = other_core(matmul(other_weight, values, dims))
-        kept = matmul(own_weight, values, dims)
-        return kept + matmul(sent, across.astype(jnp.float32), ((1,), (1,)), **exact)
-
-    before_relu = both_halves(encoder_own, encoder_other, centred, ((0,), (1,)))
-    before_relu = before_relu + enc_bias.astype(jnp.float32)[:, None]
+    products_own, products_sent = both_products(
+        core_at, centred, encoder, encoder_other, to_other, 0
+    )
+    before_relu = products_own + other_core(products_sent) + enc_bias.astype(jnp.float32)
     latents = jnp.maximum(before_relu, 0.0).astype(jnp.bfloat16)
-    across_low = across.astype(jnp.bfloat16)
-    latents_other = matmul(other_core(latents), across_low, ((1,), (1,))).astype(jnp.bfloat16)
-    latents_both = jnp.concatenate([latents, latents_other], axis=0)
-    partial = matmul(latents_both, decoder_both, ((0,), (0,))).astype(jnp.bfloat16)
+    latents_other = other_core(
+        matmul(to_other.astype(jnp.bfloat16), latents).astype(jnp.bfloat16)
+    )
+    latents_both = jnp.concatenate([latents, latents_other], axis=1)
+    partial = matmul(latents_both, decoder_both).astype(jnp.bfloat16)
     later, _ = lax.optimization_barrier((centred, partial))
     centred_other = matmul(
-        other_core(later), across_low, ((0,), (1,))
+        other_core(later), across, ((0,), (1,))
     ).astype(jnp.bfloat16)
     centred_own = later.T
     centred_full = jnp.where(
@@ -241,14 +315,23 @@
     def stepped(weight, grad):
         return (weight.astype(jnp.float32) - step_size * grad).astype(jnp.bfloat16)
 
-    decoder_own, decoder_other = decoder_both[:own], decoder_both[own:]
-    backward = both_halves(decoder_own, decoder_other, error, ((1,), (1,)))
+    products_own, products_sent = both_products(
+        core_at, error, decoder, decoder_other, to_other, 1
+    )
+    backward = products_own + other_core(products_sent)
     pre_grad = lax.optimization_barrier(
         jnp.where(before_relu > 0.0, backward, 0.0).astype(jnp.bfloat16)
     )
-    back = other_core(stepped(decoder_other, matmul(latents_other, error)))
-    new_decoder = join_columns(core, stepped(decoder_own, matmul(latents, error)), back)
-    new_encoder = stepped(encoder, matmul(centred_full, pre_grad, ((1,), (1,))))
+    over_rows = ((0,), (0,))
+    error_late, _ = lax.optimization_barrier((error, products_sent))
+    back = other_core(stepped(decoder_other, matmul(latents_other, error_late, over_rows)))
+    kept_half = stepped(decoder_both[:own], matmul(latents, error_late, over_rows))
+    new_encoder = stepped(encoder, matmul(centred_full, pre_grad))
+    new_decoder = jnp.where(
+        core == 0,
+        jnp.concatenate([kept_half, back], axis=1),
+        jnp.concatenate([back, kept_half], axis=1),
+    )
     return (owned_error, new_encoder, new_decoder)
 
 

time: 267 us -> 214 us (0.80)
  Pallas kernels: 64.6 us -> 18.6 us
  matrix products: 25.2 us -> 13.8 us
  other arithmetic: 6.36 us -> 11.7 us
  local copies, waits for them, and re-layouts: 16.2 us -> 11.3 us
  waiting for transfers between devices: 31 us -> 34.9 us
    pallas_call x1 -> x3, Pallas kernels: 64.6 us -> 18.6 us  [the longest x2 10.3 us: both_products(): pl.pallas_call(lambda *refs: products(((1,), (along,)), *refs), grid_spec...]
    all_to_all x3, waiting for transfers between devices: 12.9 us -> 26.1 us  [all_to_all(): lax.all_to_all(pieces, AXES, 0, 0, axis_index_groups=groups, tiled=True)]
    dot_general x15 -> x8, matrix products: 25.2 us -> 13.8 us  [matmul(): lax.dot_general(a, b, (dims, ((), ())), preferred_element_type=jnp.float3...]
    ppermute x12, waiting for transfers between devices: 18.1 us -> 8.81 us  [exchange(): return lax.ppermute(value, AXES, route)]
  transfers between devices with their start and end apart: 15 -> 15, of which waited for: 9 -> 9; matrix products, arithmetic and copies ran while one was open for 8% -> 9% of each run, Pallas kernels for 0% -> 2%
where the time goes in v5:
time: 214 us; the launch traced here: 213 us
  blocking collectives  84.1 us (39%)
  starting transfers between devices  37.3 us (17%)
  waiting for transfers between devices  34.9 us (16%)
  Pallas kernels  18.6 us (9%)
  matrix products  13.8 us (6%)
  other arithmetic  11.7 us (5%)
  local copies, waits for them, and re-layouts  11.3 us (5%)
    all_to_all x5, blocking collectives, all_to_all(): lax.all_to_all(pieces, AXES, 0, 0, axis_index_groups=groups, tiled=True)  84.1 us
    all_to_all x3, waiting for transfers between devices, all_to_all(): lax.all_to_all(pieces, AXES, 0, 0, axis_index_groups=groups, tiled=True)  26.1 us
    all_to_all x3, starting transfers between devices, all_to_all(): lax.all_to_all(pieces, AXES, 0, 0, axis_index_groups=groups, tiled=True)  19 us
    ppermute x12, starting transfers between devices, exchange(): return lax.ppermute(value, AXES, route)  18.3 us
    dot_general x8, matrix products, matmul(): lax.dot_general(a, b, (dims, ((), ())), preferred_element_type=jnp.float3...  13.8 us
    pallas_call x2, Pallas kernels, both_products(): pl.pallas_call(lambda *refs: products(((1,), (along,)), *refs), grid_spec...  10.3 us
    ppermute x12, waiting for transfers between devices, exchange(): return lax.ppermute(value, AXES, route)  8.81 us
    pallas_call x1, Pallas kernels, project_both(): pl.pallas_call(project, grid_spec=pltpu.PrefetchScalarGridSpec(num_scalar...  8.37 us
  transfers between devices with their start and end apart: 15, of which 9 were waited for; matrix products, arithmetic and copies ran while one was open for 9% of the time, Pallas kernels for 2%

profile of v5, /device:TPU:1, one launch (start us, length us, event | category | flops | bytes accessed | tf_op | source)
XLA Modules:
  0.0 212.9 jit_solution(15350830939142158054)
XLA Ops:
  0.7 1.3 dynamic-slice_bitcast_fusion
  2.0 3.3 %collective-permute-start.2 = (bf16[128,4096]{1,0:T(8,128)(2,1)S(1)}, bf16[128,4096]{1,0:T(8,128)(2,1)S(1)}, u32[]{:S(2)}, u32[]{:S(2)}) collective-permute-start(bf16[128,4096]{1,0:T(8,128)(2,1)S(1)} %dynamic-slice_bitcast_fusion), channel_id=1, source_target_pairs={{0,1},{1,0},{2,3},{3,2},{4,5},{5,4},{6,7},{7,6},{8,9},{9,8},{10,11... | collective-permute-start | bytes 3145736 | tf_op jit(solution)/shard_map/ppermute | solution.py:65
  6.3 1.7 and_convert_fusion
  9.7 8.4 %shard_map.112 = bf16[256,4096]{1,0:T(8,128)(2,1)} custom-call(s32[3]{0:T(128)} %pad_add_fusion.at_ref, bf16[256,256]{1,0:T(8,128)(2,1)} %get-tuple-element.42.order_ref, bf16[256,128]{1,0:T(8,128)(2,1)} %bitcast.41, bf16[256,128]{1,0:T(8,128)(2,1)} %copy-done.20, bf16[256,64]{1,0:T(8,128)(2,1)} %copy-done.16, bf16[256,64]{1,0:T(8,128)(2,1)} %copy-done.19, ...), custom_call_target="tpu_custom_call" | custom-call | flops 805306368 | bytes 4194304 | tf_op jit(solution)/shard_map/pallas_call | solution.py:138
  18.0 8.2 %all-to-all-start = ((bf16[8,32,4096]{2,1,0:T(8,128)(2,1)}), bf16[8,32,4096]{2,1,0:T(8,128)(2,1)}, u32[]{:S(2)}, u32[]{:S(2)}) async-start(bf16[8,32,4096]{2,1,0:T(8,128)(2,1)} %bitcast.38), calls=%async_computation | async-start | bytes 4194304 | tf_op jit(solution)/shard_map/all_to_all | solution.py:83
  32.0 1.8 pad_maximum_fusion
  33.8 7.6 %all-to-all-done = bf16[8,32,4096]{2,1,0:T(8,128)(2,1)} async-done(((bf16[8,32,4096]{2,1,0:T(8,128)(2,1)}), bf16[8,32,4096]{2,1,0:T(8,128)(2,1)}, u32[]{:S(2)}, u32[]{:S(2)}) %all-to-all-start) | async-done | bytes 2097184 | tf_op jit(solution)/shard_map/all_to_all | solution.py:83
  41.5 2.0 convolution_convert_fusion.3
  43.7 18.2 %all_to_all.40 = bf16[16,2,4096]{2,1,0:T(2,128)(2,1)S(1)} all-to-all(bf16[16,2,4096]{2,1,0:T(2,128)(2,1)S(1)} %reshape.125), channel_id=1, replica_groups={{0,8,16,24,32,40,48,56,64,72,80,88,96,104,112,120},{4,12,20,28,36,44,52..., dimensions={0} | all-to-all | bytes 524288 | tf_op jit(solution)/shard_map/all_to_all | solution.py:83
  62.2 1.8 collective-permute-start.5
  65.2 15.1 %all_to_all.41 = bf16[16,2,4096]{2,1,0:T(2,128)(2,1)S(1)} all-to-all(bf16[16,2,4096]{2,1,0:T(2,128)(2,1)S(1)} %broadcast_in_dim.57), channel_id=1, replica_groups={{0,8,16,24,32,40,48,56,64,72,80,88,96,104,112,120},{4,12,20,28,36,44,52..., dimensions={0} | all-to-all | bytes 524288 | tf_op jit(solution)/shard_map/all_to_all | solution.py:83
  80.6 20.6 %all_to_all.42 = bf16[8,32,4096]{2,1,0:T(8,128)(2,1)} all-to-all(bf16[8,32,4096]{2,1,0:T(8,128)(2,1)S(1)} %broadcast_in_dim.59), channel_id=1, replica_groups={{0,4,128,132,2,6,130,134},{8,12,136,140,10,14,138,142},{16,20,144,148,1..., dimensions={0} | all-to-all | bytes 4194304 | tf_op jit(solution)/shard_map/all_to_all | solution.py:83
  101.2 5.1 %shard_map.113 = (f32[256,128]{1,0:T(8,128)}, f32[256,128]{1,0:T(8,128)}) custom-call(s32[1]{0:T(128)} %bitcast.refs_0_, bf16[256,4096]{1,0:T(8,128)(2,1)} %bitcast.35, bf16[8192,128]{1,0:T(8,128)(2,1)} %refs_2_.2, bf16[4096,128]{1,0:T(8,128)(2,1)} %collective-permute-done.3.refs_3_, f32[256,256]{1,0:T(8,128)} %get-tuple-element.27.refs_4_), custom_call_target="tpu_custom_call" | custom-call | flops 536870912 | bytes 4194304 | tf_op jit(solution)/shard_map/pallas_call | solution.py:193
  106.3 3.2 %collective-permute-start.6 = (f32[256,128]{1,0:T(8,128)}, f32[256,128]{1,0:T(8,128)S(1)}, u32[]{:S(2)}, u32[]{:S(2)}) collective-permute-start(f32[256,128]{1,0:T(8,128)} %get-tuple-element.29), channel_id=1, source_target_pairs={{0,1},{1,0},{2,3},{3,2},{4,5},{5,4},{6,7},{7,6},{8,9},{9,8},{10,11... | collective-permute-start | bytes 393224 | tf_op jit(solution)/shard_map/ppermute | solution.py:65
  113.2 2.0 convolution_convert_fusion.1
  115.2 5.0 %all-to-all-start.4 = ((bf16[8,32,4096]{2,1,0:T(8,128)(2,1)}), bf16[8,32,4096]{2,1,0:T(8,128)(2,1)}, u32[]{:S(2)}, u32[]{:S(2)}) async-start(bf16[8,32,4096]{2,1,0:T(8,128)(2,1)} %bitcast.39), calls=%async_computation.4 | async-start | bytes 4194304 | tf_op jit(solution)/shard_map/all_to_all | solution.py:83
  120.4 4.1 %collective-permute-done.8 = bf16[256,4096]{1,0:T(8,128)(2,1)S(1)} collective-permute-done((bf16[256,4096]{1,0:T(8,128)(2,1)S(1)}, bf16[256,4096]{1,0:T(8,128)(2,1)S(1)}, u32[]{:S(2)}, u32[]{:S(2)}) %collective-permute-start.8) | collective-permute-done | bytes 2097184 | tf_op jit(solution)/shard_map/ppermute | solution.py:65
  125.2 2.5 %maximum_select_fusion = bf16[8192,256]{0,1:T(8,128)(2,1)} fusion(bf16[4096,256]{0,1:T(8,128)(2,1)S(1)} %convolution_convert_fusion, bf16[4096,256]{0,1:T(8,128)(2,1)S(1)} %bitcast.37, pred[]{:T(512)S(6)} %eq.84), kind=kLoop, calls=%fused_computation.9 | loop fusion | flops 18874368 | bytes 8388609 | tf_op jit(solution)/shard_map/jit(_where)/select_n | solution.py:302
  127.7 8.1 %all-to-all-done.4 = bf16[8,32,4096]{2,1,0:T(8,128)(2,1)} async-done(((bf16[8,32,4096]{2,1,0:T(8,128)(2,1)}), bf16[8,32,4096]{2,1,0:T(8,128)(2,1)}, u32[]{:S(2)}, u32[]{:S(2)}) %all-to-all-start.4) | async-done | bytes 2097184 | tf_op jit(solution)/shard_map/all_to_all | solution.py:83
  135.7 2.0 convolution_convert_fusion.2
  138.0 14.6 %all_to_all.43 = bf16[16,2,4096]{2,1,0:T(2,128)(2,1)S(1)} all-to-all(bf16[16,2,4096]{2,1,0:T(2,128)(2,1)S(1)} %reshape.129), channel_id=1, replica_groups={{0,8,16,24,32,40,48,56,64,72,80,88,96,104,112,120},{4,12,20,28,36,44,52..., dimensions={0} | all-to-all | bytes 524288 | tf_op jit(solution)/shard_map/all_to_all | solution.py:83
  154.5 15.7 %all_to_all.44 = bf16[16,2,4096]{2,1,0:T(2,128)(2,1)S(1)} all-to-all(bf16[16,2,4096]{2,1,0:T(2,128)(2,1)S(1)} %broadcast_in_dim.60), channel_id=1, replica_groups={{0,8,16,24,32,40,48,56,64,72,80,88,96,104,112,120},{4,12,20,28,36,44,52..., dimensions={0} | all-to-all | bytes 524288 | tf_op jit(solution)/shard_map/all_to_all | solution.py:83
  170.2 1.6 broadcast_in_dim.62
  171.8 5.8 %all-to-all-start.7 = ((bf16[8,32,4096]{2,1,0:T(8,128)(2,1)}), bf16[8,32,4096]{2,1,0:T(8,128)(2,1)S(1)}, u32[]{:S(2)}, u32[]{:S(2)}) async-start(bf16[8,32,4096]{2,1,0:T(8,128)(2,1)} %broadcast_in_dim.62), calls=%async_computation.7 | async-start | bytes 4194304 | tf_op jit(solution)/shard_map/all_to_all | solution.py:83
  177.6 4.9 %collective-permute-start.9 = (bf16[2,4096]{1,0:T(2,128)(2,1)}, bf16[2,4096]{1,0:T(2,128)(2,1)S(1)}, u32[]{:S(2)}, u32[]{:S(2)}) collective-permute-start(bf16[2,4096]{1,0:T(2,128)(2,1)} %multiply_convert_fusion), channel_id=1, source_target_pairs={{0,0},{1,128},{2,2},{3,130},{4,4},{5,132},{6,6},{7,134},{8,8},{9,1... | collective-permute-start | bytes 49160 | tf_op jit(solution)/shard_map/ppermute | solution.py:65
  182.5 10.5 %all-to-all-done.7 = bf16[8,32,4096]{2,1,0:T(8,128)(2,1)S(1)} async-done(((bf16[8,32,4096]{2,1,0:T(8,128)(2,1)}), bf16[8,32,4096]{2,1,0:T(8,128)(2,1)S(1)}, u32[]{:S(2)}, u32[]{:S(2)}) %all-to-all-start.7) | async-done | bytes 2097184 | tf_op jit(solution)/shard_map/all_to_all | solution.py:83
  194.3 5.2 %shard_map.114 = (f32[256,128]{1,0:T(8,128)}, f32[256,128]{1,0:T(8,128)}) custom-call(s32[1]{0:T(128)} %bitcast.refs_0_, bf16[256,4096]{1,0:T(8,128)(2,1)} %bitcast.32, bf16[128,8192]{1,0:T(8,128)(2,1)} %refs_2_.3, bf16[128,4096]{1,0:T(8,128)(2,1)} %copy-done.7, f32[256,256]{1,0:T(8,128)} %get-tuple-element.27.refs_4_), custom_call_target="tpu_custom_call" | custom-call | flops 536870912 | bytes 4194304 | tf_op jit(solution)/shard_map/pallas_call | solution.py:193
  199.5 2.3 %subtract_convert_fusion = bf16[128,4096]{1,0:T(8,128)(2,1)S(1)} fusion(bf16[128,4096]{1,0:T(8,128)(2,1)S(1)} %copy-done.8, bf16[256,128]{1,0:T(8,128)(2,1)S(1)} %collective-permute-done.7, bf16[256,4096]{1,0:T(8,128)(2,1)} %bitcast.33), kind=kOutput, calls=%fused_computation.12 | convolution fusion | flops 270532608 | bytes 4259840 | tf_op jit(solution)/shard_map/dot_general | solution.py:77
  201.9 3.2 %collective-permute-start.11 = (bf16[128,4096]{1,0:T(8,128)(2,1)S(1)}, bf16[128,4096]{1,0:T(8,128)(2,1)S(1)}, u32[]{:S(2)}, u32[]{:S(2)}) collective-permute-start(bf16[128,4096]{1,0:T(8,128)(2,1)S(1)} %subtract_convert_fusion), channel_id=1, source_target_pairs={{0,1},{1,0},{2,3},{3,2},{4,5},{5,4},{6,7},{7,6},{8,9},{9,8},{10,11... | collective-permute-start | bytes 3145736 | tf_op jit(solution)/shard_map/ppermute | solution.py:65
  205.2 1.9 subtract_convert_fusion.1
  207.7 2.6 %fusion.1 = bf16[8192,128]{1,0:T(8,128)(2,1)} fusion(bf16[8192,256]{0,1:T(8,128)(2,1)S(1)} %copy-done.2, bf16[256,128]{1,0:T(8,128)(2,1)S(1)} %select_convert_fusion, bf16[8192,128]{1,0:T(8,128)(2,1)S(1)} %copy-done.5), kind=kOutput, calls=%fused_computation.2 | convolution fusion | flops 541065216 | bytes 8454144 | tf_op jit(solution)/shard_map/dot_general | solution.py:77
  210.4 1.9 maximum_select_fusion.1
  (123 shorter events, 19.7 us)
Async XLA Ops:
  2.0 6.7 %collective-permute-start.2 = (bf16[128,4096]{1,0:T(8,128)(2,1)S(1)}, bf16[128,4096]{1,0:T(8,128)(2,1)S(1)}, u32[]{:S(2)}, u32[]{:S(2)}) collective-permute-start(bf16[128,4096]{1,0:T(8,128)(2,1)S(1)} %dynamic-slice_bitcast_fusion), channel_id=1, source_target_pairs={{0,1},{1,0},{2,3},{3,2},{4,5},{5,4},{6,7},{7,6},{8,9},{9,8},{10,11... | collective-permute-start | bytes 3145736 | tf_op jit(solution)/shard_map/ppermute | solution.py:65
  5.5 3.2 %collective-permute-start.1 = (bf16[256,64]{1,0:T(8,128)(2,1)S(1)}, bf16[256,64]{1,0:T(8,128)(2,1)S(1)}, u32[]{:S(2)}, u32[]{:S(2)}) collective-permute-start(bf16[256,64]{1,0:T(8,128)(2,1)S(1)} %copy.16.resid_ref), channel_id=1, source_target_pairs={{0,1},{1,0},{2,3},{3,2},{4,5},{5,4},{6,7},{7,6},{8,9},{9,8},{10,11... | collective-permute-start | bytes 98312 | tf_op jit(solution)/shard_map/ppermute | solution.py:65
  5.6 3.1 %collective-permute-start = (bf16[256,128]{1,0:T(8,128)(2,1)S(1)}, bf16[256,128]{1,0:T(8,128)(2,1)S(1)}, u32[]{:S(2)}, u32[]{:S(2)}) collective-permute-start(bf16[256,128]{1,0:T(8,128)(2,1)S(1)} %bitcast.42), channel_id=1, source_target_pairs={{0,1},{1,0},{2,3},{3,2},{4,5},{5,4},{6,7},{7,6},{8,9},{9,8},{10,11... | collective-permute-start | bytes 196616 | tf_op jit(solution)/shard_map/ppermute | solution.py:65
  18.0 8.2 %copy-start.4 = (bf16[8192,128]{1,0:T(8,128)(2,1)S(1)}, bf16[8192,128]{1,0:T(8,128)(2,1)}, u32[]{:S(2)}) copy-start(bf16[8192,128]{1,0:T(8,128)(2,1)} %refs_2_.2) | copy-start | bytes 6291460
  18.0 23.4 %all-to-all-start = ((bf16[8,32,4096]{2,1,0:T(8,128)(2,1)}), bf16[8,32,4096]{2,1,0:T(8,128)(2,1)}, u32[]{:S(2)}, u32[]{:S(2)}) async-start(bf16[8,32,4096]{2,1,0:T(8,128)(2,1)} %bitcast.38), calls=%async_computation | async-start | bytes 4194304 | tf_op jit(solution)/shard_map/all_to_all | solution.py:83
  29.3 2.7 %collective-permute-start.4 = (bf16[128,4096]{1,0:T(8,128)(2,1)S(1)}, bf16[128,4096]{1,0:T(8,128)(2,1)S(1)}, u32[]{:S(2)}, u32[]{:S(2)}) collective-permute-start(bf16[128,4096]{1,0:T(8,128)(2,1)S(1)} %get-tuple-element.22), channel_id=1, source_target_pairs={{0,1},{1,0},{2,3},{3,2},{4,5},{5,4},{6,7},{7,6},{8,9},{9,8},{10,11... | collective-permute-start | bytes 3145736 | tf_op jit(solution)/shard_map/ppermute | solution.py:65
  29.3 12.1 %copy-start.22 = (s32[256]{0:T(256)}, s32[256]{0:T(256)S(1)}, u32[]{:S(2)}) copy-start(s32[256]{0:T(256)S(1)} %get-tuple-element.50) | copy-start | bytes 3076
  29.3 12.1 %copy-start.24 = (s32[256]{0:T(256)}, s32[256]{0:T(256)S(1)}, u32[]{:S(2)}) copy-start(s32[256]{0:T(256)S(1)} %get-tuple-element.51) | copy-start | bytes 3076
  29.4 14.1 %collective-permute-start.3 = (bf16[4096,128]{1,0:T(8,128)(2,1)}, bf16[4096,128]{1,0:T(8,128)(2,1)}, u32[]{:S(2)}, u32[]{:S(2)}) collective-permute-start(bf16[4096,128]{1,0:T(8,128)(2,1)} %constant_dynamic-slice_fusion.2), channel_id=1, source_target_pairs={{0,1},{1,0},{2,3},{3,2},{4,5},{5,4},{6,7},{7,6},{8,9},{9,8},{10,11... | collective-permute-start | bytes 3145736 | tf_op jit(solution)/shard_map/ppermute | solution.py:65
  30.0 11.5 %copy-start.27 = (pred[256]{0:T(512)(128)(4,1)}, pred[256]{0:T(512)(128)(4,1)S(1)}, u32[]{:S(2)}) copy-start(pred[256]{0:T(512)(128)(4,1)S(1)} %compare_and_fusion.2) | copy-start | bytes 772
  33.8 79.4 %copy-start.6 = (bf16[256,4096]{1,0:T(8,128)(2,1)}, bf16[256,4096]{1,0:T(8,128)(2,1)S(1)}, u32[]{:S(2)}) copy-start(bf16[256,4096]{1,0:T(8,128)(2,1)S(1)} %pad_maximum_fusion) | copy-start | bytes 6291460
  62.2 2.7 %collective-permute-start.5 = (f32[2,1]{0,1:T(1,128)S(1)}, f32[2,1]{0,1:T(1,128)S(1)}, u32[]{:S(2)}, u32[]{:S(2)}) collective-permute-start(f32[2,1]{0,1:T(1,128)S(1)} %bitcast.43), channel_id=1, source_target_pairs={{0,1},{1,0},{2,3},{3,2},{4,5},{5,4},{6,7},{7,6},{8,9},{9,8},{10,11... | collective-permute-start | bytes 32 | tf_op jit(solution)/shard_map/ppermute | solution.py:65
  101.2 8.3 %copy-start.34 = (bf16[128]{0:T(256)(128)(2,1)S(1)}, bf16[128]{0:T(256)(128)(2,1)}, u32[]{:S(2)}) copy-start(bf16[128]{0:T(256)(128)(2,1)} %param.13) | copy-start | bytes 772
  101.2 10.4 %copy-start.10 = (f32[256,256]{1,0:T(8,128)S(1)}, f32[256,256]{1,0:T(8,128)}, u32[]{:S(2)}) copy-start(f32[256,256]{1,0:T(8,128)} %get-tuple-element.27.refs_4_) | copy-start | bytes 786436
  106.3 4.4 %collective-permute-start.6 = (f32[256,128]{1,0:T(8,128)}, f32[256,128]{1,0:T(8,128)S(1)}, u32[]{:S(2)}, u32[]{:S(2)}) collective-permute-start(f32[256,128]{1,0:T(8,128)} %get-tuple-element.29), channel_id=1, source_target_pairs={{0,1},{1,0},{2,3},{3,2},{4,5},{5,4},{6,7},{7,6},{8,9},{9,8},{10,11... | collective-permute-start | bytes 393224 | tf_op jit(solution)/shard_map/ppermute | solution.py:65
  111.8 1.4 collective-permute-start.7
  115.2 9.2 %copy-start.12 = (bf16[256,256]{1,0:T(8,128)(2,1)S(1)}, bf16[256,256]{1,0:T(8,128)(2,1)}, u32[]{:S(2)}) copy-start(bf16[256,256]{1,0:T(8,128)(2,1)} %get-tuple-element.32) | copy-start | bytes 393220
  115.2 20.5 %all-to-all-start.4 = ((bf16[8,32,4096]{2,1,0:T(8,128)(2,1)}), bf16[8,32,4096]{2,1,0:T(8,128)(2,1)}, u32[]{:S(2)}, u32[]{:S(2)}) async-start(bf16[8,32,4096]{2,1,0:T(8,128)(2,1)} %bitcast.39), calls=%async_computation.4 | async-start | bytes 4194304 | tf_op jit(solution)/shard_map/all_to_all | solution.py:83
  120.3 4.2 %collective-permute-start.8 = (bf16[256,4096]{1,0:T(8,128)(2,1)S(1)}, bf16[256,4096]{1,0:T(8,128)(2,1)S(1)}, u32[]{:S(2)}, u32[]{:S(2)}) collective-permute-start(bf16[256,4096]{1,0:T(8,128)(2,1)S(1)} %bitcast.36), channel_id=1, source_target_pairs={{0,1},{1,0},{2,3},{3,2},{4,5},{5,4},{6,7},{7,6},{8,9},{9,8},{10,11... | collective-permute-start | bytes 6291464 | tf_op jit(solution)/shard_map/ppermute | solution.py:65
  125.1 10.6 %copy-start.23 = (s32[256]{0:T(256)S(1)}, s32[256]{0:T(256)}, u32[]{:S(2)}) copy-start(s32[256]{0:T(256)} %copy-done.22) | copy-start | bytes 3076
  125.2 10.6 %copy-start.25 = (s32[256]{0:T(256)S(1)}, s32[256]{0:T(256)}, u32[]{:S(2)}) copy-start(s32[256]{0:T(256)} %copy-done.24) | copy-start | bytes 3076
  125.2 10.6 %copy-start.28 = (pred[256]{0:T(512)(128)(4,1)S(1)}, pred[256]{0:T(512)(128)(4,1)}, u32[]{:S(2)}) copy-start(pred[256]{0:T(512)(128)(4,1)} %copy-done.27) | copy-start | bytes 772
  127.7 25.2 %copy-start.29 = (f32[2]{0:T(128)S(1)}, f32[2]{0:T(128)}, u32[]{:S(2)}) copy-start(f32[2]{0:T(128)} %select_reduce_fusion) | copy-start | bytes 28
  171.8 21.2 %all-to-all-start.7 = ((bf16[8,32,4096]{2,1,0:T(8,128)(2,1)}), bf16[8,32,4096]{2,1,0:T(8,128)(2,1)S(1)}, u32[]{:S(2)}, u32[]{:S(2)}) async-start(bf16[8,32,4096]{2,1,0:T(8,128)(2,1)} %broadcast_in_dim.62), calls=%async_computation.7 | async-start | bytes 4194304 | tf_op jit(solution)/shard_map/all_to_all | solution.py:83
  177.6 27.5 %collective-permute-start.9 = (bf16[2,4096]{1,0:T(2,128)(2,1)}, bf16[2,4096]{1,0:T(2,128)(2,1)S(1)}, u32[]{:S(2)}, u32[]{:S(2)}) collective-permute-start(bf16[2,4096]{1,0:T(2,128)(2,1)} %multiply_convert_fusion), channel_id=1, source_target_pairs={{0,0},{1,128},{2,2},{3,130},{4,4},{5,132},{6,6},{7,134},{8,8},{9,1... | collective-permute-start | bytes 49160 | tf_op jit(solution)/shard_map/ppermute | solution.py:65
  199.5 8.2 %copy-start.13 = (f32[256,128]{1,0:T(8,128)S(1)}, f32[256,128]{1,0:T(8,128)}, u32[]{:S(2)}) copy-start(f32[256,128]{1,0:T(8,128)} %get-tuple-element.28) | copy-start | bytes 393220
  199.5 8.2 %copy-start.15 = (f32[256,128]{1,0:T(8,128)S(1)}, f32[256,128]{1,0:T(8,128)}, u32[]{:S(2)}) copy-start(f32[256,128]{1,0:T(8,128)} %copy-done.14) | copy-start | bytes 393220
  199.5 8.2 %copy-start.17 = (f32[256,128]{1,0:T(8,128)S(1)}, f32[256,128]{1,0:T(8,128)}, u32[]{:S(2)}) copy-start(f32[256,128]{1,0:T(8,128)} %get-tuple-element.36) | copy-start | bytes 393220
  199.5 8.1 %copy-start.31 = (f32[128]{0:T(128)S(1)}, f32[128]{0:T(128)}, u32[]{:S(2)}) copy-start(f32[128]{0:T(128)} %copy-done.30) | copy-start | bytes 1540
  199.5 8.2 %copy-start.5 = (bf16[8192,128]{1,0:T(8,128)(2,1)S(1)}, bf16[8192,128]{1,0:T(8,128)(2,1)}, u32[]{:S(2)}) copy-start(bf16[8192,128]{1,0:T(8,128)(2,1)} %refs_2_.2) | copy-start | bytes 6291460
  201.9 8.5 %collective-permute-start.11 = (bf16[128,4096]{1,0:T(8,128)(2,1)S(1)}, bf16[128,4096]{1,0:T(8,128)(2,1)S(1)}, u32[]{:S(2)}, u32[]{:S(2)}) collective-permute-start(bf16[128,4096]{1,0:T(8,128)(2,1)S(1)} %subtract_convert_fusion), channel_id=1, source_target_pairs={{0,1},{1,0},{2,3},{3,2},{4,5},{5,4},{6,7},{7,6},{8,9},{9,8},{10,11... | collective-permute-start | bytes 3145736 | tf_op jit(solution)/shard_map/ppermute | solution.py:65
  205.1 2.6 %collective-permute-start.10 = (f32[256,128]{1,0:T(8,128)}, f32[256,128]{1,0:T(8,128)S(1)}, u32[]{:S(2)}, u32[]{:S(2)}) collective-permute-start(f32[256,128]{1,0:T(8,128)} %get-tuple-element.37), channel_id=1, source_target_pairs={{0,1},{1,0},{2,3},{3,2},{4,5},{5,4},{6,7},{7,6},{8,9},{9,8},{10,11... | collective-permute-start | bytes 393224 | tf_op jit(solution)/shard_map/ppermute | solution.py:65
  (18 other events, 60.8 us)

commit v6 on v4

--- a/solution.py
+++ b/solution.py
@@ -1,8 +1,6 @@
 import jax
 import jax.numpy as jnp
 from jax import lax
-from jax.experimental import pallas as pl
-from jax.experimental.pallas import tpu as pltpu
 from jax.sharding import Mesh
 from jax.sharding import PartitionSpec as P
 
@@ -103,39 +101,6 @@
     return jnp.sum(pieces.astype(jnp.float32), axis=0)
 
 
-def place(core_ref, kept_ref, back_ref, out_ref, sems):
-    half = kept_ref.shape[1]
-    core = core_ref[0]
-    copies = [
-        pltpu.make_async_copy(
-            ref, out_ref.at[:, pl.ds(pl.multiple_of(at * half, half), half)], sems.at[i]
-        )
-        for i, (ref, at) in enumerate(((kept_ref, core), (back_ref, 1 - core)))
-    ]
-    for copy in copies:
-        copy.start()
-    for copy in copies:
-        copy.wait()
-
-
-def join_columns(core, kept, back):
-    rows, half = kept.shape
-    return pl.pallas_call(
-        place,
-        grid_spec=pltpu.PrefetchScalarGridSpec(
-            num_scalar_prefetch=1,
-            grid=(1,),
-            in_specs=[pl.BlockSpec(memory_space=pl.ANY)] * 2,
-            out_specs=pl.BlockSpec(memory_space=pl.ANY),
-            scratch_shapes=[pltpu.SemaphoreType.DMA((2,))],
-        ),
-        out_shape=jax.ShapeDtypeStruct((rows, 2 * half), kept.dtype),
-        cost_estimate=pl.CostEstimate(
-            flops=0, bytes_accessed=8 * rows * half, transcendentals=0
-        ),
-    )(jnp.reshape(core, (1,)).astype(jnp.int32), kept, back)
-
-
 def shards(
     resid_in, contexts, out_proj, encoder, enc_bias, decoder, dec_bias, token_ids, owner_map
 ):
@@ -182,6 +147,7 @@
         order,
         jnp.concatenate([contexts[0], context_other, resid_in, resid_other], axis=1),
     ).astype(jnp.bfloat16)
+    joined = lax.optimization_barrier(joined)
     proj_both = jnp.concatenate(
         [mine(proj, 1), proj_other, placed(core), placed(1 - core)], axis=0
     )
@@ -190,14 +156,12 @@
     encoder_out, decoder_out, _ = lax.optimization_barrier(
         (theirs(encoder, 0), theirs(decoder, 1), partial)
     )
-    encoder_own, encoder_other = mine(encoder, 0), other_core(encoder_out)
+    encoder_both = jnp.concatenate([mine(encoder, 0), other_core(encoder_out)], axis=1)
     decoder_both = jnp.concatenate([mine(decoder, 1), other_core(decoder_out)], axis=0)
     my_bias = mine(dec_bias, 0).astype(jnp.float32)
     chunk = near_sum(partial)
-    chunk, encoder_own, encoder_other, decoder_both, mask_rows, my_bias, across = (
-        lax.optimization_barrier(
-            (chunk, encoder_own, encoder_other, decoder_both, mask_rows, my_bias, across)
-        )
+    chunk, encoder_both, decoder_both, mask_rows, my_bias, across = lax.optimization_barrier(
+        (chunk, encoder_both, decoder_both, mask_rows, my_bias, across)
     )
     values = far_sum(chunk).astype(jnp.bfloat16).astype(jnp.float32)
     squares = jnp.sum(values * values, axis=1, keepdims=True)
@@ -208,12 +172,11 @@
 
     exact = dict(precision=lax.Precision.HIGHEST)
 
-    def both_halves(own_weight, other_weight, values, dims):
-        sent = other_core(matmul(other_weight, values, dims))
-        kept = matmul(own_weight, values, dims)
-        return kept + matmul(sent, across.astype(jnp.float32), ((1,), (1,)), **exact)
-
-    before_relu = both_halves(encoder_own, encoder_other, centred, ((0,), (1,)))
+    def in_my_order(arrived):
+        return matmul(arrived, across.astype(jnp.float32), ((1,), (1,)), **exact)
+
+    products = matmul(centred, encoder_both).T
+    before_relu = products[:own] + in_my_order(other_core(products[own:]))
     before_relu = before_relu + enc_bias.astype(jnp.float32)[:, None]
     latents = jnp.maximum(before_relu, 0.0).astype(jnp.bfloat16)
     across_low = across.astype(jnp.bfloat16)
@@ -242,13 +205,20 @@
         return (weight.astype(jnp.float32) - step_size * grad).astype(jnp.bfloat16)
 
     decoder_own, decoder_other = decoder_both[:own], decoder_both[own:]
-    backward = both_halves(decoder_own, decoder_other, error, ((1,), (1,)))
+    over_features = ((1,), (1,))
+    arrived = other_core(matmul(decoder_other, error, over_features))
+    backward = matmul(decoder_own, error, over_features) + in_my_order(arrived)
     pre_grad = lax.optimization_barrier(
         jnp.where(before_relu > 0.0, backward, 0.0).astype(jnp.bfloat16)
     )
-    back = other_core(stepped(decoder_other, matmul(latents_other, error)))
-    new_decoder = join_columns(core, stepped(decoder_own, matmul(latents, error)), back)
-    new_encoder = stepped(encoder, matmul(centred_full, pre_grad, ((1,), (1,))))
+    back_half = other_core(stepped(decoder_other, matmul(latents_other, error)))
+    kept_half = stepped(decoder_own, matmul(latents, error))
+    new_encoder = stepped(encoder, matmul(centred_full, pre_grad, over_features))
+    new_decoder = jnp.where(
+        core == 0,
+        jnp.concatenate([kept_half, back_half], axis=1),
+        jnp.concatenate([back_half, kept_half], axis=1),
+    )
     return (owned_error, new_encoder, new_decoder)
 
 

time: 267 us -> 198 us (0.74)
  Pallas kernels: 64.6 us -> 0 us
  matrix products: 25.2 us -> 21.4 us
  local copies, waits for them, and re-layouts: 16.2 us -> 12.9 us
  other arithmetic: 6.36 us -> 9.43 us
    pallas_call x1 -> x0, Pallas kernels: 64.6 us -> none  [join_columns(): pl.pallas_call(place, grid_spec=pltpu.PrefetchScalarGridSpec(num_scalar_p...]
    dot_general x15, matrix products: 25.2 us -> 21.4 us  [matmul(): lax.dot_general(a, b, (dims, ((), ())), preferred_element_type=jnp.float3...]
    concatenate x0 -> x1, other arithmetic: none -> 2.77 us  [shards(): jnp.concatenate([mine(encoder, 0), other_core(encoder_out)], axis=1)]
  transfers between devices with their start and end apart: 15 -> 15, of which waited for: 9 -> 10; matrix products, arithmetic and copies ran while one was open for 8% -> 11% of each run, Pallas kernels for 0% -> 0%
where the time goes in v6:
time: 198 us; the launch traced here: 197 us
  blocking collectives  84.8 us (43%)
  starting transfers between devices  36.7 us (19%)
  waiting for transfers between devices  30.6 us (15%)
  matrix products  21.4 us (11%)
  local copies, waits for them, and re-layouts  12.9 us (7%)
  other arithmetic  9.43 us (5%)
    all_to_all x5, blocking collectives, all_to_all(): lax.all_to_all(pieces, AXES, 0, 0, axis_index_groups=groups, tiled=True)  84.8 us
    dot_general x15, matrix products, matmul(): lax.dot_general(a, b, (dims, ((), ())), preferred_element_type=jnp.float3...  21.4 us
    all_to_all x3, starting transfers between devices, all_to_all(): lax.all_to_all(pieces, AXES, 0, 0, axis_index_groups=groups, tiled=True)  18.5 us
    ppermute x12, waiting for transfers between devices, exchange(): return lax.ppermute(value, AXES, route)  18.3 us
    ppermute x12, starting transfers between devices, exchange(): return lax.ppermute(value, AXES, route)  18.2 us
    all_to_all x3, waiting for transfers between devices, all_to_all(): lax.all_to_all(pieces, AXES, 0, 0, axis_index_groups=groups, tiled=True)  12.3 us
    dynamic_slice x3, local copies, waits for them, and re-layouts, mine(): return lax.dynamic_slice_in_dim(weight, core * half, half, axis)  4 us
  transfers between devices with their start and end apart: 15, of which 10 were waited for; matrix products, arithmetic and copies ran while one was open for 11% of the time, Pallas kernels for 0%

profile of v6, /device:TPU:1, one launch (start us, length us, event | category | flops | bytes accessed | tf_op | source)
XLA Modules:
  0.0 196.9 jit_solution(893081891964115900)
XLA Ops:
  1.5 3.3 %collective-permute-start.1 = (bf16[256,64]{1,0:T(8,128)(2,1)S(1)}, bf16[256,64]{1,0:T(8,128)(2,1)S(1)}, u32[]{:S(2)}, u32[]{:S(2)}) collective-permute-start(bf16[256,64]{1,0:T(8,128)(2,1)S(1)} %copy.16), channel_id=1, source_target_pairs={{0,1},{1,0},{2,3},{3,2},{4,5},{5,4},{6,7},{7,6},{8,9},{9,8},{10,11... | collective-permute-start | bytes 98312 | tf_op jit(solution)/shard_map/ppermute | solution.py:63
  4.9 1.7 dynamic-slice_bitcast_fusion.1
  9.6 3.8 %convolution_convert_fusion.2 = bf16[256,4096]{1,0:T(8,128)(2,1)} fusion(bf16[256,384]{1,0:T(8,128)(2,1)S(1)} %convolution_convert_fusion.5, bf16[64,4096]{1,0:T(8,128)(2,1)S(1)} %get-tuple-element.40, bf16[64,4096]{1,0:T(8,128)(2,1)S(1)} %get-tuple-element.39, bf16[128,4096]{1,0:T(8,128)(2,1)} %collective-permute-done.2, ...), kind=kOutput, calls=%fused_computation.5 | convolution fusion | flops 818937856 | bytes 5439488 | tf_op jit(solution)/shard_map/dot_general | solution.py:75
  13.4 8.2 %all-to-all-start = ((bf16[8,32,4096]{2,1,0:T(8,128)(2,1)}), bf16[8,32,4096]{2,1,0:T(8,128)(2,1)}, u32[]{:S(2)}, u32[]{:S(2)}) async-start(bf16[8,32,4096]{2,1,0:T(8,128)(2,1)} %bitcast.49), calls=%async_computation | async-start | bytes 4194304 | tf_op jit(solution)/shard_map/all_to_all | solution.py:81
  21.6 1.2 constant_dynamic-slice_fusion
  26.4 1.3 collective-permute-done.3
  27.7 2.8 %pad_maximum_fusion = bf16[4096,256]{1,0:T(8,128)(2,1)} fusion(bf16[4096,128]{1,0:T(8,128)(2,1)} %collective-permute-done.3, bf16[4096,128]{1,0:T(8,128)(2,1)S(1)} %get-tuple-element.27), kind=kLoop, calls=%fused_computation.22 | loop fusion | flops 4194304 | bytes 4194304 | tf_op jit(solution)/shard_map/concatenate | solution.py:159
  30.6 6.1 %all-to-all-done = bf16[8,32,4096]{2,1,0:T(8,128)(2,1)} async-done(((bf16[8,32,4096]{2,1,0:T(8,128)(2,1)}), bf16[8,32,4096]{2,1,0:T(8,128)(2,1)}, u32[]{:S(2)}, u32[]{:S(2)}) %all-to-all-start) | async-done | bytes 2097184 | tf_op jit(solution)/shard_map/all_to_all | solution.py:81
  36.8 2.0 %convolution_convert_fusion.4 = bf16[32,4096]{1,0:T(8,128)(2,1)S(1)} fusion(bf16[256,4096]{1,0:T(8,128)(2,1)} %bitcast.4, s32[256]{0:T(256)S(1)} %get-tuple-element.41, s32[256]{0:T(256)S(1)} %get-tuple-element.42, pred[256]{0:T(512)(128)(4,1)S(1)} %compare_and_fusion.2), kind=kOutput, calls=%fused_computation.13 | convolution fusion | flops 67256320 | bytes 2361600 | tf_op jit(solution)/shard_map/dot_general | solution.py:75
  39.0 18.1 %all_to_all.40 = bf16[16,2,4096]{2,1,0:T(2,128)(2,1)S(1)} all-to-all(bf16[16,2,4096]{2,1,0:T(2,128)(2,1)S(1)} %reshape.125), channel_id=1, replica_groups={{0,8,16,24,32,40,48,56,64,72,80,88,96,104,112,120},{4,12,20,28,36,44,52..., dimensions={0} | all-to-all | bytes 524288 | tf_op jit(solution)/shard_map/all_to_all | solution.py:81
  57.5 2.1 %collective-permute-start.5 = (f32[2,1]{0,1:T(1,128)S(1)}, f32[2,1]{0,1:T(1,128)S(1)}, u32[]{:S(2)}, u32[]{:S(2)}) collective-permute-start(f32[2,1]{0,1:T(1,128)S(1)} %bitcast.50), channel_id=1, source_target_pairs={{0,1},{1,0},{2,3},{3,2},{4,5},{5,4},{6,7},{7,6},{8,9},{9,8},{10,11... | collective-permute-start | bytes 32 | tf_op jit(solution)/shard_map/ppermute | solution.py:63
  60.7 14.7 %all_to_all.41 = bf16[16,2,4096]{2,1,0:T(2,128)(2,1)S(1)} all-to-all(bf16[16,2,4096]{2,1,0:T(2,128)(2,1)S(1)} %broadcast_in_dim.57), channel_id=1, replica_groups={{0,8,16,24,32,40,48,56,64,72,80,88,96,104,112,120},{4,12,20,28,36,44,52..., dimensions={0} | all-to-all | bytes 524288 | tf_op jit(solution)/shard_map/all_to_all | solution.py:81
  75.8 21.1 %all_to_all.42 = bf16[8,32,4096]{2,1,0:T(8,128)(2,1)S(1)} all-to-all(bf16[8,32,4096]{2,1,0:T(8,128)(2,1)S(1)} %broadcast_in_dim.59), channel_id=1, replica_groups={{0,4,128,132,2,6,130,134},{8,12,136,140,10,14,138,142},{16,20,144,148,1..., dimensions={0} | all-to-all | bytes 4194304 | tf_op jit(solution)/shard_map/all_to_all | solution.py:81
  98.3 3.2 %collective-permute-start.6 = (f32[128,256]{1,0:T(8,128)S(1)}, f32[128,256]{1,0:T(8,128)S(1)}, u32[]{:S(2)}, u32[]{:S(2)}) collective-permute-start(f32[128,256]{1,0:T(8,128)S(1)} %slice.17), channel_id=1, source_target_pairs={{0,1},{1,0},{2,3},{3,2},{4,5},{5,4},{6,7},{7,6},{8,9},{9,8},{10,11... | collective-permute-start | bytes 393224 | tf_op jit(solution)/shard_map/ppermute | solution.py:63
  104.4 2.1 %convolution_convert_fusion.1 = bf16[256,4096]{1,0:T(8,128)(2,1)} fusion(bf16[256,4096]{1,0:T(8,128)(2,1)S(1)} %pad_maximum_fusion.1, bf16[128,256]{1,0:T(8,128)(2,1)S(1)} %convolution_convert_fusion.6, bf16[128,256]{1,0:T(8,128)(2,1)S(1)} %get-tuple-element.31), kind=kOutput, calls=%fused_computation.4 | convolution fusion | flops 538181632 | bytes 4325376 | tf_op jit(solution)/shard_map/dot_general | solution.py:75
  106.4 4.7 %all-to-all-start.4 = ((bf16[8,32,4096]{2,1,0:T(8,128)(2,1)}), bf16[8,32,4096]{2,1,0:T(8,128)(2,1)}, u32[]{:S(2)}, u32[]{:S(2)}) async-start(bf16[8,32,4096]{2,1,0:T(8,128)(2,1)} %bitcast.47), calls=%async_computation.4 | async-start | bytes 4194304 | tf_op jit(solution)/shard_map/all_to_all | solution.py:81
  111.6 2.4 %copy.17 = bf16[256,4096]{0,1:T(8,128)(2,1)} copy(bf16[256,4096]{1,0:T(8,128)(2,1)S(1)} %bitcast.46) | data formatting | bytes 4194304 | tf_op jit(solution)/shard_map/optimization_barrier | solution.py:186
  114.0 1.5 collective-permute-done.8
  115.5 2.4 %convolution_convert_fusion = bf16[4096,256]{1,0:T(8,128)(2,1)S(1)} fusion(bf16[256,4096]{1,0:T(8,128)(2,1)} %collective-permute-done.8, pred[256,256]{1,0:T(32,128)(4,1)S(1)} %fusion.55), kind=kOutput, calls=%fused_computation.3 | convolution fusion | flops 537919488 | bytes 4259840 | tf_op jit(solution)/shard_map/dot_general | solution.py:75
  117.9 2.6 %maximum_select_fusion = bf16[8192,256]{1,0:T(8,128)(2,1)} fusion(bf16[4096,256]{1,0:T(8,128)(2,1)S(1)} %convolution_convert_fusion, bf16[4096,256]{1,0:T(8,128)(2,1)S(1)} %bitcast.48, pred[]{:T(512)S(6)} %eq.72), kind=kLoop, calls=%fused_computation.14 | loop fusion | flops 18874368 | bytes 8388609 | tf_op jit(solution)/shard_map/jit(_where)/select_n | solution.py:191
  120.4 6.2 %all-to-all-done.4 = bf16[8,32,4096]{2,1,0:T(8,128)(2,1)} async-done(((bf16[8,32,4096]{2,1,0:T(8,128)(2,1)}), bf16[8,32,4096]{2,1,0:T(8,128)(2,1)}, u32[]{:S(2)}, u32[]{:S(2)}) %all-to-all-start.4) | async-done | bytes 2097184 | tf_op jit(solution)/shard_map/all_to_all | solution.py:81
  126.6 2.0 %convolution_convert_fusion.3 = bf16[32,4096]{1,0:T(8,128)(2,1)S(1)} fusion(bf16[256,4096]{1,0:T(8,128)(2,1)} %bitcast.11, s32[256]{0:T(256)S(1)} %get-tuple-element.41, s32[256]{0:T(256)S(1)} %get-tuple-element.42, pred[256]{0:T(512)(128)(4,1)S(1)} %compare_and_fusion.2), kind=kOutput, calls=%fused_computation.12 | convolution fusion | flops 67256320 | bytes 2361600 | tf_op jit(solution)/shard_map/dot_general | solution.py:75
  128.8 14.9 %all_to_all.43 = bf16[16,2,4096]{2,1,0:T(2,128)(2,1)S(1)} all-to-all(bf16[16,2,4096]{2,1,0:T(2,128)(2,1)S(1)} %reshape.129), channel_id=1, replica_groups={{0,8,16,24,32,40,48,56,64,72,80,88,96,104,112,120},{4,12,20,28,36,44,52..., dimensions={0} | all-to-all | bytes 524288 | tf_op jit(solution)/shard_map/all_to_all | solution.py:81
  144.2 15.9 %all_to_all.44 = bf16[16,2,4096]{2,1,0:T(2,128)(2,1)S(1)} all-to-all(bf16[16,2,4096]{2,1,0:T(2,128)(2,1)S(1)} %broadcast_in_dim.60), channel_id=1, replica_groups={{0,8,16,24,32,40,48,56,64,72,80,88,96,104,112,120},{4,12,20,28,36,44,52..., dimensions={0} | all-to-all | bytes 524288 | tf_op jit(solution)/shard_map/all_to_all | solution.py:81
  160.2 1.6 broadcast_in_dim.62
  161.8 5.6 %all-to-all-start.7 = ((bf16[8,32,4096]{2,1,0:T(8,128)(2,1)}), bf16[8,32,4096]{2,1,0:T(8,128)(2,1)S(1)}, u32[]{:S(2)}, u32[]{:S(2)}) async-start(bf16[8,32,4096]{2,1,0:T(8,128)(2,1)} %broadcast_in_dim.62), calls=%async_computation.7 | async-start | bytes 4194304 | tf_op jit(solution)/shard_map/all_to_all | solution.py:81
  167.4 5.0 %collective-permute-start.9 = (bf16[2,4096]{1,0:T(2,128)(2,1)S(1)}, bf16[2,4096]{1,0:T(2,128)(2,1)S(1)}, u32[]{:S(2)}, u32[]{:S(2)}) collective-permute-start(bf16[2,4096]{1,0:T(2,128)(2,1)S(1)} %multiply_convert_fusion), channel_id=1, source_target_pairs={{0,0},{1,128},{2,2},{3,130},{4,4},{5,132},{6,6},{7,134},{8,8},{9,1... | collective-permute-start | bytes 49160 | tf_op jit(solution)/shard_map/ppermute | solution.py:63
  172.5 11.3 %collective-permute-done.9 = bf16[2,4096]{1,0:T(2,128)(2,1)S(1)} collective-permute-done((bf16[2,4096]{1,0:T(2,128)(2,1)S(1)}, bf16[2,4096]{1,0:T(2,128)(2,1)S(1)}, u32[]{:S(2)}, u32[]{:S(2)}) %collective-permute-start.9) | collective-permute-done | bytes 16416 | tf_op jit(solution)/shard_map/ppermute | solution.py:63
  183.7 1.9 fusion.5
  186.3 2.5 %collective-permute-start.11 = (bf16[128,4096]{1,0:T(8,128)(2,1)S(1)}, bf16[128,4096]{1,0:T(8,128)(2,1)S(1)}, u32[]{:S(2)}, u32[]{:S(2)}) collective-permute-start(bf16[128,4096]{1,0:T(8,128)(2,1)S(1)} %fusion.5), channel_id=1, source_target_pairs={{0,1},{1,0},{2,3},{3,2},{4,5},{5,4},{6,7},{7,6},{8,9},{9,8},{10,11... | collective-permute-start | bytes 3145736 | tf_op jit(solution)/shard_map/ppermute | solution.py:63
  191.8 2.6 %fusion.1 = bf16[8192,128]{1,0:T(8,128)(2,1)} fusion(bf16[8192,256]{1,0:T(8,128)(2,1)S(1)} %copy-done.2, bf16[128,256]{1,0:T(8,128)(2,1)S(1)} %select_convert_fusion, bf16[8192,128]{1,0:T(8,128)(2,1)S(1)} %copy-done.6), kind=kOutput, calls=%fused_computation.2 | convolution fusion | flops 541065216 | bytes 8454144 | tf_op jit(solution)/shard_map/dot_general | solution.py:75
  194.4 1.8 maximum_select_fusion.1
  (92 shorter events, 19.3 us)
Async XLA Ops:
  1.5 6.3 %collective-permute-start.1 = (bf16[256,64]{1,0:T(8,128)(2,1)S(1)}, bf16[256,64]{1,0:T(8,128)(2,1)S(1)}, u32[]{:S(2)}, u32[]{:S(2)}) collective-permute-start(bf16[256,64]{1,0:T(8,128)(2,1)S(1)} %copy.16), channel_id=1, source_target_pairs={{0,1},{1,0},{2,3},{3,2},{4,5},{5,4},{6,7},{7,6},{8,9},{9,8},{10,11... | collective-permute-start | bytes 98312 | tf_op jit(solution)/shard_map/ppermute | solution.py:63
  4.8 3.0 %collective-permute-start = (bf16[256,128]{1,0:T(8,128)(2,1)}, bf16[256,128]{1,0:T(8,128)(2,1)S(1)}, u32[]{:S(2)}, u32[]{:S(2)}) collective-permute-start(bf16[256,128]{1,0:T(8,128)(2,1)} %bitcast.51), channel_id=1, source_target_pairs={{0,1},{1,0},{2,3},{3,2},{4,5},{5,4},{6,7},{7,6},{8,9},{9,8},{10,11... | collective-permute-start | bytes 196616 | tf_op jit(solution)/shard_map/ppermute | solution.py:63
  4.9 2.6 %copy-start.13 = (s32[128]{0:T(128)S(1)}, s32[128]{0:T(128)}, u32[]{:S(2)}) copy-start(s32[128]{0:T(128)} %param.17) | copy-start | bytes 1540
  4.9 2.9 %copy-start.14 = (bf16[1,256,128]{2,1,0:T(8,128)(2,1)S(1)}, bf16[1,256,128]{2,1,0:T(8,128)(2,1)}, u32[]{:S(2)}) copy-start(bf16[1,256,128]{2,1,0:T(8,128)(2,1)} %param.10) | copy-start | bytes 196612
  6.6 2.9 %collective-permute-start.2 = (bf16[128,4096]{1,0:T(8,128)(2,1)S(1)}, bf16[128,4096]{1,0:T(8,128)(2,1)}, u32[]{:S(2)}, u32[]{:S(2)}) collective-permute-start(bf16[128,4096]{1,0:T(8,128)(2,1)S(1)} %get-tuple-element.30), channel_id=1, source_target_pairs={{0,1},{1,0},{2,3},{3,2},{4,5},{5,4},{6,7},{7,6},{8,9},{9,8},{10,11... | collective-permute-start | bytes 3145736 | tf_op jit(solution)/shard_map/ppermute | solution.py:63
  13.4 8.2 %copy-start.12 = (s32[256]{0:T(256)S(1)}, s32[256]{0:T(256)}, u32[]{:S(2)}) copy-start(s32[256]{0:T(256)} %param.16) | copy-start | bytes 3076
  13.4 8.2 %copy-start.9 = (bf16[128,8192]{1,0:T(8,128)(2,1)S(1)}, bf16[128,8192]{1,0:T(8,128)(2,1)}, u32[]{:S(2)}) copy-start(bf16[128,8192]{1,0:T(8,128)(2,1)} %param.14) | copy-start | bytes 6291460
  13.4 23.4 %all-to-all-start = ((bf16[8,32,4096]{2,1,0:T(8,128)(2,1)}), bf16[8,32,4096]{2,1,0:T(8,128)(2,1)}, u32[]{:S(2)}, u32[]{:S(2)}) async-start(bf16[8,32,4096]{2,1,0:T(8,128)(2,1)} %bitcast.49), calls=%async_computation | async-start | bytes 4194304 | tf_op jit(solution)/shard_map/all_to_all | solution.py:81
  21.6 2.0 %copy-start.5 = (bf16[8192,128]{1,0:T(8,128)(2,1)S(1)}, bf16[8192,128]{1,0:T(8,128)(2,1)}, u32[]{:S(2)}) copy-start(bf16[8192,128]{1,0:T(8,128)(2,1)} %param.12) | copy-start | bytes 6291460
  23.6 1.3 copy-start.11
  23.6 1.6 copy-start.10
  24.7 3.0 %collective-permute-start.3 = (bf16[4096,128]{1,0:T(8,128)(2,1)}, bf16[4096,128]{1,0:T(8,128)(2,1)}, u32[]{:S(2)}, u32[]{:S(2)}) collective-permute-start(bf16[4096,128]{1,0:T(8,128)(2,1)} %get-tuple-element.14), channel_id=1, source_target_pairs={{0,1},{1,0},{2,3},{3,2},{4,5},{5,4},{6,7},{7,6},{8,9},{9,8},{10,11... | collective-permute-start | bytes 3145736 | tf_op jit(solution)/shard_map/ppermute | solution.py:63
  25.2 5.3 %collective-permute-start.4 = (bf16[128,4096]{1,0:T(8,128)(2,1)S(1)}, bf16[128,4096]{1,0:T(8,128)(2,1)S(1)}, u32[]{:S(2)}, u32[]{:S(2)}) collective-permute-start(bf16[128,4096]{1,0:T(8,128)(2,1)S(1)} %copy-done.10), channel_id=1, source_target_pairs={{0,1},{1,0},{2,3},{3,2},{4,5},{5,4},{6,7},{7,6},{8,9},{9,8},{10,11... | collective-permute-start | bytes 3145736 | tf_op jit(solution)/shard_map/ppermute | solution.py:63
  30.6 73.7 %copy-start = (bf16[256,4096]{1,0:T(8,128)(2,1)}, bf16[256,4096]{1,0:T(8,128)(2,1)S(1)}, u32[]{:S(2)}) copy-start(bf16[256,4096]{1,0:T(8,128)(2,1)S(1)} %pad_maximum_fusion.1) | copy-start | bytes 6291460
  57.5 2.9 %collective-permute-start.5 = (f32[2,1]{0,1:T(1,128)S(1)}, f32[2,1]{0,1:T(1,128)S(1)}, u32[]{:S(2)}, u32[]{:S(2)}) collective-permute-start(f32[2,1]{0,1:T(1,128)S(1)} %bitcast.50), channel_id=1, source_target_pairs={{0,1},{1,0},{2,3},{3,2},{4,5},{5,4},{6,7},{7,6},{8,9},{9,8},{10,11... | collective-permute-start | bytes 32 | tf_op jit(solution)/shard_map/ppermute | solution.py:63
  75.8 21.1 %copy-start.7 = (bf16[4096,256]{1,0:T(8,128)(2,1)S(1)}, bf16[4096,256]{1,0:T(8,128)(2,1)}, u32[]{:S(2)}) copy-start(bf16[4096,256]{1,0:T(8,128)(2,1)} %pad_maximum_fusion) | copy-start | bytes 6291460
  97.0 1.3 copy-start.3
  97.0 4.6 %copy-start.15 = (bf16[128]{0:T(256)(128)(2,1)S(1)}, bf16[128]{0:T(256)(128)(2,1)}, u32[]{:S(2)}) copy-start(bf16[128]{0:T(256)(128)(2,1)} %param.13) | copy-start | bytes 772
  98.3 4.2 %collective-permute-start.6 = (f32[128,256]{1,0:T(8,128)S(1)}, f32[128,256]{1,0:T(8,128)S(1)}, u32[]{:S(2)}, u32[]{:S(2)}) collective-permute-start(f32[128,256]{1,0:T(8,128)S(1)} %slice.17), channel_id=1, source_target_pairs={{0,1},{1,0},{2,3},{3,2},{4,5},{5,4},{6,7},{7,6},{8,9},{9,8},{10,11... | collective-permute-start | bytes 393224 | tf_op jit(solution)/shard_map/ppermute | solution.py:63
  102.8 1.4 collective-permute-start.7
  106.4 4.7 %copy-start.4 = (bf16[8,32,4096]{2,1,0:T(8,128)(2,1)S(1)}, bf16[8,32,4096]{2,1,0:T(8,128)(2,1)}, u32[]{:S(2)}) copy-start(bf16[8,32,4096]{2,1,0:T(8,128)(2,1)} %copy-done.3) | copy-start | bytes 6291460
  106.4 20.1 %all-to-all-start.4 = ((bf16[8,32,4096]{2,1,0:T(8,128)(2,1)}), bf16[8,32,4096]{2,1,0:T(8,128)(2,1)}, u32[]{:S(2)}, u32[]{:S(2)}) async-start(bf16[8,32,4096]{2,1,0:T(8,128)(2,1)} %bitcast.47), calls=%async_computation.4 | async-start | bytes 4194304 | tf_op jit(solution)/shard_map/all_to_all | solution.py:81
  111.1 4.4 %collective-permute-start.8 = (bf16[256,4096]{1,0:T(8,128)(2,1)S(1)}, bf16[256,4096]{1,0:T(8,128)(2,1)}, u32[]{:S(2)}, u32[]{:S(2)}) collective-permute-start(bf16[256,4096]{1,0:T(8,128)(2,1)S(1)} %bitcast.45), channel_id=1, source_target_pairs={{0,1},{1,0},{2,3},{3,2},{4,5},{5,4},{6,7},{7,6},{8,9},{9,8},{10,11... | collective-permute-start | bytes 6291464 | tf_op jit(solution)/shard_map/ppermute | solution.py:63
  114.0 3.8 %copy-start.8 = (bf16[256,4096]{0,1:T(8,128)(2,1)S(1)}, bf16[256,4096]{0,1:T(8,128)(2,1)}, u32[]{:S(2)}) copy-start(bf16[256,4096]{0,1:T(8,128)(2,1)} %copy.17) | copy-start | bytes 6291460
  161.8 21.9 %all-to-all-start.7 = ((bf16[8,32,4096]{2,1,0:T(8,128)(2,1)}), bf16[8,32,4096]{2,1,0:T(8,128)(2,1)S(1)}, u32[]{:S(2)}, u32[]{:S(2)}) async-start(bf16[8,32,4096]{2,1,0:T(8,128)(2,1)} %broadcast_in_dim.62), calls=%async_computation.7 | async-start | bytes 4194304 | tf_op jit(solution)/shard_map/all_to_all | solution.py:81
  167.4 16.3 %collective-permute-start.9 = (bf16[2,4096]{1,0:T(2,128)(2,1)S(1)}, bf16[2,4096]{1,0:T(2,128)(2,1)S(1)}, u32[]{:S(2)}, u32[]{:S(2)}) collective-permute-start(bf16[2,4096]{1,0:T(2,128)(2,1)S(1)} %multiply_convert_fusion), channel_id=1, source_target_pairs={{0,0},{1,128},{2,2},{3,130},{4,4},{5,132},{6,6},{7,134},{8,8},{9,1... | collective-permute-start | bytes 49160 | tf_op jit(solution)/shard_map/ppermute | solution.py:63
  183.7 1.9 copy-start.1
  186.3 8.2 %collective-permute-start.11 = (bf16[128,4096]{1,0:T(8,128)(2,1)S(1)}, bf16[128,4096]{1,0:T(8,128)(2,1)S(1)}, u32[]{:S(2)}, u32[]{:S(2)}) collective-permute-start(bf16[128,4096]{1,0:T(8,128)(2,1)S(1)} %fusion.5), channel_id=1, source_target_pairs={{0,1},{1,0},{2,3},{3,2},{4,5},{5,4},{6,7},{7,6},{8,9},{9,8},{10,11... | collective-permute-start | bytes 3145736 | tf_op jit(solution)/shard_map/ppermute | solution.py:63
  188.7 2.8 %copy-start.2 = (bf16[8192,256]{1,0:T(8,128)(2,1)S(1)}, bf16[8192,256]{1,0:T(8,128)(2,1)}, u32[]{:S(2)}) copy-start(bf16[8192,256]{1,0:T(8,128)(2,1)} %maximum_select_fusion) | copy-start | bytes 12582916
  189.6 2.2 %copy-start.6 = (bf16[8192,128]{1,0:T(8,128)(2,1)S(1)}, bf16[8192,128]{1,0:T(8,128)(2,1)}, u32[]{:S(2)}) copy-start(bf16[8192,128]{1,0:T(8,128)(2,1)} %param.12) | copy-start | bytes 6291460
  189.6 1.6 collective-permute-start.10

commit v7 on v6

--- a/solution.py
+++ b/solution.py
@@ -86,13 +86,9 @@
     return all_to_all(stacked, groups).reshape(-1, value.shape[1])
 
 
-def near_sum(partial):
+def near_sum(partial, adds):
     tokens, width = partial.shape
-    depth = tokens // NEAR
-    pieces = all_to_all(partial.reshape(NEAR, depth, width), NEAR_GROUPS)
-    to = lax.broadcasted_iota(jnp.int32, (depth, tokens), 0)
-    of = lax.broadcasted_iota(jnp.int32, (depth, tokens), 1)
-    adds = (of % depth == to).astype(jnp.bfloat16)
+    pieces = all_to_all(partial.reshape(NEAR, tokens // NEAR, width), NEAR_GROUPS)
     return matmul(adds, pieces.reshape(tokens, width)).astype(jnp.bfloat16)
 
 
@@ -112,16 +108,19 @@
     y, z, xh, xl, core = (lax.axis_index(a) for a in ("y", "z", "xh", "xl", "c"))
     chip = (y * 8 + z) * 4 + xh * 2 + xl
 
-    def mine(weight, axis):
+    def mine(weight, axis, core):
         return lax.dynamic_slice_in_dim(weight, core * half, half, axis)
 
-    def theirs(weight, axis):
+    def theirs(weight, axis, core):
         return lax.dynamic_slice_in_dim(weight, (1 - core) * half, half, axis)
 
     proj = out_proj[0]
-    proj_other = other_core(theirs(proj, 1))
-    context_other = other_core(contexts[0])
-    resid_other = other_core(resid_in)
+    proj_out, resid, context, core_head = lax.optimization_barrier(
+        (theirs(proj, 1, core), resid_in, contexts[0], core)
+    )
+    proj_other = other_core(proj_out)
+    context_other = other_core(context)
+    resid_other = other_core(resid)
 
     row = lax.broadcasted_iota(jnp.int32, (tokens, tokens), 0)
     old = lax.broadcasted_iota(jnp.int32, (tokens, tokens), 1)
@@ -129,9 +128,6 @@
     at = chip_of(row // block_rows, core)
     owner_of_row = jnp.repeat(owner_map, block_rows)
     order = ((owner_of_row[None, :] == at) & same_place).astype(jnp.bfloat16)
-    across = (chip_of(old // block_rows, 1 - core) == at) & same_place
-    kept = (token_ids.reshape(blocks, block_rows) != BOS).astype(jnp.float32)
-    mask_rows = jnp.sum(jnp.where((owner_map == chip)[:, None], kept, 0.0), axis=0)[:, None]
 
     start = ((y * 8 + z) * 2 + xh) * 2 * width
     owns = (start // half == core) & (xl == 0)
@@ -143,27 +139,50 @@
         )
         return ((column == target) & owns).astype(jnp.bfloat16)
 
+    depth = tokens // NEAR
+    to = lax.broadcasted_iota(jnp.int32, (depth, tokens), 0)
+    of = lax.broadcasted_iota(jnp.int32, (depth, tokens), 1)
     joined = matmul(
-        order,
-        jnp.concatenate([contexts[0], context_other, resid_in, resid_other], axis=1),
+        order, jnp.concatenate([context, context_other, resid, resid_other], axis=1)
     ).astype(jnp.bfloat16)
-    joined = lax.optimization_barrier(joined)
+    joined, adds = lax.optimization_barrier(
+        (joined, (of % depth == to).astype(jnp.bfloat16))
+    )
     proj_both = jnp.concatenate(
-        [mine(proj, 1), proj_other, placed(core), placed(1 - core)], axis=0
+        [mine(proj, 1, core_head), proj_other, placed(core), placed(1 - core)], axis=0
     )
     partial = matmul(joined, proj_both).astype(jnp.bfloat16)
 
-    encoder_out, decoder_out, _ = lax.optimization_barrier(
-        (theirs(encoder, 0), theirs(decoder, 1), partial)
-    )
-    encoder_both = jnp.concatenate([mine(encoder, 0), other_core(encoder_out)], axis=1)
-    decoder_both = jnp.concatenate([mine(decoder, 1), other_core(decoder_out)], axis=0)
-    my_bias = mine(dec_bias, 0).astype(jnp.float32)
-    chunk = near_sum(partial)
-    chunk, encoder_both, decoder_both, mask_rows, my_bias, across = lax.optimization_barrier(
-        (chunk, encoder_both, decoder_both, mask_rows, my_bias, across)
-    )
-    values = far_sum(chunk).astype(jnp.bfloat16).astype(jnp.float32)
+    chunk = near_sum(partial, adds)
+    core_far, chip_far, owner_far, ids_far, bias_far, _ = lax.optimization_barrier(
+        (core, chip, owner_map, token_ids, enc_bias, chunk)
+    )
+    encoder_both = jnp.concatenate(
+        [mine(encoder, 0, core_far), other_core(theirs(encoder, 0, core_far))], axis=1
+    )
+    decoder_both = jnp.concatenate(
+        [mine(decoder, 1, core_far), other_core(theirs(decoder, 1, core_far))], axis=0
+    )
+    my_bias = mine(dec_bias, 0, core_far).astype(jnp.float32)
+    across = (
+        chip_of(old // block_rows, 1 - core_far) == chip_of(row // block_rows, core_far)
+    ) & same_place
+    kept = (ids_far.reshape(blocks, block_rows) != BOS).astype(jnp.float32)
+    mask_rows = jnp.sum(jnp.where((owner_far == chip_far)[:, None], kept, 0.0), axis=0)[:, None]
+    summed, encoder_both, decoder_both, mask_rows, my_bias, across, lat_bias = (
+        lax.optimization_barrier(
+            (
+                far_sum(chunk),
+                encoder_both,
+                decoder_both,
+                mask_rows,
+                my_bias,
+                across.astype(jnp.float32),
+                bias_far.astype(jnp.float32)[:, None],
+            )
+        )
+    )
+    values = summed.astype(jnp.bfloat16).astype(jnp.float32)
     squares = jnp.sum(values * values, axis=1, keepdims=True)
     squares = squares + other_core(squares)
     inverse_rms = lax.rsqrt(squares / features + 1e-05)
@@ -173,17 +192,18 @@
     exact = dict(precision=lax.Precision.HIGHEST)
 
     def in_my_order(arrived):
-        return matmul(arrived, across.astype(jnp.float32), ((1,), (1,)), **exact)
+        return matmul(arrived, across, ((1,), (1,)), **exact)
 
     products = matmul(centred, encoder_both).T
     before_relu = products[:own] + in_my_order(other_core(products[own:]))
-    before_relu = before_relu + enc_bias.astype(jnp.float32)[:, None]
+    before_relu = before_relu + lat_bias
     latents = jnp.maximum(before_relu, 0.0).astype(jnp.bfloat16)
     across_low = across.astype(jnp.bfloat16)
     latents_other = matmul(other_core(latents), across_low, ((1,), (1,))).astype(jnp.bfloat16)
     latents_both = jnp.concatenate([latents, latents_other], axis=0)
     partial = matmul(latents_both, decoder_both, ((0,), (0,))).astype(jnp.bfloat16)
-    later, _ = lax.optimization_barrier((centred, partial))
+    chunk = near_sum(partial, adds)
+    later, _ = lax.optimization_barrier((centred, chunk))
     centred_other = matmul(
         other_core(later), across_low, ((0,), (1,))
     ).astype(jnp.bfloat16)
@@ -193,12 +213,12 @@
         jnp.concatenate([centred_own, centred_other], axis=0),
         jnp.concatenate([centred_other, centred_own], axis=0),
     )
-    chunk = near_sum(partial)
-    chunk, centred_full = lax.optimization_barrier((chunk, centred_full))
-    rebuilt = far_sum(chunk)
+    rebuilt, centred_full = lax.optimization_barrier((far_sum(chunk), centred_full))
     my_error = (mask_rows * (rebuilt - my_centred.astype(jnp.float32))).astype(jnp.bfloat16)
-    owned_error = core_and_section(my_error)
-    error = spread(spread(my_error, FAR_GROUPS, FAR), NEAR_GROUPS, NEAR)
+    error_rows, owned_error = lax.optimization_barrier(
+        (spread(my_error, FAR_GROUPS, FAR), core_and_section(my_error))
+    )
+    error = spread(error_rows, NEAR_GROUPS, NEAR)
     step_size = STEP_RATE / tokens
 
     def stepped(weight, grad):

time: 198 us -> 216 us (1.091)
  blocking collectives: 84.8 us -> 55.6 us
  waiting for transfers between devices: 30.6 us -> 51.6 us
  starting transfers between devices: 36.7 us -> 49 us
  local copies, waits for them, and re-layouts: 12.9 us -> 17.9 us
  matrix products: 21.4 us -> 26.3 us
  other arithmetic: 9.43 us -> 14.2 us
    all_to_all x3 -> x5, waiting for transfers between devices: 12.3 us -> 48.8 us  [all_to_all(): lax.all_to_all(pieces, AXES, 0, 0, axis_index_groups=groups, tiled=True)]
    all_to_all x5 -> x3, blocking collectives: 84.8 us -> 55.6 us  [all_to_all(): lax.all_to_all(pieces, AXES, 0, 0, axis_index_groups=groups, tiled=True)]
    ppermute x12, waiting for transfers between devices: 18.3 us -> 2.73 us  [exchange(): return lax.ppermute(value, AXES, route)]
    all_to_all x3 -> x5, starting transfers between devices: 18.5 us -> 33.9 us  [all_to_all(): lax.all_to_all(pieces, AXES, 0, 0, axis_index_groups=groups, tiled=True)]
    dot_general x15, matrix products: 21.4 us -> 26.3 us  [matmul(): lax.dot_general(a, b, (dims, ((), ())), preferred_element_type=jnp.float3...]
    ppermute x12, starting transfers between devices: 18.2 us -> 15.1 us  [exchange(): return lax.ppermute(value, AXES, route)]
    concatenate x2, other arithmetic: 2.93 us -> 5.85 us  [the longest x1 3.08 us: shards(): jnp.concatenate([mine(decoder, 1, core_far), other_core(theirs(decoder, 1...]
  transfers between devices with their start and end apart: 15 -> 17, of which waited for: 10 -> 8; matrix products, arithmetic and copies ran while one was open for 11% -> 12% of each run, Pallas kernels for 0% -> 0%
where the time goes in v7:
time: 216 us
  blocking collectives  55.6 us (26%)
  waiting for transfers between devices  51.6 us (24%)
  starting transfers between devices  49 us (23%)
  matrix products  26.3 us (12%)
  local copies, waits for them, and re-layouts  17.9 us (8%)
  other arithmetic  14.2 us (7%)
    all_to_all x3, blocking collectives, all_to_all(): lax.all_to_all(pieces, AXES, 0, 0, axis_index_groups=groups, tiled=True)  55.6 us
    all_to_all x5, waiting for transfers between devices, all_to_all(): lax.all_to_all(pieces, AXES, 0, 0, axis_index_groups=groups, tiled=True)  48.8 us
    all_to_all x5, starting transfers between devices, all_to_all(): lax.all_to_all(pieces, AXES, 0, 0, axis_index_groups=groups, tiled=True)  33.9 us
    dot_general x15, matrix products, matmul(): lax.dot_general(a, b, (dims, ((), ())), preferred_element_type=jnp.float3...  26.3 us
    ppermute x12, starting transfers between devices, exchange(): return lax.ppermute(value, AXES, route)  15.1 us
    dynamic_slice x3, local copies, waits for them, and re-layouts, mine(): return lax.dynamic_slice_in_dim(weight, core * half, half, axis)  5.4 us
  transfers between devices with their start and end apart: 17, of which 8 were waited for; matrix products, arithmetic and copies ran while one was open for 12% of the time, Pallas kernels for 0%

profile of v7, /device:TPU:1, one launch (start us, length us, event | category | flops | bytes accessed | tf_op | source)
XLA Modules:
  0.0 215.5 jit_solution(14356173860586698412)
XLA Ops:
  2.5 3.3 %collective-permute-start.1 = (bf16[256,64]{1,0:T(8,128)(2,1)S(1)}, bf16[256,64]{1,0:T(8,128)(2,1)S(1)}, u32[]{:S(2)}, u32[]{:S(2)}) collective-permute-start(bf16[256,64]{1,0:T(8,128)(2,1)S(1)} %copy.16), channel_id=1, source_target_pairs={{0,1},{1,0},{2,3},{3,2},{4,5},{5,4},{6,7},{7,6},{8,9},{9,8},{10,11... | collective-permute-start | bytes 98312 | tf_op jit(solution)/shard_map/ppermute | solution.py:63
  10.5 3.8 %convolution_convert_fusion.2 = bf16[256,4096]{1,0:T(8,128)(2,1)} fusion(bf16[256,384]{1,0:T(8,128)(2,1)S(1)} %convolution_convert_fusion.5, bf16[64,4096]{1,0:T(8,128)(2,1)S(1)} %copy-done.10, bf16[64,4096]{1,0:T(8,128)(2,1)S(1)} %copy-done.9, bf16[128,4096]{1,0:T(8,128)(2,1)} %collective-permute-done.2, bf16[128,4096]{1,0:T(8,128)(2,1)S(1)} %copy-done.8), kind=kOutput, calls=%fused_computation.5 | convolution fusion | flops 818937856 | bytes 5439488 | tf_op jit(solution)/shard_map/dot_general | solution.py:75
  14.3 8.1 %all-to-all-start = ((bf16[8,32,4096]{2,1,0:T(8,128)(2,1)}), bf16[8,32,4096]{2,1,0:T(8,128)(2,1)}, u32[]{:S(2)}, u32[]{:S(2)}) async-start(bf16[8,32,4096]{2,1,0:T(8,128)(2,1)} %bitcast.47), calls=%async_computation | async-start | bytes 4194304 | tf_op jit(solution)/shard_map/all_to_all | solution.py:81
  22.4 15.2 %all-to-all-done = bf16[8,32,4096]{2,1,0:T(8,128)(2,1)} async-done(((bf16[8,32,4096]{2,1,0:T(8,128)(2,1)}), bf16[8,32,4096]{2,1,0:T(8,128)(2,1)}, u32[]{:S(2)}, u32[]{:S(2)}) %all-to-all-start) | async-done | bytes 2097184 | tf_op jit(solution)/shard_map/all_to_all | solution.py:81
  37.6 2.1 convolution_convert_fusion.4
  40.7 7.7 %all-to-all-start.1 = ((bf16[16,2,4096]{2,1,0:T(2,128)(2,1)}), bf16[16,2,4096]{2,1,0:T(2,128)(2,1)}, u32[]{:S(2)}, u32[]{:S(2)}) async-start(bf16[16,2,4096]{2,1,0:T(2,128)(2,1)} %reshape.49), calls=%async_computation.1 | async-start | bytes 524288 | tf_op jit(solution)/shard_map/all_to_all | solution.py:81
  48.4 3.2 %constant_dynamic-slice_fusion.1 = (bf16[128,4096]{1,0:T(8,128)(2,1)}, bf16[128,4096]{1,0:T(8,128)(2,1)}) fusion(bf16[128,8192]{1,0:T(8,128)(2,1)} %param.14, s32[]{:T(128)S(6)} %select_n.268, s32[]{:T(128)S(6)} %select_n.269), kind=kLoop, calls=%fused_computation.180 | loop fusion | bytes 4194312 | tf_op jit(solution)/shard_map/dynamic_slice | solution.py:112
  54.2 5.0 %all-to-all-done.1 = bf16[16,2,4096]{2,1,0:T(2,128)(2,1)} async-done(((bf16[16,2,4096]{2,1,0:T(2,128)(2,1)}), bf16[16,2,4096]{2,1,0:T(2,128)(2,1)}, u32[]{:S(2)}, u32[]{:S(2)}) %all-to-all-start.1) | async-done | bytes 262176 | tf_op jit(solution)/shard_map/all_to_all | solution.py:81
  60.4 3.1 %pad_maximum_fusion.1 = bf16[256,4096]{1,0:T(8,128)(2,1)} fusion(bf16[128,4096]{1,0:T(8,128)(2,1)} %collective-permute-done.4, bf16[128,4096]{1,0:T(8,128)(2,1)} %get-tuple-element.49), kind=kLoop, calls=%fused_computation.23 | loop fusion | flops 4194304 | bytes 4194304 | tf_op jit(solution)/shard_map/concatenate | solution.py:163
  63.5 2.8 %pad_maximum_fusion = bf16[4096,256]{1,0:T(8,128)(2,1)} fusion(bf16[4096,128]{1,0:T(8,128)(2,1)} %collective-permute-done.3, bf16[4096,128]{1,0:T(8,128)(2,1)S(1)} %get-tuple-element.51), kind=kLoop, calls=%fused_computation.22 | loop fusion | flops 4194304 | bytes 4194304 | tf_op jit(solution)/shard_map/concatenate | solution.py:160
  69.4 15.1 %all_to_all.40 = bf16[16,2,4096]{2,1,0:T(2,128)(2,1)S(1)} all-to-all(bf16[16,2,4096]{2,1,0:T(2,128)(2,1)S(1)} %broadcast_in_dim.63), channel_id=1, replica_groups={{0,8,16,24,32,40,48,56,64,72,80,88,96,104,112,120},{4,12,20,28,36,44,52..., dimensions={0} | all-to-all | bytes 524288 | tf_op jit(solution)/shard_map/all_to_all | solution.py:81
  84.8 20.7 %all_to_all.41 = bf16[8,32,4096]{2,1,0:T(8,128)(2,1)} all-to-all(bf16[8,32,4096]{2,1,0:T(8,128)(2,1)S(1)} %broadcast_in_dim.65), channel_id=1, replica_groups={{0,4,128,132,2,6,130,134},{8,12,136,140,10,14,138,142},{16,20,144,148,1..., dimensions={0} | all-to-all | bytes 4194304 | tf_op jit(solution)/shard_map/all_to_all | solution.py:81
  105.5 2.5 %fusion.108 = f32[256,256]{1,0:T(8,128)S(1)} fusion(bf16[4096,256]{1,0:T(8,128)(2,1)S(1)} %copy-done.6, bf16[256,4096]{1,0:T(8,128)(2,1)} %bitcast.10), kind=kOutput, calls=%fused_computation.205 | convolution fusion | flops 536870912 | bytes 4456448 | tf_op jit(solution)/shard_map/dot_general | solution.py:75
  108.1 3.3 %collective-permute-start.6 = (f32[128,256]{1,0:T(8,128)S(1)}, f32[128,256]{1,0:T(8,128)S(1)}, u32[]{:S(2)}, u32[]{:S(2)}) collective-permute-start(f32[128,256]{1,0:T(8,128)S(1)} %slice.17), channel_id=1, source_target_pairs={{0,1},{1,0},{2,3},{3,2},{4,5},{5,4},{6,7},{7,6},{8,9},{9,8},{10,11... | collective-permute-start | bytes 393224 | tf_op jit(solution)/shard_map/ppermute | solution.py:63
  115.2 19.8 %all_to_all.42 = bf16[8,32,4096]{2,1,0:T(8,128)(2,1)S(1)} all-to-all(bf16[8,32,4096]{2,1,0:T(8,128)(2,1)S(1)} %bitcast.45), channel_id=1, replica_groups={{0,4,128,132,2,6,130,134},{8,12,136,140,10,14,138,142},{16,20,144,148,1..., dimensions={0} | all-to-all | bytes 4194304 | tf_op jit(solution)/shard_map/all_to_all | solution.py:81
  136.6 4.2 %all-to-all-start.5 = ((bf16[16,2,4096]{2,1,0:T(2,128)(2,1)}), bf16[16,2,4096]{2,1,0:T(2,128)(2,1)S(1)}, u32[]{:S(2)}, u32[]{:S(2)}) async-start(bf16[16,2,4096]{2,1,0:T(2,128)(2,1)} %reshape.53), calls=%async_computation.5 | async-start | bytes 524288 | tf_op jit(solution)/shard_map/all_to_all | solution.py:81
  140.9 4.1 %copy.17 = bf16[256,4096]{0,1:T(8,128)(2,1)} copy(bf16[256,4096]{1,0:T(8,128)(2,1)} %bitcast.10) | data formatting | bytes 4194304 | tf_op jit(solution)/shard_map/optimization_barrier | solution.py:206
  144.9 5.8 %all-to-all-done.5 = bf16[16,2,4096]{2,1,0:T(2,128)(2,1)S(1)} async-done(((bf16[16,2,4096]{2,1,0:T(2,128)(2,1)}), bf16[16,2,4096]{2,1,0:T(2,128)(2,1)S(1)}, u32[]{:S(2)}, u32[]{:S(2)}) %all-to-all-start.5) | async-done | bytes 262176 | tf_op jit(solution)/shard_map/all_to_all | solution.py:81
  151.0 2.5 %convolution_convert_fusion = bf16[4096,256]{1,0:T(8,128)(2,1)S(1)} fusion(bf16[256,4096]{1,0:T(8,128)(2,1)} %collective-permute-done.8, f32[256,256]{1,0:T(8,128)S(1)} %and_convert_fusion), kind=kOutput, calls=%fused_computation.3 | convolution fusion | flops 537985024 | bytes 4456448 | tf_op jit(solution)/shard_map/dot_general | solution.py:75
  153.5 2.6 %maximum_select_fusion = bf16[8192,256]{1,0:T(8,128)(2,1)} fusion(bf16[4096,256]{1,0:T(8,128)(2,1)S(1)} %convolution_convert_fusion, bf16[4096,256]{1,0:T(8,128)(2,1)S(1)} %bitcast.46, pred[]{:T(512)S(6)} %eq.75), kind=kLoop, calls=%fused_computation.14 | loop fusion | flops 18874368 | bytes 8388609 | tf_op jit(solution)/shard_map/jit(_where)/select_n | solution.py:211
  157.1 6.5 %all-to-all-start.6 = ((bf16[16,2,4096]{2,1,0:T(2,128)(2,1)}), bf16[16,2,4096]{2,1,0:T(2,128)(2,1)S(1)}, u32[]{:S(2)}, u32[]{:S(2)}) async-start(bf16[16,2,4096]{2,1,0:T(2,128)(2,1)} %broadcast_in_dim.66), calls=%async_computation.6 | async-start | bytes 524288 | tf_op jit(solution)/shard_map/all_to_all | solution.py:81
  163.6 2.4 %collective-permute-start.9 = (bf16[2,4096]{1,0:T(2,128)(2,1)S(1)}, bf16[2,4096]{1,0:T(2,128)(2,1)S(1)}, u32[]{:S(2)}, u32[]{:S(2)}) collective-permute-start(bf16[2,4096]{1,0:T(2,128)(2,1)S(1)} %multiply_convert_fusion), channel_id=1, source_target_pairs={{0,0},{1,128},{2,2},{3,130},{4,4},{5,132},{6,6},{7,134},{8,8},{9,1... | collective-permute-start | bytes 49160 | tf_op jit(solution)/shard_map/ppermute | solution.py:63
  166.0 7.3 %all-to-all-done.6 = bf16[16,2,4096]{2,1,0:T(2,128)(2,1)S(1)} async-done(((bf16[16,2,4096]{2,1,0:T(2,128)(2,1)}), bf16[16,2,4096]{2,1,0:T(2,128)(2,1)S(1)}, u32[]{:S(2)}, u32[]{:S(2)}) %all-to-all-start.6) | async-done | bytes 262176 | tf_op jit(solution)/shard_map/all_to_all | solution.py:81
  174.9 7.4 %all-to-all-start.7 = ((bf16[8,32,4096]{2,1,0:T(8,128)(2,1)}), bf16[8,32,4096]{2,1,0:T(8,128)(2,1)}, u32[]{:S(2)}, u32[]{:S(2)}) async-start(bf16[8,32,4096]{2,1,0:T(8,128)(2,1)} %broadcast_in_dim.67), calls=%async_computation.7 | async-start | bytes 4194304 | tf_op jit(solution)/shard_map/all_to_all | solution.py:81
  182.3 15.5 %all-to-all-done.7 = bf16[8,32,4096]{2,1,0:T(8,128)(2,1)} async-done(((bf16[8,32,4096]{2,1,0:T(8,128)(2,1)}), bf16[8,32,4096]{2,1,0:T(8,128)(2,1)}, u32[]{:S(2)}, u32[]{:S(2)}) %all-to-all-start.7) | async-done | bytes 2097184 | tf_op jit(solution)/shard_map/all_to_all | solution.py:81
  197.8 2.5 %fusion.5 = bf16[128,4096]{1,0:T(8,128)(2,1)S(1)} fusion(bf16[128,256]{1,0:T(8,128)(2,1)S(1)} %convolution_convert_fusion.6, bf16[256,4096]{1,0:T(8,128)(2,1)} %bitcast.15, bf16[256,4096]{1,0:T(8,128)(2,1)} %pad_maximum_fusion.1), kind=kOutput, calls=%fused_computation.11 | convolution fusion | flops 270532608 | bytes 4259840 | tf_op jit(solution)/shard_map/dot_general | solution.py:75
  200.4 2.2 %fusion.4 = bf16[128,4096]{1,0:T(8,128)(2,1)S(1)} fusion(bf16[128,256]{1,0:T(8,128)(2,1)S(1)} %get-tuple-element.53, bf16[256,4096]{1,0:T(8,128)(2,1)} %bitcast.15, bf16[256,4096]{1,0:T(8,128)(2,1)S(1)} %copy-done.2), kind=kOutput, calls=%fused_computation.10 | convolution fusion | flops 270532608 | bytes 4259840 | tf_op jit(solution)/shard_map/dot_general | solution.py:75
  202.5 2.0 collective-permute-start.11
  204.6 2.6 %fusion.18 = f32[128,256]{1,0:T(8,128)S(1)} fusion(bf16[256,4096]{1,0:T(8,128)(2,1)} %bitcast.15, bf16[256,4096]{1,0:T(8,128)(2,1)S(1)} %copy-done.2), kind=kOutput, calls=%fused_computation.38 | convolution fusion | flops 268435456 | bytes 3276800 | tf_op jit(solution)/shard_map/dot_general | solution.py:75
  207.3 2.6 %fusion.20 = f32[128,256]{1,0:T(8,128)S(1)} fusion(bf16[256,4096]{1,0:T(8,128)(2,1)} %bitcast.15, bf16[256,4096]{1,0:T(8,128)(2,1)S(1)} %copy-done.2), kind=kOutput, calls=%fused_computation.40 | convolution fusion | flops 268435456 | bytes 3276800 | tf_op jit(solution)/shard_map/dot_general | solution.py:75
  210.3 2.6 %fusion.1 = bf16[8192,128]{1,0:T(8,128)(2,1)} fusion(bf16[8192,256]{1,0:T(8,128)(2,1)S(1)} %copy-done.3, bf16[128,256]{1,0:T(8,128)(2,1)S(1)} %select_convert_fusion, bf16[8192,128]{1,0:T(8,128)(2,1)S(1)} %copy-done.5), kind=kOutput, calls=%fused_computation.2 | convolution fusion | flops 541065216 | bytes 8454144 | tf_op jit(solution)/shard_map/dot_general | solution.py:75
  213.0 1.9 maximum_select_fusion.1
  (98 shorter events, 24.1 us)
Async XLA Ops:
  0.6 1.6 copy-start
  0.6 5.1 %copy-start.15 = (bf16[1,256,128]{2,1,0:T(8,128)(2,1)S(1)}, bf16[1,256,128]{2,1,0:T(8,128)(2,1)}, u32[]{:S(2)}) copy-start(bf16[1,256,128]{2,1,0:T(8,128)(2,1)} %param.10) | copy-start | bytes 196612
  0.7 1.7 copy-start.11
  2.3 6.5 %copy-start.14 = (s32[128]{0:T(128)S(1)}, s32[128]{0:T(128)}, u32[]{:S(2)}) copy-start(s32[128]{0:T(128)} %param.17) | copy-start | bytes 1540
  2.5 6.5 %collective-permute-start.1 = (bf16[256,64]{1,0:T(8,128)(2,1)S(1)}, bf16[256,64]{1,0:T(8,128)(2,1)S(1)}, u32[]{:S(2)}, u32[]{:S(2)}) collective-permute-start(bf16[256,64]{1,0:T(8,128)(2,1)S(1)} %copy.16), channel_id=1, source_target_pairs={{0,1},{1,0},{2,3},{3,2},{4,5},{5,4},{6,7},{7,6},{8,9},{9,8},{10,11... | collective-permute-start | bytes 98312 | tf_op jit(solution)/shard_map/ppermute | solution.py:63
  5.8 3.2 %collective-permute-start = (bf16[256,128]{1,0:T(8,128)(2,1)S(1)}, bf16[256,128]{1,0:T(8,128)(2,1)S(1)}, u32[]{:S(2)}, u32[]{:S(2)}) collective-permute-start(bf16[256,128]{1,0:T(8,128)(2,1)S(1)} %bitcast.50), channel_id=1, source_target_pairs={{0,1},{1,0},{2,3},{3,2},{4,5},{5,4},{6,7},{7,6},{8,9},{9,8},{10,11... | collective-permute-start | bytes 196616 | tf_op jit(solution)/shard_map/ppermute | solution.py:63
  5.9 3.9 %collective-permute-start.2 = (bf16[128,4096]{1,0:T(8,128)(2,1)S(1)}, bf16[128,4096]{1,0:T(8,128)(2,1)}, u32[]{:S(2)}, u32[]{:S(2)}) collective-permute-start(bf16[128,4096]{1,0:T(8,128)(2,1)S(1)} %dynamic-slice_bitcast_fusion.1), channel_id=1, source_target_pairs={{0,1},{1,0},{2,3},{3,2},{4,5},{5,4},{6,7},{7,6},{8,9},{9,8},{10,11... | collective-permute-start | bytes 3145736 | tf_op jit(solution)/shard_map/ppermute | solution.py:63
  9.0 1.5 copy-start.10
  14.3 23.3 %all-to-all-start = ((bf16[8,32,4096]{2,1,0:T(8,128)(2,1)}), bf16[8,32,4096]{2,1,0:T(8,128)(2,1)}, u32[]{:S(2)}, u32[]{:S(2)}) async-start(bf16[8,32,4096]{2,1,0:T(8,128)(2,1)} %bitcast.47), calls=%async_computation | async-start | bytes 4194304 | tf_op jit(solution)/shard_map/all_to_all | solution.py:81
  22.4 18.2 %copy-start.16 = (bf16[128]{0:T(256)(128)(2,1)S(1)}, bf16[128]{0:T(256)(128)(2,1)}, u32[]{:S(2)}) copy-start(bf16[128]{0:T(256)(128)(2,1)} %param.13) | copy-start | bytes 772
  22.4 18.2 %copy-start.13 = (s32[256]{0:T(256)S(1)}, s32[256]{0:T(256)}, u32[]{:S(2)}) copy-start(s32[256]{0:T(256)} %param.16) | copy-start | bytes 3076
  40.7 18.5 %all-to-all-start.1 = ((bf16[16,2,4096]{2,1,0:T(2,128)(2,1)}), bf16[16,2,4096]{2,1,0:T(2,128)(2,1)}, u32[]{:S(2)}, u32[]{:S(2)}) async-start(bf16[16,2,4096]{2,1,0:T(2,128)(2,1)} %reshape.49), calls=%async_computation.1 | async-start | bytes 524288 | tf_op jit(solution)/shard_map/all_to_all | solution.py:81
  48.4 3.9 %copy-start.4 = (bf16[8192,128]{1,0:T(8,128)(2,1)S(1)}, bf16[8192,128]{1,0:T(8,128)(2,1)}, u32[]{:S(2)}) copy-start(bf16[8192,128]{1,0:T(8,128)(2,1)} %param.12) | copy-start | bytes 6291460
  51.7 1.8 copy-start.12
  51.7 8.7 %collective-permute-start.4 = (bf16[128,4096]{1,0:T(8,128)(2,1)}, bf16[128,4096]{1,0:T(8,128)(2,1)}, u32[]{:S(2)}, u32[]{:S(2)}) collective-permute-start(bf16[128,4096]{1,0:T(8,128)(2,1)} %get-tuple-element.50), channel_id=1, source_target_pairs={{0,1},{1,0},{2,3},{3,2},{4,5},{5,4},{6,7},{7,6},{8,9},{9,8},{10,11... | collective-permute-start | bytes 3145736 | tf_op jit(solution)/shard_map/ppermute | solution.py:63
  53.5 10.0 %collective-permute-start.3 = (bf16[4096,128]{1,0:T(8,128)(2,1)}, bf16[4096,128]{1,0:T(8,128)(2,1)}, u32[]{:S(2)}, u32[]{:S(2)}) collective-permute-start(bf16[4096,128]{1,0:T(8,128)(2,1)} %get-tuple-element.52), channel_id=1, source_target_pairs={{0,1},{1,0},{2,3},{3,2},{4,5},{5,4},{6,7},{7,6},{8,9},{9,8},{10,11... | collective-permute-start | bytes 3145736 | tf_op jit(solution)/shard_map/ppermute | solution.py:63
  66.4 2.7 %collective-permute-start.5 = (f32[2,1]{0,1:T(1,128)S(1)}, f32[2,1]{0,1:T(1,128)S(1)}, u32[]{:S(2)}, u32[]{:S(2)}) collective-permute-start(f32[2,1]{0,1:T(1,128)S(1)} %bitcast.49), channel_id=1, source_target_pairs={{0,1},{1,0},{2,3},{3,2},{4,5},{5,4},{6,7},{7,6},{8,9},{9,8},{10,11... | collective-permute-start | bytes 32 | tf_op jit(solution)/shard_map/ppermute | solution.py:63
  84.8 20.7 %copy-start.6 = (bf16[4096,256]{1,0:T(8,128)(2,1)S(1)}, bf16[4096,256]{1,0:T(8,128)(2,1)}, u32[]{:S(2)}) copy-start(bf16[4096,256]{1,0:T(8,128)(2,1)} %pad_maximum_fusion) | copy-start | bytes 6291460
  105.5 8.9 %copy-start.1 = (bf16[256,4096]{1,0:T(8,128)(2,1)S(1)}, bf16[256,4096]{1,0:T(8,128)(2,1)}, u32[]{:S(2)}) copy-start(bf16[256,4096]{1,0:T(8,128)(2,1)} %pad_maximum_fusion.1) | copy-start | bytes 6291460
  108.1 4.2 %collective-permute-start.6 = (f32[128,256]{1,0:T(8,128)S(1)}, f32[128,256]{1,0:T(8,128)S(1)}, u32[]{:S(2)}, u32[]{:S(2)}) collective-permute-start(f32[128,256]{1,0:T(8,128)S(1)} %slice.17), channel_id=1, source_target_pairs={{0,1},{1,0},{2,3},{3,2},{4,5},{5,4},{6,7},{7,6},{8,9},{9,8},{10,11... | collective-permute-start | bytes 393224 | tf_op jit(solution)/shard_map/ppermute | solution.py:63
  112.7 1.5 collective-permute-start.7
  135.4 15.6 %collective-permute-start.8 = (bf16[256,4096]{1,0:T(8,128)(2,1)}, bf16[256,4096]{1,0:T(8,128)(2,1)}, u32[]{:S(2)}, u32[]{:S(2)}) collective-permute-start(bf16[256,4096]{1,0:T(8,128)(2,1)} %bitcast.10), channel_id=1, source_target_pairs={{0,1},{1,0},{2,3},{3,2},{4,5},{5,4},{6,7},{7,6},{8,9},{9,8},{10,11... | collective-permute-start | bytes 6291464 | tf_op jit(solution)/shard_map/ppermute | solution.py:63
  136.6 14.2 %all-to-all-start.5 = ((bf16[16,2,4096]{2,1,0:T(2,128)(2,1)}), bf16[16,2,4096]{2,1,0:T(2,128)(2,1)S(1)}, u32[]{:S(2)}, u32[]{:S(2)}) async-start(bf16[16,2,4096]{2,1,0:T(2,128)(2,1)} %reshape.53), calls=%async_computation.5 | async-start | bytes 524288 | tf_op jit(solution)/shard_map/all_to_all | solution.py:81
  151.0 2.5 %copy-start.7 = (bf16[256,4096]{0,1:T(8,128)(2,1)S(1)}, bf16[256,4096]{0,1:T(8,128)(2,1)}, u32[]{:S(2)}) copy-start(bf16[256,4096]{0,1:T(8,128)(2,1)} %copy.17) | copy-start | bytes 6291460
  157.1 16.1 %all-to-all-start.6 = ((bf16[16,2,4096]{2,1,0:T(2,128)(2,1)}), bf16[16,2,4096]{2,1,0:T(2,128)(2,1)S(1)}, u32[]{:S(2)}, u32[]{:S(2)}) async-start(bf16[16,2,4096]{2,1,0:T(2,128)(2,1)} %broadcast_in_dim.66), calls=%async_computation.6 | async-start | bytes 524288 | tf_op jit(solution)/shard_map/all_to_all | solution.py:81
  163.6 9.8 %collective-permute-start.9 = (bf16[2,4096]{1,0:T(2,128)(2,1)S(1)}, bf16[2,4096]{1,0:T(2,128)(2,1)S(1)}, u32[]{:S(2)}, u32[]{:S(2)}) collective-permute-start(bf16[2,4096]{1,0:T(2,128)(2,1)S(1)} %multiply_convert_fusion), channel_id=1, source_target_pairs={{0,0},{1,128},{2,2},{3,130},{4,4},{5,132},{6,6},{7,134},{8,8},{9,1... | collective-permute-start | bytes 49160 | tf_op jit(solution)/shard_map/ppermute | solution.py:63
  174.9 22.9 %all-to-all-start.7 = ((bf16[8,32,4096]{2,1,0:T(8,128)(2,1)}), bf16[8,32,4096]{2,1,0:T(8,128)(2,1)}, u32[]{:S(2)}, u32[]{:S(2)}) async-start(bf16[8,32,4096]{2,1,0:T(8,128)(2,1)} %broadcast_in_dim.67), calls=%async_computation.7 | async-start | bytes 4194304 | tf_op jit(solution)/shard_map/all_to_all | solution.py:81
  197.8 2.6 %copy-start.2 = (bf16[256,4096]{1,0:T(8,128)(2,1)S(1)}, bf16[256,4096]{1,0:T(8,128)(2,1)}, u32[]{:S(2)}) copy-start(bf16[256,4096]{1,0:T(8,128)(2,1)} %pad_maximum_fusion.1) | copy-start | bytes 6291460
  202.5 10.4 %collective-permute-start.11 = (bf16[128,4096]{1,0:T(8,128)(2,1)S(1)}, bf16[128,4096]{1,0:T(8,128)(2,1)S(1)}, u32[]{:S(2)}, u32[]{:S(2)}) collective-permute-start(bf16[128,4096]{1,0:T(8,128)(2,1)S(1)} %fusion.5), channel_id=1, source_target_pairs={{0,1},{1,0},{2,3},{3,2},{4,5},{5,4},{6,7},{7,6},{8,9},{9,8},{10,11... | collective-permute-start | bytes 3145736 | tf_op jit(solution)/shard_map/ppermute | solution.py:63
  204.6 5.8 %copy-start.3 = (bf16[8192,256]{1,0:T(8,128)(2,1)S(1)}, bf16[8192,256]{1,0:T(8,128)(2,1)}, u32[]{:S(2)}) copy-start(bf16[8192,256]{1,0:T(8,128)(2,1)} %maximum_select_fusion) | copy-start | bytes 12582916
  207.2 3.2 %copy-start.5 = (bf16[8192,128]{1,0:T(8,128)(2,1)S(1)}, bf16[8192,128]{1,0:T(8,128)(2,1)}, u32[]{:S(2)}) copy-start(bf16[8192,128]{1,0:T(8,128)(2,1)} %param.12) | copy-start | bytes 6291460
  207.2 2.7 %collective-permute-start.10 = (f32[128,256]{1,0:T(8,128)S(1)}, f32[128,256]{1,0:T(8,128)S(1)}, u32[]{:S(2)}, u32[]{:S(2)}) collective-permute-start(f32[128,256]{1,0:T(8,128)S(1)} %fusion.18), channel_id=1, source_target_pairs={{0,1},{1,0},{2,3},{3,2},{4,5},{5,4},{6,7},{7,6},{8,9},{9,8},{10,11... | collective-permute-start | bytes 393224 | tf_op jit(solution)/shard_map/ppermute | solution.py:63
  (2 other events, 2.6 us)

commit v8 on v6

--- a/solution.py
+++ b/solution.py
@@ -183,7 +183,11 @@
     latents_other = matmul(other_core(latents), across_low, ((1,), (1,))).astype(jnp.bfloat16)
     latents_both = jnp.concatenate([latents, latents_other], axis=0)
     partial = matmul(latents_both, decoder_both, ((0,), (0,))).astype(jnp.bfloat16)
-    later, _ = lax.optimization_barrier((centred, partial))
+    rebuilt = far_sum(near_sum(partial))
+    my_error = (mask_rows * (rebuilt - my_centred.astype(jnp.float32))).astype(jnp.bfloat16)
+    error_rows = spread(my_error, FAR_GROUPS, FAR)
+    later, own_rows, _ = lax.optimization_barrier((centred, my_error, error_rows))
+    owned_error = core_and_section(own_rows)
     centred_other = matmul(
         other_core(later), across_low, ((0,), (1,))
     ).astype(jnp.bfloat16)
@@ -193,12 +197,8 @@
         jnp.concatenate([centred_own, centred_other], axis=0),
         jnp.concatenate([centred_other, centred_own], axis=0),
     )
-    chunk = near_sum(partial)
-    chunk, centred_full = lax.optimization_barrier((chunk, centred_full))
-    rebuilt = far_sum(chunk)
-    my_error = (mask_rows * (rebuilt - my_centred.astype(jnp.float32))).astype(jnp.bfloat16)
-    owned_error = core_and_section(my_error)
-    error = spread(spread(my_error, FAR_GROUPS, FAR), NEAR_GROUPS, NEAR)
+    error = spread(error_rows, NEAR_GROUPS, NEAR)
+    error, centred_full = lax.optimization_barrier((error, centred_full))
     step_size = STEP_RATE / tokens
 
     def stepped(weight, grad):

time: 198 us -> 195 us (0.985)
  blocking collectives: 84.8 us -> 104 us
  waiting for transfers between devices: 30.6 us -> 17.2 us
  starting transfers between devices: 36.7 us -> 28.9 us
  matrix products: 21.4 us -> 18.4 us
    all_to_all x5 -> x6, blocking collectives: 84.8 us -> 104 us  [all_to_all(): lax.all_to_all(pieces, AXES, 0, 0, axis_index_groups=groups, tiled=True)]
    all_to_all x3 -> x2, waiting for transfers between devices: 12.3 us -> 4.48 us  [all_to_all(): lax.all_to_all(pieces, AXES, 0, 0, axis_index_groups=groups, tiled=True)]
    ppermute x12, waiting for transfers between devices: 18.3 us -> 12.7 us  [exchange(): return lax.ppermute(value, AXES, route)]
    all_to_all x3 -> x2, starting transfers between devices: 18.5 us -> 13.3 us  [all_to_all(): lax.all_to_all(pieces, AXES, 0, 0, axis_index_groups=groups, tiled=True)]
    dot_general x15, matrix products: 21.4 us -> 18.4 us  [matmul(): lax.dot_general(a, b, (dims, ((), ())), preferred_element_type=jnp.float3...]
    ppermute x12, starting transfers between devices: 18.2 us -> 15.6 us  [exchange(): return lax.ppermute(value, AXES, route)]
  transfers between devices with their start and end apart: 15 -> 14, of which waited for: 10 -> 9; matrix products, arithmetic and copies ran while one was open for 11% -> 11% of each run, Pallas kernels for 0% -> 0%
where the time goes in v8:
time: 195 us; the launch traced here: 194 us
  blocking collectives  104 us (53%)
  starting transfers between devices  28.9 us (15%)
  matrix products  18.4 us (9%)
  waiting for transfers between devices  17.2 us (9%)
  local copies, waits for them, and re-layouts  14.7 us (8%)
  other arithmetic  9.91 us (5%)
    all_to_all x6, blocking collectives, all_to_all(): lax.all_to_all(pieces, AXES, 0, 0, axis_index_groups=groups, tiled=True)  104 us
    dot_general x15, matrix products, matmul(): lax.dot_general(a, b, (dims, ((), ())), preferred_element_type=jnp.float3...  18.4 us
    ppermute x12, starting transfers between devices, exchange(): return lax.ppermute(value, AXES, route)  15.6 us
    all_to_all x2, starting transfers between devices, all_to_all(): lax.all_to_all(pieces, AXES, 0, 0, axis_index_groups=groups, tiled=True)  13.3 us
    ppermute x12, waiting for transfers between devices, exchange(): return lax.ppermute(value, AXES, route)  12.7 us
    all_to_all x2, waiting for transfers between devices, all_to_all(): lax.all_to_all(pieces, AXES, 0, 0, axis_index_groups=groups, tiled=True)  4.48 us
    dynamic_slice x3, local copies, waits for them, and re-layouts, mine(): return lax.dynamic_slice_in_dim(weight, core * half, half, axis)  4.28 us
    optimization_barrier x1, local copies, waits for them, and re-layouts, shards(): lax.optimization_barrier((centred, my_error, error_rows))  4.07 us
  transfers between devices with their start and end apart: 14, of which 9 were waited for; matrix products, arithmetic and copies ran while one was open for 11% of the time, Pallas kernels for 0%

profile of v8, /device:TPU:1, one launch (start us, length us, event | category | flops | bytes accessed | tf_op | source)
XLA Modules:
  0.0 194.4 jit_solution(16429337063232732340)
XLA Ops:
  0.7 1.7 dynamic-slice_bitcast_fusion.1
  2.4 3.3 %collective-permute-start.2 = (bf16[128,4096]{1,0:T(8,128)(2,1)S(1)}, bf16[128,4096]{1,0:T(8,128)(2,1)}, u32[]{:S(2)}, u32[]{:S(2)}) collective-permute-start(bf16[128,4096]{1,0:T(8,128)(2,1)S(1)} %get-tuple-element.32), channel_id=1, source_target_pairs={{0,1},{1,0},{2,3},{3,2},{4,5},{5,4},{6,7},{7,6},{8,9},{9,8},{10,11... | collective-permute-start | bytes 3145736 | tf_op jit(solution)/shard_map/ppermute | solution.py:63
  7.1 1.0 collective-permute-done.1
  8.9 3.8 %convolution_convert_fusion.2 = bf16[256,4096]{1,0:T(8,128)(2,1)} fusion(bf16[256,384]{1,0:T(8,128)(2,1)S(1)} %convolution_convert_fusion.5, bf16[64,4096]{1,0:T(8,128)(2,1)S(1)} %get-tuple-element.42, bf16[64,4096]{1,0:T(8,128)(2,1)S(1)} %get-tuple-element.41, bf16[128,4096]{1,0:T(8,128)(2,1)} %collective-permute-done.2, ...), kind=kOutput, calls=%fused_computation.5 | convolution fusion | flops 818937856 | bytes 5439488 | tf_op jit(solution)/shard_map/dot_general | solution.py:75
  12.7 8.2 %all-to-all-start = ((bf16[8,32,4096]{2,1,0:T(8,128)(2,1)}), bf16[8,32,4096]{2,1,0:T(8,128)(2,1)}, u32[]{:S(2)}, u32[]{:S(2)}) async-start(bf16[8,32,4096]{2,1,0:T(8,128)(2,1)} %bitcast.50), calls=%async_computation | async-start | bytes 4194304 | tf_op jit(solution)/shard_map/all_to_all | solution.py:81
  20.9 1.4 constant_dynamic-slice_fusion
  23.3 1.1 constant_dynamic-slice_fusion.3
  26.1 1.2 collective-permute-done.4
  28.2 1.7 pad_maximum_fusion.1
  29.9 1.7 pad_maximum_fusion
  31.7 4.5 %all-to-all-done = bf16[8,32,4096]{2,1,0:T(8,128)(2,1)} async-done(((bf16[8,32,4096]{2,1,0:T(8,128)(2,1)}), bf16[8,32,4096]{2,1,0:T(8,128)(2,1)}, u32[]{:S(2)}, u32[]{:S(2)}) %all-to-all-start) | async-done | bytes 2097184 | tf_op jit(solution)/shard_map/all_to_all | solution.py:81
  36.1 2.0 %convolution_convert_fusion.4 = bf16[32,4096]{1,0:T(8,128)(2,1)S(1)} fusion(bf16[256,4096]{1,0:T(8,128)(2,1)} %bitcast.4, s32[256]{0:T(256)S(1)} %get-tuple-element.43, s32[256]{0:T(256)S(1)} %get-tuple-element.44, pred[256]{0:T(512)(128)(4,1)S(1)} %compare_and_fusion.2), kind=kOutput, calls=%fused_computation.13 | convolution fusion | flops 67256320 | bytes 2361600 | tf_op jit(solution)/shard_map/dot_general | solution.py:75
  38.4 18.1 %all_to_all.40 = bf16[16,2,4096]{2,1,0:T(2,128)(2,1)S(1)} all-to-all(bf16[16,2,4096]{2,1,0:T(2,128)(2,1)S(1)} %reshape.126), channel_id=1, replica_groups={{0,8,16,24,32,40,48,56,64,72,80,88,96,104,112,120},{4,12,20,28,36,44,52..., dimensions={0} | all-to-all | bytes 524288 | tf_op jit(solution)/shard_map/all_to_all | solution.py:81
  56.9 2.1 %collective-permute-start.5 = (f32[2,1]{0,1:T(1,128)S(1)}, f32[2,1]{0,1:T(1,128)S(1)}, u32[]{:S(2)}, u32[]{:S(2)}) collective-permute-start(f32[2,1]{0,1:T(1,128)S(1)} %bitcast.51), channel_id=1, source_target_pairs={{0,1},{1,0},{2,3},{3,2},{4,5},{5,4},{6,7},{7,6},{8,9},{9,8},{10,11... | collective-permute-start | bytes 32 | tf_op jit(solution)/shard_map/ppermute | solution.py:63
  60.1 14.7 %all_to_all.41 = bf16[16,2,4096]{2,1,0:T(2,128)(2,1)S(1)} all-to-all(bf16[16,2,4096]{2,1,0:T(2,128)(2,1)S(1)} %broadcast_in_dim.57), channel_id=1, replica_groups={{0,8,16,24,32,40,48,56,64,72,80,88,96,104,112,120},{4,12,20,28,36,44,52..., dimensions={0} | all-to-all | bytes 524288 | tf_op jit(solution)/shard_map/all_to_all | solution.py:81
  75.2 21.2 %all_to_all.42 = bf16[8,32,4096]{2,1,0:T(8,128)(2,1)S(1)} all-to-all(bf16[8,32,4096]{2,1,0:T(8,128)(2,1)S(1)} %broadcast_in_dim.59), channel_id=1, replica_groups={{0,4,128,132,2,6,130,134},{8,12,136,140,10,14,138,142},{16,20,144,148,1..., dimensions={0} | all-to-all | bytes 4194304 | tf_op jit(solution)/shard_map/all_to_all | solution.py:81
  97.7 3.2 %collective-permute-start.6 = (f32[128,256]{1,0:T(8,128)S(1)}, f32[128,256]{1,0:T(8,128)S(1)}, u32[]{:S(2)}, u32[]{:S(2)}) collective-permute-start(f32[128,256]{1,0:T(8,128)S(1)} %slice.17), channel_id=1, source_target_pairs={{0,1},{1,0},{2,3},{3,2},{4,5},{5,4},{6,7},{7,6},{8,9},{9,8},{10,11... | collective-permute-start | bytes 393224 | tf_op jit(solution)/shard_map/ppermute | solution.py:63
  100.9 1.0 collective-permute-done.6
  104.5 19.7 %all_to_all.43 = bf16[8,32,4096]{2,1,0:T(8,128)(2,1)S(1)} all-to-all(bf16[8,32,4096]{2,1,0:T(8,128)(2,1)S(1)} %bitcast.48), channel_id=1, replica_groups={{0,4,128,132,2,6,130,134},{8,12,136,140,10,14,138,142},{16,20,144,148,1..., dimensions={0} | all-to-all | bytes 4194304 | tf_op jit(solution)/shard_map/all_to_all | solution.py:81
  124.8 13.7 %all_to_all.44 = bf16[16,2,4096]{2,1,0:T(2,128)(2,1)S(1)} all-to-all(bf16[16,2,4096]{2,1,0:T(2,128)(2,1)S(1)} %reshape.130), channel_id=1, replica_groups={{0,8,16,24,32,40,48,56,64,72,80,88,96,104,112,120},{4,12,20,28,36,44,52..., dimensions={0} | all-to-all | bytes 524288 | tf_op jit(solution)/shard_map/all_to_all | solution.py:81
  139.0 16.8 %all_to_all.45 = bf16[16,2,4096]{2,1,0:T(2,128)(2,1)S(1)} all-to-all(bf16[16,2,4096]{2,1,0:T(2,128)(2,1)S(1)} %broadcast_in_dim.60), channel_id=1, replica_groups={{0,8,16,24,32,40,48,56,64,72,80,88,96,104,112,120},{4,12,20,28,36,44,52..., dimensions={0} | all-to-all | bytes 524288 | tf_op jit(solution)/shard_map/all_to_all | solution.py:81
  155.9 1.6 broadcast_in_dim.62
  157.5 5.2 %all-to-all-start.7 = ((bf16[8,32,4096]{2,1,0:T(8,128)(2,1)}), bf16[8,32,4096]{2,1,0:T(8,128)(2,1)S(1)}, u32[]{:S(2)}, u32[]{:S(2)}) async-start(bf16[8,32,4096]{2,1,0:T(8,128)(2,1)} %broadcast_in_dim.62), calls=%async_computation.7 | async-start | bytes 4194304 | tf_op jit(solution)/shard_map/all_to_all | solution.py:81
  162.7 1.1 collective-permute-start.9
  163.8 3.5 %collective-permute-start.8 = (bf16[2,4096]{1,0:T(2,128)(2,1)S(1)}, bf16[2,4096]{1,0:T(2,128)(2,1)S(1)}, u32[]{:S(2)}, u32[]{:S(2)}) collective-permute-start(bf16[2,4096]{1,0:T(2,128)(2,1)S(1)} %multiply_convert_fusion), channel_id=1, source_target_pairs={{0,0},{1,128},{2,2},{3,130},{4,4},{5,132},{6,6},{7,134},{8,8},{9,1... | collective-permute-start | bytes 49160 | tf_op jit(solution)/shard_map/ppermute | solution.py:63
  167.4 4.1 %copy.17 = bf16[256,4096]{0,1:T(8,128)(2,1)} copy(bf16[256,4096]{1,0:T(8,128)(2,1)} %bitcast.46) | data formatting | bytes 4194304 | tf_op jit(solution)/shard_map/optimization_barrier | solution.py:189
  171.4 7.2 %collective-permute-done.8 = bf16[2,4096]{1,0:T(2,128)(2,1)S(1)} collective-permute-done((bf16[2,4096]{1,0:T(2,128)(2,1)S(1)}, bf16[2,4096]{1,0:T(2,128)(2,1)S(1)}, u32[]{:S(2)}, u32[]{:S(2)}) %collective-permute-start.8) | collective-permute-done | bytes 16416 | tf_op jit(solution)/shard_map/ppermute | solution.py:63
  178.6 2.4 %convolution_convert_fusion = bf16[4096,256]{1,0:T(8,128)(2,1)S(1)} fusion(bf16[256,4096]{1,0:T(8,128)(2,1)} %collective-permute-done.9, pred[256,256]{1,0:T(32,128)(4,1)S(1)} %fusion.55), kind=kOutput, calls=%fused_computation.3 | convolution fusion | flops 537919488 | bytes 4259840 | tf_op jit(solution)/shard_map/dot_general | solution.py:75
  181.0 2.6 %maximum_select_fusion = bf16[8192,256]{1,0:T(8,128)(2,1)} fusion(bf16[4096,256]{1,0:T(8,128)(2,1)S(1)} %convolution_convert_fusion, bf16[4096,256]{1,0:T(8,128)(2,1)S(1)} %bitcast.49, pred[]{:T(512)S(6)} %eq.72), kind=kLoop, calls=%fused_computation.14 | loop fusion | flops 18874368 | bytes 8388609 | tf_op jit(solution)/shard_map/jit(_where)/select_n | solution.py:195
  183.6 1.9 fusion.4
  189.4 2.6 %fusion.1 = bf16[8192,128]{1,0:T(8,128)(2,1)} fusion(bf16[8192,256]{1,0:T(8,128)(2,1)S(1)} %copy-done.2, bf16[128,256]{1,0:T(8,128)(2,1)S(1)} %select_convert_fusion, bf16[8192,128]{1,0:T(8,128)(2,1)S(1)} %copy-done.5), kind=kOutput, calls=%fused_computation.2 | convolution fusion | flops 541065216 | bytes 8454144 | tf_op jit(solution)/shard_map/dot_general | solution.py:75
  191.9 1.8 maximum_select_fusion.1
  (91 shorter events, 17.2 us)
Async XLA Ops:
  0.6 5.1 %copy-start.10 = (bf16[256,64]{0,1:T(8,128)(2,1)S(1)}, bf16[256,64]{0,1:T(8,128)(2,1)}, u32[]{:S(2)}) copy-start(bf16[256,64]{0,1:T(8,128)(2,1)} %param.9) | copy-start | bytes 98308
  0.7 5.3 %copy-start.14 = (bf16[1,256,128]{2,1,0:T(8,128)(2,1)S(1)}, bf16[1,256,128]{2,1,0:T(8,128)(2,1)}, u32[]{:S(2)}) copy-start(bf16[1,256,128]{2,1,0:T(8,128)(2,1)} %param.10) | copy-start | bytes 196612
  0.7 6.2 %copy-start.13 = (s32[128]{0:T(128)S(1)}, s32[128]{0:T(128)}, u32[]{:S(2)}) copy-start(s32[128]{0:T(128)} %param.17) | copy-start | bytes 1540
  2.4 6.5 %collective-permute-start.2 = (bf16[128,4096]{1,0:T(8,128)(2,1)S(1)}, bf16[128,4096]{1,0:T(8,128)(2,1)}, u32[]{:S(2)}, u32[]{:S(2)}) collective-permute-start(bf16[128,4096]{1,0:T(8,128)(2,1)S(1)} %get-tuple-element.32), channel_id=1, source_target_pairs={{0,1},{1,0},{2,3},{3,2},{4,5},{5,4},{6,7},{7,6},{8,9},{9,8},{10,11... | collective-permute-start | bytes 3145736 | tf_op jit(solution)/shard_map/ppermute | solution.py:63
  5.8 2.3 %collective-permute-start.1 = (bf16[256,64]{1,0:T(8,128)(2,1)S(1)}, bf16[256,64]{1,0:T(8,128)(2,1)S(1)}, u32[]{:S(2)}, u32[]{:S(2)}) collective-permute-start(bf16[256,64]{1,0:T(8,128)(2,1)S(1)} %copy.16), channel_id=1, source_target_pairs={{0,1},{1,0},{2,3},{3,2},{4,5},{5,4},{6,7},{7,6},{8,9},{9,8},{10,11... | collective-permute-start | bytes 98312 | tf_op jit(solution)/shard_map/ppermute | solution.py:63
  5.9 2.2 %collective-permute-start = (bf16[256,128]{1,0:T(8,128)(2,1)S(1)}, bf16[256,128]{1,0:T(8,128)(2,1)S(1)}, u32[]{:S(2)}, u32[]{:S(2)}) collective-permute-start(bf16[256,128]{1,0:T(8,128)(2,1)S(1)} %bitcast.52), channel_id=1, source_target_pairs={{0,1},{1,0},{2,3},{3,2},{4,5},{5,4},{6,7},{7,6},{8,9},{9,8},{10,11... | collective-permute-start | bytes 196616 | tf_op jit(solution)/shard_map/ppermute | solution.py:63
  12.7 8.2 %copy-start.12 = (s32[256]{0:T(256)S(1)}, s32[256]{0:T(256)}, u32[]{:S(2)}) copy-start(s32[256]{0:T(256)} %param.16) | copy-start | bytes 3076
  12.7 8.2 %copy-start.8 = (bf16[128,8192]{1,0:T(8,128)(2,1)S(1)}, bf16[128,8192]{1,0:T(8,128)(2,1)}, u32[]{:S(2)}) copy-start(bf16[128,8192]{1,0:T(8,128)(2,1)} %param.14) | copy-start | bytes 6291460
  12.7 23.4 %all-to-all-start = ((bf16[8,32,4096]{2,1,0:T(8,128)(2,1)}), bf16[8,32,4096]{2,1,0:T(8,128)(2,1)}, u32[]{:S(2)}, u32[]{:S(2)}) async-start(bf16[8,32,4096]{2,1,0:T(8,128)(2,1)} %bitcast.50), calls=%async_computation | async-start | bytes 4194304 | tf_op jit(solution)/shard_map/all_to_all | solution.py:81
  20.9 2.4 %copy-start.4 = (bf16[8192,128]{1,0:T(8,128)(2,1)S(1)}, bf16[8192,128]{1,0:T(8,128)(2,1)}, u32[]{:S(2)}) copy-start(bf16[8192,128]{1,0:T(8,128)(2,1)} %param.12) | copy-start | bytes 6291460
  23.3 1.3 copy-start.11
  24.4 2.9 %collective-permute-start.4 = (bf16[128,4096]{1,0:T(8,128)(2,1)}, bf16[128,4096]{1,0:T(8,128)(2,1)S(1)}, u32[]{:S(2)}, u32[]{:S(2)}) collective-permute-start(bf16[128,4096]{1,0:T(8,128)(2,1)} %get-tuple-element.16), channel_id=1, source_target_pairs={{0,1},{1,0},{2,3},{3,2},{4,5},{5,4},{6,7},{7,6},{8,9},{9,8},{10,11... | collective-permute-start | bytes 3145736 | tf_op jit(solution)/shard_map/ppermute | solution.py:63
  24.7 5.2 %collective-permute-start.3 = (bf16[4096,128]{1,0:T(8,128)(2,1)}, bf16[4096,128]{1,0:T(8,128)(2,1)S(1)}, u32[]{:S(2)}, u32[]{:S(2)}) collective-permute-start(bf16[4096,128]{1,0:T(8,128)(2,1)} %get-tuple-element.15), channel_id=1, source_target_pairs={{0,1},{1,0},{2,3},{3,2},{4,5},{5,4},{6,7},{7,6},{8,9},{9,8},{10,11... | collective-permute-start | bytes 3145736 | tf_op jit(solution)/shard_map/ppermute | solution.py:63
  27.3 1.0 copy-start.9
  29.9 73.8 %copy-start = (bf16[256,4096]{1,0:T(8,128)(2,1)}, bf16[256,4096]{1,0:T(8,128)(2,1)S(1)}, u32[]{:S(2)}) copy-start(bf16[256,4096]{1,0:T(8,128)(2,1)S(1)} %pad_maximum_fusion.1) | copy-start | bytes 6291460
  56.9 2.9 %collective-permute-start.5 = (f32[2,1]{0,1:T(1,128)S(1)}, f32[2,1]{0,1:T(1,128)S(1)}, u32[]{:S(2)}, u32[]{:S(2)}) collective-permute-start(f32[2,1]{0,1:T(1,128)S(1)} %bitcast.51), channel_id=1, source_target_pairs={{0,1},{1,0},{2,3},{3,2},{4,5},{5,4},{6,7},{7,6},{8,9},{9,8},{10,11... | collective-permute-start | bytes 32 | tf_op jit(solution)/shard_map/ppermute | solution.py:63
  75.2 21.2 %copy-start.6 = (bf16[4096,256]{1,0:T(8,128)(2,1)S(1)}, bf16[4096,256]{1,0:T(8,128)(2,1)}, u32[]{:S(2)}) copy-start(bf16[4096,256]{1,0:T(8,128)(2,1)} %pad_maximum_fusion) | copy-start | bytes 6291460
  96.4 1.3 copy-start.3
  96.4 4.5 %copy-start.15 = (bf16[128]{0:T(256)(128)(2,1)S(1)}, bf16[128]{0:T(256)(128)(2,1)}, u32[]{:S(2)}) copy-start(bf16[128]{0:T(256)(128)(2,1)} %param.13) | copy-start | bytes 772
  97.7 4.2 %collective-permute-start.6 = (f32[128,256]{1,0:T(8,128)S(1)}, f32[128,256]{1,0:T(8,128)S(1)}, u32[]{:S(2)}, u32[]{:S(2)}) collective-permute-start(f32[128,256]{1,0:T(8,128)S(1)} %slice.17), channel_id=1, source_target_pairs={{0,1},{1,0},{2,3},{3,2},{4,5},{5,4},{6,7},{7,6},{8,9},{9,8},{10,11... | collective-permute-start | bytes 393224 | tf_op jit(solution)/shard_map/ppermute | solution.py:63
  102.2 1.4 collective-permute-start.7
  157.5 26.0 %all-to-all-start.7 = ((bf16[8,32,4096]{2,1,0:T(8,128)(2,1)}), bf16[8,32,4096]{2,1,0:T(8,128)(2,1)S(1)}, u32[]{:S(2)}, u32[]{:S(2)}) async-start(bf16[8,32,4096]{2,1,0:T(8,128)(2,1)} %broadcast_in_dim.62), calls=%async_computation.7 | async-start | bytes 4194304 | tf_op jit(solution)/shard_map/all_to_all | solution.py:81
  162.7 15.9 %collective-permute-start.9 = (bf16[256,4096]{1,0:T(8,128)(2,1)}, bf16[256,4096]{1,0:T(8,128)(2,1)}, u32[]{:S(2)}, u32[]{:S(2)}) collective-permute-start(bf16[256,4096]{1,0:T(8,128)(2,1)} %bitcast.45), channel_id=1, source_target_pairs={{0,1},{1,0},{2,3},{3,2},{4,5},{5,4},{6,7},{7,6},{8,9},{9,8},{10,11... | collective-permute-start | bytes 6291464 | tf_op jit(solution)/shard_map/ppermute | solution.py:63
  163.8 14.8 %collective-permute-start.8 = (bf16[2,4096]{1,0:T(2,128)(2,1)S(1)}, bf16[2,4096]{1,0:T(2,128)(2,1)S(1)}, u32[]{:S(2)}, u32[]{:S(2)}) collective-permute-start(bf16[2,4096]{1,0:T(2,128)(2,1)S(1)} %multiply_convert_fusion), channel_id=1, source_target_pairs={{0,0},{1,128},{2,2},{3,130},{4,4},{5,132},{6,6},{7,134},{8,8},{9,1... | collective-permute-start | bytes 49160 | tf_op jit(solution)/shard_map/ppermute | solution.py:63
  171.4 9.5 %copy-start.7 = (bf16[256,4096]{0,1:T(8,128)(2,1)S(1)}, bf16[256,4096]{0,1:T(8,128)(2,1)}, u32[]{:S(2)}) copy-start(bf16[256,4096]{0,1:T(8,128)(2,1)} %copy.17) | copy-start | bytes 6291460
  183.6 1.9 copy-start.1
  186.1 5.8 %collective-permute-start.11 = (bf16[128,4096]{1,0:T(8,128)(2,1)S(1)}, bf16[128,4096]{1,0:T(8,128)(2,1)S(1)}, u32[]{:S(2)}, u32[]{:S(2)}) collective-permute-start(bf16[128,4096]{1,0:T(8,128)(2,1)S(1)} %fusion.5), channel_id=1, source_target_pairs={{0,1},{1,0},{2,3},{3,2},{4,5},{5,4},{6,7},{7,6},{8,9},{9,8},{10,11... | collective-permute-start | bytes 3145736 | tf_op jit(solution)/shard_map/ppermute | solution.py:63
  186.2 3.1 %copy-start.2 = (bf16[8192,256]{1,0:T(8,128)(2,1)S(1)}, bf16[8192,256]{1,0:T(8,128)(2,1)}, u32[]{:S(2)}) copy-start(bf16[8192,256]{1,0:T(8,128)(2,1)} %maximum_select_fusion) | copy-start | bytes 12582916
  187.0 2.3 %copy-start.5 = (bf16[8192,128]{1,0:T(8,128)(2,1)S(1)}, bf16[8192,128]{1,0:T(8,128)(2,1)}, u32[]{:S(2)}) copy-start(bf16[8192,128]{1,0:T(8,128)(2,1)} %param.12) | copy-start | bytes 6291460
  187.1 2.0 %collective-permute-start.10 = (f32[128,256]{1,0:T(8,128)S(1)}, f32[128,256]{1,0:T(8,128)S(1)}, u32[]{:S(2)}, u32[]{:S(2)}) collective-permute-start(f32[128,256]{1,0:T(8,128)S(1)} %fusion.18), channel_id=1, source_target_pairs={{0,1},{1,0},{2,3},{3,2},{4,5},{5,4},{6,7},{7,6},{8,9},{9,8},{10,11... | collective-permute-start | bytes 393224 | tf_op jit(solution)/shard_map/ppermute | solution.py:63

commit v9 on v8

--- a/solution.py
+++ b/solution.py
@@ -145,11 +145,11 @@
 
     joined = matmul(
         order,
-        jnp.concatenate([contexts[0], context_other, resid_in, resid_other], axis=1),
+        jnp.concatenate([contexts[0], resid_in, context_other, resid_other], axis=1),
     ).astype(jnp.bfloat16)
     joined = lax.optimization_barrier(joined)
     proj_both = jnp.concatenate(
-        [mine(proj, 1), proj_other, placed(core), placed(1 - core)], axis=0
+        [mine(proj, 1), placed(core), proj_other, placed(1 - core)], axis=0
     )
     partial = matmul(joined, proj_both).astype(jnp.bfloat16)
 
@@ -186,8 +186,7 @@
     rebuilt = far_sum(near_sum(partial))
     my_error = (mask_rows * (rebuilt - my_centred.astype(jnp.float32))).astype(jnp.bfloat16)
     error_rows = spread(my_error, FAR_GROUPS, FAR)
-    later, own_rows, _ = lax.optimization_barrier((centred, my_error, error_rows))
-    owned_error = core_and_section(own_rows)
+    later, _ = lax.optimization_barrier((centred, error_rows))
     centred_other = matmul(
         other_core(later), across_low, ((0,), (1,))
     ).astype(jnp.bfloat16)
@@ -197,6 +196,8 @@
         jnp.concatenate([centred_own, centred_other], axis=0),
         jnp.concatenate([centred_other, centred_own], axis=0),
     )
+    own_rows, centred_full = lax.optimization_barrier((my_error, centred_full))
+    owned_error = core_and_section(own_rows)
     error = spread(error_rows, NEAR_GROUPS, NEAR)
     error, centred_full = lax.optimization_barrier((error, centred_full))
     step_size = STEP_RATE / tokens
@@ -206,7 +207,9 @@
 
     decoder_own, decoder_other = decoder_both[:own], decoder_both[own:]
     over_features = ((1,), (1,))
-    arrived = other_core(matmul(decoder_other, error, over_features))
+    sent = matmul(decoder_other, error, over_features)
+    arrived = other_core(sent)
+    error, _ = lax.optimization_barrier((error, sent))
     backward = matmul(decoder_own, error, over_features) + in_my_order(arrived)
     pre_grad = lax.optimization_barrier(
         jnp.where(before_relu > 0.0, backward, 0.0).astype(jnp.bfloat16)

time: 195 us -> 194 us (level)
  waiting for transfers between devices: 17.2 us -> 13.4 us
  starting transfers between devices: 28.9 us -> 31 us
    ppermute x12, waiting for transfers between devices: 12.7 us -> 6.72 us  [exchange(): return lax.ppermute(value, AXES, route)]
    all_to_all x2, waiting for transfers between devices: 4.48 us -> 6.66 us  [all_to_all(): lax.all_to_all(pieces, AXES, 0, 0, axis_index_groups=groups, tiled=True)]
    ppermute x12, starting transfers between devices: 15.6 us -> 17.7 us  [exchange(): return lax.ppermute(value, AXES, route)]
    unnamed x34 -> x32, local copies, waits for them, and re-layouts: 3.18 us -> 4.5 us
  transfers between devices with their start and end apart: 14 -> 14, of which waited for: 9 -> 8; matrix products, arithmetic and copies ran while one was open for 11% -> 12% of each run, Pallas kernels for 0% -> 0%
where the time goes in v9:
time: 194 us; the launch traced here: 193 us
  blocking collectives  104 us (54%)
  starting transfers between devices  31 us (16%)
  matrix products  18.6 us (10%)
  local copies, waits for them, and re-layouts  15.1 us (8%)
  waiting for transfers between devices  13.4 us (7%)
  other arithmetic  9.43 us (5%)
    all_to_all x6, blocking collectives, all_to_all(): lax.all_to_all(pieces, AXES, 0, 0, axis_index_groups=groups, tiled=True)  104 us
    dot_general x15, matrix products, matmul(): lax.dot_general(a, b, (dims, ((), ())), preferred_element_type=jnp.float3...  18.6 us
    ppermute x12, starting transfers between devices, exchange(): return lax.ppermute(value, AXES, route)  17.7 us
    all_to_all x2, starting transfers between devices, all_to_all(): lax.all_to_all(pieces, AXES, 0, 0, axis_index_groups=groups, tiled=True)  13.4 us
    ppermute x12, waiting for transfers between devices, exchange(): return lax.ppermute(value, AXES, route)  6.72 us
    all_to_all x2, waiting for transfers between devices, all_to_all(): lax.all_to_all(pieces, AXES, 0, 0, axis_index_groups=groups, tiled=True)  6.66 us
    unnamed x32, local copies, waits for them, and re-layouts  4.5 us
    optimization_barrier x1, local copies, waits for them, and re-layouts, shards(): later, _ = lax.optimization_barrier((centred, error_rows))  4.06 us
  transfers between devices with their start and end apart: 14, of which 8 were waited for; matrix products, arithmetic and copies ran while one was open for 12% of the time, Pallas kernels for 0%

profile of v9, /device:TPU:1, one launch (start us, length us, event | category | flops | bytes accessed | tf_op | source)
XLA Modules:
  0.0 192.7 jit_solution(2961971107465826903)
XLA Ops:
  1.5 3.3 %collective-permute-start.1 = (bf16[256,64]{1,0:T(8,128)(2,1)S(1)}, bf16[256,64]{1,0:T(8,128)(2,1)S(1)}, u32[]{:S(2)}, u32[]{:S(2)}) collective-permute-start(bf16[256,64]{1,0:T(8,128)(2,1)S(1)} %copy.16), channel_id=1, source_target_pairs={{0,1},{1,0},{2,3},{3,2},{4,5},{5,4},{6,7},{7,6},{8,9},{9,8},{10,11... | collective-permute-start | bytes 98312 | tf_op jit(solution)/shard_map/ppermute | solution.py:63
  4.9 1.7 dynamic-slice_bitcast_fusion.1
  8.6 0.9 collective-permute-done.2
  9.6 3.8 %convolution_convert_fusion.2 = bf16[256,4096]{1,0:T(8,128)(2,1)} fusion(bf16[256,384]{1,0:T(8,128)(2,1)S(1)} %convolution_convert_fusion.5, bf16[64,4096]{1,0:T(8,128)(2,1)S(1)} %get-tuple-element.44, bf16[128,4096]{1,0:T(8,128)(2,1)} %collective-permute-done.2, bf16[64,4096]{1,0:T(8,128)(2,1)S(1)} %get-tuple-element.43, ...), kind=kOutput, calls=%fused_computation.5 | convolution fusion | flops 818937856 | bytes 5439488 | tf_op jit(solution)/shard_map/dot_general | solution.py:75
  13.4 8.2 %all-to-all-start = ((bf16[8,32,4096]{2,1,0:T(8,128)(2,1)}), bf16[8,32,4096]{2,1,0:T(8,128)(2,1)}, u32[]{:S(2)}, u32[]{:S(2)}) async-start(bf16[8,32,4096]{2,1,0:T(8,128)(2,1)} %bitcast.50), calls=%async_computation | async-start | bytes 4194304 | tf_op jit(solution)/shard_map/all_to_all | solution.py:81
  21.6 1.5 constant_dynamic-slice_fusion.3
  25.9 1.3 collective-permute-done.3
  27.2 2.8 %pad_maximum_fusion = bf16[4096,256]{1,0:T(8,128)(2,1)} fusion(bf16[4096,128]{1,0:T(8,128)(2,1)} %collective-permute-done.3, bf16[4096,128]{1,0:T(8,128)(2,1)S(1)} %copy-done.8), kind=kLoop, calls=%fused_computation.22 | loop fusion | flops 4194304 | bytes 4194304 | tf_op jit(solution)/shard_map/concatenate | solution.py:159
  30.1 6.7 %all-to-all-done = bf16[8,32,4096]{2,1,0:T(8,128)(2,1)} async-done(((bf16[8,32,4096]{2,1,0:T(8,128)(2,1)}), bf16[8,32,4096]{2,1,0:T(8,128)(2,1)}, u32[]{:S(2)}, u32[]{:S(2)}) %all-to-all-start) | async-done | bytes 2097184 | tf_op jit(solution)/shard_map/all_to_all | solution.py:81
  36.8 2.0 %convolution_convert_fusion.4 = bf16[32,4096]{1,0:T(8,128)(2,1)S(1)} fusion(bf16[256,4096]{1,0:T(8,128)(2,1)} %bitcast.4, s32[256]{0:T(256)S(1)} %get-tuple-element.45, s32[256]{0:T(256)S(1)} %get-tuple-element.46, pred[256]{0:T(512)(128)(4,1)S(1)} %compare_and_fusion.2), kind=kOutput, calls=%fused_computation.13 | convolution fusion | flops 67256320 | bytes 2361600 | tf_op jit(solution)/shard_map/dot_general | solution.py:75
  39.0 18.1 %all_to_all.40 = bf16[16,2,4096]{2,1,0:T(2,128)(2,1)S(1)} all-to-all(bf16[16,2,4096]{2,1,0:T(2,128)(2,1)S(1)} %reshape.126), channel_id=1, replica_groups={{0,8,16,24,32,40,48,56,64,72,80,88,96,104,112,120},{4,12,20,28,36,44,52..., dimensions={0} | all-to-all | bytes 524288 | tf_op jit(solution)/shard_map/all_to_all | solution.py:81
  57.5 2.1 %collective-permute-start.5 = (f32[2,1]{0,1:T(1,128)S(1)}, f32[2,1]{0,1:T(1,128)S(1)}, u32[]{:S(2)}, u32[]{:S(2)}) collective-permute-start(f32[2,1]{0,1:T(1,128)S(1)} %bitcast.51), channel_id=1, source_target_pairs={{0,1},{1,0},{2,3},{3,2},{4,5},{5,4},{6,7},{7,6},{8,9},{9,8},{10,11... | collective-permute-start | bytes 32 | tf_op jit(solution)/shard_map/ppermute | solution.py:63
  60.7 14.7 %all_to_all.41 = bf16[16,2,4096]{2,1,0:T(2,128)(2,1)S(1)} all-to-all(bf16[16,2,4096]{2,1,0:T(2,128)(2,1)S(1)} %broadcast_in_dim.57), channel_id=1, replica_groups={{0,8,16,24,32,40,48,56,64,72,80,88,96,104,112,120},{4,12,20,28,36,44,52..., dimensions={0} | all-to-all | bytes 524288 | tf_op jit(solution)/shard_map/all_to_all | solution.py:81
  75.8 21.1 %all_to_all.42 = bf16[8,32,4096]{2,1,0:T(8,128)(2,1)S(1)} all-to-all(bf16[8,32,4096]{2,1,0:T(8,128)(2,1)S(1)} %broadcast_in_dim.59), channel_id=1, replica_groups={{0,4,128,132,2,6,130,134},{8,12,136,140,10,14,138,142},{16,20,144,148,1..., dimensions={0} | all-to-all | bytes 4194304 | tf_op jit(solution)/shard_map/all_to_all | solution.py:81
  98.3 3.2 %collective-permute-start.6 = (f32[128,256]{1,0:T(8,128)S(1)}, f32[128,256]{1,0:T(8,128)S(1)}, u32[]{:S(2)}, u32[]{:S(2)}) collective-permute-start(f32[128,256]{1,0:T(8,128)S(1)} %slice.17), channel_id=1, source_target_pairs={{0,1},{1,0},{2,3},{3,2},{4,5},{5,4},{6,7},{7,6},{8,9},{9,8},{10,11... | collective-permute-start | bytes 393224 | tf_op jit(solution)/shard_map/ppermute | solution.py:63
  101.5 1.0 collective-permute-done.6
  103.3 0.9 collective-permute-done.7
  105.1 19.7 %all_to_all.43 = bf16[8,32,4096]{2,1,0:T(8,128)(2,1)S(1)} all-to-all(bf16[8,32,4096]{2,1,0:T(8,128)(2,1)S(1)} %bitcast.48), channel_id=1, replica_groups={{0,4,128,132,2,6,130,134},{8,12,136,140,10,14,138,142},{16,20,144,148,1..., dimensions={0} | all-to-all | bytes 4194304 | tf_op jit(solution)/shard_map/all_to_all | solution.py:81
  125.4 13.7 %all_to_all.44 = bf16[16,2,4096]{2,1,0:T(2,128)(2,1)S(1)} all-to-all(bf16[16,2,4096]{2,1,0:T(2,128)(2,1)S(1)} %reshape.130), channel_id=1, replica_groups={{0,8,16,24,32,40,48,56,64,72,80,88,96,104,112,120},{4,12,20,28,36,44,52..., dimensions={0} | all-to-all | bytes 524288 | tf_op jit(solution)/shard_map/all_to_all | solution.py:81
  139.6 16.8 %all_to_all.45 = bf16[16,2,4096]{2,1,0:T(2,128)(2,1)S(1)} all-to-all(bf16[16,2,4096]{2,1,0:T(2,128)(2,1)S(1)} %broadcast_in_dim.60), channel_id=1, replica_groups={{0,8,16,24,32,40,48,56,64,72,80,88,96,104,112,120},{4,12,20,28,36,44,52..., dimensions={0} | all-to-all | bytes 524288 | tf_op jit(solution)/shard_map/all_to_all | solution.py:81
  156.6 1.6 broadcast_in_dim.62
  158.2 5.2 %all-to-all-start.7 = ((bf16[8,32,4096]{2,1,0:T(8,128)(2,1)}), bf16[8,32,4096]{2,1,0:T(8,128)(2,1)S(1)}, u32[]{:S(2)}, u32[]{:S(2)}) async-start(bf16[8,32,4096]{2,1,0:T(8,128)(2,1)} %broadcast_in_dim.62), calls=%async_computation.7 | async-start | bytes 4194304 | tf_op jit(solution)/shard_map/all_to_all | solution.py:81
  163.4 1.1 collective-permute-start.8
  164.5 4.1 %copy.17 = bf16[256,4096]{0,1:T(8,128)(2,1)} copy(bf16[256,4096]{1,0:T(8,128)(2,1)} %bitcast.46) | data formatting | bytes 4194304 | tf_op jit(solution)/shard_map/optimization_barrier | solution.py:189
  168.6 2.5 %convolution_convert_fusion = bf16[4096,256]{1,0:T(8,128)(2,1)S(1)} fusion(bf16[256,4096]{1,0:T(8,128)(2,1)} %collective-permute-done.8, pred[256,256]{1,0:T(32,128)(4,1)S(1)} %fusion.55), kind=kOutput, calls=%fused_computation.3 | convolution fusion | flops 537919488 | bytes 4259840 | tf_op jit(solution)/shard_map/dot_general | solution.py:75
  171.1 2.6 %maximum_select_fusion = bf16[8192,256]{1,0:T(8,128)(2,1)} fusion(bf16[4096,256]{1,0:T(8,128)(2,1)S(1)} %convolution_convert_fusion, bf16[4096,256]{1,0:T(8,128)(2,1)S(1)} %bitcast.49, pred[]{:T(512)S(6)} %eq.72), kind=kLoop, calls=%fused_computation.14 | loop fusion | flops 18874368 | bytes 8388609 | tf_op jit(solution)/shard_map/jit(_where)/select_n | solution.py:194
  173.7 4.0 %collective-permute-start.9 = (bf16[2,4096]{1,0:T(2,128)(2,1)S(1)}, bf16[2,4096]{1,0:T(2,128)(2,1)S(1)}, u32[]{:S(2)}, u32[]{:S(2)}) collective-permute-start(bf16[2,4096]{1,0:T(2,128)(2,1)S(1)} %multiply_convert_fusion), channel_id=1, source_target_pairs={{0,0},{1,128},{2,2},{3,130},{4,4},{5,132},{6,6},{7,134},{8,8},{9,1... | collective-permute-start | bytes 49160 | tf_op jit(solution)/shard_map/ppermute | solution.py:63
  177.7 1.7 collective-permute-done.9
  179.4 2.2 %fusion.18 = f32[128,256]{1,0:T(8,128)S(1)} fusion(bf16[256,4096]{1,0:T(8,128)(2,1)S(1)} %bitcast.40, bf16[256,4096]{1,0:T(8,128)(2,1)} %copy-done), kind=kOutput, calls=%fused_computation.38 | convolution fusion | flops 268435456 | bytes 3276800 | tf_op jit(solution)/shard_map/dot_general | solution.py:75
  181.6 2.4 %collective-permute-start.10 = (f32[128,256]{1,0:T(8,128)S(1)}, f32[128,256]{1,0:T(8,128)S(1)}, u32[]{:S(2)}, u32[]{:S(2)}) collective-permute-start(f32[128,256]{1,0:T(8,128)S(1)} %fusion.18), channel_id=1, source_target_pairs={{0,1},{1,0},{2,3},{3,2},{4,5},{5,4},{6,7},{7,6},{8,9},{9,8},{10,11... | collective-permute-start | bytes 393224 | tf_op jit(solution)/shard_map/ppermute | solution.py:63
  187.6 2.6 %fusion.1 = bf16[8192,128]{1,0:T(8,128)(2,1)} fusion(bf16[8192,256]{1,0:T(8,128)(2,1)S(1)} %copy-done.2, bf16[128,256]{1,0:T(8,128)(2,1)S(1)} %select_convert_fusion, bf16[8192,128]{1,0:T(8,128)(2,1)S(1)} %copy-done.5), kind=kOutput, calls=%fused_computation.2 | convolution fusion | flops 541065216 | bytes 8454144 | tf_op jit(solution)/shard_map/dot_general | solution.py:75
  190.2 1.8 maximum_select_fusion.1
  (89 shorter events, 16.3 us)
Async XLA Ops:
  1.5 6.3 %collective-permute-start.1 = (bf16[256,64]{1,0:T(8,128)(2,1)S(1)}, bf16[256,64]{1,0:T(8,128)(2,1)S(1)}, u32[]{:S(2)}, u32[]{:S(2)}) collective-permute-start(bf16[256,64]{1,0:T(8,128)(2,1)S(1)} %copy.16), channel_id=1, source_target_pairs={{0,1},{1,0},{2,3},{3,2},{4,5},{5,4},{6,7},{7,6},{8,9},{9,8},{10,11... | collective-permute-start | bytes 98312 | tf_op jit(solution)/shard_map/ppermute | solution.py:63
  4.8 3.0 %collective-permute-start = (bf16[256,128]{1,0:T(8,128)(2,1)}, bf16[256,128]{1,0:T(8,128)(2,1)S(1)}, u32[]{:S(2)}, u32[]{:S(2)}) collective-permute-start(bf16[256,128]{1,0:T(8,128)(2,1)} %bitcast.52), channel_id=1, source_target_pairs={{0,1},{1,0},{2,3},{3,2},{4,5},{5,4},{6,7},{7,6},{8,9},{9,8},{10,11... | collective-permute-start | bytes 196616 | tf_op jit(solution)/shard_map/ppermute | solution.py:63
  4.9 2.7 %copy-start.12 = (s32[128]{0:T(128)S(1)}, s32[128]{0:T(128)}, u32[]{:S(2)}) copy-start(s32[128]{0:T(128)} %param.17) | copy-start | bytes 1540
  4.9 2.9 %copy-start.13 = (bf16[1,256,128]{2,1,0:T(8,128)(2,1)S(1)}, bf16[1,256,128]{2,1,0:T(8,128)(2,1)}, u32[]{:S(2)}) copy-start(bf16[1,256,128]{2,1,0:T(8,128)(2,1)} %param.10) | copy-start | bytes 196612
  6.6 2.9 %collective-permute-start.2 = (bf16[128,4096]{1,0:T(8,128)(2,1)S(1)}, bf16[128,4096]{1,0:T(8,128)(2,1)}, u32[]{:S(2)}, u32[]{:S(2)}) collective-permute-start(bf16[128,4096]{1,0:T(8,128)(2,1)S(1)} %get-tuple-element.34), channel_id=1, source_target_pairs={{0,1},{1,0},{2,3},{3,2},{4,5},{5,4},{6,7},{7,6},{8,9},{9,8},{10,11... | collective-permute-start | bytes 3145736 | tf_op jit(solution)/shard_map/ppermute | solution.py:63
  13.4 8.2 %copy-start.11 = (s32[256]{0:T(256)S(1)}, s32[256]{0:T(256)}, u32[]{:S(2)}) copy-start(s32[256]{0:T(256)} %param.16) | copy-start | bytes 3076
  13.4 8.2 %copy-start.4 = (bf16[8192,128]{1,0:T(8,128)(2,1)S(1)}, bf16[8192,128]{1,0:T(8,128)(2,1)}, u32[]{:S(2)}) copy-start(bf16[8192,128]{1,0:T(8,128)(2,1)} %param.12) | copy-start | bytes 6291460
  13.4 23.4 %all-to-all-start = ((bf16[8,32,4096]{2,1,0:T(8,128)(2,1)}), bf16[8,32,4096]{2,1,0:T(8,128)(2,1)}, u32[]{:S(2)}, u32[]{:S(2)}) async-start(bf16[8,32,4096]{2,1,0:T(8,128)(2,1)} %bitcast.50), calls=%async_computation | async-start | bytes 4194304 | tf_op jit(solution)/shard_map/all_to_all | solution.py:81
  21.6 2.4 %copy-start.9 = (bf16[128,8192]{1,0:T(8,128)(2,1)S(1)}, bf16[128,8192]{1,0:T(8,128)(2,1)}, u32[]{:S(2)}) copy-start(bf16[128,8192]{1,0:T(8,128)(2,1)} %param.14) | copy-start | bytes 6291460
  23.9 0.7 copy-start.10
  24.0 3.2 %copy-start.8 = (bf16[4096,128]{1,0:T(8,128)(2,1)S(1)}, bf16[4096,128]{1,0:T(8,128)(2,1)}, u32[]{:S(2)}) copy-start(bf16[4096,128]{1,0:T(8,128)(2,1)} %get-tuple-element.31) | copy-start | bytes 3145732
  24.1 3.1 %collective-permute-start.3 = (bf16[4096,128]{1,0:T(8,128)(2,1)}, bf16[4096,128]{1,0:T(8,128)(2,1)}, u32[]{:S(2)}, u32[]{:S(2)}) collective-permute-start(bf16[4096,128]{1,0:T(8,128)(2,1)} %get-tuple-element.16), channel_id=1, source_target_pairs={{0,1},{1,0},{2,3},{3,2},{4,5},{5,4},{6,7},{7,6},{8,9},{9,8},{10,11... | collective-permute-start | bytes 3145736 | tf_op jit(solution)/shard_map/ppermute | solution.py:63
  24.8 5.2 %collective-permute-start.4 = (bf16[128,4096]{1,0:T(8,128)(2,1)S(1)}, bf16[128,4096]{1,0:T(8,128)(2,1)S(1)}, u32[]{:S(2)}, u32[]{:S(2)}) collective-permute-start(bf16[128,4096]{1,0:T(8,128)(2,1)S(1)} %get-tuple-element.17), channel_id=1, source_target_pairs={{0,1},{1,0},{2,3},{3,2},{4,5},{5,4},{6,7},{7,6},{8,9},{9,8},{10,11... | collective-permute-start | bytes 3145736 | tf_op jit(solution)/shard_map/ppermute | solution.py:63
  30.1 74.2 %copy-start = (bf16[256,4096]{1,0:T(8,128)(2,1)}, bf16[256,4096]{1,0:T(8,128)(2,1)S(1)}, u32[]{:S(2)}) copy-start(bf16[256,4096]{1,0:T(8,128)(2,1)S(1)} %pad_maximum_fusion.1) | copy-start | bytes 6291460
  57.5 2.9 %collective-permute-start.5 = (f32[2,1]{0,1:T(1,128)S(1)}, f32[2,1]{0,1:T(1,128)S(1)}, u32[]{:S(2)}, u32[]{:S(2)}) collective-permute-start(f32[2,1]{0,1:T(1,128)S(1)} %bitcast.51), channel_id=1, source_target_pairs={{0,1},{1,0},{2,3},{3,2},{4,5},{5,4},{6,7},{7,6},{8,9},{9,8},{10,11... | collective-permute-start | bytes 32 | tf_op jit(solution)/shard_map/ppermute | solution.py:63
  75.8 21.1 %copy-start.6 = (bf16[4096,256]{1,0:T(8,128)(2,1)S(1)}, bf16[4096,256]{1,0:T(8,128)(2,1)}, u32[]{:S(2)}) copy-start(bf16[4096,256]{1,0:T(8,128)(2,1)} %pad_maximum_fusion) | copy-start | bytes 6291460
  97.0 1.3 copy-start.3
  97.0 4.6 %copy-start.14 = (bf16[128]{0:T(256)(128)(2,1)S(1)}, bf16[128]{0:T(256)(128)(2,1)}, u32[]{:S(2)}) copy-start(bf16[128]{0:T(256)(128)(2,1)} %param.13) | copy-start | bytes 772
  98.3 4.2 %collective-permute-start.6 = (f32[128,256]{1,0:T(8,128)S(1)}, f32[128,256]{1,0:T(8,128)S(1)}, u32[]{:S(2)}, u32[]{:S(2)}) collective-permute-start(f32[128,256]{1,0:T(8,128)S(1)} %slice.17), channel_id=1, source_target_pairs={{0,1},{1,0},{2,3},{3,2},{4,5},{5,4},{6,7},{7,6},{8,9},{9,8},{10,11... | collective-permute-start | bytes 393224 | tf_op jit(solution)/shard_map/ppermute | solution.py:63
  102.8 1.4 collective-permute-start.7
  158.2 21.2 %all-to-all-start.7 = ((bf16[8,32,4096]{2,1,0:T(8,128)(2,1)}), bf16[8,32,4096]{2,1,0:T(8,128)(2,1)S(1)}, u32[]{:S(2)}, u32[]{:S(2)}) async-start(bf16[8,32,4096]{2,1,0:T(8,128)(2,1)} %broadcast_in_dim.62), calls=%async_computation.7 | async-start | bytes 4194304 | tf_op jit(solution)/shard_map/all_to_all | solution.py:81
  163.4 5.3 %collective-permute-start.8 = (bf16[256,4096]{1,0:T(8,128)(2,1)}, bf16[256,4096]{1,0:T(8,128)(2,1)}, u32[]{:S(2)}, u32[]{:S(2)}) collective-permute-start(bf16[256,4096]{1,0:T(8,128)(2,1)} %bitcast.45), channel_id=1, source_target_pairs={{0,1},{1,0},{2,3},{3,2},{4,5},{5,4},{6,7},{7,6},{8,9},{9,8},{10,11... | collective-permute-start | bytes 6291464 | tf_op jit(solution)/shard_map/ppermute | solution.py:63
  168.5 2.6 %copy-start.7 = (bf16[256,4096]{0,1:T(8,128)(2,1)S(1)}, bf16[256,4096]{0,1:T(8,128)(2,1)}, u32[]{:S(2)}) copy-start(bf16[256,4096]{0,1:T(8,128)(2,1)} %copy.17) | copy-start | bytes 6291460
  173.7 5.7 %collective-permute-start.9 = (bf16[2,4096]{1,0:T(2,128)(2,1)S(1)}, bf16[2,4096]{1,0:T(2,128)(2,1)S(1)}, u32[]{:S(2)}, u32[]{:S(2)}) collective-permute-start(bf16[2,4096]{1,0:T(2,128)(2,1)S(1)} %multiply_convert_fusion), channel_id=1, source_target_pairs={{0,0},{1,128},{2,2},{3,130},{4,4},{5,132},{6,6},{7,134},{8,8},{9,1... | collective-permute-start | bytes 49160 | tf_op jit(solution)/shard_map/ppermute | solution.py:63
  179.4 4.6 %copy-start.1 = (bf16[256,4096]{1,0:T(8,128)(2,1)S(1)}, bf16[256,4096]{1,0:T(8,128)(2,1)}, u32[]{:S(2)}) copy-start(bf16[256,4096]{1,0:T(8,128)(2,1)} %copy-done) | copy-start | bytes 6291460
  181.6 4.5 %collective-permute-start.10 = (f32[128,256]{1,0:T(8,128)S(1)}, f32[128,256]{1,0:T(8,128)S(1)}, u32[]{:S(2)}, u32[]{:S(2)}) collective-permute-start(f32[128,256]{1,0:T(8,128)S(1)} %fusion.18), channel_id=1, source_target_pairs={{0,1},{1,0},{2,3},{3,2},{4,5},{5,4},{6,7},{7,6},{8,9},{9,8},{10,11... | collective-permute-start | bytes 393224 | tf_op jit(solution)/shard_map/ppermute | solution.py:63
  184.5 5.7 %collective-permute-start.11 = (bf16[128,4096]{1,0:T(8,128)(2,1)S(1)}, bf16[128,4096]{1,0:T(8,128)(2,1)S(1)}, u32[]{:S(2)}, u32[]{:S(2)}) collective-permute-start(bf16[128,4096]{1,0:T(8,128)(2,1)S(1)} %fusion.5), channel_id=1, source_target_pairs={{0,1},{1,0},{2,3},{3,2},{4,5},{5,4},{6,7},{7,6},{8,9},{9,8},{10,11... | collective-permute-start | bytes 3145736 | tf_op jit(solution)/shard_map/ppermute | solution.py:63
  184.6 2.2 %copy-start.2 = (bf16[8192,256]{1,0:T(8,128)(2,1)S(1)}, bf16[8192,256]{1,0:T(8,128)(2,1)}, u32[]{:S(2)}) copy-start(bf16[8192,256]{1,0:T(8,128)(2,1)} %maximum_select_fusion) | copy-start | bytes 12582916
  185.2 2.4 %copy-start.5 = (bf16[8192,128]{1,0:T(8,128)(2,1)S(1)}, bf16[8192,128]{1,0:T(8,128)(2,1)}, u32[]{:S(2)}) copy-start(bf16[8192,128]{1,0:T(8,128)(2,1)} %param.12) | copy-start | bytes 6291460

commit v10 on v9

--- a/solution.py
+++ b/solution.py
@@ -120,15 +120,17 @@
 
     proj = out_proj[0]
     proj_other = other_core(theirs(proj, 1))
-    context_other = other_core(contexts[0])
-    resid_other = other_core(resid_in)
 
     row = lax.broadcasted_iota(jnp.int32, (tokens, tokens), 0)
     old = lax.broadcasted_iota(jnp.int32, (tokens, tokens), 1)
     same_place = row % block_rows == old % block_rows
     at = chip_of(row // block_rows, core)
+    at_other = chip_of(row // block_rows, 1 - core)
     owner_of_row = jnp.repeat(owner_map, block_rows)
-    order = ((owner_of_row[None, :] == at) & same_place).astype(jnp.bfloat16)
+    orders = [
+        ((owner_of_row[None, :] == to) & same_place).astype(jnp.bfloat16)
+        for to in (at, at_other)
+    ]
     across = (chip_of(old // block_rows, 1 - core) == at) & same_place
     kept = (token_ids.reshape(blocks, block_rows) != BOS).astype(jnp.float32)
     mask_rows = jnp.sum(jnp.where((owner_map == chip)[:, None], kept, 0.0), axis=0)[:, None]
@@ -143,11 +145,11 @@
         )
         return ((column == target) & owns).astype(jnp.bfloat16)
 
-    joined = matmul(
-        order,
-        jnp.concatenate([contexts[0], resid_in, context_other, resid_other], axis=1),
-    ).astype(jnp.bfloat16)
-    joined = lax.optimization_barrier(joined)
+    given = jnp.concatenate([contexts[0], resid_in], axis=1)
+    joined, joined_out = lax.optimization_barrier(
+        [matmul(order, given).astype(jnp.bfloat16) for order in orders]
+    )
+    joined = jnp.concatenate([joined, other_core(joined_out)], axis=1)
     proj_both = jnp.concatenate(
         [mine(proj, 1), placed(core), proj_other, placed(1 - core)], axis=0
     )
@@ -216,12 +218,13 @@
     )
     back_half = other_core(stepped(decoder_other, matmul(latents_other, error)))
     kept_half = stepped(decoder_own, matmul(latents, error))
-    new_encoder = stepped(encoder, matmul(centred_full, pre_grad, over_features))
     new_decoder = jnp.where(
         core == 0,
         jnp.concatenate([kept_half, back_half], axis=1),
         jnp.concatenate([back_half, kept_half], axis=1),
     )
+    pre_grad, _ = lax.optimization_barrier((pre_grad, new_decoder))
+    new_encoder = stepped(encoder, matmul(centred_full, pre_grad, over_features))
     return (owned_error, new_encoder, new_decoder)
 
 

time: 194 us -> 198 us (1.021)
  waiting for transfers between devices: 13.4 us -> 18.8 us
    all_to_all x2, waiting for transfers between devices: 6.66 us -> 10.8 us  [all_to_all(): lax.all_to_all(pieces, AXES, 0, 0, axis_index_groups=groups, tiled=True)]
    ppermute x12 -> x11, waiting for transfers between devices: 6.72 us -> 8.02 us  [exchange(): return lax.ppermute(value, AXES, route)]
    unnamed x32 -> x34, local copies, waits for them, and re-layouts: 4.5 us -> 3.69 us
    dot_general x15 -> x16, matrix products: 18.6 us -> 19.4 us  [matmul(): lax.dot_general(a, b, (dims, ((), ())), preferred_element_type=jnp.float3...]
    ppermute x12 -> x11, starting transfers between devices: 17.7 us -> 16.9 us  [exchange(): return lax.ppermute(value, AXES, route)]
  transfers between devices with their start and end apart: 14 -> 13, of which waited for: 8 -> 9; matrix products, arithmetic and copies ran while one was open for 12% -> 9% of each run, Pallas kernels for 0% -> 0%
where the time goes in v10:
time: 198 us; the launch traced here: 197 us
  blocking collectives  105 us (53%)
  starting transfers between devices  29.5 us (15%)
  matrix products  19.4 us (10%)
  waiting for transfers between devices  18.8 us (9%)
  local copies, waits for them, and re-layouts  14.3 us (7%)
  other arithmetic  9.43 us (5%)
    all_to_all x6, blocking collectives, all_to_all(): lax.all_to_all(pieces, AXES, 0, 0, axis_index_groups=groups, tiled=True)  105 us
    dot_general x16, matrix products, matmul(): lax.dot_general(a, b, (dims, ((), ())), preferred_element_type=jnp.float3...  19.4 us
    ppermute x11, starting transfers between devices, exchange(): return lax.ppermute(value, AXES, route)  16.9 us
    all_to_all x2, starting transfers between devices, all_to_all(): lax.all_to_all(pieces, AXES, 0, 0, axis_index_groups=groups, tiled=True)  12.6 us
    all_to_all x2, waiting for transfers between devices, all_to_all(): lax.all_to_all(pieces, AXES, 0, 0, axis_index_groups=groups, tiled=True)  10.8 us
    ppermute x11, waiting for transfers between devices, exchange(): return lax.ppermute(value, AXES, route)  8.02 us
    optimization_barrier x1, local copies, waits for them, and re-layouts, shards(): later, _ = lax.optimization_barrier((centred, error_rows))  4.06 us
  transfers between devices with their start and end apart: 13, of which 9 were waited for; matrix products, arithmetic and copies ran while one was open for 9% of the time, Pallas kernels for 0%

profile of v10, /device:TPU:1, one launch (start us, length us, event | category | flops | bytes accessed | tf_op | source)
XLA Modules:
  0.0 197.5 jit_solution(556285436511342037)
XLA Ops:
  0.7 1.7 dynamic-slice_bitcast_fusion.1
  2.4 3.3 %collective-permute-start.1 = (bf16[128,4096]{1,0:T(8,128)(2,1)S(1)}, bf16[128,4096]{1,0:T(8,128)(2,1)}, u32[]{:S(2)}, u32[]{:S(2)}) collective-permute-start(bf16[128,4096]{1,0:T(8,128)(2,1)S(1)} %get-tuple-element.40), channel_id=1, source_target_pairs={{0,1},{1,0},{2,3},{3,2},{4,5},{5,4},{6,7},{7,6},{8,9},{9,8},{10,11... | collective-permute-start | bytes 3145736 | tf_op jit(solution)/shard_map/ppermute | solution.py:63
  9.0 3.8 %convolution_convert_fusion.2 = bf16[256,4096]{1,0:T(8,128)(2,1)} fusion(bf16[64,4096]{1,0:T(8,128)(2,1)S(1)} %get-tuple-element.46, bf16[128,4096]{1,0:T(8,128)(2,1)} %collective-permute-done.1, bf16[64,4096]{1,0:T(8,128)(2,1)S(1)} %get-tuple-element.45, bf16[128,4096]{1,0:T(8,128)(2,1)S(1)} %get-tuple-element.39, ...), kind=kOutput, calls=%fused_computation.5 | convolution fusion | flops 819331072 | bytes 5439488 | tf_op jit(solution)/shard_map/dot_general | solution.py:75
  12.9 8.2 %all-to-all-start = ((bf16[8,32,4096]{2,1,0:T(8,128)(2,1)}), bf16[8,32,4096]{2,1,0:T(8,128)(2,1)}, u32[]{:S(2)}, u32[]{:S(2)}) async-start(bf16[8,32,4096]{2,1,0:T(8,128)(2,1)} %bitcast.49), calls=%async_computation | async-start | bytes 4194304 | tf_op jit(solution)/shard_map/all_to_all | solution.py:81
  21.1 1.5 constant_dynamic-slice_fusion.3
  25.4 1.3 collective-permute-done.2
  26.7 2.8 %pad_maximum_fusion = bf16[4096,256]{1,0:T(8,128)(2,1)} fusion(bf16[4096,128]{1,0:T(8,128)(2,1)} %collective-permute-done.2, bf16[4096,128]{1,0:T(8,128)(2,1)S(1)} %copy-done.8), kind=kLoop, calls=%fused_computation.22 | loop fusion | flops 4194304 | bytes 4194304 | tf_op jit(solution)/shard_map/concatenate | solution.py:161
  29.6 6.7 %all-to-all-done = bf16[8,32,4096]{2,1,0:T(8,128)(2,1)} async-done(((bf16[8,32,4096]{2,1,0:T(8,128)(2,1)}), bf16[8,32,4096]{2,1,0:T(8,128)(2,1)}, u32[]{:S(2)}, u32[]{:S(2)}) %all-to-all-start) | async-done | bytes 2097184 | tf_op jit(solution)/shard_map/all_to_all | solution.py:81
  36.3 2.0 %convolution_convert_fusion.4 = bf16[32,4096]{1,0:T(8,128)(2,1)S(1)} fusion(bf16[256,4096]{1,0:T(8,128)(2,1)} %bitcast.4, s32[256]{0:T(256)S(1)} %get-tuple-element.51, s32[256]{0:T(256)S(1)} %get-tuple-element.52, pred[256]{0:T(512)(128)(4,1)S(1)} %compare_and_fusion.2), kind=kOutput, calls=%fused_computation.13 | convolution fusion | flops 67256320 | bytes 2361600 | tf_op jit(solution)/shard_map/dot_general | solution.py:75
  38.5 18.1 %all_to_all.40 = bf16[16,2,4096]{2,1,0:T(2,128)(2,1)S(1)} all-to-all(bf16[16,2,4096]{2,1,0:T(2,128)(2,1)S(1)} %reshape.126), channel_id=1, replica_groups={{0,8,16,24,32,40,48,56,64,72,80,88,96,104,112,120},{4,12,20,28,36,44,52..., dimensions={0} | all-to-all | bytes 524288 | tf_op jit(solution)/shard_map/all_to_all | solution.py:81
  57.0 1.9 collective-permute-start.4
  60.0 15.1 %all_to_all.41 = bf16[16,2,4096]{2,1,0:T(2,128)(2,1)S(1)} all-to-all(bf16[16,2,4096]{2,1,0:T(2,128)(2,1)S(1)} %broadcast_in_dim.57), channel_id=1, replica_groups={{0,8,16,24,32,40,48,56,64,72,80,88,96,104,112,120},{4,12,20,28,36,44,52..., dimensions={0} | all-to-all | bytes 524288 | tf_op jit(solution)/shard_map/all_to_all | solution.py:81
  75.5 21.2 %all_to_all.42 = bf16[8,32,4096]{2,1,0:T(8,128)(2,1)S(1)} all-to-all(bf16[8,32,4096]{2,1,0:T(8,128)(2,1)S(1)} %broadcast_in_dim.59), channel_id=1, replica_groups={{0,4,128,132,2,6,130,134},{8,12,136,140,10,14,138,142},{16,20,144,148,1..., dimensions={0} | all-to-all | bytes 4194304 | tf_op jit(solution)/shard_map/all_to_all | solution.py:81
  98.0 2.7 %collective-permute-start.5 = (f32[128,256]{1,0:T(8,128)S(1)}, f32[128,256]{1,0:T(8,128)S(1)}, u32[]{:S(2)}, u32[]{:S(2)}) collective-permute-start(f32[128,256]{1,0:T(8,128)S(1)} %slice.17), channel_id=1, source_target_pairs={{0,1},{1,0},{2,3},{3,2},{4,5},{5,4},{6,7},{7,6},{8,9},{9,8},{10,11... | collective-permute-start | bytes 393224 | tf_op jit(solution)/shard_map/ppermute | solution.py:63
  100.7 1.0 collective-permute-done.5
  104.5 19.7 %all_to_all.43 = bf16[8,32,4096]{2,1,0:T(8,128)(2,1)S(1)} all-to-all(bf16[8,32,4096]{2,1,0:T(8,128)(2,1)S(1)} %bitcast.47), channel_id=1, replica_groups={{0,4,128,132,2,6,130,134},{8,12,136,140,10,14,138,142},{16,20,144,148,1..., dimensions={0} | all-to-all | bytes 4194304 | tf_op jit(solution)/shard_map/all_to_all | solution.py:81
  124.8 13.0 %all_to_all.44 = bf16[16,2,4096]{2,1,0:T(2,128)(2,1)S(1)} all-to-all(bf16[16,2,4096]{2,1,0:T(2,128)(2,1)S(1)} %reshape.130), channel_id=1, replica_groups={{0,8,16,24,32,40,48,56,64,72,80,88,96,104,112,120},{4,12,20,28,36,44,52..., dimensions={0} | all-to-all | bytes 524288 | tf_op jit(solution)/shard_map/all_to_all | solution.py:81
  138.3 18.0 %all_to_all.45 = bf16[16,2,4096]{2,1,0:T(2,128)(2,1)S(1)} all-to-all(bf16[16,2,4096]{2,1,0:T(2,128)(2,1)S(1)} %broadcast_in_dim.60), channel_id=1, replica_groups={{0,8,16,24,32,40,48,56,64,72,80,88,96,104,112,120},{4,12,20,28,36,44,52..., dimensions={0} | all-to-all | bytes 524288 | tf_op jit(solution)/shard_map/all_to_all | solution.py:81
  156.4 1.6 broadcast_in_dim.62
  158.1 4.4 %all-to-all-start.7 = ((bf16[8,32,4096]{2,1,0:T(8,128)(2,1)}), bf16[8,32,4096]{2,1,0:T(8,128)(2,1)S(1)}, u32[]{:S(2)}, u32[]{:S(2)}) async-start(bf16[8,32,4096]{2,1,0:T(8,128)(2,1)} %broadcast_in_dim.62), calls=%async_computation.7 | async-start | bytes 4194304 | tf_op jit(solution)/shard_map/all_to_all | solution.py:81
  162.5 1.9 collective-permute-start.7
  164.4 4.1 %copy.15 = bf16[256,4096]{0,1:T(8,128)(2,1)} copy(bf16[256,4096]{1,0:T(8,128)(2,1)} %bitcast.45) | data formatting | bytes 4194304 | tf_op jit(solution)/shard_map/optimization_barrier | solution.py:191
  168.5 2.5 %convolution_convert_fusion = bf16[4096,256]{1,0:T(8,128)(2,1)S(1)} fusion(bf16[256,4096]{1,0:T(8,128)(2,1)} %collective-permute-done.7, pred[256,256]{1,0:T(32,128)(4,1)S(1)} %fusion.61), kind=kOutput, calls=%fused_computation.3 | convolution fusion | flops 537919488 | bytes 4259840 | tf_op jit(solution)/shard_map/dot_general | solution.py:75
  171.0 2.6 %maximum_select_fusion = bf16[8192,256]{1,0:T(8,128)(2,1)} fusion(bf16[4096,256]{1,0:T(8,128)(2,1)S(1)} %convolution_convert_fusion, bf16[4096,256]{1,0:T(8,128)(2,1)S(1)} %bitcast.48, pred[]{:T(512)S(6)} %eq.86), kind=kLoop, calls=%fused_computation.14 | loop fusion | flops 18874368 | bytes 8388609 | tf_op jit(solution)/shard_map/jit(_where)/select_n | solution.py:196
  173.6 4.1 %all-to-all-done.7 = bf16[8,32,4096]{2,1,0:T(8,128)(2,1)S(1)} async-done(((bf16[8,32,4096]{2,1,0:T(8,128)(2,1)}), bf16[8,32,4096]{2,1,0:T(8,128)(2,1)S(1)}, u32[]{:S(2)}, u32[]{:S(2)}) %all-to-all-start.7) | async-done | bytes 2097184 | tf_op jit(solution)/shard_map/all_to_all | solution.py:81
  177.7 2.2 %fusion.18 = f32[128,256]{1,0:T(8,128)S(1)} fusion(bf16[256,4096]{1,0:T(8,128)(2,1)S(1)} %bitcast.39, bf16[256,4096]{1,0:T(8,128)(2,1)} %copy-done), kind=kOutput, calls=%fused_computation.39 | convolution fusion | flops 268435456 | bytes 3276800 | tf_op jit(solution)/shard_map/dot_general | solution.py:75
  180.5 3.9 %collective-permute-start.10 = (bf16[128,4096]{1,0:T(8,128)(2,1)S(1)}, bf16[128,4096]{1,0:T(8,128)(2,1)S(1)}, u32[]{:S(2)}, u32[]{:S(2)}) collective-permute-start(bf16[128,4096]{1,0:T(8,128)(2,1)S(1)} %fusion.5), channel_id=1, source_target_pairs={{0,1},{1,0},{2,3},{3,2},{4,5},{5,4},{6,7},{7,6},{8,9},{9,8},{10,11... | collective-permute-start | bytes 3145736 | tf_op jit(solution)/shard_map/ppermute | solution.py:63
  184.5 1.9 collective-permute-start.8
  186.4 3.1 %collective-permute-done.8 = bf16[2,4096]{1,0:T(2,128)(2,1)S(1)} collective-permute-done((bf16[2,4096]{1,0:T(2,128)(2,1)S(1)}, bf16[2,4096]{1,0:T(2,128)(2,1)S(1)}, u32[]{:S(2)}, u32[]{:S(2)}) %collective-permute-start.8) | collective-permute-done | bytes 16416 | tf_op jit(solution)/shard_map/ppermute | solution.py:63
  191.3 1.8 maximum_select_fusion.1
  193.1 1.2 copy-done.2
  194.3 2.6 %fusion.1 = bf16[8192,128]{1,0:T(8,128)(2,1)} fusion(bf16[8192,256]{1,0:T(8,128)(2,1)S(1)} %copy-done.2, bf16[128,256]{1,0:T(8,128)(2,1)S(1)} %select_convert_fusion, bf16[8192,128]{1,0:T(8,128)(2,1)S(1)} %copy-done.5), kind=kOutput, calls=%fused_computation.2 | convolution fusion | flops 541065216 | bytes 8454144 | tf_op jit(solution)/shard_map/dot_general | solution.py:75
  (90 shorter events, 16.4 us)
Async XLA Ops:
  0.6 5.1 %copy-start.13 = (s32[128]{0:T(128)S(1)}, s32[128]{0:T(128)}, u32[]{:S(2)}) copy-start(s32[128]{0:T(128)} %param.17) | copy-start | bytes 1540
  0.7 5.3 %copy-start.10 = (bf16[256,64]{0,1:T(8,128)(2,1)S(1)}, bf16[256,64]{0,1:T(8,128)(2,1)}, u32[]{:S(2)}) copy-start(bf16[256,64]{0,1:T(8,128)(2,1)} %param.9) | copy-start | bytes 98308
  0.7 5.4 %copy-start.14 = (bf16[1,256,128]{2,1,0:T(8,128)(2,1)S(1)}, bf16[1,256,128]{2,1,0:T(8,128)(2,1)}, u32[]{:S(2)}) copy-start(bf16[1,256,128]{2,1,0:T(8,128)(2,1)} %param.10) | copy-start | bytes 196612
  2.4 6.7 %collective-permute-start.1 = (bf16[128,4096]{1,0:T(8,128)(2,1)S(1)}, bf16[128,4096]{1,0:T(8,128)(2,1)}, u32[]{:S(2)}, u32[]{:S(2)}) collective-permute-start(bf16[128,4096]{1,0:T(8,128)(2,1)S(1)} %get-tuple-element.40), channel_id=1, source_target_pairs={{0,1},{1,0},{2,3},{3,2},{4,5},{5,4},{6,7},{7,6},{8,9},{9,8},{10,11... | collective-permute-start | bytes 3145736 | tf_op jit(solution)/shard_map/ppermute | solution.py:63
  7.7 1.4 collective-permute-start
  12.9 8.2 %copy-start.12 = (s32[256]{0:T(256)S(1)}, s32[256]{0:T(256)}, u32[]{:S(2)}) copy-start(s32[256]{0:T(256)} %param.16) | copy-start | bytes 3076
  12.9 8.2 %copy-start.4 = (bf16[8192,128]{1,0:T(8,128)(2,1)S(1)}, bf16[8192,128]{1,0:T(8,128)(2,1)}, u32[]{:S(2)}) copy-start(bf16[8192,128]{1,0:T(8,128)(2,1)} %param.12) | copy-start | bytes 6291460
  12.9 23.4 %all-to-all-start = ((bf16[8,32,4096]{2,1,0:T(8,128)(2,1)}), bf16[8,32,4096]{2,1,0:T(8,128)(2,1)}, u32[]{:S(2)}, u32[]{:S(2)}) async-start(bf16[8,32,4096]{2,1,0:T(8,128)(2,1)} %bitcast.49), calls=%async_computation | async-start | bytes 4194304 | tf_op jit(solution)/shard_map/all_to_all | solution.py:81
  21.1 2.4 %copy-start.9 = (bf16[128,8192]{1,0:T(8,128)(2,1)S(1)}, bf16[128,8192]{1,0:T(8,128)(2,1)}, u32[]{:S(2)}) copy-start(bf16[128,8192]{1,0:T(8,128)(2,1)} %param.14) | copy-start | bytes 6291460
  23.5 0.7 copy-start.11
  23.5 3.2 %copy-start.8 = (bf16[4096,128]{1,0:T(8,128)(2,1)S(1)}, bf16[4096,128]{1,0:T(8,128)(2,1)}, u32[]{:S(2)}) copy-start(bf16[4096,128]{1,0:T(8,128)(2,1)} %get-tuple-element.37) | copy-start | bytes 3145732
  23.6 3.1 %collective-permute-start.2 = (bf16[4096,128]{1,0:T(8,128)(2,1)}, bf16[4096,128]{1,0:T(8,128)(2,1)}, u32[]{:S(2)}, u32[]{:S(2)}) collective-permute-start(bf16[4096,128]{1,0:T(8,128)(2,1)} %get-tuple-element.21), channel_id=1, source_target_pairs={{0,1},{1,0},{2,3},{3,2},{4,5},{5,4},{6,7},{7,6},{8,9},{9,8},{10,11... | collective-permute-start | bytes 3145736 | tf_op jit(solution)/shard_map/ppermute | solution.py:63
  24.3 5.2 %collective-permute-start.3 = (bf16[128,4096]{1,0:T(8,128)(2,1)S(1)}, bf16[128,4096]{1,0:T(8,128)(2,1)S(1)}, u32[]{:S(2)}, u32[]{:S(2)}) collective-permute-start(bf16[128,4096]{1,0:T(8,128)(2,1)S(1)} %get-tuple-element.22), channel_id=1, source_target_pairs={{0,1},{1,0},{2,3},{3,2},{4,5},{5,4},{6,7},{7,6},{8,9},{9,8},{10,11... | collective-permute-start | bytes 3145736 | tf_op jit(solution)/shard_map/ppermute | solution.py:63
  29.6 74.1 %copy-start = (bf16[256,4096]{1,0:T(8,128)(2,1)}, bf16[256,4096]{1,0:T(8,128)(2,1)S(1)}, u32[]{:S(2)}) copy-start(bf16[256,4096]{1,0:T(8,128)(2,1)S(1)} %pad_maximum_fusion.1) | copy-start | bytes 6291460
  57.0 2.7 %collective-permute-start.4 = (f32[2,1]{0,1:T(1,128)S(1)}, f32[2,1]{0,1:T(1,128)S(1)}, u32[]{:S(2)}, u32[]{:S(2)}) collective-permute-start(f32[2,1]{0,1:T(1,128)S(1)} %bitcast.50), channel_id=1, source_target_pairs={{0,1},{1,0},{2,3},{3,2},{4,5},{5,4},{6,7},{7,6},{8,9},{9,8},{10,11... | collective-permute-start | bytes 32 | tf_op jit(solution)/shard_map/ppermute | solution.py:63
  75.5 21.2 %copy-start.6 = (bf16[4096,256]{1,0:T(8,128)(2,1)S(1)}, bf16[4096,256]{1,0:T(8,128)(2,1)}, u32[]{:S(2)}) copy-start(bf16[4096,256]{1,0:T(8,128)(2,1)} %pad_maximum_fusion) | copy-start | bytes 6291460
  96.6 1.3 copy-start.3
  96.6 4.0 %copy-start.15 = (bf16[128]{0:T(256)(128)(2,1)S(1)}, bf16[128]{0:T(256)(128)(2,1)}, u32[]{:S(2)}) copy-start(bf16[128]{0:T(256)(128)(2,1)} %param.13) | copy-start | bytes 772
  98.0 3.7 %collective-permute-start.5 = (f32[128,256]{1,0:T(8,128)S(1)}, f32[128,256]{1,0:T(8,128)S(1)}, u32[]{:S(2)}, u32[]{:S(2)}) collective-permute-start(f32[128,256]{1,0:T(8,128)S(1)} %slice.17), channel_id=1, source_target_pairs={{0,1},{1,0},{2,3},{3,2},{4,5},{5,4},{6,7},{7,6},{8,9},{9,8},{10,11... | collective-permute-start | bytes 393224 | tf_op jit(solution)/shard_map/ppermute | solution.py:63
  102.0 1.5 collective-permute-start.6
  158.1 19.6 %all-to-all-start.7 = ((bf16[8,32,4096]{2,1,0:T(8,128)(2,1)}), bf16[8,32,4096]{2,1,0:T(8,128)(2,1)S(1)}, u32[]{:S(2)}, u32[]{:S(2)}) async-start(bf16[8,32,4096]{2,1,0:T(8,128)(2,1)} %broadcast_in_dim.62), calls=%async_computation.7 | async-start | bytes 4194304 | tf_op jit(solution)/shard_map/all_to_all | solution.py:81
  162.5 6.1 %collective-permute-start.7 = (bf16[256,4096]{1,0:T(8,128)(2,1)}, bf16[256,4096]{1,0:T(8,128)(2,1)}, u32[]{:S(2)}, u32[]{:S(2)}) collective-permute-start(bf16[256,4096]{1,0:T(8,128)(2,1)} %bitcast.44), channel_id=1, source_target_pairs={{0,1},{1,0},{2,3},{3,2},{4,5},{5,4},{6,7},{7,6},{8,9},{9,8},{10,11... | collective-permute-start | bytes 6291464 | tf_op jit(solution)/shard_map/ppermute | solution.py:63
  168.5 2.6 %copy-start.7 = (bf16[256,4096]{0,1:T(8,128)(2,1)S(1)}, bf16[256,4096]{0,1:T(8,128)(2,1)}, u32[]{:S(2)}) copy-start(bf16[256,4096]{0,1:T(8,128)(2,1)} %copy.15) | copy-start | bytes 6291460
  177.7 2.2 %copy-start.1 = (bf16[256,4096]{1,0:T(8,128)(2,1)S(1)}, bf16[256,4096]{1,0:T(8,128)(2,1)}, u32[]{:S(2)}) copy-start(bf16[256,4096]{1,0:T(8,128)(2,1)} %copy-done) | copy-start | bytes 6291460
  180.5 10.8 %collective-permute-start.10 = (bf16[128,4096]{1,0:T(8,128)(2,1)S(1)}, bf16[128,4096]{1,0:T(8,128)(2,1)S(1)}, u32[]{:S(2)}, u32[]{:S(2)}) collective-permute-start(bf16[128,4096]{1,0:T(8,128)(2,1)S(1)} %fusion.5), channel_id=1, source_target_pairs={{0,1},{1,0},{2,3},{3,2},{4,5},{5,4},{6,7},{7,6},{8,9},{9,8},{10,11... | collective-permute-start | bytes 3145736 | tf_op jit(solution)/shard_map/ppermute | solution.py:63
  184.5 5.0 %collective-permute-start.8 = (bf16[2,4096]{1,0:T(2,128)(2,1)S(1)}, bf16[2,4096]{1,0:T(2,128)(2,1)S(1)}, u32[]{:S(2)}, u32[]{:S(2)}) collective-permute-start(bf16[2,4096]{1,0:T(2,128)(2,1)S(1)} %multiply_convert_fusion), channel_id=1, source_target_pairs={{0,0},{1,128},{2,2},{3,130},{4,4},{5,132},{6,6},{7,134},{8,8},{9,1... | collective-permute-start | bytes 49160 | tf_op jit(solution)/shard_map/ppermute | solution.py:63
  189.5 1.4 collective-permute-start.9
  190.1 3.0 %copy-start.5 = (bf16[8192,128]{1,0:T(8,128)(2,1)S(1)}, bf16[8192,128]{1,0:T(8,128)(2,1)}, u32[]{:S(2)}) copy-start(bf16[8192,128]{1,0:T(8,128)(2,1)} %param.12) | copy-start | bytes 6291460
  191.3 3.0 %copy-start.2 = (bf16[8192,256]{1,0:T(8,128)(2,1)S(1)}, bf16[8192,256]{1,0:T(8,128)(2,1)}, u32[]{:S(2)}) copy-start(bf16[8192,256]{1,0:T(8,128)(2,1)} %maximum_select_fusion) | copy-start | bytes 12582916

commit v11 on v10

--- a/solution.py
+++ b/solution.py
@@ -201,7 +201,9 @@
     own_rows, centred_full = lax.optimization_barrier((my_error, centred_full))
     owned_error = core_and_section(own_rows)
     error = spread(error_rows, NEAR_GROUPS, NEAR)
-    error, centred_full = lax.optimization_barrier((error, centred_full))
+    error, centred_full, owned_error = lax.optimization_barrier(
+        (error, centred_full, owned_error)
+    )
     step_size = STEP_RATE / tokens
 
     def stepped(weight, grad):
@@ -218,13 +220,12 @@
     )
     back_half = other_core(stepped(decoder_other, matmul(latents_other, error)))
     kept_half = stepped(decoder_own, matmul(latents, error))
+    new_encoder = stepped(encoder, matmul(centred_full, pre_grad, over_features))
     new_decoder = jnp.where(
         core == 0,
         jnp.concatenate([kept_half, back_half], axis=1),
         jnp.concatenate([back_half, kept_half], axis=1),
     )
-    pre_grad, _ = lax.optimization_barrier((pre_grad, new_decoder))
-    new_encoder = stepped(encoder, matmul(centred_full, pre_grad, over_features))
     return (owned_error, new_encoder, new_decoder)
 
 

time: 198 us -> 195 us (0.985)
  waiting for transfers between devices: 18.8 us -> 14 us
    all_to_all x2, waiting for transfers between devices: 10.8 us -> 6.14 us  [all_to_all(): lax.all_to_all(pieces, AXES, 0, 0, axis_index_groups=groups, tiled=True)]
  transfers between devices with their start and end apart: 13 -> 13, of which waited for: 9 -> 8; matrix products, arithmetic and copies ran while one was open for 9% -> 11% of each run, Pallas kernels for 0% -> 0%
where the time goes in v11:
time: 195 us; the launch traced here: 194 us
  blocking collectives  104 us (53%)
  starting transfers between devices  31.1 us (16%)
  matrix products  18.9 us (10%)
  local copies, waits for them, and re-layouts  15.7 us (8%)
  waiting for transfers between devices  14 us (7%)
  other arithmetic  9.44 us (5%)
    all_to_all x6, blocking collectives, all_to_all(): lax.all_to_all(pieces, AXES, 0, 0, axis_index_groups=groups, tiled=True)  104 us
    dot_general x16, matrix products, matmul(): lax.dot_general(a, b, (dims, ((), ())), preferred_element_type=jnp.float3...  18.9 us
    ppermute x11, starting transfers between devices, exchange(): return lax.ppermute(value, AXES, route)  18 us
    all_to_all x2, starting transfers between devices, all_to_all(): lax.all_to_all(pieces, AXES, 0, 0, axis_index_groups=groups, tiled=True)  13.1 us
    ppermute x11, waiting for transfers between devices, exchange(): return lax.ppermute(value, AXES, route)  7.86 us
    all_to_all x2, waiting for transfers between devices, all_to_all(): lax.all_to_all(pieces, AXES, 0, 0, axis_index_groups=groups, tiled=True)  6.14 us
    unnamed x34, local copies, waits for them, and re-layouts  4.35 us
    optimization_barrier x1, local copies, waits for them, and re-layouts, shards(): later, _ = lax.optimization_barrier((centred, error_rows))  4.06 us
  transfers between devices with their start and end apart: 13, of which 8 were waited for; matrix products, arithmetic and copies ran while one was open for 11% of the time, Pallas kernels for 0%

profile of v11, /device:TPU:1, one launch (start us, length us, event | category | flops | bytes accessed | tf_op | source)
XLA Modules:
  0.0 194.4 jit_solution(1020386953779010551)
XLA Ops:
  2.5 1.7 convolution_convert_fusion.5
  4.9 3.3 %collective-permute-start = (bf16[256,192]{0,1:T(8,128)(2,1)S(1)}, bf16[256,192]{0,1:T(8,128)(2,1)S(1)}, u32[]{:S(2)}, u32[]{:S(2)}) collective-permute-start(bf16[256,192]{0,1:T(8,128)(2,1)S(1)} %convolution_convert_fusion.5), channel_id=1, source_target_pairs={{0,1},{1,0},{2,3},{3,2},{4,5},{5,4},{6,7},{7,6},{8,9},{9,8},{10,11... | collective-permute-start | bytes 294920 | tf_op jit(solution)/shard_map/ppermute | solution.py:63
  8.2 1.2 dynamic-slice_bitcast_fusion.1
  10.5 2.1 %collective-permute-done.1 = bf16[128,4096]{1,0:T(8,128)(2,1)S(1)} collective-permute-done((bf16[128,4096]{1,0:T(8,128)(2,1)}, bf16[128,4096]{1,0:T(8,128)(2,1)S(1)}, u32[]{:S(2)}, u32[]{:S(2)}) %collective-permute-start.1) | collective-permute-done | bytes 1048608 | tf_op jit(solution)/shard_map/ppermute | solution.py:63
  12.6 2.4 %convolution_convert_fusion.2 = bf16[256,4096]{1,0:T(8,128)(2,1)} fusion(bf16[64,4096]{1,0:T(8,128)(2,1)S(1)} %get-tuple-element.46, bf16[128,4096]{1,0:T(8,128)(2,1)S(1)} %collective-permute-done.1, bf16[64,4096]{1,0:T(8,128)(2,1)S(1)} %get-tuple-element.45, bf16[128,4096]{1,0:T(8,128)(2,1)S(1)} %get-tuple-element.39, ...), kind=kOutput, calls=%fused_computation.5 | convolution fusion | flops 819331072 | bytes 5439488 | tf_op jit(solution)/shard_map/dot_general | solution.py:75
  15.1 8.2 %all-to-all-start = ((bf16[8,32,4096]{2,1,0:T(8,128)(2,1)}), bf16[8,32,4096]{2,1,0:T(8,128)(2,1)}, u32[]{:S(2)}, u32[]{:S(2)}) async-start(bf16[8,32,4096]{2,1,0:T(8,128)(2,1)} %bitcast.49), calls=%async_computation | async-start | bytes 4194304 | tf_op jit(solution)/shard_map/all_to_all | solution.py:81
  23.3 1.2 constant_dynamic-slice_fusion
  25.3 1.1 constant_dynamic-slice_fusion.3
  28.1 1.3 collective-permute-done.2
  29.4 2.8 %pad_maximum_fusion = bf16[4096,256]{1,0:T(8,128)(2,1)} fusion(bf16[4096,128]{1,0:T(8,128)(2,1)} %collective-permute-done.2, bf16[4096,128]{1,0:T(8,128)(2,1)S(1)} %get-tuple-element.37), kind=kLoop, calls=%fused_computation.22 | loop fusion | flops 4194304 | bytes 4194304 | tf_op jit(solution)/shard_map/concatenate | solution.py:161
  32.3 6.1 %all-to-all-done = bf16[8,32,4096]{2,1,0:T(8,128)(2,1)} async-done(((bf16[8,32,4096]{2,1,0:T(8,128)(2,1)}), bf16[8,32,4096]{2,1,0:T(8,128)(2,1)}, u32[]{:S(2)}, u32[]{:S(2)}) %all-to-all-start) | async-done | bytes 2097184 | tf_op jit(solution)/shard_map/all_to_all | solution.py:81
  38.5 2.0 %convolution_convert_fusion.4 = bf16[32,4096]{1,0:T(8,128)(2,1)S(1)} fusion(bf16[256,4096]{1,0:T(8,128)(2,1)} %bitcast.4, s32[256]{0:T(256)S(1)} %get-tuple-element.51, s32[256]{0:T(256)S(1)} %get-tuple-element.52, pred[256]{0:T(512)(128)(4,1)S(1)} %compare_and_fusion.2), kind=kOutput, calls=%fused_computation.13 | convolution fusion | flops 67256320 | bytes 2361600 | tf_op jit(solution)/shard_map/dot_general | solution.py:75
  40.7 18.1 %all_to_all.40 = bf16[16,2,4096]{2,1,0:T(2,128)(2,1)S(1)} all-to-all(bf16[16,2,4096]{2,1,0:T(2,128)(2,1)S(1)} %reshape.126), channel_id=1, replica_groups={{0,8,16,24,32,40,48,56,64,72,80,88,96,104,112,120},{4,12,20,28,36,44,52..., dimensions={0} | all-to-all | bytes 524288 | tf_op jit(solution)/shard_map/all_to_all | solution.py:81
  59.2 2.1 %collective-permute-start.4 = (f32[2,1]{0,1:T(1,128)S(1)}, f32[2,1]{0,1:T(1,128)S(1)}, u32[]{:S(2)}, u32[]{:S(2)}) collective-permute-start(f32[2,1]{0,1:T(1,128)S(1)} %bitcast.50), channel_id=1, source_target_pairs={{0,1},{1,0},{2,3},{3,2},{4,5},{5,4},{6,7},{7,6},{8,9},{9,8},{10,11... | collective-permute-start | bytes 32 | tf_op jit(solution)/shard_map/ppermute | solution.py:63
  62.4 14.7 %all_to_all.41 = bf16[16,2,4096]{2,1,0:T(2,128)(2,1)S(1)} all-to-all(bf16[16,2,4096]{2,1,0:T(2,128)(2,1)S(1)} %broadcast_in_dim.57), channel_id=1, replica_groups={{0,8,16,24,32,40,48,56,64,72,80,88,96,104,112,120},{4,12,20,28,36,44,52..., dimensions={0} | all-to-all | bytes 524288 | tf_op jit(solution)/shard_map/all_to_all | solution.py:81
  77.5 21.2 %all_to_all.42 = bf16[8,32,4096]{2,1,0:T(8,128)(2,1)S(1)} all-to-all(bf16[8,32,4096]{2,1,0:T(8,128)(2,1)S(1)} %broadcast_in_dim.59), channel_id=1, replica_groups={{0,4,128,132,2,6,130,134},{8,12,136,140,10,14,138,142},{16,20,144,148,1..., dimensions={0} | all-to-all | bytes 4194304 | tf_op jit(solution)/shard_map/all_to_all | solution.py:81
  100.0 3.2 %collective-permute-start.5 = (f32[128,256]{1,0:T(8,128)S(1)}, f32[128,256]{1,0:T(8,128)S(1)}, u32[]{:S(2)}, u32[]{:S(2)}) collective-permute-start(f32[128,256]{1,0:T(8,128)S(1)} %slice.17), channel_id=1, source_target_pairs={{0,1},{1,0},{2,3},{3,2},{4,5},{5,4},{6,7},{7,6},{8,9},{9,8},{10,11... | collective-permute-start | bytes 393224 | tf_op jit(solution)/shard_map/ppermute | solution.py:63
  106.8 19.6 %all_to_all.43 = bf16[8,32,4096]{2,1,0:T(8,128)(2,1)S(1)} all-to-all(bf16[8,32,4096]{2,1,0:T(8,128)(2,1)S(1)} %bitcast.47), channel_id=1, replica_groups={{0,4,128,132,2,6,130,134},{8,12,136,140,10,14,138,142},{16,20,144,148,1..., dimensions={0} | all-to-all | bytes 4194304 | tf_op jit(solution)/shard_map/all_to_all | solution.py:81
  127.1 13.7 %all_to_all.44 = bf16[16,2,4096]{2,1,0:T(2,128)(2,1)S(1)} all-to-all(bf16[16,2,4096]{2,1,0:T(2,128)(2,1)S(1)} %reshape.130), channel_id=1, replica_groups={{0,8,16,24,32,40,48,56,64,72,80,88,96,104,112,120},{4,12,20,28,36,44,52..., dimensions={0} | all-to-all | bytes 524288 | tf_op jit(solution)/shard_map/all_to_all | solution.py:81
  141.2 17.0 %all_to_all.45 = bf16[16,2,4096]{2,1,0:T(2,128)(2,1)S(1)} all-to-all(bf16[16,2,4096]{2,1,0:T(2,128)(2,1)S(1)} %broadcast_in_dim.60), channel_id=1, replica_groups={{0,8,16,24,32,40,48,56,64,72,80,88,96,104,112,120},{4,12,20,28,36,44,52..., dimensions={0} | all-to-all | bytes 524288 | tf_op jit(solution)/shard_map/all_to_all | solution.py:81
  158.3 1.6 broadcast_in_dim.62
  160.0 4.9 %all-to-all-start.7 = ((bf16[8,32,4096]{2,1,0:T(8,128)(2,1)}), bf16[8,32,4096]{2,1,0:T(8,128)(2,1)S(1)}, u32[]{:S(2)}, u32[]{:S(2)}) async-start(bf16[8,32,4096]{2,1,0:T(8,128)(2,1)} %broadcast_in_dim.62), calls=%async_computation.7 | async-start | bytes 4194304 | tf_op jit(solution)/shard_map/all_to_all | solution.py:81
  164.9 1.3 collective-permute-start.7
  166.2 4.1 %copy.15 = bf16[256,4096]{0,1:T(8,128)(2,1)} copy(bf16[256,4096]{1,0:T(8,128)(2,1)} %bitcast.45) | data formatting | bytes 4194304 | tf_op jit(solution)/shard_map/optimization_barrier | solution.py:191
  170.3 2.5 %convolution_convert_fusion = bf16[4096,256]{1,0:T(8,128)(2,1)S(1)} fusion(bf16[256,4096]{1,0:T(8,128)(2,1)} %collective-permute-done.7, pred[256,256]{1,0:T(32,128)(4,1)S(1)} %fusion.61), kind=kOutput, calls=%fused_computation.3 | convolution fusion | flops 537919488 | bytes 4259840 | tf_op jit(solution)/shard_map/dot_general | solution.py:75
  172.8 2.6 %maximum_select_fusion = bf16[8192,256]{1,0:T(8,128)(2,1)} fusion(bf16[4096,256]{1,0:T(8,128)(2,1)S(1)} %convolution_convert_fusion, bf16[4096,256]{1,0:T(8,128)(2,1)S(1)} %bitcast.48, pred[]{:T(512)S(6)} %eq.86), kind=kLoop, calls=%fused_computation.14 | loop fusion | flops 18874368 | bytes 8388609 | tf_op jit(solution)/shard_map/jit(_where)/select_n | solution.py:196
  175.4 4.0 %collective-permute-start.8 = (bf16[2,4096]{1,0:T(2,128)(2,1)S(1)}, bf16[2,4096]{1,0:T(2,128)(2,1)S(1)}, u32[]{:S(2)}, u32[]{:S(2)}) collective-permute-start(bf16[2,4096]{1,0:T(2,128)(2,1)S(1)} %multiply_convert_fusion), channel_id=1, source_target_pairs={{0,0},{1,128},{2,2},{3,130},{4,4},{5,132},{6,6},{7,134},{8,8},{9,1... | collective-permute-start | bytes 49160 | tf_op jit(solution)/shard_map/ppermute | solution.py:63
  179.4 1.7 collective-permute-done.8
  181.1 2.2 %fusion.18 = f32[128,256]{1,0:T(8,128)S(1)} fusion(bf16[256,4096]{1,0:T(8,128)(2,1)S(1)} %bitcast.39, bf16[256,4096]{1,0:T(8,128)(2,1)} %copy-done), kind=kOutput, calls=%fused_computation.39 | convolution fusion | flops 268435456 | bytes 3276800 | tf_op jit(solution)/shard_map/dot_general | solution.py:75
  183.3 2.4 %collective-permute-start.9 = (f32[128,256]{1,0:T(8,128)S(1)}, f32[128,256]{1,0:T(8,128)S(1)}, u32[]{:S(2)}, u32[]{:S(2)}) collective-permute-start(f32[128,256]{1,0:T(8,128)S(1)} %fusion.18), channel_id=1, source_target_pairs={{0,1},{1,0},{2,3},{3,2},{4,5},{5,4},{6,7},{7,6},{8,9},{9,8},{10,11... | collective-permute-start | bytes 393224 | tf_op jit(solution)/shard_map/ppermute | solution.py:63
  189.4 2.6 %fusion.1 = bf16[8192,128]{1,0:T(8,128)(2,1)} fusion(bf16[8192,256]{1,0:T(8,128)(2,1)S(1)} %copy-done.2, bf16[128,256]{1,0:T(8,128)(2,1)S(1)} %select_convert_fusion, bf16[8192,128]{1,0:T(8,128)(2,1)S(1)} %copy-done.5), kind=kOutput, calls=%fused_computation.2 | convolution fusion | flops 541065216 | bytes 8454144 | tf_op jit(solution)/shard_map/dot_general | solution.py:75
  191.9 1.8 maximum_select_fusion.1
  (90 shorter events, 18.8 us)
Async XLA Ops:
  2.4 1.7 copy-start.14
  4.1 4.1 %copy-start.8 = (bf16[1,128,8192]{2,1,0:T(8,128)(2,1)S(1)}, bf16[1,128,8192]{2,1,0:T(8,128)(2,1)}, u32[]{:S(2)}) copy-start(bf16[1,128,8192]{2,1,0:T(8,128)(2,1)} %param.11) | copy-start | bytes 6291460
  4.9 5.6 %collective-permute-start = (bf16[256,192]{0,1:T(8,128)(2,1)S(1)}, bf16[256,192]{0,1:T(8,128)(2,1)S(1)}, u32[]{:S(2)}, u32[]{:S(2)}) collective-permute-start(bf16[256,192]{0,1:T(8,128)(2,1)S(1)} %convolution_convert_fusion.5), channel_id=1, source_target_pairs={{0,1},{1,0},{2,3},{3,2},{4,5},{5,4},{6,7},{7,6},{8,9},{9,8},{10,11... | collective-permute-start | bytes 294920 | tf_op jit(solution)/shard_map/ppermute | solution.py:63
  9.4 3.2 %collective-permute-start.1 = (bf16[128,4096]{1,0:T(8,128)(2,1)}, bf16[128,4096]{1,0:T(8,128)(2,1)S(1)}, u32[]{:S(2)}, u32[]{:S(2)}) collective-permute-start(bf16[128,4096]{1,0:T(8,128)(2,1)} %get-tuple-element.40), channel_id=1, source_target_pairs={{0,1},{1,0},{2,3},{3,2},{4,5},{5,4},{6,7},{7,6},{8,9},{9,8},{10,11... | collective-permute-start | bytes 3145736 | tf_op jit(solution)/shard_map/ppermute | solution.py:63
  15.0 8.2 %copy-start.12 = (s32[256]{0:T(256)S(1)}, s32[256]{0:T(256)}, u32[]{:S(2)}) copy-start(s32[256]{0:T(256)} %param.16) | copy-start | bytes 3076
  15.1 8.2 %copy-start.9 = (bf16[128,8192]{1,0:T(8,128)(2,1)S(1)}, bf16[128,8192]{1,0:T(8,128)(2,1)}, u32[]{:S(2)}) copy-start(bf16[128,8192]{1,0:T(8,128)(2,1)} %param.14) | copy-start | bytes 6291460
  15.1 23.4 %all-to-all-start = ((bf16[8,32,4096]{2,1,0:T(8,128)(2,1)}), bf16[8,32,4096]{2,1,0:T(8,128)(2,1)}, u32[]{:S(2)}, u32[]{:S(2)}) async-start(bf16[8,32,4096]{2,1,0:T(8,128)(2,1)} %bitcast.49), calls=%async_computation | async-start | bytes 4194304 | tf_op jit(solution)/shard_map/all_to_all | solution.py:81
  23.3 2.0 %copy-start.4 = (bf16[8192,128]{1,0:T(8,128)(2,1)S(1)}, bf16[8192,128]{1,0:T(8,128)(2,1)}, u32[]{:S(2)}) copy-start(bf16[8192,128]{1,0:T(8,128)(2,1)} %param.12) | copy-start | bytes 6291460
  25.3 1.3 copy-start.11
  25.3 1.3 copy-start.13
  25.3 1.6 copy-start.10
  26.4 3.0 %collective-permute-start.2 = (bf16[4096,128]{1,0:T(8,128)(2,1)}, bf16[4096,128]{1,0:T(8,128)(2,1)}, u32[]{:S(2)}, u32[]{:S(2)}) collective-permute-start(bf16[4096,128]{1,0:T(8,128)(2,1)} %get-tuple-element.21), channel_id=1, source_target_pairs={{0,1},{1,0},{2,3},{3,2},{4,5},{5,4},{6,7},{7,6},{8,9},{9,8},{10,11... | collective-permute-start | bytes 3145736 | tf_op jit(solution)/shard_map/ppermute | solution.py:63
  26.9 5.3 %collective-permute-start.3 = (bf16[128,4096]{1,0:T(8,128)(2,1)S(1)}, bf16[128,4096]{1,0:T(8,128)(2,1)S(1)}, u32[]{:S(2)}, u32[]{:S(2)}) collective-permute-start(bf16[128,4096]{1,0:T(8,128)(2,1)S(1)} %copy-done.10), channel_id=1, source_target_pairs={{0,1},{1,0},{2,3},{3,2},{4,5},{5,4},{6,7},{7,6},{8,9},{9,8},{10,11... | collective-permute-start | bytes 3145736 | tf_op jit(solution)/shard_map/ppermute | solution.py:63
  32.3 73.7 %copy-start = (bf16[256,4096]{1,0:T(8,128)(2,1)}, bf16[256,4096]{1,0:T(8,128)(2,1)S(1)}, u32[]{:S(2)}) copy-start(bf16[256,4096]{1,0:T(8,128)(2,1)S(1)} %pad_maximum_fusion.1) | copy-start | bytes 6291460
  59.2 2.9 %collective-permute-start.4 = (f32[2,1]{0,1:T(1,128)S(1)}, f32[2,1]{0,1:T(1,128)S(1)}, u32[]{:S(2)}, u32[]{:S(2)}) collective-permute-start(f32[2,1]{0,1:T(1,128)S(1)} %bitcast.50), channel_id=1, source_target_pairs={{0,1},{1,0},{2,3},{3,2},{4,5},{5,4},{6,7},{7,6},{8,9},{9,8},{10,11... | collective-permute-start | bytes 32 | tf_op jit(solution)/shard_map/ppermute | solution.py:63
  77.5 21.2 %copy-start.6 = (bf16[4096,256]{1,0:T(8,128)(2,1)S(1)}, bf16[4096,256]{1,0:T(8,128)(2,1)}, u32[]{:S(2)}) copy-start(bf16[4096,256]{1,0:T(8,128)(2,1)} %pad_maximum_fusion) | copy-start | bytes 6291460
  98.7 1.3 copy-start.3
  98.7 4.5 %copy-start.15 = (bf16[128]{0:T(256)(128)(2,1)S(1)}, bf16[128]{0:T(256)(128)(2,1)}, u32[]{:S(2)}) copy-start(bf16[128]{0:T(256)(128)(2,1)} %param.13) | copy-start | bytes 772
  100.0 4.2 %collective-permute-start.5 = (f32[128,256]{1,0:T(8,128)S(1)}, f32[128,256]{1,0:T(8,128)S(1)}, u32[]{:S(2)}, u32[]{:S(2)}) collective-permute-start(f32[128,256]{1,0:T(8,128)S(1)} %slice.17), channel_id=1, source_target_pairs={{0,1},{1,0},{2,3},{3,2},{4,5},{5,4},{6,7},{7,6},{8,9},{9,8},{10,11... | collective-permute-start | bytes 393224 | tf_op jit(solution)/shard_map/ppermute | solution.py:63
  104.5 1.4 collective-permute-start.6
  160.0 21.1 %all-to-all-start.7 = ((bf16[8,32,4096]{2,1,0:T(8,128)(2,1)}), bf16[8,32,4096]{2,1,0:T(8,128)(2,1)S(1)}, u32[]{:S(2)}, u32[]{:S(2)}) async-start(bf16[8,32,4096]{2,1,0:T(8,128)(2,1)} %broadcast_in_dim.62), calls=%async_computation.7 | async-start | bytes 4194304 | tf_op jit(solution)/shard_map/all_to_all | solution.py:81
  164.9 5.5 %collective-permute-start.7 = (bf16[256,4096]{1,0:T(8,128)(2,1)}, bf16[256,4096]{1,0:T(8,128)(2,1)}, u32[]{:S(2)}, u32[]{:S(2)}) collective-permute-start(bf16[256,4096]{1,0:T(8,128)(2,1)} %bitcast.44), channel_id=1, source_target_pairs={{0,1},{1,0},{2,3},{3,2},{4,5},{5,4},{6,7},{7,6},{8,9},{9,8},{10,11... | collective-permute-start | bytes 6291464 | tf_op jit(solution)/shard_map/ppermute | solution.py:63
  170.3 2.6 %copy-start.7 = (bf16[256,4096]{0,1:T(8,128)(2,1)S(1)}, bf16[256,4096]{0,1:T(8,128)(2,1)}, u32[]{:S(2)}) copy-start(bf16[256,4096]{0,1:T(8,128)(2,1)} %copy.15) | copy-start | bytes 6291460
  175.4 5.7 %collective-permute-start.8 = (bf16[2,4096]{1,0:T(2,128)(2,1)S(1)}, bf16[2,4096]{1,0:T(2,128)(2,1)S(1)}, u32[]{:S(2)}, u32[]{:S(2)}) collective-permute-start(bf16[2,4096]{1,0:T(2,128)(2,1)S(1)} %multiply_convert_fusion), channel_id=1, source_target_pairs={{0,0},{1,128},{2,2},{3,130},{4,4},{5,132},{6,6},{7,134},{8,8},{9,1... | collective-permute-start | bytes 49160 | tf_op jit(solution)/shard_map/ppermute | solution.py:63
  181.1 4.6 %copy-start.1 = (bf16[256,4096]{1,0:T(8,128)(2,1)S(1)}, bf16[256,4096]{1,0:T(8,128)(2,1)}, u32[]{:S(2)}) copy-start(bf16[256,4096]{1,0:T(8,128)(2,1)} %copy-done) | copy-start | bytes 6291460
  183.3 4.5 %collective-permute-start.9 = (f32[128,256]{1,0:T(8,128)S(1)}, f32[128,256]{1,0:T(8,128)S(1)}, u32[]{:S(2)}, u32[]{:S(2)}) collective-permute-start(f32[128,256]{1,0:T(8,128)S(1)} %fusion.18), channel_id=1, source_target_pairs={{0,1},{1,0},{2,3},{3,2},{4,5},{5,4},{6,7},{7,6},{8,9},{9,8},{10,11... | collective-permute-start | bytes 393224 | tf_op jit(solution)/shard_map/ppermute | solution.py:63
  186.2 5.7 %collective-permute-start.10 = (bf16[128,4096]{1,0:T(8,128)(2,1)S(1)}, bf16[128,4096]{1,0:T(8,128)(2,1)S(1)}, u32[]{:S(2)}, u32[]{:S(2)}) collective-permute-start(bf16[128,4096]{1,0:T(8,128)(2,1)S(1)} %fusion.5), channel_id=1, source_target_pairs={{0,1},{1,0},{2,3},{3,2},{4,5},{5,4},{6,7},{7,6},{8,9},{9,8},{10,11... | collective-permute-start | bytes 3145736 | tf_op jit(solution)/shard_map/ppermute | solution.py:63
  186.4 2.2 %copy-start.2 = (bf16[8192,256]{1,0:T(8,128)(2,1)S(1)}, bf16[8192,256]{1,0:T(8,128)(2,1)}, u32[]{:S(2)}) copy-start(bf16[8192,256]{1,0:T(8,128)(2,1)} %maximum_select_fusion) | copy-start | bytes 12582916
  186.9 2.4 %copy-start.5 = (bf16[8192,128]{1,0:T(8,128)(2,1)S(1)}, bf16[8192,128]{1,0:T(8,128)(2,1)}, u32[]{:S(2)}) copy-start(bf16[8192,128]{1,0:T(8,128)(2,1)} %param.12) | copy-start | bytes 6291460

commit v12 on v10

--- a/solution.py
+++ b/solution.py
@@ -218,13 +218,12 @@
     )
     back_half = other_core(stepped(decoder_other, matmul(latents_other, error)))
     kept_half = stepped(decoder_own, matmul(latents, error))
+    new_encoder = stepped(encoder, matmul(centred_full, pre_grad, over_features))
     new_decoder = jnp.where(
         core == 0,
         jnp.concatenate([kept_half, back_half], axis=1),
         jnp.concatenate([back_half, kept_half], axis=1),
     )
-    pre_grad, _ = lax.optimization_barrier((pre_grad, new_decoder))
-    new_encoder = stepped(encoder, matmul(centred_full, pre_grad, over_features))
     return (owned_error, new_encoder, new_decoder)
 
 

time: 198 us -> 193 us (0.975)
  waiting for transfers between devices: 18.8 us -> 13.3 us
    all_to_all x2, waiting for transfers between devices: 10.8 us -> 6.66 us  [all_to_all(): lax.all_to_all(pieces, AXES, 0, 0, axis_index_groups=groups, tiled=True)]
  transfers between devices with their start and end apart: 13 -> 13, of which waited for: 9 -> 8; matrix products, arithmetic and copies ran while one was open for 9% -> 11% of each run, Pallas kernels for 0% -> 0%
where the time goes in v12:
time: 193 us
  blocking collectives  105 us (54%)
  starting transfers between devices  30.1 us (16%)
  matrix products  19.4 us (10%)
  local copies, waits for them, and re-layouts  14.4 us (7%)
  waiting for transfers between devices  13.3 us (7%)
  other arithmetic  9.43 us (5%)
    all_to_all x6, blocking collectives, all_to_all(): lax.all_to_all(pieces, AXES, 0, 0, axis_index_groups=groups, tiled=True)  105 us
    dot_general x16, matrix products, matmul(): lax.dot_general(a, b, (dims, ((), ())), preferred_element_type=jnp.float3...  19.4 us
    ppermute x11, starting transfers between devices, exchange(): return lax.ppermute(value, AXES, route)  17.5 us
    all_to_all x2, starting transfers between devices, all_to_all(): lax.all_to_all(pieces, AXES, 0, 0, axis_index_groups=groups, tiled=True)  12.6 us
    all_to_all x2, waiting for transfers between devices, all_to_all(): lax.all_to_all(pieces, AXES, 0, 0, axis_index_groups=groups, tiled=True)  6.66 us
    ppermute x11, waiting for transfers between devices, exchange(): return lax.ppermute(value, AXES, route)  6.6 us
    optimization_barrier x1, local copies, waits for them, and re-layouts, shards(): later, _ = lax.optimization_barrier((centred, error_rows))  4.06 us
  transfers between devices with their start and end apart: 13, of which 8 were waited for; matrix products, arithmetic and copies ran while one was open for 11% of the time, Pallas kernels for 0%

profile of v12, /device:TPU:1, one launch (start us, length us, event | category | flops | bytes accessed | tf_op | source)
XLA Modules:
  0.0 192.6 jit_solution(13944715076013160582)
XLA Ops:
  0.7 1.7 dynamic-slice_bitcast_fusion.1
  2.4 3.3 %collective-permute-start.1 = (bf16[128,4096]{1,0:T(8,128)(2,1)S(1)}, bf16[128,4096]{1,0:T(8,128)(2,1)}, u32[]{:S(2)}, u32[]{:S(2)}) collective-permute-start(bf16[128,4096]{1,0:T(8,128)(2,1)S(1)} %get-tuple-element.38), channel_id=1, source_target_pairs={{0,1},{1,0},{2,3},{3,2},{4,5},{5,4},{6,7},{7,6},{8,9},{9,8},{10,11... | collective-permute-start | bytes 3145736 | tf_op jit(solution)/shard_map/ppermute | solution.py:63
  9.0 3.8 %convolution_convert_fusion.2 = bf16[256,4096]{1,0:T(8,128)(2,1)} fusion(bf16[64,4096]{1,0:T(8,128)(2,1)S(1)} %get-tuple-element.44, bf16[128,4096]{1,0:T(8,128)(2,1)} %collective-permute-done.1, bf16[64,4096]{1,0:T(8,128)(2,1)S(1)} %get-tuple-element.43, bf16[128,4096]{1,0:T(8,128)(2,1)S(1)} %get-tuple-element.37, ...), kind=kOutput, calls=%fused_computation.5 | convolution fusion | flops 819331072 | bytes 5439488 | tf_op jit(solution)/shard_map/dot_general | solution.py:75
  12.9 8.2 %all-to-all-start = ((bf16[8,32,4096]{2,1,0:T(8,128)(2,1)}), bf16[8,32,4096]{2,1,0:T(8,128)(2,1)}, u32[]{:S(2)}, u32[]{:S(2)}) async-start(bf16[8,32,4096]{2,1,0:T(8,128)(2,1)} %bitcast.49), calls=%async_computation | async-start | bytes 4194304 | tf_op jit(solution)/shard_map/all_to_all | solution.py:81
  21.1 1.5 constant_dynamic-slice_fusion.3
  22.6 0.9 copy-done.9
  25.4 1.3 collective-permute-done.2
  26.7 2.8 %pad_maximum_fusion = bf16[4096,256]{1,0:T(8,128)(2,1)} fusion(bf16[4096,128]{1,0:T(8,128)(2,1)} %collective-permute-done.2, bf16[4096,128]{1,0:T(8,128)(2,1)S(1)} %copy-done.8), kind=kLoop, calls=%fused_computation.22 | loop fusion | flops 4194304 | bytes 4194304 | tf_op jit(solution)/shard_map/concatenate | solution.py:161
  29.6 6.7 %all-to-all-done = bf16[8,32,4096]{2,1,0:T(8,128)(2,1)} async-done(((bf16[8,32,4096]{2,1,0:T(8,128)(2,1)}), bf16[8,32,4096]{2,1,0:T(8,128)(2,1)}, u32[]{:S(2)}, u32[]{:S(2)}) %all-to-all-start) | async-done | bytes 2097184 | tf_op jit(solution)/shard_map/all_to_all | solution.py:81
  36.3 2.0 %convolution_convert_fusion.4 = bf16[32,4096]{1,0:T(8,128)(2,1)S(1)} fusion(bf16[256,4096]{1,0:T(8,128)(2,1)} %bitcast.4, s32[256]{0:T(256)S(1)} %get-tuple-element.49, s32[256]{0:T(256)S(1)} %get-tuple-element.50, pred[256]{0:T(512)(128)(4,1)S(1)} %compare_and_fusion.2), kind=kOutput, calls=%fused_computation.13 | convolution fusion | flops 67256320 | bytes 2361600 | tf_op jit(solution)/shard_map/dot_general | solution.py:75
  38.5 18.1 %all_to_all.40 = bf16[16,2,4096]{2,1,0:T(2,128)(2,1)S(1)} all-to-all(bf16[16,2,4096]{2,1,0:T(2,128)(2,1)S(1)} %reshape.126), channel_id=1, replica_groups={{0,8,16,24,32,40,48,56,64,72,80,88,96,104,112,120},{4,12,20,28,36,44,52..., dimensions={0} | all-to-all | bytes 524288 | tf_op jit(solution)/shard_map/all_to_all | solution.py:81
  57.0 1.9 %collective-permute-start.4 = (f32[2,1]{0,1:T(1,128)S(1)}, f32[2,1]{0,1:T(1,128)S(1)}, u32[]{:S(2)}, u32[]{:S(2)}) collective-permute-start(f32[2,1]{0,1:T(1,128)S(1)} %bitcast.50), channel_id=1, source_target_pairs={{0,1},{1,0},{2,3},{3,2},{4,5},{5,4},{6,7},{7,6},{8,9},{9,8},{10,11... | collective-permute-start | bytes 32 | tf_op jit(solution)/shard_map/ppermute | solution.py:63
  60.0 15.1 %all_to_all.41 = bf16[16,2,4096]{2,1,0:T(2,128)(2,1)S(1)} all-to-all(bf16[16,2,4096]{2,1,0:T(2,128)(2,1)S(1)} %broadcast_in_dim.57), channel_id=1, replica_groups={{0,8,16,24,32,40,48,56,64,72,80,88,96,104,112,120},{4,12,20,28,36,44,52..., dimensions={0} | all-to-all | bytes 524288 | tf_op jit(solution)/shard_map/all_to_all | solution.py:81
  75.5 21.2 %all_to_all.42 = bf16[8,32,4096]{2,1,0:T(8,128)(2,1)S(1)} all-to-all(bf16[8,32,4096]{2,1,0:T(8,128)(2,1)S(1)} %broadcast_in_dim.59), channel_id=1, replica_groups={{0,4,128,132,2,6,130,134},{8,12,136,140,10,14,138,142},{16,20,144,148,1..., dimensions={0} | all-to-all | bytes 4194304 | tf_op jit(solution)/shard_map/all_to_all | solution.py:81
  98.0 2.7 %collective-permute-start.5 = (f32[128,256]{1,0:T(8,128)S(1)}, f32[128,256]{1,0:T(8,128)S(1)}, u32[]{:S(2)}, u32[]{:S(2)}) collective-permute-start(f32[128,256]{1,0:T(8,128)S(1)} %slice.17), channel_id=1, source_target_pairs={{0,1},{1,0},{2,3},{3,2},{4,5},{5,4},{6,7},{7,6},{8,9},{9,8},{10,11... | collective-permute-start | bytes 393224 | tf_op jit(solution)/shard_map/ppermute | solution.py:63
  100.7 1.0 collective-permute-done.5
  102.6 0.9 collective-permute-done.6
  104.5 19.7 %all_to_all.43 = bf16[8,32,4096]{2,1,0:T(8,128)(2,1)S(1)} all-to-all(bf16[8,32,4096]{2,1,0:T(8,128)(2,1)S(1)} %bitcast.47), channel_id=1, replica_groups={{0,4,128,132,2,6,130,134},{8,12,136,140,10,14,138,142},{16,20,144,148,1..., dimensions={0} | all-to-all | bytes 4194304 | tf_op jit(solution)/shard_map/all_to_all | solution.py:81
  124.8 13.0 %all_to_all.44 = bf16[16,2,4096]{2,1,0:T(2,128)(2,1)S(1)} all-to-all(bf16[16,2,4096]{2,1,0:T(2,128)(2,1)S(1)} %reshape.130), channel_id=1, replica_groups={{0,8,16,24,32,40,48,56,64,72,80,88,96,104,112,120},{4,12,20,28,36,44,52..., dimensions={0} | all-to-all | bytes 524288 | tf_op jit(solution)/shard_map/all_to_all | solution.py:81
  138.3 18.0 %all_to_all.45 = bf16[16,2,4096]{2,1,0:T(2,128)(2,1)S(1)} all-to-all(bf16[16,2,4096]{2,1,0:T(2,128)(2,1)S(1)} %broadcast_in_dim.60), channel_id=1, replica_groups={{0,8,16,24,32,40,48,56,64,72,80,88,96,104,112,120},{4,12,20,28,36,44,52..., dimensions={0} | all-to-all | bytes 524288 | tf_op jit(solution)/shard_map/all_to_all | solution.py:81
  156.4 1.6 broadcast_in_dim.62
  158.1 4.4 %all-to-all-start.7 = ((bf16[8,32,4096]{2,1,0:T(8,128)(2,1)}), bf16[8,32,4096]{2,1,0:T(8,128)(2,1)S(1)}, u32[]{:S(2)}, u32[]{:S(2)}) async-start(bf16[8,32,4096]{2,1,0:T(8,128)(2,1)} %broadcast_in_dim.62), calls=%async_computation.7 | async-start | bytes 4194304 | tf_op jit(solution)/shard_map/all_to_all | solution.py:81
  162.5 1.9 collective-permute-start.7
  164.4 4.1 %copy.15 = bf16[256,4096]{0,1:T(8,128)(2,1)} copy(bf16[256,4096]{1,0:T(8,128)(2,1)} %bitcast.45) | data formatting | bytes 4194304 | tf_op jit(solution)/shard_map/optimization_barrier | solution.py:191
  168.5 2.5 %convolution_convert_fusion = bf16[4096,256]{1,0:T(8,128)(2,1)S(1)} fusion(bf16[256,4096]{1,0:T(8,128)(2,1)} %collective-permute-done.7, pred[256,256]{1,0:T(32,128)(4,1)S(1)} %fusion.61), kind=kOutput, calls=%fused_computation.3 | convolution fusion | flops 537919488 | bytes 4259840 | tf_op jit(solution)/shard_map/dot_general | solution.py:75
  171.0 2.6 %maximum_select_fusion = bf16[8192,256]{1,0:T(8,128)(2,1)} fusion(bf16[4096,256]{1,0:T(8,128)(2,1)S(1)} %convolution_convert_fusion, bf16[4096,256]{1,0:T(8,128)(2,1)S(1)} %bitcast.48, pred[]{:T(512)S(6)} %eq.86), kind=kLoop, calls=%fused_computation.14 | loop fusion | flops 18874368 | bytes 8388609 | tf_op jit(solution)/shard_map/jit(_where)/select_n | solution.py:196
  173.6 4.0 %collective-permute-start.8 = (bf16[2,4096]{1,0:T(2,128)(2,1)S(1)}, bf16[2,4096]{1,0:T(2,128)(2,1)S(1)}, u32[]{:S(2)}, u32[]{:S(2)}) collective-permute-start(bf16[2,4096]{1,0:T(2,128)(2,1)S(1)} %multiply_convert_fusion), channel_id=1, source_target_pairs={{0,0},{1,128},{2,2},{3,130},{4,4},{5,132},{6,6},{7,134},{8,8},{9,1... | collective-permute-start | bytes 49160 | tf_op jit(solution)/shard_map/ppermute | solution.py:63
  177.6 1.7 collective-permute-done.8
  179.3 2.2 %fusion.18 = f32[128,256]{1,0:T(8,128)S(1)} fusion(bf16[256,4096]{1,0:T(8,128)(2,1)S(1)} %bitcast.39, bf16[256,4096]{1,0:T(8,128)(2,1)} %copy-done), kind=kOutput, calls=%fused_computation.39 | convolution fusion | flops 268435456 | bytes 3276800 | tf_op jit(solution)/shard_map/dot_general | solution.py:75
  181.5 2.4 %collective-permute-start.9 = (f32[128,256]{1,0:T(8,128)S(1)}, f32[128,256]{1,0:T(8,128)S(1)}, u32[]{:S(2)}, u32[]{:S(2)}) collective-permute-start(f32[128,256]{1,0:T(8,128)S(1)} %fusion.18), channel_id=1, source_target_pairs={{0,1},{1,0},{2,3},{3,2},{4,5},{5,4},{6,7},{7,6},{8,9},{9,8},{10,11... | collective-permute-start | bytes 393224 | tf_op jit(solution)/shard_map/ppermute | solution.py:63
  187.6 2.6 %fusion.1 = bf16[8192,128]{1,0:T(8,128)(2,1)} fusion(bf16[8192,256]{1,0:T(8,128)(2,1)S(1)} %copy-done.2, bf16[128,256]{1,0:T(8,128)(2,1)S(1)} %select_convert_fusion, bf16[8192,128]{1,0:T(8,128)(2,1)S(1)} %copy-done.5), kind=kOutput, calls=%fused_computation.2 | convolution fusion | flops 541065216 | bytes 8454144 | tf_op jit(solution)/shard_map/dot_general | solution.py:75
  190.1 1.8 maximum_select_fusion.1
  (90 shorter events, 16.0 us)
Async XLA Ops:
  0.6 5.1 %copy-start.13 = (s32[128]{0:T(128)S(1)}, s32[128]{0:T(128)}, u32[]{:S(2)}) copy-start(s32[128]{0:T(128)} %param.17) | copy-start | bytes 1540
  0.7 5.3 %copy-start.10 = (bf16[256,64]{0,1:T(8,128)(2,1)S(1)}, bf16[256,64]{0,1:T(8,128)(2,1)}, u32[]{:S(2)}) copy-start(bf16[256,64]{0,1:T(8,128)(2,1)} %param.9) | copy-start | bytes 98308
  0.7 5.4 %copy-start.14 = (bf16[1,256,128]{2,1,0:T(8,128)(2,1)S(1)}, bf16[1,256,128]{2,1,0:T(8,128)(2,1)}, u32[]{:S(2)}) copy-start(bf16[1,256,128]{2,1,0:T(8,128)(2,1)} %param.10) | copy-start | bytes 196612
  2.4 6.7 %collective-permute-start.1 = (bf16[128,4096]{1,0:T(8,128)(2,1)S(1)}, bf16[128,4096]{1,0:T(8,128)(2,1)}, u32[]{:S(2)}, u32[]{:S(2)}) collective-permute-start(bf16[128,4096]{1,0:T(8,128)(2,1)S(1)} %get-tuple-element.38), channel_id=1, source_target_pairs={{0,1},{1,0},{2,3},{3,2},{4,5},{5,4},{6,7},{7,6},{8,9},{9,8},{10,11... | collective-permute-start | bytes 3145736 | tf_op jit(solution)/shard_map/ppermute | solution.py:63
  7.7 1.4 collective-permute-start
  12.9 8.2 %copy-start.12 = (s32[256]{0:T(256)S(1)}, s32[256]{0:T(256)}, u32[]{:S(2)}) copy-start(s32[256]{0:T(256)} %param.16) | copy-start | bytes 3076
  12.9 8.2 %copy-start.4 = (bf16[8192,128]{1,0:T(8,128)(2,1)S(1)}, bf16[8192,128]{1,0:T(8,128)(2,1)}, u32[]{:S(2)}) copy-start(bf16[8192,128]{1,0:T(8,128)(2,1)} %param.12) | copy-start | bytes 6291460
  12.9 23.4 %all-to-all-start = ((bf16[8,32,4096]{2,1,0:T(8,128)(2,1)}), bf16[8,32,4096]{2,1,0:T(8,128)(2,1)}, u32[]{:S(2)}, u32[]{:S(2)}) async-start(bf16[8,32,4096]{2,1,0:T(8,128)(2,1)} %bitcast.49), calls=%async_computation | async-start | bytes 4194304 | tf_op jit(solution)/shard_map/all_to_all | solution.py:81
  21.1 2.4 %copy-start.9 = (bf16[128,8192]{1,0:T(8,128)(2,1)S(1)}, bf16[128,8192]{1,0:T(8,128)(2,1)}, u32[]{:S(2)}) copy-start(bf16[128,8192]{1,0:T(8,128)(2,1)} %param.14) | copy-start | bytes 6291460
  23.5 0.7 copy-start.11
  23.5 3.2 %copy-start.8 = (bf16[4096,128]{1,0:T(8,128)(2,1)S(1)}, bf16[4096,128]{1,0:T(8,128)(2,1)}, u32[]{:S(2)}) copy-start(bf16[4096,128]{1,0:T(8,128)(2,1)} %get-tuple-element.35) | copy-start | bytes 3145732
  23.6 3.1 %collective-permute-start.2 = (bf16[4096,128]{1,0:T(8,128)(2,1)}, bf16[4096,128]{1,0:T(8,128)(2,1)}, u32[]{:S(2)}, u32[]{:S(2)}) collective-permute-start(bf16[4096,128]{1,0:T(8,128)(2,1)} %get-tuple-element.20), channel_id=1, source_target_pairs={{0,1},{1,0},{2,3},{3,2},{4,5},{5,4},{6,7},{7,6},{8,9},{9,8},{10,11... | collective-permute-start | bytes 3145736 | tf_op jit(solution)/shard_map/ppermute | solution.py:63
  24.3 5.2 %collective-permute-start.3 = (bf16[128,4096]{1,0:T(8,128)(2,1)S(1)}, bf16[128,4096]{1,0:T(8,128)(2,1)S(1)}, u32[]{:S(2)}, u32[]{:S(2)}) collective-permute-start(bf16[128,4096]{1,0:T(8,128)(2,1)S(1)} %get-tuple-element.21), channel_id=1, source_target_pairs={{0,1},{1,0},{2,3},{3,2},{4,5},{5,4},{6,7},{7,6},{8,9},{9,8},{10,11... | collective-permute-start | bytes 3145736 | tf_op jit(solution)/shard_map/ppermute | solution.py:63
  29.6 74.1 %copy-start = (bf16[256,4096]{1,0:T(8,128)(2,1)}, bf16[256,4096]{1,0:T(8,128)(2,1)S(1)}, u32[]{:S(2)}) copy-start(bf16[256,4096]{1,0:T(8,128)(2,1)S(1)} %pad_maximum_fusion.1) | copy-start | bytes 6291460
  57.0 2.7 %collective-permute-start.4 = (f32[2,1]{0,1:T(1,128)S(1)}, f32[2,1]{0,1:T(1,128)S(1)}, u32[]{:S(2)}, u32[]{:S(2)}) collective-permute-start(f32[2,1]{0,1:T(1,128)S(1)} %bitcast.50), channel_id=1, source_target_pairs={{0,1},{1,0},{2,3},{3,2},{4,5},{5,4},{6,7},{7,6},{8,9},{9,8},{10,11... | collective-permute-start | bytes 32 | tf_op jit(solution)/shard_map/ppermute | solution.py:63
  75.5 21.2 %copy-start.6 = (bf16[4096,256]{1,0:T(8,128)(2,1)S(1)}, bf16[4096,256]{1,0:T(8,128)(2,1)}, u32[]{:S(2)}) copy-start(bf16[4096,256]{1,0:T(8,128)(2,1)} %pad_maximum_fusion) | copy-start | bytes 6291460
  96.6 1.3 copy-start.3
  96.6 4.0 %copy-start.15 = (bf16[128]{0:T(256)(128)(2,1)S(1)}, bf16[128]{0:T(256)(128)(2,1)}, u32[]{:S(2)}) copy-start(bf16[128]{0:T(256)(128)(2,1)} %param.13) | copy-start | bytes 772
  98.0 3.7 %collective-permute-start.5 = (f32[128,256]{1,0:T(8,128)S(1)}, f32[128,256]{1,0:T(8,128)S(1)}, u32[]{:S(2)}, u32[]{:S(2)}) collective-permute-start(f32[128,256]{1,0:T(8,128)S(1)} %slice.17), channel_id=1, source_target_pairs={{0,1},{1,0},{2,3},{3,2},{4,5},{5,4},{6,7},{7,6},{8,9},{9,8},{10,11... | collective-permute-start | bytes 393224 | tf_op jit(solution)/shard_map/ppermute | solution.py:63
  102.0 1.5 collective-permute-start.6
  158.1 21.2 %all-to-all-start.7 = ((bf16[8,32,4096]{2,1,0:T(8,128)(2,1)}), bf16[8,32,4096]{2,1,0:T(8,128)(2,1)S(1)}, u32[]{:S(2)}, u32[]{:S(2)}) async-start(bf16[8,32,4096]{2,1,0:T(8,128)(2,1)} %broadcast_in_dim.62), calls=%async_computation.7 | async-start | bytes 4194304 | tf_op jit(solution)/shard_map/all_to_all | solution.py:81
  162.5 6.1 %collective-permute-start.7 = (bf16[256,4096]{1,0:T(8,128)(2,1)}, bf16[256,4096]{1,0:T(8,128)(2,1)}, u32[]{:S(2)}, u32[]{:S(2)}) collective-permute-start(bf16[256,4096]{1,0:T(8,128)(2,1)} %bitcast.44), channel_id=1, source_target_pairs={{0,1},{1,0},{2,3},{3,2},{4,5},{5,4},{6,7},{7,6},{8,9},{9,8},{10,11... | collective-permute-start | bytes 6291464 | tf_op jit(solution)/shard_map/ppermute | solution.py:63
  168.5 2.6 %copy-start.7 = (bf16[256,4096]{0,1:T(8,128)(2,1)S(1)}, bf16[256,4096]{0,1:T(8,128)(2,1)}, u32[]{:S(2)}) copy-start(bf16[256,4096]{0,1:T(8,128)(2,1)} %copy.15) | copy-start | bytes 6291460
  173.6 5.7 %collective-permute-start.8 = (bf16[2,4096]{1,0:T(2,128)(2,1)S(1)}, bf16[2,4096]{1,0:T(2,128)(2,1)S(1)}, u32[]{:S(2)}, u32[]{:S(2)}) collective-permute-start(bf16[2,4096]{1,0:T(2,128)(2,1)S(1)} %multiply_convert_fusion), channel_id=1, source_target_pairs={{0,0},{1,128},{2,2},{3,130},{4,4},{5,132},{6,6},{7,134},{8,8},{9,1... | collective-permute-start | bytes 49160 | tf_op jit(solution)/shard_map/ppermute | solution.py:63
  179.3 4.6 %copy-start.1 = (bf16[256,4096]{1,0:T(8,128)(2,1)S(1)}, bf16[256,4096]{1,0:T(8,128)(2,1)}, u32[]{:S(2)}) copy-start(bf16[256,4096]{1,0:T(8,128)(2,1)} %copy-done) | copy-start | bytes 6291460
  181.5 4.5 %collective-permute-start.9 = (f32[128,256]{1,0:T(8,128)S(1)}, f32[128,256]{1,0:T(8,128)S(1)}, u32[]{:S(2)}, u32[]{:S(2)}) collective-permute-start(f32[128,256]{1,0:T(8,128)S(1)} %fusion.18), channel_id=1, source_target_pairs={{0,1},{1,0},{2,3},{3,2},{4,5},{5,4},{6,7},{7,6},{8,9},{9,8},{10,11... | collective-permute-start | bytes 393224 | tf_op jit(solution)/shard_map/ppermute | solution.py:63
  184.4 5.7 %collective-permute-start.10 = (bf16[128,4096]{1,0:T(8,128)(2,1)S(1)}, bf16[128,4096]{1,0:T(8,128)(2,1)S(1)}, u32[]{:S(2)}, u32[]{:S(2)}) collective-permute-start(bf16[128,4096]{1,0:T(8,128)(2,1)S(1)} %fusion.5), channel_id=1, source_target_pairs={{0,1},{1,0},{2,3},{3,2},{4,5},{5,4},{6,7},{7,6},{8,9},{9,8},{10,11... | collective-permute-start | bytes 3145736 | tf_op jit(solution)/shard_map/ppermute | solution.py:63
  184.6 2.2 %copy-start.2 = (bf16[8192,256]{1,0:T(8,128)(2,1)S(1)}, bf16[8192,256]{1,0:T(8,128)(2,1)}, u32[]{:S(2)}) copy-start(bf16[8192,256]{1,0:T(8,128)(2,1)} %maximum_select_fusion) | copy-start | bytes 12582916
  185.1 2.4 %copy-start.5 = (bf16[8192,128]{1,0:T(8,128)(2,1)S(1)}, bf16[8192,128]{1,0:T(8,128)(2,1)}, u32[]{:S(2)}) copy-start(bf16[8192,128]{1,0:T(8,128)(2,1)} %param.12) | copy-start | bytes 6291460
